TPU v7x, 32 devices: a whole 2x2x4 slice. The times are simulated.
32 devices in a mesh: aux: 4 (over x, core), pair: 8 (over z, y).
Axes of the slice: x: 2, y: 2, z: 4, core: 2. Of those that a mesh axis runs over, the one named last changes fastest.
Arguments:
- chol_vv: bfloat16 [32, 896, 2304], P(None, 'pair', 'aux'), may hold values from -0.625 to 0.625
- chol_ov: bfloat16 [100, 896, 2304], P(None, 'pair', 'aux'), may hold values from -0.625 to 0.625
- t1_window: bfloat16 [100, 32], replicated, may hold values from -0.625 to 0.625
- amplitudes: bfloat16 [64, 896, 896], P(None, 'aux'), may hold values from -0.0068359375 to 0.0068359375
- assignment: int32 [8, 2], replicated, may hold values from 0 to 7
Outputs:
- residual: float32 [64, 128], P('aux', 'pair')
All inputs are finite; a program needn't handle non-finite values.
Results may differ from a plain program's by a relative error of at most 0.0049.
Values may be sent and summed in bfloat16 or wider, within the bound.
No kernel may reach another device: no remote copies, remote signals or barrier semaphores. Data moves between devices by JAX's collectives and lax.ppermute only.
A program may use at most 256 MiB of HBM per device.

v0:
```python
import jax
import jax.numpy as jnp
from jax import lax
from jax.sharding import PartitionSpec as P

BLK = 4


def picker(blocks, window):
    offsets = jnp.arange(2 * BLK, dtype=jnp.int32)
    chosen = jnp.where(offsets[None, :] < BLK, blocks[:, 0:1], blocks[:, 1:2])
    column = chosen * BLK + offsets[None, :] % BLK
    return (column[:, :, None] == jnp.arange(window, dtype=jnp.int32)[None, None, :]).astype(
        jnp.bfloat16
    )


def shards(chol_vv, chol_ov, t1_window, amplitudes, assignment):
    window, cols_dev, aux_dev = chol_vv.shape
    occupied = chol_ov.shape[0]
    groups = lax.axis_size("pair")
    shift = jnp.dot(
        t1_window.T,
        chol_ov.reshape(occupied, cols_dev * aux_dev),
        preferred_element_type=jnp.float32,
    )
    dressed = (chol_vv.astype(jnp.float32).reshape(window, cols_dev * aux_dev) - shift).astype(
        jnp.bfloat16
    )
    onehot = picker(assignment, window).reshape(groups * 2 * BLK, window)
    outgoing = jnp.dot(onehot, dressed, preferred_element_type=jnp.float32).astype(jnp.bfloat16)
    outgoing = outgoing.reshape(groups, 2 * BLK, cols_dev, aux_dev)
    incoming = lax.all_to_all(outgoing, "pair", split_axis=0, concat_axis=2, tiled=True)
    slab_vectors = incoming[0]
    first_block = slab_vectors[:BLK]
    second_block = slab_vectors[BLK:]
    first_all = lax.all_to_all(first_block, "aux", split_axis=1, concat_axis=2, tiled=True)
    tiles = jnp.einsum(
        "acp,bdp->cabd",
        first_all,
        lax.all_gather(second_block, "aux", axis=2, tiled=True),
        preferred_element_type=jnp.float32,
    ).astype(jnp.bfloat16)
    pairs_all = amplitudes.shape[0]
    partial_terms = jnp.einsum(
        "icd,cabd->iab", amplitudes, tiles, preferred_element_type=jnp.float32
    )
    partial_terms = partial_terms.reshape(pairs_all, BLK * BLK)
    summed = lax.psum(partial_terms, "aux")
    share_rows = pairs_all // lax.axis_size("aux")
    return lax.dynamic_slice_in_dim(summed, lax.axis_index("aux") * share_rows, share_rows, 0)


def solution(mesh):
    in_specs = (P(None, "pair", "aux"), P(None, "pair", "aux"), P(), P(None, "aux", None), P())
    out_specs = P("aux", "pair")
    return jax.shard_map(shards, mesh=mesh, in_specs=in_specs, out_specs=out_specs, check_vma=False)
```

profile of v0, /device:TPU:0, one launch (start us, length us, event | category | flops | bytes accessed | tf_op | source)
XLA Modules:
  0.0 502.1 jit_solution(16094479755060905764)
XLA Ops:
  6.5 0.0 copy-start
  6.5 0.0 all-gather.2.cloned.1.call-start
  6.5 0.8 slice_bitcast_fusion
  7.3 0.1 broadcast_in_dim.41
  7.4 0.1 broadcast_in_dim.42
  7.5 0.1 broadcast_in_dim.44
  7.5 0.1 broadcast_in_dim.45
  7.6 0.1 add.32
  7.7 0.1 broadcast_in_dim.39
  7.8 20.0 %reshape.92 = bf16[100,64512]{1,0:T(8,128)(2,1)} reshape(bf16[100,112,576]{2,1,0:T(8,128)(2,1)} %param.6) | data formatting | bytes 25804800 | tf_op jit(solution)/shard_map/reshape | solution.py:24
  27.7 7.9 %reshape.96 = f32[32,64512]{1,0:T(8,128)} reshape(bf16[32,112,576]{2,1,0:T(8,128)(2,1)} %param.5) | data formatting | bytes 12386304 | tf_op jit(solution)/shard_map/reshape | solution.py:27
  35.6 0.0 copy-done
  35.6 11.5 %convolution_convert_fusion = bf16[64,64512]{1,0:T(8,128)(2,1)} fusion(f32[32,64512]{1,0:T(8,128)} %reshape.96, bf16[100,32]{0,1:T(8,128)(2,1)S(1)} %copy-done, bf16[100,64512]{1,0:T(8,128)(2,1)} %reshape.92, s32[64]{0:T(128)S(1)} %multiply_add_fusion), kind=kOutput, calls=%fused_computation | convolution fusion | flops 685377536 | bytes 29424128 | tf_op jit(solution)/shard_map/dot_general | solution.py:31
  47.1 12.3 %reshape.93 = bf16[8,8,112,576]{3,2,1,0:T(8,128)(2,1)} reshape(bf16[64,64512]{1,0:T(8,128)(2,1)} %convolution_convert_fusion) | data formatting | bytes 16515072 | tf_op jit(solution)/shard_map/reshape | solution.py:32
  59.4 207.2 %all_to_all.33 = bf16[8,8,112,576]{3,2,1,0:T(8,128)(2,1)S(1)} all-to-all(bf16[8,8,112,576]{3,2,1,0:T(8,128)(2,1)} %reshape.93), channel_id=1, replica_groups=mesh['aux'=4,'pair'=8] {'pair'}, dimensions={0} | all-to-all | bytes 16515072 | tf_op jit(solution)/shard_map/all_to_all | solution.py:33
  266.6 4.3 fusion.10
  270.9 8.6 %copy.18 = bf16[1,4,8,112,576]{3,2,4,1,0:T(8,128)(2,1)} copy(bf16[1,4,8,112,576]{4,3,1,2,0:T(8,128)(2,1)} %get-tuple-element.5) | data formatting | bytes 8257536 | tf_op jit(solution)/shard_map/slice | solution.py:36
  279.5 8.7 %slice.21 = bf16[4,896,576]{1,2,0:T(8,128)(2,1)} reshape(bf16[1,4,8,112,576]{3,2,4,1,0:T(8,128)(2,1)} %copy.18) | data formatting | bytes 8257536 | tf_op jit(solution)/shard_map/slice | solution.py:36
  288.2 0.0 all-gather.2.cloned.1.call-update
  288.3 6.5 %copy.28 = bf16[1,4,8,112,576]{4,1,3,2,0:T(4,128)(2,1)} copy(bf16[1,4,8,112,576]{4,3,1,2,0:T(8,128)(2,1)} %get-tuple-element.6) | data formatting | bytes 8257536 | tf_op jit(solution)/shard_map/slice | solution.py:35
  294.8 5.3 %all-to-all-start.1 = ((bf16[4,896,576]{2,0,1:T(4,128)(2,1)}), bf16[4,896,576]{2,0,1:T(4,128)(2,1)}, u32[]{:S(2)}, u32[]{:S(2)}) async-start(bf16[4,896,576]{2,0,1:T(4,128)(2,1)} %bitcast.41), calls=%async_computation.1 | async-start | bytes 9175040 | tf_op jit(solution)/shard_map/all_to_all | solution.py:37
  300.1 101.7 %all-to-all-done.1 = bf16[4,896,576]{2,0,1:T(4,128)(2,1)} async-done(((bf16[4,896,576]{2,0,1:T(4,128)(2,1)}), bf16[4,896,576]{2,0,1:T(4,128)(2,1)}, u32[]{:S(2)}, u32[]{:S(2)}) %all-to-all-start.1) | async-done | bytes 4128800 | tf_op jit(solution)/shard_map/all_to_all | solution.py:37
  401.8 2.9 copy.21
  404.7 4.4 copy.22
  409.1 8.3 %reshape.98 = bf16[4,224,2304,1]{2,1,0,3:T(8,128)(2,1)} reshape(bf16[4,224,4,576]{3,2,1,0:T(4,128)(2,1)} %copy.22) | data formatting | bytes 8257536 | tf_op jit(solution)/shard_map/all_to_all | solution.py:37
  417.5 23.6 %all-gather.2.cloned.1.call-done = bf16[4,896,2304]{1,2,0:T(8,128)(2,1)} async-done(((bf16[4,896,576]{1,2,0:T(8,128)(2,1)}), bf16[4,896,2304]{1,2,0:T(8,128)(2,1)}) %all-gather.2.cloned.1.call-update) | async-done | bytes 16515088 | tf_op jit(solution)/shard_map/all_gather | solution.py:41
  441.0 19.9 %convert_bitcast_fusion = bf16[224,4,4,896]{3,0,1,2:T(8,128)(2,1)S(1)} fusion(bf16[4,224,2304,1]{2,1,0,3:T(8,128)(2,1)} %reshape.98, bf16[4,896,2304]{1,2,0:T(8,128)(2,1)} %all-gather.2.cloned.1.call-done), kind=kOutput, calls=%fused_computation.9 | convolution fusion | flops 14800715776 | bytes 27066368 | tf_op jit(solution)/shard_map/acp,bdp->cabd/dot_general | solution.py:38
  460.9 0.0 copy-start.1
  460.9 23.2 %fusion.1 = f32[4,4,64,1]{2,1,3,0:T(4,128)S(1)} fusion(bf16[64,224,896]{2,1,0:T(8,128)(2,1)} %param.8, bf16[224,4,4,896]{3,0,1,2:T(8,128)(2,1)S(1)} %convert_bitcast_fusion), kind=kOutput, calls=%fused_computation.3 | convolution fusion | flops 411041792 | bytes 32116736 | tf_op jit(solution)/shard_map/icd,cabd->iab/dot_general | solution.py:45
  484.1 0.1 copy.25
  484.2 10.4 %psum.7 = f32[64,16]{1,0:T(8,128)S(1)} all-reduce(f32[64,16]{1,0:T(8,128)S(1)} %copy.25), channel_id=1, replica_groups=mesh['aux'=4,'pair'=8] {'aux'}, use_global_device_ids=true, to_apply=%region_0.1 | all-reduce | flops 1024 | bytes 8192 | tf_op jit(solution)/shard_map/psum | solution.py:49
  494.6 0.6 constant_dynamic-slice_fusion
  495.2 0.0 copy-done.1
  (5 shorter events, 0.0 us)
Async XLA Ops:
  6.5 29.1 %copy-start = (bf16[100,32]{0,1:T(8,128)(2,1)S(1)}, bf16[100,32]{0,1:T(8,128)(2,1)}, u32[]{:S(2)}) copy-start(bf16[100,32]{0,1:T(8,128)(2,1)} %param.7) | copy-start | bytes 19204
  6.5 434.5 %all-gather.2.cloned.1.call-start = ((), (), s32[]{:S(2)}) async-start(), calls=%async_computation.2 | async-start | bytes 20643840 | tf_op jit(solution)/shard_map/all_gather | solution.py:41
  294.8 107.0 %all-to-all-start.1 = ((bf16[4,896,576]{2,0,1:T(4,128)(2,1)}), bf16[4,896,576]{2,0,1:T(4,128)(2,1)}, u32[]{:S(2)}, u32[]{:S(2)}) async-start(bf16[4,896,576]{2,0,1:T(4,128)(2,1)} %bitcast.41), calls=%async_computation.1 | async-start | bytes 9175040 | tf_op jit(solution)/shard_map/all_to_all | solution.py:37
  460.9 34.3 %copy-start.1 = (bf16[100,32]{0,1:T(8,128)(2,1)S(1)}, bf16[100,32]{0,1:T(8,128)(2,1)}, u32[]{:S(2)}) copy-start(bf16[100,32]{0,1:T(8,128)(2,1)} %param.7) | copy-start | bytes 19204
Sparse Core Ops, SparseCore 0:
  288.4 152.5 all-gather.1
where the time goes:
time: 504 us; the launch traced here: 502 us
  blocking collectives  218 us (43%)
  waiting for transfers between devices  125 us (25%)
  local copies, waits for them, and re-layouts  85.8 us (17%)
  matrix products  54.6 us (11%)
  between operations  13.5 us (3%)
  starting transfers between devices  5.3 us (1%)
    all_to_all x1, blocking collectives, shards(): lax.all_to_all(outgoing, 'pair', split_axis=0, concat_axis=2, tiled=True)  207 us
    all_to_all x1, waiting for transfers between devices, shards(): lax.all_to_all(first_block, 'aux', split_axis=1, concat_axis=2, tiled=True)  102 us
    all_gather x1, waiting for transfers between devices, shards(): lax.all_gather(second_block, 'aux', axis=2, tiled=True)  23.6 us
    dot_general x1, matrix products, shards(): jnp.einsum('icd,cabd->iab', amplitudes, tiles, preferred_element_type=jnp...  23.2 us
    slice x3, local copies, waits for them, and re-layouts, shards(): second_block = slab_vectors[BLK:]  21.6 us
    reshape x1, local copies, waits for them, and re-layouts, shards(): chol_ov.reshape(occupied, cols_dev * aux_dev)  20 us
    dot_general x1, matrix products, shards(): jnp.einsum('acp,bdp->cabd', first_all, lax.all_gather(second_block, 'aux'...  19.9 us
    all_to_all x3, local copies, waits for them, and re-layouts, shards(): lax.all_to_all(first_block, 'aux', split_axis=1, concat_axis=2, tiled=True)  15.6 us
  transfers between devices with their start and end apart: 2, of which 2 were waited for; matrix products, arithmetic and copies ran while one was open for 4% of the time, Pallas kernels for 0%

commit v1 on v0

v1 whole, which is shorter than its diff:
```python
import functools

import jax
import jax.numpy as jnp
from jax import lax
from jax.experimental import pallas as pl
from jax.experimental.pallas import tpu as pltpu
from jax.sharding import PartitionSpec as P

BLK = 4
QUAD = 4
ROWS = 16
LANES = 128
CORES = 2
NT = (((1,), (1,)), ((), ()))
NN = (((1,), (0,)), ((), ()))


def round_up(value, unit):
    return (value + unit - 1) // unit * unit


class Plan:
    def __init__(self, window, occupied, cols, aux_dev, n_aux, n_pair, pairs_all):
        self.window, self.occupied, self.cols, self.aux_dev = window, occupied, cols, aux_dev
        self.n_aux, self.n_pair, self.ij = n_aux, n_pair, pairs_all
        self.xs = n_aux // CORES
        self.js = n_pair // CORES
        self.cpad = round_up(cols, ROWS)
        chunk = aux_dev // self.js
        self.main = chunk // LANES * LANES
        self.tail = chunk - self.main
        self.slot = 1
        while self.slot < self.tail:
            self.slot *= 2
        self.per_row = LANES // self.slot
        self.nm = self.main // LANES
        self.nt = window // self.per_row
        self.planes = self.nm * window + self.nt
        self.per = n_pair // n_aux
        self.c = self.per * self.cpad
        self.d = n_pair * self.cpad
        self.k = self.xs * LANES
        self.groups = n_pair
        self.blocks = window // BLK
        self.gf = self.groups * BLK
        self.tail_from = self.js * self.main
        self.tail_width = round_up(self.js * self.tail, LANES)


def dress_kernel(p, z_ref, a_ref, ov_ref, vv_ref, *refs):
    outs, (dressed, packed) = refs[: p.js], refs[p.js :]
    w = p.window

    @pl.when(pl.program_id(0) == 0)
    def _():
        dressed[...] = jnp.zeros_like(dressed)

    shift = lax.dot_general(
        a_ref[...],
        ov_ref[...].reshape(p.occupied * ROWS, p.aux_dev),
        NN,
        preferred_element_type=jnp.float32,
    )
    vv = vv_ref[...].astype(jnp.float32)
    dressed[:, :, : p.aux_dev] = vv - shift.reshape(w, ROWS, p.aux_dev)
    lane = lax.broadcasted_iota(jnp.int32, (p.nt, ROWS, LANES), 2)
    for j in range(p.js):
        for m in range(p.nm):
            low = j * p.main + m * LANES
            packed[j, m * w : (m + 1) * w] = dressed[:, :, low : low + LANES].astype(jnp.bfloat16)
        rest = jnp.zeros((p.nt, ROWS, LANES), jnp.float32)
        source = dressed[:, :, p.tail_from : p.tail_from + p.tail_width]
        source = source.reshape(p.nt, p.per_row, ROWS, p.tail_width)
        for s in range(p.per_row):
            turn = (s * p.slot - j * p.tail) % p.tail_width
            moved = pltpu.roll(source[:, s].reshape(p.nt * ROWS, p.tail_width), turn, 1)
            moved = moved[:, :LANES].reshape(p.nt, ROWS, LANES)
            here = (lane >= s * p.slot) & (lane < s * p.slot + p.tail)
            rest = jnp.where(here, moved, rest)
        packed[j, p.nm * w :] = rest.astype(jnp.bfloat16)
    z = z_ref[0]
    for o, out in enumerate(outs):
        out[...] = packed[lax.rem(z + o, p.js)]


def dress(p, z, chol_vv, chol_ov, t1_window):
    spread = jnp.einsum(
        "kw,cd->wckd", t1_window, jnp.eye(ROWS, dtype=jnp.bfloat16)
    ).reshape(p.window * ROWS, p.occupied * ROWS)
    message = jax.ShapeDtypeStruct((p.planes, p.cpad, LANES), jnp.bfloat16)
    return pl.pallas_call(
        functools.partial(dress_kernel, p),
        out_shape=[message] * p.js,
        grid_spec=pltpu.PrefetchScalarGridSpec(
            num_scalar_prefetch=1,
            grid=(p.cpad // ROWS,),
            in_specs=[
                pl.BlockSpec((p.window * ROWS, p.occupied * ROWS), lambda i, z: (0, 0)),
                pl.BlockSpec((p.occupied, ROWS, p.aux_dev), lambda i, z: (0, i, 0)),
                pl.BlockSpec((p.window, ROWS, p.aux_dev), lambda i, z: (0, i, 0)),
            ],
            out_specs=[pl.BlockSpec((p.planes, ROWS, LANES), lambda i, z: (0, i, 0))] * p.js,
            scratch_shapes=[
                pltpu.VMEM((p.window, ROWS, p.tail_from + p.tail_width), jnp.float32),
                pltpu.VMEM((p.js, p.planes, ROWS, LANES), jnp.bfloat16),
            ],
        ),
        compiler_params=pltpu.CompilerParams(vmem_limit_bytes=48 * 2**20),
        cost_estimate=pl.CostEstimate(
            flops=2 * p.window * p.occupied * p.cpad * p.aux_dev * ROWS,
            bytes_accessed=2 * (p.occupied + 2 * p.window) * p.cpad * p.aux_dev,
            transcendentals=0,
        ),
        name="dress",
    )(z, spread, chol_ov, chol_vv)


def ladder_kernel(p, parts, group, place_ref, blocks_ref, *refs):
    count = 2 * p.js * p.xs
    pieces, (amps, out), scratch = refs[:count], refs[count : count + 2], refs[count + 2 :]
    vectors, left_main, left_tail, spread_tail, tiles, held, total, piece_sem, amp_sem = scratch
    w, z, core, chunk = p.window, place_ref[0], place_ref[1], place_ref[2]
    quads = p.c // QUAD
    here = quads // parts
    rows = here * ROWS
    steps = here // group
    wide = group * QUAD * p.ij

    def fetch(step, slot):
        return pltpu.make_async_copy(
            amps.at[pl.ds(pl.multiple_of(step * wide, wide), wide)], held.at[slot], amp_sem.at[slot]
        )

    copies = []
    for o in range(p.js):
        for r in range(p.xs):
            for other in range(CORES):
                parity = core if other == 0 else 1 - core
                origin = CORES * lax.rem(z - o + p.js, p.js) + parity
                row = pl.multiple_of(origin * p.cpad, ROWS)
                copies.append(
                    pltpu.make_async_copy(
                        pieces[(o * p.xs + r) * CORES + other],
                        vectors.at[:, pl.ds(row, p.cpad), r * LANES : (r + 1) * LANES],
                        piece_sem.at[(o * p.xs + r) * CORES + other],
                    )
                )
    for copy in copies:
        copy.start()
    fetch(0, 0).start()
    for copy in copies:
        copy.wait()

    mixed = QUAD * ROWS
    to = lax.broadcasted_iota(jnp.int32, (mixed, mixed), 0)
    frm = lax.broadcasted_iota(jnp.int32, (mixed, mixed), 1)
    weave = ((to % BLK) * ROWS + to // BLK == frm).astype(jnp.float32).astype(jnp.bfloat16)
    lane_in = lax.broadcasted_iota(jnp.int32, (LANES, LANES), 0)
    lane_out = lax.broadcasted_iota(jnp.int32, (LANES, LANES), 1)
    same = lane_in % p.slot == lane_out % p.slot
    first = pl.multiple_of(chunk * p.c, ROWS)

    def woven(stack):
        return lax.dot_general(weave, stack, NN, preferred_element_type=jnp.float32).astype(
            jnp.bfloat16
        )

    @pl.loop(0, p.blocks)
    def _(b):
        for e in range(BLK):
            index = b * BLK + e
            plane = p.nm * w + index // p.per_row
            copier = (same & (lane_in // p.slot == index % p.per_row)).astype(jnp.float32)
            copier = copier.astype(jnp.bfloat16)
            for r in range(p.xs):
                span = slice(r * LANES, (r + 1) * LANES)
                spread_tail[e, :, span] = lax.dot_general(
                    vectors[plane, pl.ds(first, p.c), span],
                    copier,
                    NN,
                    preferred_element_type=jnp.float32,
                ).astype(jnp.bfloat16)
        for i in range(p.c // ROWS):
            span = slice(i * mixed, (i + 1) * mixed)
            tail = [spread_tail[e, i * ROWS : (i + 1) * ROWS, :] for e in range(BLK)]
            left_tail[b, span] = woven(jnp.concatenate(tail, axis=0))
            for m in range(p.nm):
                at = pl.ds(pl.multiple_of(first + i * ROWS, ROWS), ROWS)
                stack = [vectors[m * w + b * BLK + e, at] for e in range(BLK)]
                left_main[m, b, span] = woven(jnp.concatenate(stack, axis=0))

    total[...] = jnp.zeros_like(total)
    slot_of = lax.broadcasted_iota(jnp.int32, (1, p.k), 1) % LANES // p.slot

    @pl.loop(0, parts)
    def _(part):
        part_rows = pl.ds(pl.multiple_of(part * rows, rows), rows)

        @pl.loop(0, p.gf)
        def _(gf):
            left = blocks_ref[gf // BLK, 0]
            index = blocks_ref[gf // BLK, 1] * BLK + gf % BLK
            only = (slot_of == index % p.per_row).astype(jnp.float32).astype(jnp.bfloat16)
            lhs = [left_tail[left, part_rows] * only]
            planes = [p.nm * w + index // p.per_row]
            for m in range(p.nm):
                lhs.append(left_main[m, left, part_rows])
                planes.append(m * w + index)
            lhs = jnp.concatenate(lhs, axis=1)
            for low in range(0, p.d, 256):
                span = slice(low, min(low + 256, p.d))
                rhs = jnp.concatenate([vectors[plane, span] for plane in planes], axis=1)
                block = lax.dot_general(lhs, rhs, NT, preferred_element_type=jnp.float32)
                block = block.astype(jnp.bfloat16).reshape(here, ROWS, span.stop - low)
                tiles[:, gf, :, span] = block

        @pl.loop(0, steps)
        def _(step):
            at = part * steps + step
            slot = lax.rem(at, 2)

            @pl.when(at + 1 < parts * steps)
            def _():
                fetch(at + 1, 1 - slot).start()

            fetch(at, slot).wait()
            width = QUAD * p.ij
            for n in range(group):
                total[...] += lax.dot_general(
                    tiles[step * group + n].reshape(p.gf * ROWS, p.d),
                    held[slot, n * width : (n + 1) * width],
                    NT,
                    preferred_element_type=jnp.float32,
                )

    width = QUAD * p.ij
    row = lax.broadcasted_iota(jnp.int32, (p.gf * ROWS, width), 0) % ROWS // BLK
    col = lax.broadcasted_iota(jnp.int32, (p.gf * ROWS, width), 1) // p.ij
    kept = jnp.where(row == col, total[...], 0.0)
    folded = kept[:, :LANES]
    for low in range(LANES, width, LANES):
        folded += kept[:, low : low + LANES]
    shift = LANES
    while shift > p.ij:
        shift //= 2
        folded += pltpu.roll(folded, shift, 1)
    folded = folded.reshape(p.gf, 2, 8, LANES).sum(axis=1)
    out[...] = folded[:, :4] + folded[:, 4:]


def ladder(p, place, blocks, pieces, amps):
    parts, group = 2, 1
    quads = p.c // QUAD
    for wanted in (4, 2):
        if quads // parts % wanted == 0:
            group = wanted
            break
    width = QUAD * p.ij
    return pl.pallas_call(
        functools.partial(ladder_kernel, p, parts, group),
        out_shape=jax.ShapeDtypeStruct((p.gf, BLK, LANES), jnp.float32),
        in_specs=[pl.BlockSpec(memory_space=pltpu.SMEM)] * 2
        + [pl.BlockSpec(memory_space=pl.ANY)] * (len(pieces) + 1),
        out_specs=pl.BlockSpec(memory_space=pltpu.VMEM),
        scratch_shapes=[
            pltpu.VMEM((p.planes, p.d, p.k), jnp.bfloat16),
            pltpu.VMEM((max(p.nm, 1), p.blocks, BLK * p.c if p.nm else ROWS, p.k), jnp.bfloat16),
            pltpu.VMEM((p.blocks, BLK * p.c, p.k), jnp.bfloat16),
            pltpu.VMEM((BLK, p.c, p.k), jnp.bfloat16),
            pltpu.VMEM((quads // parts, p.gf, ROWS, p.d), jnp.bfloat16),
            pltpu.VMEM((2, group * width, p.d), jnp.bfloat16),
            pltpu.VMEM((p.gf * ROWS, width), jnp.float32),
            pltpu.SemaphoreType.DMA((len(pieces),)),
            pltpu.SemaphoreType.DMA((2,)),
        ],
        compiler_params=pltpu.CompilerParams(vmem_limit_bytes=63 * 2**20),
        cost_estimate=pl.CostEstimate(
            flops=2 * p.gf * BLK * p.c * p.d * p.k,
            bytes_accessed=2 * (len(pieces) * p.planes * p.cpad * LANES + p.c * p.ij * p.d),
            transcendentals=0,
        ),
        name="ladder",
    )(place, blocks, *pieces, amps)


def pad_columns(array, axis, cols, cpad):
    if cols == cpad:
        return array
    shape = array.shape
    split = array.reshape(shape[:axis] + (shape[axis] // cols, cols) + shape[axis + 1 :])
    widths = [(0, 0)] * split.ndim
    widths[axis + 1] = (0, cpad - cols)
    split = jnp.pad(split, widths)
    return split.reshape(shape[:axis] + (shape[axis] // cols * cpad,) + shape[axis + 1 :])


def shards(chol_vv, chol_ov, t1_window, amplitudes, assignment):
    window, cols, aux_dev = chol_vv.shape
    n_aux, n_pair = lax.axis_size("aux"), lax.axis_size("pair")
    p = Plan(window, chol_ov.shape[0], cols, aux_dev, n_aux, n_pair, amplitudes.shape[0])
    me_aux, me_pair = lax.axis_index("aux"), lax.axis_index("pair")
    z = me_pair // CORES
    place = jnp.stack([z, me_aux % CORES, me_aux]).astype(jnp.int32)

    chol_vv = pad_columns(chol_vv, 1, cols, p.cpad)
    chol_ov = pad_columns(chol_ov, 1, cols, p.cpad)
    messages = dress(p, place, chol_vv, chol_ov, t1_window)

    def permute(array, target):
        pairs = []
        for a in range(n_aux):
            for q in range(n_pair):
                to_a, to_q = target(a, q)
                pairs.append((a * n_pair + q, to_a * n_pair + to_q))
        return lax.ppermute(array, ("aux", "pair"), pairs)

    pieces = []
    for o in range(p.js):
        own = permute(
            messages[o],
            lambda a, q: (
                a // CORES * CORES + q % CORES,
                CORES * ((q // CORES + o) % p.js) + a % CORES,
            ),
        )
        for r in range(p.xs):
            turned = own
            if r:
                turned = permute(
                    own, lambda a, q: (CORES * ((a // CORES + r) % p.xs) + a % CORES, q)
                )
            pieces += [turned, permute(turned, lambda a, q: (a ^ 1, q))]

    amps = pad_columns(pad_columns(amplitudes, 1, cols, p.cpad), 2, cols, p.cpad)
    amps = jnp.transpose(amps, (1, 0, 2)).reshape(p.c * p.ij, p.d)

    partial_terms = ladder(p, place, assignment, pieces, amps)
    share = p.ij // n_aux
    terms = partial_terms[:, :, : p.ij].reshape(n_pair, BLK, BLK, n_aux, share)
    terms = terms.transpose(3, 0, 4, 2, 1).reshape(n_aux * n_pair, share, BLK * BLK)
    terms = lax.all_to_all(terms, ("aux", "pair"), split_axis=0, concat_axis=0, tiled=True)
    return terms.sum(axis=0)


def solution(mesh):
    in_specs = (P(None, "pair", "aux"), P(None, "pair", "aux"), P(), P(None, "aux", None), P())
    out_specs = P("aux", "pair")
    return jax.shard_map(shards, mesh=mesh, in_specs=in_specs, out_specs=out_specs, check_vma=False)
```

time: 504 us -> 334 us (0.66)
  blocking collectives: 218 us -> 33.8 us
  Pallas kernels: 0 us -> 91.5 us
  matrix products: 54.6 us -> 0 us
  local copies, waits for them, and re-layouts: 85.8 us -> 58.2 us
  starting transfers between devices: 5.3 us -> 19.2 us
  between operations: 13.5 us -> 0.17 us
  other arithmetic: 0.01 us -> 6.49 us
    all_to_all x1, blocking collectives: 207 us -> 33.8 us  [shards(): lax.all_to_all(terms, ('aux', 'pair'), split_axis=0, concat_axis=0, tiled...]
    ppermute x0 -> x16, waiting for transfers between devices: none -> 123 us  [permute(): return lax.ppermute(array, ('aux', 'pair'), pairs)]
    all_to_all x1 -> x0, waiting for transfers between devices: 102 us -> none  [shards(): lax.all_to_all(first_block, 'aux', split_axis=1, concat_axis=2, tiled=True)]
    pallas_call x0 -> x2, Pallas kernels: none -> 91.5 us  [the longest x1 75.7 us: ladder(): pl.pallas_call(functools.partial(ladder_kernel, p, parts, group), out_sha...]
    dot_general x3 -> x0, matrix products: 54.6 us -> none  [the longest x1 23.2 us: shards(): jnp.einsum('icd,cabd->iab', amplitudes, tiles, preferred_element_type=jnp...]
    transpose x0 -> x1, local copies, waits for them, and re-layouts: none -> 29.7 us  [shards(): amps = jnp.transpose(amps, (1, 0, 2)).reshape(p.c * p.ij, p.d)]
    slice x4 -> x0, local copies, waits for them, and re-layouts: 28.2 us -> none  [the longest x3 21.6 us: shards(): second_block = slab_vectors[BLK:]]
    all_gather x1 -> x0, waiting for transfers between devices: 23.6 us -> none  [shards(): lax.all_gather(second_block, 'aux', axis=2, tiled=True)]
  transfers between devices with their start and end apart: 2 -> 16, of which waited for: 2 -> 5; matrix products, arithmetic and copies ran while one was open for 4% -> 9% of each run, Pallas kernels for 0% -> 0%
where the time goes in v1:
time: 334 us; the launch traced here: 333 us
  waiting for transfers between devices  123 us (37%)
  Pallas kernels  91.5 us (27%)
  local copies, waits for them, and re-layouts  58.2 us (17%)
  blocking collectives  33.8 us (10%)
  starting transfers between devices  19.2 us (6%)
  other arithmetic  6.49 us (2%)
    ppermute x16, waiting for transfers between devices, permute(): return lax.ppermute(array, ('aux', 'pair'), pairs)  123 us
    pallas_call x1, Pallas kernels, ladder(): pl.pallas_call(functools.partial(ladder_kernel, p, parts, group), out_sha...  75.7 us
    all_to_all x1, blocking collectives, shards(): lax.all_to_all(terms, ('aux', 'pair'), split_axis=0, concat_axis=0, tiled...  33.8 us
    transpose x1, local copies, waits for them, and re-layouts, shards(): amps = jnp.transpose(amps, (1, 0, 2)).reshape(p.c * p.ij, p.d)  29.7 us
    reshape x2, local copies, waits for them, and re-layouts, dress(): spread = jnp.einsum('kw,cd->wckd', t1_window, jnp.eye(ROWS, dtype=jnp.bfl...  23.3 us
    ppermute x16, starting transfers between devices, permute(): return lax.ppermute(array, ('aux', 'pair'), pairs)  19.2 us
    pallas_call x1, Pallas kernels, dress(): pl.pallas_call(functools.partial(dress_kernel, p), out_shape=[message] *...  15.8 us
  transfers between devices with their start and end apart: 16, of which 5 were waited for; matrix products, arithmetic and copies ran while one was open for 9% of the time, Pallas kernels for 0%

profile of v1, /device:TPU:0, one launch (start us, length us, event | category | flops | bytes accessed | tf_op | source)
XLA Modules:
  0.0 332.8 jit_solution(403562932468368732)
XLA Ops:
  0.0 0.8 copy.13
  0.8 5.6 %multiply_bitcast_fusion = bf16[32,16,100,16]{1,0,3,2:T(8,128)(2,1)} fusion(bf16[100,32]{1,0:T(8,128)(2,1)S(1)} %copy.13, bf16[16,16]{0,1:T(8,128)(2,1)S(1)} %fusion), kind=kLoop, calls=%fused_computation | loop fusion | flops 819200 | bytes 1645312 | tf_op jit(solution)/shard_map/kw,cd->wckd/transpose | solution.py:88
  6.5 21.9 %reshape.12 = bf16[512,1600]{0,1:T(8,128)(2,1)S(1)} reshape(bf16[32,16,100,16]{1,0,3,2:T(8,128)(2,1)} %multiply_bitcast_fusion) | data formatting | bytes 3276800 | tf_op jit(solution)/shard_map/reshape | solution.py:90
  28.4 1.4 copy.14.a_ref
  29.8 0.1 pad_add_fusion.z_ref.place_ref
  29.9 15.8 %dress.1 = (bf16[36,112,128]{2,1,0:T(8,128)(2,1)S(1)}, bf16[36,112,128]{2,1,0:T(8,128)(2,1)S(1)}, bf16[36,112,128]{2,1,0:T(8,128)(2,1)S(1)}, bf16[36,112,128]{2,1,0:T(8,128)(2,1)S(1)}) custom-call(s32[3]{0:T(128)S(1)} %pad_add_fusion.z_ref.place_ref, bf16[512,1600]{1,0:T(8,128)(2,1)S(1)} %copy.14.a_ref, bf16[100,112,576]{2,1,0:T(8,128)(2,1)} %ov_ref.1, ...), custom_call_target="tpu_custom_call" | custom-call | flops 6606028800 | bytes 21159936 | tf_op jit(solution)/shard_map/dress/pallas_call | solution.py:92
  45.7 4.5 %collective-permute-start.8 = (bf16[36,112,128]{2,1,0:T(8,128)(2,1)S(1)}, bf16[36,112,128]{2,1,0:T(8,128)(2,1)S(1)}, u32[]{:S(2)}, u32[]{:S(2)}) collective-permute-start(bf16[36,112,128]{2,1,0:T(8,128)(2,1)S(1)} %get-tuple-element.11), channel_id=1, source_target_pairs={{0,4},{1,12},{2,6},{3,14},{4,0},{5,8},{6,2},{7,10},{8,5},{9,13},{1... | collective-permute-start | bytes 3096584 | tf_op jit(solution)/shard_map/ppermute | solution.py:316
  50.2 1.2 collective-permute-start.12
  51.4 0.7 collective-permute-start
  52.1 0.9 collective-permute-start.4
  53.0 42.7 %collective-permute-done.8.refs_8_ = bf16[36,112,128]{2,1,0:T(8,128)(2,1)S(1)} collective-permute-done((bf16[36,112,128]{2,1,0:T(8,128)(2,1)S(1)}, bf16[36,112,128]{2,1,0:T(8,128)(2,1)S(1)}, u32[]{:S(2)}, u32[]{:S(2)}) %collective-permute-start.8) | collective-permute-done | bytes 1032224 | tf_op jit(solution)/shard_map/ppermute | solution.py:316
  95.7 1.6 collective-permute-start.10
  97.3 0.0 collective-permute-done.12.refs_12_
  97.3 0.8 collective-permute-start.14
  98.0 0.0 collective-permute-done.refs_0_
  98.0 1.3 collective-permute-start.2
  99.3 19.8 %collective-permute-done.4.refs_4_ = bf16[36,112,128]{2,1,0:T(8,128)(2,1)S(1)} collective-permute-done((bf16[36,112,128]{2,1,0:T(8,128)(2,1)S(1)}, bf16[36,112,128]{2,1,0:T(8,128)(2,1)S(1)}, u32[]{:S(2)}, u32[]{:S(2)}) %collective-permute-start.4) | collective-permute-done | bytes 1032224 | tf_op jit(solution)/shard_map/ppermute | solution.py:316
  119.1 1.5 collective-permute-start.6
  120.6 0.0 collective-permute-start.1
  120.6 1.7 collective-permute-start.13
  122.4 20.3 %collective-permute-done.14.refs_14_ = bf16[36,112,128]{2,1,0:T(8,128)(2,1)S(1)} collective-permute-done((bf16[36,112,128]{2,1,0:T(8,128)(2,1)S(1)}, bf16[36,112,128]{2,1,0:T(8,128)(2,1)S(1)}, u32[]{:S(2)}, u32[]{:S(2)}) %collective-permute-start.14) | collective-permute-done | bytes 1032224 | tf_op jit(solution)/shard_map/ppermute | solution.py:316
  142.6 1.9 collective-permute-start.5
  144.6 20.3 %collective-permute-done.2.refs_2_ = bf16[36,112,128]{2,1,0:T(8,128)(2,1)} collective-permute-done((bf16[36,112,128]{2,1,0:T(8,128)(2,1)S(1)}, bf16[36,112,128]{2,1,0:T(8,128)(2,1)}, u32[]{:S(2)}, u32[]{:S(2)}) %collective-permute-start.2) | collective-permute-done | bytes 1032224 | tf_op jit(solution)/shard_map/ppermute | solution.py:316
  164.9 1.8 collective-permute-start.9
  166.7 20.3 %collective-permute-done.6.refs_6_ = bf16[36,112,128]{2,1,0:T(8,128)(2,1)} collective-permute-done((bf16[36,112,128]{2,1,0:T(8,128)(2,1)S(1)}, bf16[36,112,128]{2,1,0:T(8,128)(2,1)}, u32[]{:S(2)}, u32[]{:S(2)}) %collective-permute-start.6) | collective-permute-done | bytes 1032224 | tf_op jit(solution)/shard_map/ppermute | solution.py:316
  187.0 0.7 collective-permute-start.11
  187.7 0.1 collective-permute-start.15
  187.7 0.4 collective-permute-start.3
  188.2 0.0 collective-permute-done.5.refs_5_
  188.2 0.1 collective-permute-start.7
  188.3 0.3 copy-done.8
  188.6 0.4 copy-done.9
  189.0 0.3 copy-done.10
  189.3 29.7 %copy.15 = bf16[224,64,896]{2,1,0:T(8,128)(2,1)} copy(bf16[224,64,896]{2,0,1:T(8,128)(2,1)} %bitcast.20) | data formatting | bytes 51380224 | tf_op jit(solution)/shard_map/transpose | solution.py:336
  219.0 0.7 copy.16.blocks_ref
  219.6 0.0 collective-permute-done.15.refs_15_
  219.6 0.0 collective-permute-done.3.refs_3_
  219.7 0.0 collective-permute-done.7.refs_7_
  219.7 75.7 %ladder.1 = f32[32,4,128]{2,1,0:T(4,128)} custom-call(s32[3]{0:T(128)} %copy-done, s32[8,2]{1,0:T(8,128)} %copy.16.blocks_ref, bf16[36,112,128]{2,1,0:T(8,128)(2,1)} %copy-done.4, bf16[36,112,128]{2,1,0:T(8,128)(2,1)} %copy-done.8, bf16[36,112,128]{2,1,0:T(8,128)(2,1)} %collective-permute-done.2.refs_2_, ...), custom_call_target="tpu_custom_call" | custom-call | flops 13153337344 | bytes 42205184 | tf_op jit(solution)/shard_map/ladder/pallas_call | solution.py:260
  295.4 1.0 reshape.14
  296.4 0.2 copy.17
  296.5 0.2 copy.23
  296.7 0.1 reshape.16
  296.9 33.8 %all_to_all.5 = f32[32,1,256]{2,1,0:T(1,128)S(1)} all-to-all(f32[32,1,256]{2,1,0:T(1,128)S(1)} %reshape.16), channel_id=1, replica_groups=mesh['aux'=4,'pair'=8] {'aux','pair'}, dimensions={0} | all-to-all | bytes 65536 | tf_op jit(solution)/shard_map/all_to_all | solution.py:342
  330.7 0.5 broadcast.4
  331.2 0.7 reduce
  331.9 0.1 reshape.17
  332.1 0.7 copy.20
  (26 shorter events, 0.1 us)
Async XLA Ops:
  29.9 189.1 %copy-start = (s32[3]{0:T(128)}, s32[3]{0:T(128)S(1)}, u32[]{:S(2)}) copy-start(s32[3]{0:T(128)S(1)} %pad_add_fusion.z_ref.place_ref) | copy-start | bytes 40
  45.7 50.0 %collective-permute-start.8 = (bf16[36,112,128]{2,1,0:T(8,128)(2,1)S(1)}, bf16[36,112,128]{2,1,0:T(8,128)(2,1)S(1)}, u32[]{:S(2)}, u32[]{:S(2)}) collective-permute-start(bf16[36,112,128]{2,1,0:T(8,128)(2,1)S(1)} %get-tuple-element.11), channel_id=1, source_target_pairs={{0,4},{1,12},{2,6},{3,14},{4,0},{5,8},{6,2},{7,10},{8,5},{9,13},{1... | collective-permute-start | bytes 3096584 | tf_op jit(solution)/shard_map/ppermute | solution.py:316
  50.2 47.1 %collective-permute-start.12 = (bf16[36,112,128]{2,1,0:T(8,128)(2,1)S(1)}, bf16[36,112,128]{2,1,0:T(8,128)(2,1)S(1)}, u32[]{:S(2)}, u32[]{:S(2)}) collective-permute-start(bf16[36,112,128]{2,1,0:T(8,128)(2,1)S(1)} %get-tuple-element.12), channel_id=1, source_target_pairs={{0,6},{1,14},{2,0},{3,8},{4,2},{5,10},{6,4},{7,12},{8,7},{9,15},{1... | collective-permute-start | bytes 3096584 | tf_op jit(solution)/shard_map/ppermute | solution.py:316
  51.4 46.7 %collective-permute-start = (bf16[36,112,128]{2,1,0:T(8,128)(2,1)S(1)}, bf16[36,112,128]{2,1,0:T(8,128)(2,1)S(1)}, u32[]{:S(2)}, u32[]{:S(2)}) collective-permute-start(bf16[36,112,128]{2,1,0:T(8,128)(2,1)S(1)} %get-tuple-element.9), channel_id=1, source_target_pairs={{0,0},{1,8},{2,2},{3,10},{4,4},{5,12},{6,6},{7,14},{8,1},{9,9},{10... | collective-permute-start | bytes 3096584 | tf_op jit(solution)/shard_map/ppermute | solution.py:316
  52.1 67.0 %collective-permute-start.4 = (bf16[36,112,128]{2,1,0:T(8,128)(2,1)S(1)}, bf16[36,112,128]{2,1,0:T(8,128)(2,1)S(1)}, u32[]{:S(2)}, u32[]{:S(2)}) collective-permute-start(bf16[36,112,128]{2,1,0:T(8,128)(2,1)S(1)} %get-tuple-element.10), channel_id=1, source_target_pairs={{0,2},{1,10},{2,4},{3,12},{4,6},{5,14},{6,0},{7,8},{8,3},{9,11},{1... | collective-permute-start | bytes 3096584 | tf_op jit(solution)/shard_map/ppermute | solution.py:316
  95.7 123.2 %copy-start.2 = (bf16[36,112,128]{2,1,0:T(8,128)(2,1)}, bf16[36,112,128]{2,1,0:T(8,128)(2,1)S(1)}, u32[]{:S(2)}) copy-start(bf16[36,112,128]{2,1,0:T(8,128)(2,1)S(1)} %collective-permute-done.8.refs_8_) | copy-start | bytes 3096580
  95.7 24.9 %collective-permute-start.10 = (bf16[36,112,128]{2,1,0:T(8,128)(2,1)S(1)}, bf16[36,112,128]{2,1,0:T(8,128)(2,1)S(1)}, u32[]{:S(2)}, u32[]{:S(2)}) collective-permute-start(bf16[36,112,128]{2,1,0:T(8,128)(2,1)S(1)} %collective-permute-done.8.refs_8_), channel_id=1, source_target_pairs={{0,16},{1,17},{2,18},{3,19},{4,20},{5,21},{6,22},{7,23},{8,24},{9,... | collective-permute-start | bytes 3096584 | tf_op jit(solution)/shard_map/ppermute | solution.py:316
  97.3 91.0 %copy-start.3 = (bf16[36,112,128]{2,1,0:T(8,128)(2,1)}, bf16[36,112,128]{2,1,0:T(8,128)(2,1)S(1)}, u32[]{:S(2)}) copy-start(bf16[36,112,128]{2,1,0:T(8,128)(2,1)S(1)} %collective-permute-done.12.refs_12_) | copy-start | bytes 3096580
  97.3 45.4 %collective-permute-start.14 = (bf16[36,112,128]{2,1,0:T(8,128)(2,1)S(1)}, bf16[36,112,128]{2,1,0:T(8,128)(2,1)S(1)}, u32[]{:S(2)}, u32[]{:S(2)}) collective-permute-start(bf16[36,112,128]{2,1,0:T(8,128)(2,1)S(1)} %collective-permute-done.12.refs_12_), channel_id=1, source_target_pairs={{0,16},{1,17},{2,18},{3,19},{4,20},{5,21},{6,22},{7,23},{8,24},{9,... | collective-permute-start | bytes 3096584 | tf_op jit(solution)/shard_map/ppermute | solution.py:316
  98.0 90.2 %copy-start.4 = (bf16[36,112,128]{2,1,0:T(8,128)(2,1)}, bf16[36,112,128]{2,1,0:T(8,128)(2,1)S(1)}, u32[]{:S(2)}) copy-start(bf16[36,112,128]{2,1,0:T(8,128)(2,1)S(1)} %collective-permute-done.refs_0_) | copy-start | bytes 3096580
  98.0 66.8 %collective-permute-start.2 = (bf16[36,112,128]{2,1,0:T(8,128)(2,1)S(1)}, bf16[36,112,128]{2,1,0:T(8,128)(2,1)}, u32[]{:S(2)}, u32[]{:S(2)}) collective-permute-start(bf16[36,112,128]{2,1,0:T(8,128)(2,1)S(1)} %collective-permute-done.refs_0_), channel_id=1, source_target_pairs={{0,16},{1,17},{2,18},{3,19},{4,20},{5,21},{6,22},{7,23},{8,24},{9,... | collective-permute-start | bytes 3096584 | tf_op jit(solution)/shard_map/ppermute | solution.py:316
  119.1 69.2 %copy-start.5 = (bf16[36,112,128]{2,1,0:T(8,128)(2,1)}, bf16[36,112,128]{2,1,0:T(8,128)(2,1)S(1)}, u32[]{:S(2)}) copy-start(bf16[36,112,128]{2,1,0:T(8,128)(2,1)S(1)} %collective-permute-done.4.refs_4_) | copy-start | bytes 3096580
  119.1 67.9 %collective-permute-start.6 = (bf16[36,112,128]{2,1,0:T(8,128)(2,1)S(1)}, bf16[36,112,128]{2,1,0:T(8,128)(2,1)}, u32[]{:S(2)}, u32[]{:S(2)}) collective-permute-start(bf16[36,112,128]{2,1,0:T(8,128)(2,1)S(1)} %collective-permute-done.4.refs_4_), channel_id=1, source_target_pairs={{0,16},{1,17},{2,18},{3,19},{4,20},{5,21},{6,22},{7,23},{8,24},{9,... | collective-permute-start | bytes 3096584 | tf_op jit(solution)/shard_map/ppermute | solution.py:316
  120.6 67.0 %collective-permute-start.1 = (bf16[36,112,128]{2,1,0:T(8,128)(2,1)S(1)}, bf16[36,112,128]{2,1,0:T(8,128)(2,1)S(1)}, u32[]{:S(2)}, u32[]{:S(2)}) collective-permute-start(bf16[36,112,128]{2,1,0:T(8,128)(2,1)S(1)} %collective-permute-done.refs_0_), channel_id=1, source_target_pairs={{0,8},{1,9},{2,10},{3,11},{4,12},{5,13},{6,14},{7,15},{8,0},{9,1},... | collective-permute-start | bytes 3096584 | tf_op jit(solution)/shard_map/ppermute | solution.py:316
  120.6 98.3 %copy-start.6 = (bf16[36,112,128]{2,1,0:T(8,128)(2,1)}, bf16[36,112,128]{2,1,0:T(8,128)(2,1)S(1)}, u32[]{:S(2)}) copy-start(bf16[36,112,128]{2,1,0:T(8,128)(2,1)S(1)} %collective-permute-done.10.refs_10_) | copy-start | bytes 3096580
  120.6 67.1 %collective-permute-start.13 = (bf16[36,112,128]{2,1,0:T(8,128)(2,1)S(1)}, bf16[36,112,128]{2,1,0:T(8,128)(2,1)S(1)}, u32[]{:S(2)}, u32[]{:S(2)}) collective-permute-start(bf16[36,112,128]{2,1,0:T(8,128)(2,1)S(1)} %collective-permute-done.12.refs_12_), channel_id=1, source_target_pairs={{0,8},{1,9},{2,10},{3,11},{4,12},{5,13},{6,14},{7,15},{8,0},{9,1},... | collective-permute-start | bytes 3096584 | tf_op jit(solution)/shard_map/ppermute | solution.py:316
  142.6 76.3 %copy-start.7 = (bf16[36,112,128]{2,1,0:T(8,128)(2,1)}, bf16[36,112,128]{2,1,0:T(8,128)(2,1)S(1)}, u32[]{:S(2)}) copy-start(bf16[36,112,128]{2,1,0:T(8,128)(2,1)S(1)} %collective-permute-done.14.refs_14_) | copy-start | bytes 3096580
  142.6 45.6 %collective-permute-start.5 = (bf16[36,112,128]{2,1,0:T(8,128)(2,1)S(1)}, bf16[36,112,128]{2,1,0:T(8,128)(2,1)S(1)}, u32[]{:S(2)}, u32[]{:S(2)}) collective-permute-start(bf16[36,112,128]{2,1,0:T(8,128)(2,1)S(1)} %collective-permute-done.4.refs_4_), channel_id=1, source_target_pairs={{0,8},{1,9},{2,10},{3,11},{4,12},{5,13},{6,14},{7,15},{8,0},{9,1},... | collective-permute-start | bytes 3096584 | tf_op jit(solution)/shard_map/ppermute | solution.py:316
  164.9 54.8 %collective-permute-start.9 = (bf16[36,112,128]{2,1,0:T(8,128)(2,1)S(1)}, bf16[36,112,128]{2,1,0:T(8,128)(2,1)}, u32[]{:S(2)}, u32[]{:S(2)}) collective-permute-start(bf16[36,112,128]{2,1,0:T(8,128)(2,1)S(1)} %collective-permute-done.8.refs_8_), channel_id=1, source_target_pairs={{0,8},{1,9},{2,10},{3,11},{4,12},{5,13},{6,14},{7,15},{8,0},{9,1},... | collective-permute-start | bytes 3096584 | tf_op jit(solution)/shard_map/ppermute | solution.py:316
  187.0 32.7 %collective-permute-start.11 = (bf16[36,112,128]{2,1,0:T(8,128)(2,1)S(1)}, bf16[36,112,128]{2,1,0:T(8,128)(2,1)}, u32[]{:S(2)}, u32[]{:S(2)}) collective-permute-start(bf16[36,112,128]{2,1,0:T(8,128)(2,1)S(1)} %collective-permute-done.10.refs_10_), channel_id=1, source_target_pairs={{0,8},{1,9},{2,10},{3,11},{4,12},{5,13},{6,14},{7,15},{8,0},{9,1},... | collective-permute-start | bytes 3096584 | tf_op jit(solution)/shard_map/ppermute | solution.py:316
  187.7 1.0 copy-start.8
  187.7 32.0 %collective-permute-start.15 = (bf16[36,112,128]{2,1,0:T(8,128)(2,1)S(1)}, bf16[36,112,128]{2,1,0:T(8,128)(2,1)}, u32[]{:S(2)}, u32[]{:S(2)}) collective-permute-start(bf16[36,112,128]{2,1,0:T(8,128)(2,1)S(1)} %collective-permute-done.14.refs_14_), channel_id=1, source_target_pairs={{0,8},{1,9},{2,10},{3,11},{4,12},{5,13},{6,14},{7,15},{8,0},{9,1},... | collective-permute-start | bytes 3096584 | tf_op jit(solution)/shard_map/ppermute | solution.py:316
  187.7 1.3 copy-start.9
  187.7 31.9 %collective-permute-start.3 = (bf16[36,112,128]{2,1,0:T(8,128)(2,1)}, bf16[36,112,128]{2,1,0:T(8,128)(2,1)}, u32[]{:S(2)}, u32[]{:S(2)}) collective-permute-start(bf16[36,112,128]{2,1,0:T(8,128)(2,1)} %collective-permute-done.2.refs_2_), channel_id=1, source_target_pairs={{0,8},{1,9},{2,10},{3,11},{4,12},{5,13},{6,14},{7,15},{8,0},{9,1},... | collective-permute-start | bytes 3096584 | tf_op jit(solution)/shard_map/ppermute | solution.py:316
  188.2 1.1 copy-start.10
  188.2 31.5 %collective-permute-start.7 = (bf16[36,112,128]{2,1,0:T(8,128)(2,1)}, bf16[36,112,128]{2,1,0:T(8,128)(2,1)}, u32[]{:S(2)}, u32[]{:S(2)}) collective-permute-start(bf16[36,112,128]{2,1,0:T(8,128)(2,1)} %collective-permute-done.6.refs_6_), channel_id=1, source_target_pairs={{0,8},{1,9},{2,10},{3,11},{4,12},{5,13},{6,14},{7,15},{8,0},{9,1},... | collective-permute-start | bytes 3096584 | tf_op jit(solution)/shard_map/ppermute | solution.py:316
  189.3 29.7 %copy-start.1 = (s32[8,2]{0,1:T(2,128)S(1)}, s32[8,2]{0,1:T(2,128)}, u32[]{:S(2)}) copy-start(s32[8,2]{0,1:T(2,128)} %param.9) | copy-start | bytes 196

commit v2 on v1

--- a/solution.py
+++ b/solution.py
@@ -48,72 +48,93 @@
         self.tail_width = round_up(self.js * self.tail, LANES)
 
 
-def dress_kernel(p, z_ref, a_ref, ov_ref, vv_ref, *refs):
-    outs, (dressed, packed) = refs[: p.js], refs[p.js :]
+def spread_kernel(p, t1_ref, out_ref):
+    def repeat(rows, cols, per_row, per_col):
+        row = lax.broadcasted_iota(jnp.int32, (rows, cols), 0) // per_row
+        col = lax.broadcasted_iota(jnp.int32, (rows, cols), 1) // per_col
+        return (row == col).astype(jnp.float32).astype(jnp.bfloat16)
+
+    rows, cols = p.window * ROWS, p.occupied * ROWS
+    tall = lax.dot_general(
+        repeat(rows, p.window, ROWS, 1), t1_ref[...], NT, preferred_element_type=jnp.float32
+    ).astype(jnp.bfloat16)
+    full = jnp.dot(
+        tall, repeat(p.occupied, cols, 1, ROWS), preferred_element_type=jnp.float32
+    )
+    row = lax.broadcasted_iota(jnp.int32, (rows, cols), 0) % ROWS
+    col = lax.broadcasted_iota(jnp.int32, (rows, cols), 1) % ROWS
+    out_ref[...] = jnp.where(row == col, full, 0.0).astype(jnp.bfloat16)
+
+
+def spread_amplitudes(p, t1_window):
+    return pl.pallas_call(
+        functools.partial(spread_kernel, p),
+        out_shape=jax.ShapeDtypeStruct((p.window * ROWS, p.occupied * ROWS), jnp.bfloat16),
+        compiler_params=pltpu.CompilerParams(vmem_limit_bytes=48 * 2**20),
+        name="spread",
+    )(t1_window)
+
+
+def dress_kernel(p, offset, z_ref, a_ref, *refs):
+    ov, vv, out = refs[: p.nm + 1], refs[p.nm + 1 : 2 * p.nm + 2], refs[-1]
     w = p.window
-
-    @pl.when(pl.program_id(0) == 0)
-    def _():
-        dressed[...] = jnp.zeros_like(dressed)
-
-    shift = lax.dot_general(
-        a_ref[...],
-        ov_ref[...].reshape(p.occupied * ROWS, p.aux_dev),
-        NN,
-        preferred_element_type=jnp.float32,
-    )
-    vv = vv_ref[...].astype(jnp.float32)
-    dressed[:, :, : p.aux_dev] = vv - shift.reshape(w, ROWS, p.aux_dev)
+    j = lax.rem(z_ref[0] + offset, p.js)
+    vectors = jnp.concatenate([ref[...].reshape(p.occupied * ROWS, -1) for ref in ov], axis=1)
+    shift = lax.dot_general(a_ref[...], vectors, NN, preferred_element_type=jnp.float32)
+    for m in range(p.nm):
+        here = shift[:, m * LANES : (m + 1) * LANES].reshape(w, ROWS, LANES)
+        out[m * w : (m + 1) * w] = (vv[m][...].astype(jnp.float32) - here).astype(jnp.bfloat16)
+    here = shift[:, p.nm * LANES :].reshape(w, ROWS, p.tail_width)
+    source = vv[p.nm][...].astype(jnp.float32) - here
+    source = source.reshape(p.nt, p.per_row, ROWS, p.tail_width)
     lane = lax.broadcasted_iota(jnp.int32, (p.nt, ROWS, LANES), 2)
-    for j in range(p.js):
+    rest = jnp.zeros((p.nt, ROWS, LANES), jnp.float32)
+    for s in range(p.per_row):
+        turn = lax.rem(s * p.slot - j * p.tail + 2 * p.tail_width, p.tail_width)
+        moved = pltpu.roll(source[:, s].reshape(p.nt * ROWS, p.tail_width), turn, 1)
+        moved = moved[:, :LANES].reshape(p.nt, ROWS, LANES)
+        keep = (lane >= s * p.slot) & (lane < s * p.slot + p.tail)
+        rest = jnp.where(keep, moved, rest)
+    out[p.nm * w :] = rest.astype(jnp.bfloat16)
+
+
+def dress(p, offset, z, spread, chol_vv, chol_ov):
+    def specs(lead):
+        found = []
         for m in range(p.nm):
-            low = j * p.main + m * LANES
-            packed[j, m * w : (m + 1) * w] = dressed[:, :, low : low + LANES].astype(jnp.bfloat16)
-        rest = jnp.zeros((p.nt, ROWS, LANES), jnp.float32)
-        source = dressed[:, :, p.tail_from : p.tail_from + p.tail_width]
-        source = source.reshape(p.nt, p.per_row, ROWS, p.tail_width)
-        for s in range(p.per_row):
-            turn = (s * p.slot - j * p.tail) % p.tail_width
-            moved = pltpu.roll(source[:, s].reshape(p.nt * ROWS, p.tail_width), turn, 1)
-            moved = moved[:, :LANES].reshape(p.nt, ROWS, LANES)
-            here = (lane >= s * p.slot) & (lane < s * p.slot + p.tail)
-            rest = jnp.where(here, moved, rest)
-        packed[j, p.nm * w :] = rest.astype(jnp.bfloat16)
-    z = z_ref[0]
-    for o, out in enumerate(outs):
-        out[...] = packed[lax.rem(z + o, p.js)]
-
-
-def dress(p, z, chol_vv, chol_ov, t1_window):
-    spread = jnp.einsum(
-        "kw,cd->wckd", t1_window, jnp.eye(ROWS, dtype=jnp.bfloat16)
-    ).reshape(p.window * ROWS, p.occupied * ROWS)
-    message = jax.ShapeDtypeStruct((p.planes, p.cpad, LANES), jnp.bfloat16)
+            found.append(
+                pl.BlockSpec(
+                    (lead, ROWS, LANES),
+                    lambda i, z, m=m: (0, i, lax.rem(z[0] + offset, p.js) * p.nm + m),
+                )
+            )
+        found.append(
+            pl.BlockSpec(
+                (lead, ROWS, p.tail_width), lambda i, z: (0, i, p.tail_from // p.tail_width)
+            )
+        )
+        return found
+
+    count = p.nm + 1
     return pl.pallas_call(
-        functools.partial(dress_kernel, p),
-        out_shape=[message] * p.js,
+        functools.partial(dress_kernel, p, offset),
+        out_shape=jax.ShapeDtypeStruct((p.planes, p.cpad, LANES), jnp.bfloat16),
         grid_spec=pltpu.PrefetchScalarGridSpec(
             num_scalar_prefetch=1,
             grid=(p.cpad // ROWS,),
-            in_specs=[
-                pl.BlockSpec((p.window * ROWS, p.occupied * ROWS), lambda i, z: (0, 0)),
-                pl.BlockSpec((p.occupied, ROWS, p.aux_dev), lambda i, z: (0, i, 0)),
-                pl.BlockSpec((p.window, ROWS, p.aux_dev), lambda i, z: (0, i, 0)),
-            ],
-            out_specs=[pl.BlockSpec((p.planes, ROWS, LANES), lambda i, z: (0, i, 0))] * p.js,
-            scratch_shapes=[
-                pltpu.VMEM((p.window, ROWS, p.tail_from + p.tail_width), jnp.float32),
-                pltpu.VMEM((p.js, p.planes, ROWS, LANES), jnp.bfloat16),
-            ],
+            in_specs=[pl.BlockSpec((p.window * ROWS, p.occupied * ROWS), lambda i, z: (0, 0))]
+            + specs(p.occupied)
+            + specs(p.window),
+            out_specs=pl.BlockSpec((p.planes, ROWS, LANES), lambda i, z: (0, i, 0)),
         ),
         compiler_params=pltpu.CompilerParams(vmem_limit_bytes=48 * 2**20),
         cost_estimate=pl.CostEstimate(
-            flops=2 * p.window * p.occupied * p.cpad * p.aux_dev * ROWS,
-            bytes_accessed=2 * (p.occupied + 2 * p.window) * p.cpad * p.aux_dev,
+            flops=2 * p.window * p.occupied * p.cpad * LANES * count * ROWS,
+            bytes_accessed=2 * (p.occupied + 2 * p.window) * p.cpad * LANES * count,
             transcendentals=0,
         ),
         name="dress",
-    )(z, spread, chol_ov, chol_vv)
+    )(z, spread, *([chol_ov] * count), *([chol_vv] * count))
 
 
 def ladder_kernel(p, parts, group, place_ref, blocks_ref, *refs):
@@ -305,7 +326,7 @@
 
     chol_vv = pad_columns(chol_vv, 1, cols, p.cpad)
     chol_ov = pad_columns(chol_ov, 1, cols, p.cpad)
-    messages = dress(p, place, chol_vv, chol_ov, t1_window)
+    spread = spread_amplitudes(p, t1_window)
 
     def permute(array, target):
         pairs = []
@@ -315,25 +336,55 @@
                 pairs.append((a * n_pair + q, to_a * n_pair + to_q))
         return lax.ppermute(array, ("aux", "pair"), pairs)
 
-    pieces = []
-    for o in range(p.js):
-        own = permute(
-            messages[o],
+    def to_slice(array, o):
+        return permute(
+            array,
             lambda a, q: (
                 a // CORES * CORES + q % CORES,
                 CORES * ((q // CORES + o) % p.js) + a % CORES,
             ),
         )
-        for r in range(p.xs):
-            turned = own
-            if r:
-                turned = permute(
-                    own, lambda a, q: (CORES * ((a // CORES + r) % p.xs) + a % CORES, q)
-                )
-            pieces += [turned, permute(turned, lambda a, q: (a ^ 1, q))]
-
+
+    def along_x(array, r):
+        return permute(array, lambda a, q: (CORES * ((a // CORES + r) % p.xs) + a % CORES, q))
+
+    def to_core(array):
+        return permute(array, lambda a, q: (a ^ 1, q))
+
+    order = sorted(range(p.js), key=lambda o: min(o, p.js - o))
+    messages = {}
+    for place_in_order, o in enumerate(order):
+        messages[o] = dress(p, o, place, spread, chol_vv, chol_ov)
+        if o == 0:
+            turned_here = to_slice(messages[0], 0)
+        if place_in_order == 1:
+            spread, messages[o], turned_here = lax.optimization_barrier(
+                (spread, messages[o], turned_here)
+            )
+        else:
+            spread, messages[o] = lax.optimization_barrier((spread, messages[o]))
+
+    messages[order[-1]], amplitudes = lax.optimization_barrier((messages[order[-1]], amplitudes))
     amps = pad_columns(pad_columns(amplitudes, 1, cols, p.cpad), 2, cols, p.cpad)
     amps = jnp.transpose(amps, (1, 0, 2)).reshape(p.c * p.ij, p.d)
+
+    found = {}
+    before = None
+    for place_in_order, o in enumerate(order):
+        if o == 0:
+            turned = [turned_here]
+            turned += [to_slice(along_x(messages[0], r), 0) for r in range(1, p.xs)]
+        else:
+            message = messages[o]
+            if before is not None:
+                message, before = lax.optimization_barrier((message, before))
+            own = to_slice(message, o)
+            before = own
+            if place_in_order == p.js - 2:
+                own, amps = lax.optimization_barrier((own, amps))
+            turned = [own] + [along_x(own, r) for r in range(1, p.xs)]
+        found[o] = [piece for array in turned for piece in (array, to_core(array))]
+    pieces = [piece for o in range(p.js) for piece in found[o]]
 
     partial_terms = ladder(p, place, assignment, pieces, amps)
     share = p.ij // n_aux

time: 334 us -> 268 us (0.80)
  waiting for transfers between devices: 123 us -> 62.4 us
  starting transfers between devices: 19.2 us -> 46.5 us
  local copies, waits for them, and re-layouts: 58.2 us -> 34.4 us
  blocking collectives: 33.8 us -> 11.6 us
  Pallas kernels: 91.5 us -> 110 us
  other arithmetic: 6.49 us -> 0.84 us
    ppermute x16 -> x17, waiting for transfers between devices: 123 us -> 62.4 us  [permute(): return lax.ppermute(array, ('aux', 'pair'), pairs)]
    ppermute x16 -> x17, starting transfers between devices: 19.2 us -> 46.5 us  [permute(): return lax.ppermute(array, ('aux', 'pair'), pairs)]
    reshape x2 -> x0, local copies, waits for them, and re-layouts: 23.3 us -> none  [dress(): spread = jnp.einsum('kw,cd->wckd', t1_window, jnp.eye(ROWS, dtype=jnp.bfl...]
    all_to_all x1, blocking collectives: 33.8 us -> 11.6 us  [shards(): lax.all_to_all(terms, ('aux', 'pair'), split_axis=0, concat_axis=0, tiled...]
    pallas_call x1 -> x5, Pallas kernels: 15.8 us -> 34.7 us  [the longest x4 33.9 us: dress(): pl.pallas_call(functools.partial(dress_kernel, p, offset), out_shape=jax....]
    transpose x1 -> x0, other arithmetic: 5.64 us -> none  [dress(): jnp.einsum('kw,cd->wckd', t1_window, jnp.eye(ROWS, dtype=jnp.bfloat16))]
  transfers between devices with their start and end apart: 16 -> 17, of which waited for: 5 -> 6; matrix products, arithmetic and copies ran while one was open for 9% -> 12% of each run, Pallas kernels for 0% -> 10%
where the time goes in v2:
time: 268 us; the launch traced here: 266 us
  Pallas kernels  110 us (41%)
  waiting for transfers between devices  62.4 us (23%)
  starting transfers between devices  46.5 us (17%)
  local copies, waits for them, and re-layouts  34.4 us (13%)
  blocking collectives  11.6 us (4%)
    pallas_call x1, Pallas kernels, ladder(): pl.pallas_call(functools.partial(ladder_kernel, p, parts, group), out_sha...  75.7 us
    ppermute x17, waiting for transfers between devices, permute(): return lax.ppermute(array, ('aux', 'pair'), pairs)  62.4 us
    ppermute x17, starting transfers between devices, permute(): return lax.ppermute(array, ('aux', 'pair'), pairs)  46.5 us
    pallas_call x4, Pallas kernels, dress(): pl.pallas_call(functools.partial(dress_kernel, p, offset), out_shape=jax....  33.9 us
    transpose x1, local copies, waits for them, and re-layouts, shards(): amps = jnp.transpose(amps, (1, 0, 2)).reshape(p.c * p.ij, p.d)  30.1 us
    all_to_all x1, blocking collectives, shards(): lax.all_to_all(terms, ('aux', 'pair'), split_axis=0, concat_axis=0, tiled...  11.6 us
  transfers between devices with their start and end apart: 17, of which 6 were waited for; matrix products, arithmetic and copies ran while one was open for 12% of the time, Pallas kernels for 10%

profile of v2, /device:TPU:0, one launch (start us, length us, event | category | flops | bytes accessed | tf_op | source)
XLA Modules:
  0.0 266.3 jit_solution(16809110134377638532)
XLA Ops:
  0.0 0.8 copy.13.t1_ref
  0.8 0.8 spread.1.a_ref
  1.6 0.1 pad_add_fusion.z_ref.place_ref
  1.7 8.5 %dress.4 = bf16[36,112,128]{2,1,0:T(8,128)(2,1)S(1)} custom-call(s32[3]{0:T(128)S(1)} %pad_add_fusion.z_ref.place_ref, bf16[512,1600]{1,0:T(8,128)(2,1)S(1)} %spread.1.a_ref, bf16[100,112,576]{2,1,0:T(8,128)(2,1)} %refs_1_.7, bf16[100,112,576]{2,1,0:T(8,128)(2,1)} %refs_1_.7, bf16[32,112,576]{2,1,0:T(8,128)(2,1)} %refs_3_.7, bf16[32,112,576]{2,1,0:T(8,128)(2,1)} %refs_3_.7), custom_call_target="tpu_custom_call" | custom-call | flops 2936012800 | bytes 9404416 | tf_op jit(solution)/shard_map/dress/pallas_call | solution.py:119
  10.2 0.7 collective-permute-start
  10.9 8.5 %dress.5 = bf16[36,112,128]{2,1,0:T(8,128)(2,1)S(1)} custom-call(s32[3]{0:T(128)S(1)} %pad_add_fusion.z_ref.place_ref, bf16[512,1600]{1,0:T(8,128)(2,1)S(1)} %spread.1.a_ref, bf16[100,112,576]{2,1,0:T(8,128)(2,1)} %refs_1_.7, bf16[100,112,576]{2,1,0:T(8,128)(2,1)} %refs_1_.7, bf16[32,112,576]{2,1,0:T(8,128)(2,1)} %refs_3_.7, bf16[32,112,576]{2,1,0:T(8,128)(2,1)} %refs_3_.7), custom_call_target="tpu_custom_call" | custom-call | flops 2936012800 | bytes 9404416 | tf_op jit(solution)/shard_map/dress/pallas_call | solution.py:119
  19.4 0.0 collective-permute-done.refs_0_
  19.4 3.1 %collective-permute-start.5 = (bf16[36,112,128]{2,1,0:T(8,128)(2,1)S(1)}, bf16[36,112,128]{2,1,0:T(8,128)(2,1)S(1)}, u32[]{:S(2)}, u32[]{:S(2)}) collective-permute-start(bf16[36,112,128]{2,1,0:T(8,128)(2,1)S(1)} %dress.5), channel_id=1, source_target_pairs={{0,2},{1,10},{2,4},{3,12},{4,6},{5,14},{6,0},{7,8},{8,3},{9,11},{1... | collective-permute-start | bytes 3096584 | tf_op jit(solution)/shard_map/ppermute | solution.py:337
  22.5 1.5 collective-permute-start.2
  24.0 8.5 %dress.6 = bf16[36,112,128]{2,1,0:T(8,128)(2,1)S(1)} custom-call(s32[3]{0:T(128)S(1)} %pad_add_fusion.z_ref.place_ref, bf16[512,1600]{1,0:T(8,128)(2,1)S(1)} %spread.1.a_ref, bf16[100,112,576]{2,1,0:T(8,128)(2,1)} %refs_1_.7, bf16[100,112,576]{2,1,0:T(8,128)(2,1)} %refs_1_.7, bf16[32,112,576]{2,1,0:T(8,128)(2,1)} %refs_3_.7, bf16[32,112,576]{2,1,0:T(8,128)(2,1)} %refs_3_.7), custom_call_target="tpu_custom_call" | custom-call | flops 2936012800 | bytes 9404416 | tf_op jit(solution)/shard_map/dress/pallas_call | solution.py:119
  32.5 8.4 %collective-permute-done.5.refs_4_ = bf16[36,112,128]{2,1,0:T(8,128)(2,1)S(1)} collective-permute-done((bf16[36,112,128]{2,1,0:T(8,128)(2,1)S(1)}, bf16[36,112,128]{2,1,0:T(8,128)(2,1)S(1)}, u32[]{:S(2)}, u32[]{:S(2)}) %collective-permute-start.5) | collective-permute-done | bytes 1032224 | tf_op jit(solution)/shard_map/ppermute | solution.py:337
  40.9 2.2 collective-permute-start.9
  43.1 8.5 %dress.7 = bf16[36,112,128]{2,1,0:T(8,128)(2,1)S(1)} custom-call(s32[3]{0:T(128)S(1)} %pad_add_fusion.z_ref.place_ref, bf16[512,1600]{1,0:T(8,128)(2,1)S(1)} %spread.1.a_ref, bf16[100,112,576]{2,1,0:T(8,128)(2,1)} %refs_1_.7, bf16[100,112,576]{2,1,0:T(8,128)(2,1)} %refs_1_.7, bf16[32,112,576]{2,1,0:T(8,128)(2,1)} %refs_3_.7, bf16[32,112,576]{2,1,0:T(8,128)(2,1)} %refs_3_.7), custom_call_target="tpu_custom_call" | custom-call | flops 2936012800 | bytes 9404416 | tf_op jit(solution)/shard_map/dress/pallas_call | solution.py:119
  51.6 0.0 collective-permute-done.2
  51.6 0.7 collective-permute-start.3
  52.4 20.5 %collective-permute-start.1 = (bf16[36,112,128]{2,1,0:T(8,128)(2,1)S(1)}, bf16[36,112,128]{2,1,0:T(8,128)(2,1)S(1)}, u32[]{:S(2)}, u32[]{:S(2)}) collective-permute-start(bf16[36,112,128]{2,1,0:T(8,128)(2,1)S(1)} %collective-permute-done.refs_0_), channel_id=1, source_target_pairs={{0,8},{1,9},{2,10},{3,11},{4,12},{5,13},{6,14},{7,15},{8,0},{9,1},... | collective-permute-start | bytes 3096584 | tf_op jit(solution)/shard_map/ppermute | solution.py:337
  72.9 0.0 collective-permute-start.10
  72.9 0.0 copy-start.1
  72.9 30.1 %copy.14 = bf16[224,64,896]{2,1,0:T(8,128)(2,1)} copy(bf16[224,64,896]{2,0,1:T(8,128)(2,1)} %bitcast.14) | data formatting | bytes 51380224 | tf_op jit(solution)/shard_map/transpose | solution.py:369
  103.0 1.5 collective-permute-start.7
  104.5 2.8 %collective-permute-start.6 = (bf16[36,112,128]{2,1,0:T(8,128)(2,1)S(1)}, bf16[36,112,128]{2,1,0:T(8,128)(2,1)S(1)}, u32[]{:S(2)}, u32[]{:S(2)}) collective-permute-start(bf16[36,112,128]{2,1,0:T(8,128)(2,1)S(1)} %collective-permute-done.5.refs_4_), channel_id=1, source_target_pairs={{0,8},{1,9},{2,10},{3,11},{4,12},{5,13},{6,14},{7,15},{8,0},{9,1},... | collective-permute-start | bytes 3096584 | tf_op jit(solution)/shard_map/ppermute | solution.py:337
  107.3 0.0 collective-permute-done.3.refs_2_
  107.3 0.1 collective-permute-start.4
  107.4 0.0 collective-permute-done.1.refs_1_
  107.4 0.5 collective-permute-start.15
  107.9 11.3 %collective-permute-done.10.refs_8_ = bf16[36,112,128]{2,1,0:T(8,128)(2,1)} collective-permute-done((bf16[36,112,128]{2,1,0:T(8,128)(2,1)S(1)}, bf16[36,112,128]{2,1,0:T(8,128)(2,1)}, u32[]{:S(2)}, u32[]{:S(2)}) %collective-permute-start.10) | collective-permute-done | bytes 1032224 | tf_op jit(solution)/shard_map/ppermute | solution.py:337
  119.2 1.5 collective-permute-start.12
  120.7 5.9 %collective-permute-done.7.refs_6_ = bf16[36,112,128]{2,1,0:T(8,128)(2,1)} collective-permute-done((bf16[36,112,128]{2,1,0:T(8,128)(2,1)S(1)}, bf16[36,112,128]{2,1,0:T(8,128)(2,1)}, u32[]{:S(2)}, u32[]{:S(2)}) %collective-permute-start.7) | collective-permute-done | bytes 1032224 | tf_op jit(solution)/shard_map/ppermute | solution.py:337
  126.6 4.4 %collective-permute-start.14 = (bf16[36,112,128]{2,1,0:T(8,128)(2,1)S(1)}, bf16[36,112,128]{2,1,0:T(8,128)(2,1)}, u32[]{:S(2)}, u32[]{:S(2)}) collective-permute-start(bf16[36,112,128]{2,1,0:T(8,128)(2,1)S(1)} %collective-permute-done.9.refs_12_), channel_id=1, source_target_pairs={{0,8},{1,9},{2,10},{3,11},{4,12},{5,13},{6,14},{7,15},{8,0},{9,1},... | collective-permute-start | bytes 3096584 | tf_op jit(solution)/shard_map/ppermute | solution.py:337
  131.1 0.0 collective-permute-done.6.refs_5_
  131.1 0.1 collective-permute-start.8
  131.2 0.4 collective-permute-start.11
  131.6 17.2 %collective-permute-done.15.refs_14_ = bf16[36,112,128]{2,1,0:T(8,128)(2,1)} collective-permute-done((bf16[36,112,128]{2,1,0:T(8,128)(2,1)S(1)}, bf16[36,112,128]{2,1,0:T(8,128)(2,1)}, u32[]{:S(2)}, u32[]{:S(2)}) %collective-permute-start.15) | collective-permute-done | bytes 1032224 | tf_op jit(solution)/shard_map/ppermute | solution.py:337
  148.8 4.4 %collective-permute-start.16 = (bf16[36,112,128]{2,1,0:T(8,128)(2,1)}, bf16[36,112,128]{2,1,0:T(8,128)(2,1)}, u32[]{:S(2)}, u32[]{:S(2)}) collective-permute-start(bf16[36,112,128]{2,1,0:T(8,128)(2,1)} %collective-permute-done.15.refs_14_), channel_id=1, source_target_pairs={{0,8},{1,9},{2,10},{3,11},{4,12},{5,13},{6,14},{7,15},{8,0},{9,1},... | collective-permute-start | bytes 3096584 | tf_op jit(solution)/shard_map/ppermute | solution.py:337
  153.2 17.7 %collective-permute-done.12.refs_10_ = bf16[36,112,128]{2,1,0:T(8,128)(2,1)} collective-permute-done((bf16[36,112,128]{2,1,0:T(8,128)(2,1)}, bf16[36,112,128]{2,1,0:T(8,128)(2,1)}, u32[]{:S(2)}, u32[]{:S(2)}) %collective-permute-start.12) | collective-permute-done | bytes 1032224 | tf_op jit(solution)/shard_map/ppermute | solution.py:337
  170.9 2.0 collective-permute-start.13
  172.9 0.7 copy.15.blocks_ref
  173.6 1.9 collective-permute-done.13.refs_11_
  175.5 75.7 %ladder.1 = f32[32,4,128]{2,1,0:T(4,128)} custom-call(s32[3]{0:T(128)} %copy-done, s32[8,2]{1,0:T(8,128)} %copy.15.blocks_ref, bf16[36,112,128]{2,1,0:T(8,128)(2,1)} %copy-done.2, bf16[36,112,128]{2,1,0:T(8,128)(2,1)} %copy-done.6, bf16[36,112,128]{2,1,0:T(8,128)(2,1)} %copy-done.5, bf16[36,112,128]{2,1,0:T(8,128)(2,1)} %copy-done.8, ...), custom_call_target="tpu_custom_call" | custom-call | flops 13153337344 | bytes 42205184 | tf_op jit(solution)/shard_map/ladder/pallas_call | solution.py:281
  251.1 1.0 reshape.10
  252.2 0.2 copy.16
  252.3 0.2 copy.22
  252.5 0.1 reshape.12
  252.6 11.6 %all_to_all.5 = f32[32,1,256]{2,1,0:T(1,128)S(1)} all-to-all(f32[32,1,256]{2,1,0:T(1,128)S(1)} %reshape.12), channel_id=1, replica_groups=mesh['aux'=4,'pair'=8] {'aux','pair'}, dimensions={0} | all-to-all | bytes 65536 | tf_op jit(solution)/shard_map/all_to_all | solution.py:393
  264.2 0.5 broadcast.2
  264.7 0.7 reduce
  265.5 0.1 reshape.13
  265.6 0.7 copy.19
  (24 shorter events, 0.1 us)
Async XLA Ops:
  1.7 41.4 %copy-start = (s32[3]{0:T(128)}, s32[3]{0:T(128)S(1)}, u32[]{:S(2)}) copy-start(s32[3]{0:T(128)S(1)} %pad_add_fusion.z_ref.place_ref) | copy-start | bytes 40
  10.2 9.2 %collective-permute-start = (bf16[36,112,128]{2,1,0:T(8,128)(2,1)S(1)}, bf16[36,112,128]{2,1,0:T(8,128)(2,1)S(1)}, u32[]{:S(2)}, u32[]{:S(2)}) collective-permute-start(bf16[36,112,128]{2,1,0:T(8,128)(2,1)S(1)} %dress.4), channel_id=1, source_target_pairs={{0,0},{1,8},{2,2},{3,10},{4,4},{5,12},{6,6},{7,14},{8,1},{9,9},{10... | collective-permute-start | bytes 3096584 | tf_op jit(solution)/shard_map/ppermute | solution.py:337
  19.4 32.9 %copy-start.2 = (bf16[36,112,128]{2,1,0:T(8,128)(2,1)}, bf16[36,112,128]{2,1,0:T(8,128)(2,1)S(1)}, u32[]{:S(2)}) copy-start(bf16[36,112,128]{2,1,0:T(8,128)(2,1)S(1)} %collective-permute-done.refs_0_) | copy-start | bytes 3096580
  19.4 21.5 %collective-permute-start.5 = (bf16[36,112,128]{2,1,0:T(8,128)(2,1)S(1)}, bf16[36,112,128]{2,1,0:T(8,128)(2,1)S(1)}, u32[]{:S(2)}, u32[]{:S(2)}) collective-permute-start(bf16[36,112,128]{2,1,0:T(8,128)(2,1)S(1)} %dress.5), channel_id=1, source_target_pairs={{0,2},{1,10},{2,4},{3,12},{4,6},{5,14},{6,0},{7,8},{8,3},{9,11},{1... | collective-permute-start | bytes 3096584 | tf_op jit(solution)/shard_map/ppermute | solution.py:337
  22.5 29.1 %collective-permute-start.2 = (bf16[36,112,128]{2,1,0:T(8,128)(2,1)S(1)}, bf16[36,112,128]{2,1,0:T(8,128)(2,1)S(1)}, u32[]{:S(2)}, u32[]{:S(2)}) collective-permute-start(bf16[36,112,128]{2,1,0:T(8,128)(2,1)S(1)} %dress.4), channel_id=1, source_target_pairs={{0,16},{1,17},{2,18},{3,19},{4,20},{5,21},{6,22},{7,23},{8,24},{9,... | collective-permute-start | bytes 3096584 | tf_op jit(solution)/shard_map/ppermute | solution.py:337
  40.9 63.6 %copy-start.3 = (bf16[36,112,128]{2,1,0:T(8,128)(2,1)}, bf16[36,112,128]{2,1,0:T(8,128)(2,1)S(1)}, u32[]{:S(2)}) copy-start(bf16[36,112,128]{2,1,0:T(8,128)(2,1)S(1)} %collective-permute-done.5.refs_4_) | copy-start | bytes 3096580
  40.9 32.0 %collective-permute-start.9 = (bf16[36,112,128]{2,1,0:T(8,128)(2,1)S(1)}, bf16[36,112,128]{2,1,0:T(8,128)(2,1)S(1)}, u32[]{:S(2)}, u32[]{:S(2)}) collective-permute-start(bf16[36,112,128]{2,1,0:T(8,128)(2,1)S(1)} %dress.6), channel_id=1, source_target_pairs={{0,6},{1,14},{2,0},{3,8},{4,2},{5,10},{6,4},{7,12},{8,7},{9,15},{1... | collective-permute-start | bytes 3096584 | tf_op jit(solution)/shard_map/ppermute | solution.py:337
  51.6 55.7 %collective-permute-start.3 = (bf16[36,112,128]{2,1,0:T(8,128)(2,1)S(1)}, bf16[36,112,128]{2,1,0:T(8,128)(2,1)S(1)}, u32[]{:S(2)}, u32[]{:S(2)}) collective-permute-start(bf16[36,112,128]{2,1,0:T(8,128)(2,1)S(1)} %collective-permute-done.2), channel_id=1, source_target_pairs={{0,0},{1,8},{2,2},{3,10},{4,4},{5,12},{6,6},{7,14},{8,1},{9,9},{10... | collective-permute-start | bytes 3096584 | tf_op jit(solution)/shard_map/ppermute | solution.py:337
  52.4 55.0 %collective-permute-start.1 = (bf16[36,112,128]{2,1,0:T(8,128)(2,1)S(1)}, bf16[36,112,128]{2,1,0:T(8,128)(2,1)S(1)}, u32[]{:S(2)}, u32[]{:S(2)}) collective-permute-start(bf16[36,112,128]{2,1,0:T(8,128)(2,1)S(1)} %collective-permute-done.refs_0_), channel_id=1, source_target_pairs={{0,8},{1,9},{2,10},{3,11},{4,12},{5,13},{6,14},{7,15},{8,0},{9,1},... | collective-permute-start | bytes 3096584 | tf_op jit(solution)/shard_map/ppermute | solution.py:337
  72.9 53.8 %copy-start.4 = (bf16[36,112,128]{2,1,0:T(8,128)(2,1)}, bf16[36,112,128]{2,1,0:T(8,128)(2,1)S(1)}, u32[]{:S(2)}) copy-start(bf16[36,112,128]{2,1,0:T(8,128)(2,1)S(1)} %collective-permute-done.9.refs_12_) | copy-start | bytes 3096580
  72.9 46.3 %collective-permute-start.10 = (bf16[36,112,128]{2,1,0:T(8,128)(2,1)S(1)}, bf16[36,112,128]{2,1,0:T(8,128)(2,1)}, u32[]{:S(2)}, u32[]{:S(2)}) collective-permute-start(bf16[36,112,128]{2,1,0:T(8,128)(2,1)S(1)} %dress.7), channel_id=1, source_target_pairs={{0,4},{1,12},{2,6},{3,14},{4,0},{5,8},{6,2},{7,10},{8,5},{9,13},{1... | collective-permute-start | bytes 3096584 | tf_op jit(solution)/shard_map/ppermute | solution.py:337
  72.9 100.0 %copy-start.1 = (s32[8,2]{0,1:T(2,128)S(1)}, s32[8,2]{0,1:T(2,128)}, u32[]{:S(2)}) copy-start(s32[8,2]{0,1:T(2,128)} %param.9) | copy-start | bytes 196
  103.0 23.6 %collective-permute-start.7 = (bf16[36,112,128]{2,1,0:T(8,128)(2,1)S(1)}, bf16[36,112,128]{2,1,0:T(8,128)(2,1)}, u32[]{:S(2)}, u32[]{:S(2)}) collective-permute-start(bf16[36,112,128]{2,1,0:T(8,128)(2,1)S(1)} %collective-permute-done.5.refs_4_), channel_id=1, source_target_pairs={{0,16},{1,17},{2,18},{3,19},{4,20},{5,21},{6,22},{7,23},{8,24},{9,... | collective-permute-start | bytes 3096584 | tf_op jit(solution)/shard_map/ppermute | solution.py:337
  104.5 26.6 %collective-permute-start.6 = (bf16[36,112,128]{2,1,0:T(8,128)(2,1)S(1)}, bf16[36,112,128]{2,1,0:T(8,128)(2,1)S(1)}, u32[]{:S(2)}, u32[]{:S(2)}) collective-permute-start(bf16[36,112,128]{2,1,0:T(8,128)(2,1)S(1)} %collective-permute-done.5.refs_4_), channel_id=1, source_target_pairs={{0,8},{1,9},{2,10},{3,11},{4,12},{5,13},{6,14},{7,15},{8,0},{9,1},... | collective-permute-start | bytes 3096584 | tf_op jit(solution)/shard_map/ppermute | solution.py:337
  107.3 41.5 %copy-start.5 = (bf16[36,112,128]{2,1,0:T(8,128)(2,1)}, bf16[36,112,128]{2,1,0:T(8,128)(2,1)S(1)}, u32[]{:S(2)}) copy-start(bf16[36,112,128]{2,1,0:T(8,128)(2,1)S(1)} %collective-permute-done.3.refs_2_) | copy-start | bytes 3096580
  107.3 23.9 %collective-permute-start.4 = (bf16[36,112,128]{2,1,0:T(8,128)(2,1)S(1)}, bf16[36,112,128]{2,1,0:T(8,128)(2,1)S(1)}, u32[]{:S(2)}, u32[]{:S(2)}) collective-permute-start(bf16[36,112,128]{2,1,0:T(8,128)(2,1)S(1)} %collective-permute-done.3.refs_2_), channel_id=1, source_target_pairs={{0,8},{1,9},{2,10},{3,11},{4,12},{5,13},{6,14},{7,15},{8,0},{9,1},... | collective-permute-start | bytes 3096584 | tf_op jit(solution)/shard_map/ppermute | solution.py:337
  107.4 66.2 %copy-start.6 = (bf16[36,112,128]{2,1,0:T(8,128)(2,1)}, bf16[36,112,128]{2,1,0:T(8,128)(2,1)S(1)}, u32[]{:S(2)}) copy-start(bf16[36,112,128]{2,1,0:T(8,128)(2,1)S(1)} %collective-permute-done.1.refs_1_) | copy-start | bytes 3096580
  107.4 41.4 %collective-permute-start.15 = (bf16[36,112,128]{2,1,0:T(8,128)(2,1)S(1)}, bf16[36,112,128]{2,1,0:T(8,128)(2,1)}, u32[]{:S(2)}, u32[]{:S(2)}) collective-permute-start(bf16[36,112,128]{2,1,0:T(8,128)(2,1)S(1)} %collective-permute-done.9.refs_12_), channel_id=1, source_target_pairs={{0,16},{1,17},{2,18},{3,19},{4,20},{5,21},{6,22},{7,23},{8,24},{9,... | collective-permute-start | bytes 3096584 | tf_op jit(solution)/shard_map/ppermute | solution.py:337
  119.2 51.7 %collective-permute-start.12 = (bf16[36,112,128]{2,1,0:T(8,128)(2,1)}, bf16[36,112,128]{2,1,0:T(8,128)(2,1)}, u32[]{:S(2)}, u32[]{:S(2)}) collective-permute-start(bf16[36,112,128]{2,1,0:T(8,128)(2,1)} %collective-permute-done.10.refs_8_), channel_id=1, source_target_pairs={{0,16},{1,17},{2,18},{3,19},{4,20},{5,21},{6,22},{7,23},{8,24},{9,... | collective-permute-start | bytes 3096584 | tf_op jit(solution)/shard_map/ppermute | solution.py:337
  126.6 46.9 %collective-permute-start.14 = (bf16[36,112,128]{2,1,0:T(8,128)(2,1)S(1)}, bf16[36,112,128]{2,1,0:T(8,128)(2,1)}, u32[]{:S(2)}, u32[]{:S(2)}) collective-permute-start(bf16[36,112,128]{2,1,0:T(8,128)(2,1)S(1)} %collective-permute-done.9.refs_12_), channel_id=1, source_target_pairs={{0,8},{1,9},{2,10},{3,11},{4,12},{5,13},{6,14},{7,15},{8,0},{9,1},... | collective-permute-start | bytes 3096584 | tf_op jit(solution)/shard_map/ppermute | solution.py:337
  131.1 22.1 %copy-start.7 = (bf16[36,112,128]{2,1,0:T(8,128)(2,1)}, bf16[36,112,128]{2,1,0:T(8,128)(2,1)S(1)}, u32[]{:S(2)}) copy-start(bf16[36,112,128]{2,1,0:T(8,128)(2,1)S(1)} %collective-permute-done.6.refs_5_) | copy-start | bytes 3096580
  131.1 42.5 %collective-permute-start.8 = (bf16[36,112,128]{2,1,0:T(8,128)(2,1)}, bf16[36,112,128]{2,1,0:T(8,128)(2,1)}, u32[]{:S(2)}, u32[]{:S(2)}) collective-permute-start(bf16[36,112,128]{2,1,0:T(8,128)(2,1)} %collective-permute-done.7.refs_6_), channel_id=1, source_target_pairs={{0,8},{1,9},{2,10},{3,11},{4,12},{5,13},{6,14},{7,15},{8,0},{9,1},... | collective-permute-start | bytes 3096584 | tf_op jit(solution)/shard_map/ppermute | solution.py:337
  131.2 39.7 %copy-start.8 = (bf16[36,112,128]{2,1,0:T(8,128)(2,1)}, bf16[36,112,128]{2,1,0:T(8,128)(2,1)S(1)}, u32[]{:S(2)}) copy-start(bf16[36,112,128]{2,1,0:T(8,128)(2,1)S(1)} %collective-permute-done.4.refs_3_) | copy-start | bytes 3096580
  131.2 42.4 %collective-permute-start.11 = (bf16[36,112,128]{2,1,0:T(8,128)(2,1)}, bf16[36,112,128]{2,1,0:T(8,128)(2,1)}, u32[]{:S(2)}, u32[]{:S(2)}) collective-permute-start(bf16[36,112,128]{2,1,0:T(8,128)(2,1)} %collective-permute-done.10.refs_8_), channel_id=1, source_target_pairs={{0,8},{1,9},{2,10},{3,11},{4,12},{5,13},{6,14},{7,15},{8,0},{9,1},... | collective-permute-start | bytes 3096584 | tf_op jit(solution)/shard_map/ppermute | solution.py:337
  148.8 24.8 %collective-permute-start.16 = (bf16[36,112,128]{2,1,0:T(8,128)(2,1)}, bf16[36,112,128]{2,1,0:T(8,128)(2,1)}, u32[]{:S(2)}, u32[]{:S(2)}) collective-permute-start(bf16[36,112,128]{2,1,0:T(8,128)(2,1)} %collective-permute-done.15.refs_14_), channel_id=1, source_target_pairs={{0,8},{1,9},{2,10},{3,11},{4,12},{5,13},{6,14},{7,15},{8,0},{9,1},... | collective-permute-start | bytes 3096584 | tf_op jit(solution)/shard_map/ppermute | solution.py:337
  170.9 4.6 %collective-permute-start.13 = (bf16[36,112,128]{2,1,0:T(8,128)(2,1)}, bf16[36,112,128]{2,1,0:T(8,128)(2,1)}, u32[]{:S(2)}, u32[]{:S(2)}) collective-permute-start(bf16[36,112,128]{2,1,0:T(8,128)(2,1)} %collective-permute-done.12.refs_10_), channel_id=1, source_target_pairs={{0,8},{1,9},{2,10},{3,11},{4,12},{5,13},{6,14},{7,15},{8,0},{9,1},... | collective-permute-start | bytes 3096584 | tf_op jit(solution)/shard_map/ppermute | solution.py:337

commit v3 on v2

--- a/solution.py
+++ b/solution.py
@@ -9,6 +9,7 @@
 
 BLK = 4
 QUAD = 4
+AMPS = 2
 ROWS = 16
 LANES = 128
 CORES = 2
@@ -137,39 +138,81 @@
     )(z, spread, *([chol_ov] * count), *([chol_vv] * count))
 
 
+def relayout_kernel(p, in_ref, out_ref):
+    rows = ROWS * ROWS
+    to = lax.broadcasted_iota(jnp.int32, (rows, rows), 0)
+    frm = lax.broadcasted_iota(jnp.int32, (rows, rows), 1)
+    turn = (to % ROWS * ROWS + to // ROWS == frm).astype(jnp.float32).astype(jnp.bfloat16)
+    turned = lax.dot_general(
+        turn, in_ref[...].reshape(rows, p.d), NN, preferred_element_type=jnp.float32
+    )
+    out_ref[...] = turned.astype(jnp.bfloat16).reshape(ROWS, ROWS, p.d)
+
+
+def relayout(p, amplitudes, part):
+    count = p.c // AMPS
+    blocks = count // ROWS
+    return pl.pallas_call(
+        functools.partial(relayout_kernel, p),
+        out_shape=jax.ShapeDtypeStruct((count, p.ij, p.d), jnp.bfloat16),
+        grid=(blocks, p.ij // ROWS),
+        in_specs=[pl.BlockSpec((ROWS, ROWS, p.d), lambda c, i: (i, part * blocks + c, 0))],
+        out_specs=pl.BlockSpec((ROWS, ROWS, p.d), lambda c, i: (c, i, 0)),
+        cost_estimate=pl.CostEstimate(
+            flops=2 * count * p.ij * p.d * ROWS * ROWS,
+            bytes_accessed=4 * count * p.ij * p.d,
+            transcendentals=0,
+        ),
+        name="relayout",
+    )(amplitudes)
+
+
 def ladder_kernel(p, parts, group, place_ref, blocks_ref, *refs):
-    count = 2 * p.js * p.xs
-    pieces, (amps, out), scratch = refs[:count], refs[count : count + 2], refs[count + 2 :]
+    pieces, amps, out = refs[: p.js], refs[p.js : p.js + AMPS], refs[p.js + AMPS]
+    scratch = refs[p.js + AMPS + 1 :]
     vectors, left_main, left_tail, spread_tail, tiles, held, total, piece_sem, amp_sem = scratch
-    w, z, core, chunk = p.window, place_ref[0], place_ref[1], place_ref[2]
+    w, z, chunk = p.window, place_ref[0], place_ref[1]
     quads = p.c // QUAD
     here = quads // parts
     rows = here * ROWS
     steps = here // group
     wide = group * QUAD * p.ij
-
-    def fetch(step, slot):
-        return pltpu.make_async_copy(
-            amps.at[pl.ds(pl.multiple_of(step * wide, wide), wide)], held.at[slot], amp_sem.at[slot]
-        )
+    each = parts * steps // AMPS
+
+    class Fetch:
+        def __init__(self, step, slot):
+            self.step, self.slot = step, slot
+
+        def copy(self, amp, step):
+            at = pl.ds(pl.multiple_of(step * wide, wide), wide)
+            return pltpu.make_async_copy(amp.at[at], held.at[self.slot], amp_sem.at[self.slot])
+
+        def start(self):
+            for n, amp in enumerate(amps):
+
+                @pl.when(self.step // each == n)
+                def _():
+                    self.copy(amp, self.step - n * each).start()
+
+        def wait(self):
+            self.copy(amps[0], 0).wait()
 
     copies = []
     for o in range(p.js):
-        for r in range(p.xs):
-            for other in range(CORES):
-                parity = core if other == 0 else 1 - core
-                origin = CORES * lax.rem(z - o + p.js, p.js) + parity
-                row = pl.multiple_of(origin * p.cpad, ROWS)
-                copies.append(
-                    pltpu.make_async_copy(
-                        pieces[(o * p.xs + r) * CORES + other],
-                        vectors.at[:, pl.ds(row, p.cpad), r * LANES : (r + 1) * LANES],
-                        piece_sem.at[(o * p.xs + r) * CORES + other],
-                    )
+        for source in range(p.n_aux):
+            r, parity = source // CORES, source % CORES
+            origin = CORES * lax.rem(z - o + p.js, p.js) + parity
+            row = pl.multiple_of(origin * p.cpad, ROWS)
+            copies.append(
+                pltpu.make_async_copy(
+                    pieces[o].at[source],
+                    vectors.at[:, pl.ds(row, p.cpad), r * LANES : (r + 1) * LANES],
+                    piece_sem.at[o * p.n_aux + source],
                 )
+            )
     for copy in copies:
         copy.start()
-    fetch(0, 0).start()
+    Fetch(jnp.int32(0), 0).start()
     for copy in copies:
         copy.wait()
 
@@ -243,9 +286,9 @@
 
             @pl.when(at + 1 < parts * steps)
             def _():
-                fetch(at + 1, 1 - slot).start()
-
-            fetch(at, slot).wait()
+                Fetch(at + 1, 1 - slot).start()
+
+            Fetch(at, slot).wait()
             width = QUAD * p.ij
             for n in range(group):
                 total[...] += lax.dot_general(
@@ -282,7 +325,7 @@
         functools.partial(ladder_kernel, p, parts, group),
         out_shape=jax.ShapeDtypeStruct((p.gf, BLK, LANES), jnp.float32),
         in_specs=[pl.BlockSpec(memory_space=pltpu.SMEM)] * 2
-        + [pl.BlockSpec(memory_space=pl.ANY)] * (len(pieces) + 1),
+        + [pl.BlockSpec(memory_space=pl.ANY)] * (len(pieces) + AMPS),
         out_specs=pl.BlockSpec(memory_space=pltpu.VMEM),
         scratch_shapes=[
             pltpu.VMEM((p.planes, p.d, p.k), jnp.bfloat16),
@@ -292,17 +335,17 @@
             pltpu.VMEM((quads // parts, p.gf, ROWS, p.d), jnp.bfloat16),
             pltpu.VMEM((2, group * width, p.d), jnp.bfloat16),
             pltpu.VMEM((p.gf * ROWS, width), jnp.float32),
-            pltpu.SemaphoreType.DMA((len(pieces),)),
+            pltpu.SemaphoreType.DMA((p.js * p.n_aux,)),
             pltpu.SemaphoreType.DMA((2,)),
         ],
         compiler_params=pltpu.CompilerParams(vmem_limit_bytes=63 * 2**20),
         cost_estimate=pl.CostEstimate(
             flops=2 * p.gf * BLK * p.c * p.d * p.k,
-            bytes_accessed=2 * (len(pieces) * p.planes * p.cpad * LANES + p.c * p.ij * p.d),
+            bytes_accessed=2 * (p.js * p.n_aux * p.planes * p.cpad * LANES + p.c * p.ij * p.d),
             transcendentals=0,
         ),
         name="ladder",
-    )(place, blocks, *pieces, amps)
+    )(place, blocks, *pieces, *amps)
 
 
 def pad_columns(array, axis, cols, cpad):
@@ -322,7 +365,7 @@
     p = Plan(window, chol_ov.shape[0], cols, aux_dev, n_aux, n_pair, amplitudes.shape[0])
     me_aux, me_pair = lax.axis_index("aux"), lax.axis_index("pair")
     z = me_pair // CORES
-    place = jnp.stack([z, me_aux % CORES, me_aux]).astype(jnp.int32)
+    place = jnp.stack([z, me_aux]).astype(jnp.int32)
 
     chol_vv = pad_columns(chol_vv, 1, cols, p.cpad)
     chol_ov = pad_columns(chol_ov, 1, cols, p.cpad)
@@ -344,12 +387,6 @@
                 CORES * ((q // CORES + o) % p.js) + a % CORES,
             ),
         )
-
-    def along_x(array, r):
-        return permute(array, lambda a, q: (CORES * ((a // CORES + r) % p.xs) + a % CORES, q))
-
-    def to_core(array):
-        return permute(array, lambda a, q: (a ^ 1, q))
 
     order = sorted(range(p.js), key=lambda o: min(o, p.js - o))
     messages = {}
@@ -365,26 +402,25 @@
             spread, messages[o] = lax.optimization_barrier((spread, messages[o]))
 
     messages[order[-1]], amplitudes = lax.optimization_barrier((messages[order[-1]], amplitudes))
-    amps = pad_columns(pad_columns(amplitudes, 1, cols, p.cpad), 2, cols, p.cpad)
-    amps = jnp.transpose(amps, (1, 0, 2)).reshape(p.c * p.ij, p.d)
+    amplitudes = pad_columns(pad_columns(amplitudes, 1, cols, p.cpad), 2, cols, p.cpad)
+    amps = [relayout(p, amplitudes, part) for part in range(AMPS)]
 
     found = {}
-    before = None
+    before = turned_here
     for place_in_order, o in enumerate(order):
         if o == 0:
-            turned = [turned_here]
-            turned += [to_slice(along_x(messages[0], r), 0) for r in range(1, p.xs)]
+            own = turned_here
         else:
-            message = messages[o]
-            if before is not None:
-                message, before = lax.optimization_barrier((message, before))
-            own = to_slice(message, o)
-            before = own
-            if place_in_order == p.js - 2:
-                own, amps = lax.optimization_barrier((own, amps))
-            turned = [own] + [along_x(own, r) for r in range(1, p.xs)]
-        found[o] = [piece for array in turned for piece in (array, to_core(array))]
-    pieces = [piece for o in range(p.js) for piece in found[o]]
+            message, before = lax.optimization_barrier((messages[o], before))
+            own = before = to_slice(message, o)
+        if place_in_order == 1:
+            own, messages[order[2]] = lax.optimization_barrier((own, messages[order[2]]))
+        part = place_in_order - (p.js - AMPS)
+        if part >= 0:
+            own, amps[part] = lax.optimization_barrier((own, amps[part]))
+        found[o] = lax.all_gather(own, "aux", axis=0, tiled=False)
+    amps = [amp.reshape(-1, p.d) for amp in amps]
+    pieces = [found[o] for o in range(p.js)]
 
     partial_terms = ladder(p, place, assignment, pieces, amps)
     share = p.ij // n_aux

time: 268 us -> 277 us (1.034)
  Pallas kernels: 110 us -> 157 us
  starting transfers between devices: 46.5 us -> 6.28 us
  local copies, waits for them, and re-layouts: 34.4 us -> 7.18 us
  waiting for transfers between devices: 62.4 us -> 78.8 us
  between operations: 0.21 us -> 13.3 us
    all_gather x0 -> x4, waiting for transfers between devices: none -> 47.5 us  [shards(): found[o] = lax.all_gather(own, 'aux', axis=0, tiled=False)]
    pallas_call x0 -> x2, Pallas kernels: none -> 45.8 us  [relayout(): pl.pallas_call(functools.partial(relayout_kernel, p), out_shape=jax.Shape...]
    ppermute x17 -> x4, starting transfers between devices: 46.5 us -> 6.16 us  [permute(): return lax.ppermute(array, ('aux', 'pair'), pairs)]
    ppermute x17 -> x4, waiting for transfers between devices: 62.4 us -> 31.2 us  [permute(): return lax.ppermute(array, ('aux', 'pair'), pairs)]
    transpose x1 -> x0, local copies, waits for them, and re-layouts: 30.1 us -> none  [shards(): amps = jnp.transpose(amps, (1, 0, 2)).reshape(p.c * p.ij, p.d)]
    unnamed x22 -> x14, local copies, waits for them, and re-layouts: 1.79 us -> 4.67 us
  transfers between devices with their start and end apart: 17 -> 8, of which waited for: 6 -> 4; matrix products, arithmetic and copies ran while one was open for 12% -> 0% of each run, Pallas kernels for 10% -> 26%
where the time goes in v3:
time: 277 us; the launch traced here: 275 us
  Pallas kernels  157 us (57%)
  waiting for transfers between devices  78.8 us (28%)
  between operations  13.3 us (5%)
  blocking collectives  11.6 us (4%)
  local copies, waits for them, and re-layouts  7.18 us (3%)
  starting transfers between devices  6.28 us (2%)
    pallas_call x1, Pallas kernels, ladder(): pl.pallas_call(functools.partial(ladder_kernel, p, parts, group), out_sha...  75.7 us
    all_gather x4, waiting for transfers between devices, shards(): found[o] = lax.all_gather(own, 'aux', axis=0, tiled=False)  47.5 us
    pallas_call x2, Pallas kernels, relayout(): pl.pallas_call(functools.partial(relayout_kernel, p), out_shape=jax.Shape...  45.8 us
    pallas_call x4, Pallas kernels, dress(): pl.pallas_call(functools.partial(dress_kernel, p, offset), out_shape=jax....  34.8 us
    ppermute x4, waiting for transfers between devices, permute(): return lax.ppermute(array, ('aux', 'pair'), pairs)  31.2 us
    all_to_all x1, blocking collectives, shards(): lax.all_to_all(terms, ('aux', 'pair'), split_axis=0, concat_axis=0, tiled...  11.6 us
    ppermute x4, starting transfers between devices, permute(): return lax.ppermute(array, ('aux', 'pair'), pairs)  6.16 us
  transfers between devices with their start and end apart: 8, of which 4 were waited for; matrix products, arithmetic and copies ran while one was open for 0% of the time, Pallas kernels for 26%

profile of v3, /device:TPU:0, one launch (start us, length us, event | category | flops | bytes accessed | tf_op | source)
XLA Modules:
  0.0 275.0 jit_solution(11348886237841951189)
XLA Ops:
  6.5 0.0 all-gather.9.cloned.1.call-start
  6.5 0.8 copy.11.t1_ref
  7.3 0.8 spread.1.a_ref
  8.1 0.1 pad_add_fusion.z_ref.place_ref
  8.2 0.0 copy-start.1
  8.2 8.5 %dress.4 = bf16[36,112,128]{2,1,0:T(8,128)(2,1)S(1)} custom-call(s32[2]{0:T(128)S(1)} %pad_add_fusion.z_ref.place_ref, bf16[512,1600]{1,0:T(8,128)(2,1)S(1)} %spread.1.a_ref, bf16[100,112,576]{2,1,0:T(8,128)(2,1)} %refs_1_.7, bf16[100,112,576]{2,1,0:T(8,128)(2,1)} %refs_1_.7, bf16[32,112,576]{2,1,0:T(8,128)(2,1)} %refs_3_.7, bf16[32,112,576]{2,1,0:T(8,128)(2,1)} %refs_3_.7), custom_call_target="tpu_custom_call" | custom-call | flops 2936012800 | bytes 9404416 | tf_op jit(solution)/shard_map/dress/pallas_call | solution.py:120
  16.7 0.7 collective-permute-start
  17.4 9.3 %dress.5 = bf16[36,112,128]{2,1,0:T(8,128)(2,1)} custom-call(s32[2]{0:T(128)S(1)} %pad_add_fusion.z_ref.place_ref, bf16[512,1600]{1,0:T(8,128)(2,1)S(1)} %spread.1.a_ref, bf16[100,112,576]{2,1,0:T(8,128)(2,1)} %refs_1_.7, bf16[100,112,576]{2,1,0:T(8,128)(2,1)} %refs_1_.7, bf16[32,112,576]{2,1,0:T(8,128)(2,1)} %refs_3_.7, bf16[32,112,576]{2,1,0:T(8,128)(2,1)} %refs_3_.7), custom_call_target="tpu_custom_call" | custom-call | flops 2936012800 | bytes 9404416 | tf_op jit(solution)/shard_map/dress/pallas_call | solution.py:120
  26.8 0.0 collective-permute-done
  26.8 0.0 copy-start.2
  26.8 1.0 copy-done.2
  27.7 0.0 all-gather.9.cloned.1.call-update
  27.8 0.0 all-gather.11.cloned.1.call-start
  27.8 3.1 %collective-permute-start.1 = (bf16[36,112,128]{2,1,0:T(8,128)(2,1)}, bf16[36,112,128]{2,1,0:T(8,128)(2,1)}, u32[]{:S(2)}, u32[]{:S(2)}) collective-permute-start(bf16[36,112,128]{2,1,0:T(8,128)(2,1)} %dress.5), channel_id=1, source_target_pairs={{0,2},{1,10},{2,4},{3,12},{4,6},{5,14},{6,0},{7,8},{8,3},{9,11},{1... | collective-permute-start | bytes 3096584 | tf_op jit(solution)/shard_map/ppermute | solution.py:380
  30.9 8.5 %dress.6 = bf16[36,112,128]{2,1,0:T(8,128)(2,1)S(1)} custom-call(s32[2]{0:T(128)S(1)} %pad_add_fusion.z_ref.place_ref, bf16[512,1600]{1,0:T(8,128)(2,1)S(1)} %spread.1.a_ref, bf16[100,112,576]{2,1,0:T(8,128)(2,1)} %refs_1_.7, bf16[100,112,576]{2,1,0:T(8,128)(2,1)} %refs_1_.7, bf16[32,112,576]{2,1,0:T(8,128)(2,1)} %refs_3_.7, bf16[32,112,576]{2,1,0:T(8,128)(2,1)} %refs_3_.7), custom_call_target="tpu_custom_call" | custom-call | flops 2936012800 | bytes 9404416 | tf_op jit(solution)/shard_map/dress/pallas_call | solution.py:120
  39.4 11.0 %collective-permute-done.1 = bf16[36,112,128]{2,1,0:T(8,128)(2,1)} collective-permute-done((bf16[36,112,128]{2,1,0:T(8,128)(2,1)}, bf16[36,112,128]{2,1,0:T(8,128)(2,1)}, u32[]{:S(2)}, u32[]{:S(2)}) %collective-permute-start.1) | collective-permute-done | bytes 1032224 | tf_op jit(solution)/shard_map/ppermute | solution.py:380
  50.4 0.0 all-gather.11.cloned.1.call-update
  50.4 0.0 all-gather.15.cloned.1.call-start
  50.5 2.3 collective-permute-start.2
  52.7 0.0 copy-done.1
  52.7 8.5 %dress.7 = bf16[36,112,128]{2,1,0:T(8,128)(2,1)S(1)} custom-call(s32[2]{0:T(128)S(1)} %pad_add_fusion.z_ref.place_ref, bf16[512,1600]{1,0:T(8,128)(2,1)S(1)} %spread.1.a_ref, bf16[100,112,576]{2,1,0:T(8,128)(2,1)} %refs_1_.7, bf16[100,112,576]{2,1,0:T(8,128)(2,1)} %refs_1_.7, bf16[32,112,576]{2,1,0:T(8,128)(2,1)} %refs_3_.7, bf16[32,112,576]{2,1,0:T(8,128)(2,1)} %refs_3_.7), custom_call_target="tpu_custom_call" | custom-call | flops 2936012800 | bytes 9404416 | tf_op jit(solution)/shard_map/dress/pallas_call | solution.py:120
  61.2 0.0 copy-start
  61.2 1.0 copy-done
  62.2 23.0 %relayout.3 = bf16[112,64,896]{2,1,0:T(8,128)(2,1)} custom-call(bf16[64,224,896]{2,1,0:T(8,128)(2,1)} %in_ref.1), custom_call_target="tpu_custom_call" | custom-call | flops 3288334336 | bytes 25690112 | tf_op jit(solution)/shard_map/relayout/pallas_call | solution.py:155
  85.2 0.0 collective-permute-done.2
  85.2 0.0 all-gather.15.cloned.1.call-update
  85.2 0.0 copy-start.4
  85.3 0.0 all-gather.13.cloned.1.call-start
  85.3 0.1 collective-permute-start.3
  85.4 22.8 %relayout.2 = bf16[112,64,896]{2,1,0:T(8,128)(2,1)} custom-call(bf16[64,224,896]{2,1,0:T(8,128)(2,1)} %in_ref.1), custom_call_target="tpu_custom_call" | custom-call | flops 3288334336 | bytes 25690112 | tf_op jit(solution)/shard_map/relayout/pallas_call | solution.py:155
  108.2 20.2 %collective-permute-done.3 = bf16[36,112,128]{2,1,0:T(8,128)(2,1)S(1)} collective-permute-done((bf16[36,112,128]{2,1,0:T(8,128)(2,1)}, bf16[36,112,128]{2,1,0:T(8,128)(2,1)S(1)}, u32[]{:S(2)}, u32[]{:S(2)}) %collective-permute-start.3) | collective-permute-done | bytes 1032224 | tf_op jit(solution)/shard_map/ppermute | solution.py:380
  128.4 0.0 copy-start.3
  128.4 1.0 copy-done.3
  129.3 0.0 all-gather.13.cloned.1.call-update
  129.4 0.0 copy-done.4
  129.4 0.7 copy.12.blocks_ref
  130.1 12.0 %all-gather.15.cloned.1.call-done = bf16[144,112,128]{2,1,0:T(8,128)(2,1)} async-done(((bf16[36,112,128]{2,1,0:T(8,128)(2,1)}), bf16[144,112,128]{2,1,0:T(8,128)(2,1)}) %all-gather.15.cloned.1.call-update) | async-done | bytes 4128784 | tf_op jit(solution)/shard_map/all_gather | solution.py:421
  142.0 35.6 %all-gather.13.cloned.1.call-done = bf16[144,112,128]{2,1,0:T(8,128)(2,1)} async-done(((bf16[36,112,128]{2,1,0:T(8,128)(2,1)}), bf16[144,112,128]{2,1,0:T(8,128)(2,1)}) %all-gather.13.cloned.1.call-update) | async-done | bytes 4128784 | tf_op jit(solution)/shard_map/all_gather | solution.py:421
  177.6 75.7 %ladder.1 = f32[32,4,128]{2,1,0:T(4,128)} custom-call(s32[2]{0:T(128)} %copy-done.1, s32[8,2]{1,0:T(8,128)} %copy.12.blocks_ref, bf16[4,36,112,128]{3,2,1,0:T(8,128)(2,1)} %bitcast.22, bf16[4,36,112,128]{3,2,1,0:T(8,128)(2,1)} %bitcast.23, bf16[4,36,112,128]{3,2,1,0:T(8,128)(2,1)} %bitcast.25, bf16[4,36,112,128]{3,2,1,0:T(8,128)(2,1)} %bitcast.24, ...), custom_call_target="tpu_custom_call" | custom-call | flops 13153337344 | bytes 42205184 | tf_op jit(solution)/shard_map/ladder/pallas_call | solution.py:324
  253.3 1.0 reshape.14
  254.4 0.2 copy.13
  254.5 0.2 copy.19
  254.7 0.1 reshape.20
  254.8 11.6 %all_to_all.5 = f32[32,1,256]{2,1,0:T(1,128)S(1)} all-to-all(f32[32,1,256]{2,1,0:T(1,128)S(1)} %reshape.20), channel_id=1, replica_groups=mesh['aux'=4,'pair'=8] {'aux','pair'}, dimensions={0} | all-to-all | bytes 65536 | tf_op jit(solution)/shard_map/all_to_all | solution.py:429
  266.4 0.5 broadcast.1
  266.9 0.7 reduce
  267.7 0.1 reshape.21
  267.8 0.7 copy.16
  (3 shorter events, 0.0 us)
Async XLA Ops:
  6.5 123.5 %all-gather.9.cloned.1.call-start = ((), (), s32[]{:S(2)}) async-start(), calls=%async_computation.1 | async-start | bytes 5160960 | tf_op jit(solution)/shard_map/all_gather | solution.py:421
  8.2 44.5 %copy-start.1 = (s32[2]{0:T(128)}, s32[2]{0:T(128)S(1)}, u32[]{:S(2)}) copy-start(s32[2]{0:T(128)S(1)} %pad_add_fusion.z_ref.place_ref) | copy-start | bytes 28
  16.7 10.1 %collective-permute-start = (bf16[36,112,128]{2,1,0:T(8,128)(2,1)S(1)}, bf16[36,112,128]{2,1,0:T(8,128)(2,1)S(1)}, u32[]{:S(2)}, u32[]{:S(2)}) collective-permute-start(bf16[36,112,128]{2,1,0:T(8,128)(2,1)S(1)} %dress.4), channel_id=1, source_target_pairs={{0,0},{1,8},{2,2},{3,10},{4,4},{5,12},{6,6},{7,14},{8,1},{9,9},{10... | collective-permute-start | bytes 3096584 | tf_op jit(solution)/shard_map/ppermute | solution.py:380
  26.8 1.0 copy-start.2
  27.8 102.3 %all-gather.11.cloned.1.call-start = ((), (), s32[]{:S(2)}) async-start(), calls=%async_computation.2 | async-start | bytes 5160960 | tf_op jit(solution)/shard_map/all_gather | solution.py:421
  27.8 22.6 %collective-permute-start.1 = (bf16[36,112,128]{2,1,0:T(8,128)(2,1)}, bf16[36,112,128]{2,1,0:T(8,128)(2,1)}, u32[]{:S(2)}, u32[]{:S(2)}) collective-permute-start(bf16[36,112,128]{2,1,0:T(8,128)(2,1)} %dress.5), channel_id=1, source_target_pairs={{0,2},{1,10},{2,4},{3,12},{4,6},{5,14},{6,0},{7,8},{8,3},{9,11},{1... | collective-permute-start | bytes 3096584 | tf_op jit(solution)/shard_map/ppermute | solution.py:380
  50.4 91.6 %all-gather.15.cloned.1.call-start = ((), (), s32[]{:S(2)}) async-start(), calls=%async_computation.4 | async-start | bytes 5160960 | tf_op jit(solution)/shard_map/all_gather | solution.py:421
  50.5 34.8 %collective-permute-start.2 = (bf16[36,112,128]{2,1,0:T(8,128)(2,1)S(1)}, bf16[36,112,128]{2,1,0:T(8,128)(2,1)}, u32[]{:S(2)}, u32[]{:S(2)}) collective-permute-start(bf16[36,112,128]{2,1,0:T(8,128)(2,1)S(1)} %dress.6), channel_id=1, source_target_pairs={{0,6},{1,14},{2,0},{3,8},{4,2},{5,10},{6,4},{7,12},{8,7},{9,15},{1... | collective-permute-start | bytes 3096584 | tf_op jit(solution)/shard_map/ppermute | solution.py:380
  61.2 1.0 copy-start
  85.2 44.1 %copy-start.4 = (s32[8,2]{0,1:T(2,128)S(1)}, s32[8,2]{0,1:T(2,128)}, u32[]{:S(2)}) copy-start(s32[8,2]{0,1:T(2,128)} %param.9) | copy-start | bytes 196
  85.3 92.3 %all-gather.13.cloned.1.call-start = ((), (), s32[]{:S(2)}) async-start(), calls=%async_computation.3 | async-start | bytes 5160960 | tf_op jit(solution)/shard_map/all_gather | solution.py:421
  85.3 43.1 %collective-permute-start.3 = (bf16[36,112,128]{2,1,0:T(8,128)(2,1)}, bf16[36,112,128]{2,1,0:T(8,128)(2,1)S(1)}, u32[]{:S(2)}, u32[]{:S(2)}) collective-permute-start(bf16[36,112,128]{2,1,0:T(8,128)(2,1)} %copy-done), channel_id=1, source_target_pairs={{0,4},{1,12},{2,6},{3,14},{4,0},{5,8},{6,2},{7,10},{8,5},{9,13},{1... | collective-permute-start | bytes 3096584 | tf_op jit(solution)/shard_map/ppermute | solution.py:380
  128.4 1.0 copy-start.3
Sparse Core Ops, SparseCore 0:
  27.9 42.6 all-gather.8
  72.2 34.1 all-gather.10
  107.9 34.0 all-gather.14
  143.4 34.1 all-gather.12

commit v4 on v3

--- a/solution.py
+++ b/solution.py
@@ -10,6 +10,7 @@
 BLK = 4
 QUAD = 4
 AMPS = 2
+DEEP = 256
 ROWS = 16
 LANES = 128
 CORES = 2
@@ -111,7 +112,8 @@
             )
         found.append(
             pl.BlockSpec(
-                (lead, ROWS, p.tail_width), lambda i, z: (0, i, p.tail_from // p.tail_width)
+                (lead, ROWS, p.tail_width),
+                lambda i, z: (0, i, p.tail_from // p.tail_width),
             )
         )
         return found
@@ -143,10 +145,10 @@
     to = lax.broadcasted_iota(jnp.int32, (rows, rows), 0)
     frm = lax.broadcasted_iota(jnp.int32, (rows, rows), 1)
     turn = (to % ROWS * ROWS + to // ROWS == frm).astype(jnp.float32).astype(jnp.bfloat16)
-    turned = lax.dot_general(
-        turn, in_ref[...].reshape(rows, p.d), NN, preferred_element_type=jnp.float32
-    )
-    out_ref[...] = turned.astype(jnp.bfloat16).reshape(ROWS, ROWS, p.d)
+    for low in range(0, p.ij, ROWS):
+        block = in_ref[low : low + ROWS].reshape(rows, p.d)
+        turned = lax.dot_general(turn, block, NN, preferred_element_type=jnp.float32)
+        out_ref[:, low : low + ROWS] = turned.astype(jnp.bfloat16).reshape(ROWS, ROWS, p.d)
 
 
 def relayout(p, amplitudes, part):
@@ -155,9 +157,10 @@
     return pl.pallas_call(
         functools.partial(relayout_kernel, p),
         out_shape=jax.ShapeDtypeStruct((count, p.ij, p.d), jnp.bfloat16),
-        grid=(blocks, p.ij // ROWS),
-        in_specs=[pl.BlockSpec((ROWS, ROWS, p.d), lambda c, i: (i, part * blocks + c, 0))],
-        out_specs=pl.BlockSpec((ROWS, ROWS, p.d), lambda c, i: (c, i, 0)),
+        grid=(blocks,),
+        in_specs=[pl.BlockSpec((p.ij, ROWS, p.d), lambda c: (0, part * blocks + c, 0))],
+        out_specs=pl.BlockSpec((ROWS, p.ij, p.d), lambda c: (c, 0, 0)),
+        compiler_params=pltpu.CompilerParams(vmem_limit_bytes=40 * 2**20),
         cost_estimate=pl.CostEstimate(
             flops=2 * count * p.ij * p.d * ROWS * ROWS,
             bytes_accessed=4 * count * p.ij * p.d,
@@ -167,138 +170,124 @@
     )(amplitudes)
 
 
-def ladder_kernel(p, parts, group, place_ref, blocks_ref, *refs):
-    pieces, amps, out = refs[: p.js], refs[p.js : p.js + AMPS], refs[p.js + AMPS]
-    scratch = refs[p.js + AMPS + 1 :]
-    vectors, left_main, left_tail, spread_tail, tiles, held, total, piece_sem, amp_sem = scratch
+def ladder_kernel(p, group, place_ref, blocks_ref, *refs):
+    count = p.js * p.xs
+    pieces, amps, out = refs[:count], refs[count : count + AMPS], refs[count + AMPS]
+    scratch = refs[count + AMPS + 1 :]
+    vectors, left, strided, tiles, held, total, piece_sem, amp_sem = scratch
     w, z, chunk = p.window, place_ref[0], place_ref[1]
     quads = p.c // QUAD
-    here = quads // parts
-    rows = here * ROWS
-    steps = here // group
-    wide = group * QUAD * p.ij
-    each = parts * steps // AMPS
-
-    class Fetch:
-        def __init__(self, step, slot):
-            self.step, self.slot = step, slot
-
-        def copy(self, amp, step):
-            at = pl.ds(pl.multiple_of(step * wide, wide), wide)
-            return pltpu.make_async_copy(amp.at[at], held.at[self.slot], amp_sem.at[self.slot])
-
-        def start(self):
-            for n, amp in enumerate(amps):
-
-                @pl.when(self.step // each == n)
-                def _():
-                    self.copy(amp, self.step - n * each).start()
-
-        def wait(self):
-            self.copy(amps[0], 0).wait()
+    width = QUAD * p.ij
+    steps = quads // group
+    each = steps // AMPS
+    spans = [slice(low, min(low + DEEP, p.d)) for low in range(0, p.d, DEEP)]
+
+    def fetch(span, step, slot, act):
+        for n, amp in enumerate(amps):
+
+            @pl.when(step // each == n)
+            def _():
+                at = pl.multiple_of((step - n * each) * group * width, group * width)
+                copy = pltpu.make_async_copy(
+                    amp.at[pl.ds(at, group * width), span],
+                    held.at[slot, :, : span.stop - span.start],
+                    amp_sem.at[slot],
+                )
+                copy.start() if act == "start" else copy.wait()
 
     copies = []
     for o in range(p.js):
-        for source in range(p.n_aux):
-            r, parity = source // CORES, source % CORES
-            origin = CORES * lax.rem(z - o + p.js, p.js) + parity
-            row = pl.multiple_of(origin * p.cpad, ROWS)
-            copies.append(
-                pltpu.make_async_copy(
-                    pieces[o].at[source],
-                    vectors.at[:, pl.ds(row, p.cpad), r * LANES : (r + 1) * LANES],
-                    piece_sem.at[o * p.n_aux + source],
+        for r in range(p.xs):
+            for parity in range(CORES):
+                origin = CORES * lax.rem(z - o + p.js, p.js) + parity
+                row = pl.multiple_of(origin * p.cpad, ROWS)
+                copies.append(
+                    pltpu.make_async_copy(
+                        pieces[o * p.xs + r].at[parity],
+                        vectors.at[:, pl.ds(row, p.cpad), r * LANES : (r + 1) * LANES],
+                        piece_sem.at[(o * p.xs + r) * CORES + parity],
+                    )
                 )
-            )
     for copy in copies:
         copy.start()
-    Fetch(jnp.int32(0), 0).start()
+    fetch(spans[0], 0, 0, "start")
+    total[...] = jnp.zeros_like(total)
     for copy in copies:
         copy.wait()
 
-    mixed = QUAD * ROWS
-    to = lax.broadcasted_iota(jnp.int32, (mixed, mixed), 0)
-    frm = lax.broadcasted_iota(jnp.int32, (mixed, mixed), 1)
-    weave = ((to % BLK) * ROWS + to // BLK == frm).astype(jnp.float32).astype(jnp.bfloat16)
-    lane_in = lax.broadcasted_iota(jnp.int32, (LANES, LANES), 0)
-    lane_out = lax.broadcasted_iota(jnp.int32, (LANES, LANES), 1)
-    same = lane_in % p.slot == lane_out % p.slot
     first = pl.multiple_of(chunk * p.c, ROWS)
-
-    def woven(stack):
-        return lax.dot_general(weave, stack, NN, preferred_element_type=jnp.float32).astype(
-            jnp.bfloat16
-        )
+    lane = lax.broadcasted_iota(jnp.int32, (p.c, LANES), 1)
 
     @pl.loop(0, p.blocks)
     def _(b):
-        for e in range(BLK):
-            index = b * BLK + e
-            plane = p.nm * w + index // p.per_row
-            copier = (same & (lane_in // p.slot == index % p.per_row)).astype(jnp.float32)
-            copier = copier.astype(jnp.bfloat16)
-            for r in range(p.xs):
-                span = slice(r * LANES, (r + 1) * LANES)
-                spread_tail[e, :, span] = lax.dot_general(
-                    vectors[plane, pl.ds(first, p.c), span],
-                    copier,
-                    NN,
-                    preferred_element_type=jnp.float32,
-                ).astype(jnp.bfloat16)
-        for i in range(p.c // ROWS):
-            span = slice(i * mixed, (i + 1) * mixed)
-            tail = [spread_tail[e, i * ROWS : (i + 1) * ROWS, :] for e in range(BLK)]
-            left_tail[b, span] = woven(jnp.concatenate(tail, axis=0))
-            for m in range(p.nm):
-                at = pl.ds(pl.multiple_of(first + i * ROWS, ROWS), ROWS)
-                stack = [vectors[m * w + b * BLK + e, at] for e in range(BLK)]
-                left_main[m, b, span] = woven(jnp.concatenate(stack, axis=0))
-
-    total[...] = jnp.zeros_like(total)
+        for r in range(p.xs):
+            span = slice(r * LANES, (r + 1) * LANES)
+            for m in range(p.nm + 1):
+                for e in range(BLK):
+                    index = b * BLK + e
+                    plane = m * w + index if m < p.nm else m * w + index // p.per_row
+                    rows = vectors[plane, pl.ds(first, p.c), span].astype(jnp.float32)
+                    if m == p.nm:
+                        rows = jnp.where(lane // p.slot == index % p.per_row, rows, 0.0)
+                        turn = p.slot
+                        while turn < LANES:
+                            rows += pltpu.roll(rows, turn, 1)
+                            turn *= 2
+                    strided[pl.ds(e, p.c, stride=BLK), :] = rows
+                at = slice((m * p.xs + r) * LANES, (m * p.xs + r + 1) * LANES)
+                left[b, :, at] = strided[...].astype(jnp.bfloat16)
+
     slot_of = lax.broadcasted_iota(jnp.int32, (1, p.k), 1) % LANES // p.slot
 
-    @pl.loop(0, parts)
-    def _(part):
-        part_rows = pl.ds(pl.multiple_of(part * rows, rows), rows)
+    for number, span in enumerate(spans):
+        size = span.stop - span.start
 
         @pl.loop(0, p.gf)
         def _(gf):
-            left = blocks_ref[gf // BLK, 0]
+            block = blocks_ref[gf // BLK, 0]
             index = blocks_ref[gf // BLK, 1] * BLK + gf % BLK
             only = (slot_of == index % p.per_row).astype(jnp.float32).astype(jnp.bfloat16)
-            lhs = [left_tail[left, part_rows] * only]
-            planes = [p.nm * w + index // p.per_row]
+            lhs, rhs = [], []
             for m in range(p.nm):
-                lhs.append(left_main[m, left, part_rows])
-                planes.append(m * w + index)
-            lhs = jnp.concatenate(lhs, axis=1)
-            for low in range(0, p.d, 256):
-                span = slice(low, min(low + 256, p.d))
-                rhs = jnp.concatenate([vectors[plane, span] for plane in planes], axis=1)
-                block = lax.dot_general(lhs, rhs, NT, preferred_element_type=jnp.float32)
-                block = block.astype(jnp.bfloat16).reshape(here, ROWS, span.stop - low)
-                tiles[:, gf, :, span] = block
+                lhs.append(left[block, :, m * p.k : (m + 1) * p.k])
+                rhs.append(vectors[m * w + index, span])
+            lhs.append(left[block, :, p.nm * p.k :] * only)
+            rhs.append(vectors[p.nm * w + index // p.per_row, span])
+            tile = lax.dot_general(
+                jnp.concatenate(lhs, axis=1),
+                jnp.concatenate(rhs, axis=1),
+                NT,
+                preferred_element_type=jnp.float32,
+            )
+            tiles[:, gf, :, :size] = tile.astype(jnp.bfloat16).reshape(quads, ROWS, size)
 
         @pl.loop(0, steps)
         def _(step):
-            at = part * steps + step
-            slot = lax.rem(at, 2)
-
-            @pl.when(at + 1 < parts * steps)
+            slot = lax.rem(number * steps + step, 2)
+
+            @pl.when(step + 1 < steps)
             def _():
-                Fetch(at + 1, 1 - slot).start()
-
-            Fetch(at, slot).wait()
-            width = QUAD * p.ij
-            for n in range(group):
-                total[...] += lax.dot_general(
-                    tiles[step * group + n].reshape(p.gf * ROWS, p.d),
-                    held[slot, n * width : (n + 1) * width],
-                    NT,
-                    preferred_element_type=jnp.float32,
-                )
-
-    width = QUAD * p.ij
+                fetch(span, step + 1, 1 - slot, "start")
+
+            if number + 1 < len(spans):
+
+                @pl.when(step + 1 == steps)
+                def _():
+                    fetch(spans[number + 1], 0, 1 - slot, "start")
+
+            fetch(span, step, slot, "wait")
+            lhs = [
+                tiles[step * group + n, :, :, :size].reshape(p.gf * ROWS, size)
+                for n in range(group)
+            ]
+            rhs = [held[slot, n * width : (n + 1) * width, :size] for n in range(group)]
+            total[...] += lax.dot_general(
+                jnp.concatenate(lhs, axis=1),
+                jnp.concatenate(rhs, axis=1),
+                NT,
+                preferred_element_type=jnp.float32,
+            )
+
     row = lax.broadcasted_iota(jnp.int32, (p.gf * ROWS, width), 0) % ROWS // BLK
     col = lax.broadcasted_iota(jnp.int32, (p.gf * ROWS, width), 1) // p.ij
     kept = jnp.where(row == col, total[...], 0.0)
@@ -314,34 +303,29 @@
 
 
 def ladder(p, place, blocks, pieces, amps):
-    parts, group = 2, 1
     quads = p.c // QUAD
-    for wanted in (4, 2):
-        if quads // parts % wanted == 0:
-            group = wanted
-            break
+    group = 4 if quads // AMPS % 4 == 0 else 2
     width = QUAD * p.ij
     return pl.pallas_call(
-        functools.partial(ladder_kernel, p, parts, group),
+        functools.partial(ladder_kernel, p, group),
         out_shape=jax.ShapeDtypeStruct((p.gf, BLK, LANES), jnp.float32),
         in_specs=[pl.BlockSpec(memory_space=pltpu.SMEM)] * 2
         + [pl.BlockSpec(memory_space=pl.ANY)] * (len(pieces) + AMPS),
         out_specs=pl.BlockSpec(memory_space=pltpu.VMEM),
         scratch_shapes=[
             pltpu.VMEM((p.planes, p.d, p.k), jnp.bfloat16),
-            pltpu.VMEM((max(p.nm, 1), p.blocks, BLK * p.c if p.nm else ROWS, p.k), jnp.bfloat16),
-            pltpu.VMEM((p.blocks, BLK * p.c, p.k), jnp.bfloat16),
-            pltpu.VMEM((BLK, p.c, p.k), jnp.bfloat16),
-            pltpu.VMEM((quads // parts, p.gf, ROWS, p.d), jnp.bfloat16),
-            pltpu.VMEM((2, group * width, p.d), jnp.bfloat16),
+            pltpu.VMEM((p.blocks, BLK * p.c, (p.nm + 1) * p.k), jnp.bfloat16),
+            pltpu.VMEM((BLK * p.c, LANES), jnp.float32),
+            pltpu.VMEM((quads, p.gf, ROWS, DEEP), jnp.bfloat16),
+            pltpu.VMEM((2, group * width, DEEP), jnp.bfloat16),
             pltpu.VMEM((p.gf * ROWS, width), jnp.float32),
-            pltpu.SemaphoreType.DMA((p.js * p.n_aux,)),
+            pltpu.SemaphoreType.DMA((len(pieces) * CORES,)),
             pltpu.SemaphoreType.DMA((2,)),
         ],
-        compiler_params=pltpu.CompilerParams(vmem_limit_bytes=63 * 2**20),
+        compiler_params=pltpu.CompilerParams(vmem_limit_bytes=60 * 2**20),
         cost_estimate=pl.CostEstimate(
             flops=2 * p.gf * BLK * p.c * p.d * p.k,
-            bytes_accessed=2 * (p.js * p.n_aux * p.planes * p.cpad * LANES + p.c * p.ij * p.d),
+            bytes_accessed=2 * (p.planes * p.d * p.k + p.c * p.ij * p.d),
             transcendentals=0,
         ),
         name="ladder",
@@ -405,22 +389,42 @@
     amplitudes = pad_columns(pad_columns(amplitudes, 1, cols, p.cpad), 2, cols, p.cpad)
     amps = [relayout(p, amplitudes, part) for part in range(AMPS)]
 
+    def along_x(array, r):
+        return permute(array, lambda a, q: (CORES * ((a // CORES + r) % p.xs) + a % CORES, q))
+
+    cores = [list(range(a, a + CORES)) for a in range(0, n_aux, CORES)]
+
+    def share(array):
+        return lax.all_gather(array, "aux", axis_index_groups=cores, axis=0, tiled=False)
+
+    def beside(array, work):
+        return lax.optimization_barrier((array, work))[0]
+
+    late = [messages[o] for o in order[2:]]
     found = {}
-    before = turned_here
+    before = earlier = swapped = None
     for place_in_order, o in enumerate(order):
         if o == 0:
             own = turned_here
         else:
-            message, before = lax.optimization_barrier((messages[o], before))
-            own = before = to_slice(message, o)
+            message, before, earlier = lax.optimization_barrier((messages[o], before, earlier))
+            own = to_slice(message, o)
+        last = p.js - 1 - place_in_order
         if place_in_order == 1:
-            own, messages[order[2]] = lax.optimization_barrier((own, messages[order[2]]))
-        part = place_in_order - (p.js - AMPS)
-        if part >= 0:
-            own, amps[part] = lax.optimization_barrier((own, amps[part]))
-        found[o] = lax.all_gather(own, "aux", axis=0, tiled=False)
+            own = beside(own, late)
+        turned = [own] + [along_x(own, r) for r in range(1, p.xs)]
+        if place_in_order == 0:
+            turned[1:] = beside(turned[1:], late)
+        if last == 2:
+            turned[1:] = beside(turned[1:], amps[0])
+        if last == 1:
+            turned[0] = beside(turned[0], amps[0])
+        if last == 0:
+            turned[1:] = beside(turned[1:], amps[1:])
+        before, earlier, swapped = own, swapped, turned[1:]
+        found[o] = [share(array) for array in turned]
     amps = [amp.reshape(-1, p.d) for amp in amps]
-    pieces = [found[o] for o in range(p.js)]
+    pieces = [piece for o in range(p.js) for piece in found[o]]
 
     partial_terms = ladder(p, place, assignment, pieces, amps)
     share = p.ij // n_aux

time: 277 us -> 368 us (1.33)
  waiting for transfers between devices: 78.8 us -> 132 us
  Pallas kernels: 157 us -> 171 us
  local copies, waits for them, and re-layouts: 7.18 us -> 20.5 us
  starting transfers between devices: 6.28 us -> 15.6 us
    ppermute x4 -> x8, waiting for transfers between devices: 31.2 us -> 114 us  [permute(): return lax.ppermute(array, ('aux', 'pair'), pairs)]
    pallas_call x1, Pallas kernels: 75.7 us -> 117 us  [ladder(): pl.pallas_call(functools.partial(ladder_kernel, p, group), out_shape=jax....]
    all_gather x4 -> x8, waiting for transfers between devices: 47.5 us -> 17.9 us  [share(): lax.all_gather(array, 'aux', axis_index_groups=cores, axis=0, tiled=False)]
    pallas_call x2, Pallas kernels: 45.8 us -> 18.5 us  [relayout(): pl.pallas_call(functools.partial(relayout_kernel, p), out_shape=jax.Shape...]
    unnamed x14 -> x32, local copies, waits for them, and re-layouts: 4.67 us -> 18 us
    ppermute x4 -> x8, starting transfers between devices: 6.16 us -> 15.3 us  [permute(): return lax.ppermute(array, ('aux', 'pair'), pairs)]
  transfers between devices with their start and end apart: 8 -> 16, of which waited for: 4 -> 7; matrix products, arithmetic and copies ran while one was open for 0% -> 0% of each run, Pallas kernels for 26% -> 12%
where the time goes in v4:
time: 368 us; the launch traced here: 366 us
  Pallas kernels  171 us (46%)
  waiting for transfers between devices  132 us (36%)
  local copies, waits for them, and re-layouts  20.5 us (6%)
  starting transfers between devices  15.6 us (4%)
  between operations  13.7 us (4%)
  blocking collectives  12.8 us (3%)
    pallas_call x1, Pallas kernels, ladder(): pl.pallas_call(functools.partial(ladder_kernel, p, group), out_shape=jax....  117 us
    ppermute x8, waiting for transfers between devices, permute(): return lax.ppermute(array, ('aux', 'pair'), pairs)  114 us
    pallas_call x4, Pallas kernels, dress(): pl.pallas_call(functools.partial(dress_kernel, p, offset), out_shape=jax....  35 us
    pallas_call x2, Pallas kernels, relayout(): pl.pallas_call(functools.partial(relayout_kernel, p), out_shape=jax.Shape...  18.5 us
    unnamed x32, local copies, waits for them, and re-layouts  18 us
    all_gather x8, waiting for transfers between devices, share(): lax.all_gather(array, 'aux', axis_index_groups=cores, axis=0, tiled=False)  17.9 us
    ppermute x8, starting transfers between devices, permute(): return lax.ppermute(array, ('aux', 'pair'), pairs)  15.3 us
    all_to_all x1, blocking collectives, shards(): lax.all_to_all(terms, ('aux', 'pair'), split_axis=0, concat_axis=0, tiled...  12.8 us
  transfers between devices with their start and end apart: 16, of which 7 were waited for; matrix products, arithmetic and copies ran while one was open for 0% of the time, Pallas kernels for 12%

profile of v4, /device:TPU:0, one launch (start us, length us, event | category | flops | bytes accessed | tf_op | source)
XLA Modules:
  0.0 366.1 jit_solution(4548583671522090188)
XLA Ops:
  6.5 0.8 copy.11.t1_ref
  7.3 0.8 spread.1.a_ref
  8.1 0.1 pad_add_fusion.z_ref.place_ref
  8.2 8.5 %dress.4 = bf16[36,112,128]{2,1,0:T(8,128)(2,1)S(1)} custom-call(s32[2]{0:T(128)S(1)} %pad_add_fusion.z_ref.place_ref, bf16[512,1600]{1,0:T(8,128)(2,1)S(1)} %spread.1.a_ref, bf16[100,112,576]{2,1,0:T(8,128)(2,1)} %refs_1_.7, bf16[100,112,576]{2,1,0:T(8,128)(2,1)} %refs_1_.7, bf16[32,112,576]{2,1,0:T(8,128)(2,1)} %refs_3_.7, bf16[32,112,576]{2,1,0:T(8,128)(2,1)} %refs_3_.7), custom_call_target="tpu_custom_call" | custom-call | flops 2936012800 | bytes 9404416 | tf_op jit(solution)/shard_map/dress/pallas_call | solution.py:122
  16.7 0.7 collective-permute-start
  17.4 9.3 %dress.5 = bf16[36,112,128]{2,1,0:T(8,128)(2,1)} custom-call(s32[2]{0:T(128)S(1)} %pad_add_fusion.z_ref.place_ref, bf16[512,1600]{1,0:T(8,128)(2,1)S(1)} %spread.1.a_ref, bf16[100,112,576]{2,1,0:T(8,128)(2,1)} %refs_1_.7, bf16[100,112,576]{2,1,0:T(8,128)(2,1)} %refs_1_.7, bf16[32,112,576]{2,1,0:T(8,128)(2,1)} %refs_3_.7, bf16[32,112,576]{2,1,0:T(8,128)(2,1)} %refs_3_.7), custom_call_target="tpu_custom_call" | custom-call | flops 2936012800 | bytes 9404416 | tf_op jit(solution)/shard_map/dress/pallas_call | solution.py:122
  26.8 1.0 copy-done.5
  27.8 0.0 all-gather.21.cloned.1.call-start
  27.8 3.1 collective-permute-start.2
  30.9 8.5 %dress.6 = bf16[36,112,128]{2,1,0:T(8,128)(2,1)S(1)} custom-call(s32[2]{0:T(128)S(1)} %pad_add_fusion.z_ref.place_ref, bf16[512,1600]{1,0:T(8,128)(2,1)S(1)} %spread.1.a_ref, bf16[100,112,576]{2,1,0:T(8,128)(2,1)} %refs_1_.7, bf16[100,112,576]{2,1,0:T(8,128)(2,1)} %refs_1_.7, bf16[32,112,576]{2,1,0:T(8,128)(2,1)} %refs_3_.7, bf16[32,112,576]{2,1,0:T(8,128)(2,1)} %refs_3_.7), custom_call_target="tpu_custom_call" | custom-call | flops 2936012800 | bytes 9404416 | tf_op jit(solution)/shard_map/dress/pallas_call | solution.py:122
  39.4 8.7 %dress.7 = bf16[36,112,128]{2,1,0:T(8,128)(2,1)S(1)} custom-call(s32[2]{0:T(128)S(1)} %pad_add_fusion.z_ref.place_ref, bf16[512,1600]{1,0:T(8,128)(2,1)S(1)} %spread.1.a_ref, bf16[100,112,576]{2,1,0:T(8,128)(2,1)} %refs_1_.7, bf16[100,112,576]{2,1,0:T(8,128)(2,1)} %refs_1_.7, bf16[32,112,576]{2,1,0:T(8,128)(2,1)} %refs_3_.7, bf16[32,112,576]{2,1,0:T(8,128)(2,1)} %refs_3_.7), custom_call_target="tpu_custom_call" | custom-call | flops 2936012800 | bytes 9404416 | tf_op jit(solution)/shard_map/dress/pallas_call | solution.py:122
  48.1 2.2 collective-permute-done.2
  50.4 0.0 all-gather.19.cloned.1.call-start
  50.4 2.0 collective-permute-start.1
  52.4 18.4 %collective-permute-done.1 = bf16[36,112,128]{2,1,0:T(8,128)(2,1)S(1)} collective-permute-done((bf16[36,112,128]{2,1,0:T(8,128)(2,1)}, bf16[36,112,128]{2,1,0:T(8,128)(2,1)S(1)}, u32[]{:S(2)}, u32[]{:S(2)}) %collective-permute-start.1) | collective-permute-done | bytes 1032224 | tf_op jit(solution)/shard_map/ppermute | solution.py:364
  70.8 1.0 copy-done.6
  71.9 2.8 collective-permute-start.4
  74.7 9.2 %relayout.2 = bf16[112,64,896]{2,1,0:T(8,128)(2,1)S(1)} custom-call(bf16[64,224,896]{2,1,0:T(8,128)(2,1)} %in_ref.1), custom_call_target="tpu_custom_call" | custom-call | flops 3288334336 | bytes 25690112 | tf_op jit(solution)/shard_map/relayout/pallas_call | solution.py:157
  83.9 4.6 %copy-done = bf16[112,64,896]{2,1,0:T(8,128)(2,1)} copy-done((bf16[112,64,896]{2,1,0:T(8,128)(2,1)}, bf16[112,64,896]{2,1,0:T(8,128)(2,1)S(1)}, u32[]{:S(2)}) %copy-start) | copy-done | bytes 12845080
  88.6 6.4 %collective-permute-done.4 = bf16[36,112,128]{2,1,0:T(8,128)(2,1)S(1)} collective-permute-done((bf16[36,112,128]{2,1,0:T(8,128)(2,1)S(1)}, bf16[36,112,128]{2,1,0:T(8,128)(2,1)S(1)}, u32[]{:S(2)}, u32[]{:S(2)}) %collective-permute-start.4) | collective-permute-done | bytes 1032224 | tf_op jit(solution)/shard_map/ppermute | solution.py:364
  95.0 1.0 copy-done.7
  96.0 0.0 all-gather.23.cloned.1.call-start
  96.0 1.9 collective-permute-start.3
  97.9 21.9 %collective-permute-done.3 = bf16[36,112,128]{2,1,0:T(8,128)(2,1)S(1)} collective-permute-done((bf16[36,112,128]{2,1,0:T(8,128)(2,1)}, bf16[36,112,128]{2,1,0:T(8,128)(2,1)S(1)}, u32[]{:S(2)}, u32[]{:S(2)}) %collective-permute-start.3) | collective-permute-done | bytes 1032224 | tf_op jit(solution)/shard_map/ppermute | solution.py:364
  119.9 1.0 copy-done.9
  120.9 1.5 collective-permute-start.5
  122.4 46.0 %collective-permute-done.5 = bf16[36,112,128]{2,1,0:T(8,128)(2,1)S(1)} collective-permute-done((bf16[36,112,128]{2,1,0:T(8,128)(2,1)S(1)}, bf16[36,112,128]{2,1,0:T(8,128)(2,1)S(1)}, u32[]{:S(2)}, u32[]{:S(2)}) %collective-permute-start.5) | collective-permute-done | bytes 1032224 | tf_op jit(solution)/shard_map/ppermute | solution.py:364
  168.4 1.0 copy-done.10
  169.4 1.6 collective-permute-start.7
  171.0 18.9 %collective-permute-done.7 = bf16[36,112,128]{2,1,0:T(8,128)(2,1)S(1)} collective-permute-done((bf16[36,112,128]{2,1,0:T(8,128)(2,1)S(1)}, bf16[36,112,128]{2,1,0:T(8,128)(2,1)S(1)}, u32[]{:S(2)}, u32[]{:S(2)}) %collective-permute-start.7) | collective-permute-done | bytes 1032224 | tf_op jit(solution)/shard_map/ppermute | solution.py:364
  189.9 1.0 copy-done.11
  190.9 0.0 all-gather.27.cloned.1.call-start
  191.0 1.8 collective-permute-start.6
  192.8 9.3 %relayout.3 = bf16[112,64,896]{2,1,0:T(8,128)(2,1)S(1)} custom-call(bf16[64,224,896]{2,1,0:T(8,128)(2,1)} %in_ref.1), custom_call_target="tpu_custom_call" | custom-call | flops 3288334336 | bytes 25690112 | tf_op jit(solution)/shard_map/relayout/pallas_call | solution.py:157
  202.1 4.6 %copy-done.1 = bf16[112,64,896]{2,1,0:T(8,128)(2,1)} copy-done((bf16[112,64,896]{2,1,0:T(8,128)(2,1)}, bf16[112,64,896]{2,1,0:T(8,128)(2,1)S(1)}, u32[]{:S(2)}) %copy-start.1) | copy-done | bytes 12845080
  206.7 1.0 copy-done.12
  207.7 0.7 copy.12.blocks_ref
  208.5 17.8 %all-gather.27.cloned.1.call-done = bf16[72,112,128]{2,1,0:T(8,128)(2,1)} async-done(((bf16[36,112,128]{2,1,0:T(8,128)(2,1)}), bf16[72,112,128]{2,1,0:T(8,128)(2,1)}) %all-gather.27.cloned.1.call-update) | async-done | bytes 2064400 | tf_op jit(solution)/shard_map/all_gather | solution.py:398
  226.3 116.6 %ladder.1 = f32[32,4,128]{2,1,0:T(4,128)} custom-call(s32[2]{0:T(128)} %copy-done.4, s32[8,2]{1,0:T(8,128)} %copy.12.blocks_ref, bf16[2,36,112,128]{3,2,1,0:T(8,128)(2,1)} %bitcast.26, bf16[2,36,112,128]{3,2,1,0:T(8,128)(2,1)} %bitcast.28, bf16[2,36,112,128]{3,2,1,0:T(8,128)(2,1)} %bitcast.27, bf16[2,36,112,128]{3,2,1,0:T(8,128)(2,1)} %bitcast.30, ...), custom_call_target="tpu_custom_call" | custom-call | flops 13153337344 | bytes 42205184 | tf_op jit(solution)/shard_map/ladder/pallas_call | solution.py:309
  342.9 1.0 reshape.14
  343.9 0.2 copy.13
  344.1 0.2 copy.19
  344.3 0.1 reshape.24
  344.4 12.8 %all_to_all.5 = f32[32,1,256]{2,1,0:T(1,128)S(1)} all-to-all(f32[32,1,256]{2,1,0:T(1,128)S(1)} %reshape.24), channel_id=1, replica_groups=mesh['aux'=4,'pair'=8] {'aux','pair'}, dimensions={0} | all-to-all | bytes 65536 | tf_op jit(solution)/shard_map/all_to_all | solution.py:433
  357.2 0.5 broadcast.1
  357.7 0.7 reduce
  358.4 0.1 reshape.25
  358.6 0.7 copy.16
  (41 shorter events, 0.4 us)
Async XLA Ops:
  6.5 201.9 %all-gather.17.cloned.1.call-start = ((), (), s32[]{:S(2)}) async-start(), calls=%async_computation.1 | async-start | bytes 3096576 | tf_op jit(solution)/shard_map/all_gather | solution.py:398
  8.2 31.2 %copy-start.4 = (s32[2]{0:T(128)}, s32[2]{0:T(128)S(1)}, u32[]{:S(2)}) copy-start(s32[2]{0:T(128)S(1)} %pad_add_fusion.z_ref.place_ref) | copy-start | bytes 28
  16.7 10.1 %collective-permute-start = (bf16[36,112,128]{2,1,0:T(8,128)(2,1)S(1)}, bf16[36,112,128]{2,1,0:T(8,128)(2,1)S(1)}, u32[]{:S(2)}, u32[]{:S(2)}) collective-permute-start(bf16[36,112,128]{2,1,0:T(8,128)(2,1)S(1)} %dress.4), channel_id=1, source_target_pairs={{0,0},{1,8},{2,2},{3,10},{4,4},{5,12},{6,6},{7,14},{8,1},{9,9},{10... | collective-permute-start | bytes 3096584 | tf_op jit(solution)/shard_map/ppermute | solution.py:364
  26.8 1.0 copy-start.5
  27.8 180.6 %all-gather.21.cloned.1.call-start = ((), (), s32[]{:S(2)}) async-start(), calls=%async_computation.3 | async-start | bytes 3096576 | tf_op jit(solution)/shard_map/all_gather | solution.py:398
  27.8 22.5 %collective-permute-start.2 = (bf16[36,112,128]{2,1,0:T(8,128)(2,1)}, bf16[36,112,128]{2,1,0:T(8,128)(2,1)}, u32[]{:S(2)}, u32[]{:S(2)}) collective-permute-start(bf16[36,112,128]{2,1,0:T(8,128)(2,1)} %dress.5), channel_id=1, source_target_pairs={{0,2},{1,10},{2,4},{3,12},{4,6},{5,14},{6,0},{7,8},{8,3},{9,11},{1... | collective-permute-start | bytes 3096584 | tf_op jit(solution)/shard_map/ppermute | solution.py:364
  39.4 8.7 %copy-start.2 = (bf16[36,112,128]{2,1,0:T(8,128)(2,1)}, bf16[36,112,128]{2,1,0:T(8,128)(2,1)S(1)}, u32[]{:S(2)}) copy-start(bf16[36,112,128]{2,1,0:T(8,128)(2,1)S(1)} %dress.6) | copy-start | bytes 3096580
  50.4 21.5 %copy-start.3 = (bf16[36,112,128]{2,1,0:T(8,128)(2,1)S(1)}, bf16[36,112,128]{2,1,0:T(8,128)(2,1)}, u32[]{:S(2)}) copy-start(bf16[36,112,128]{2,1,0:T(8,128)(2,1)} %copy-done.2) | copy-start | bytes 3096580
  50.4 158.0 %all-gather.19.cloned.1.call-start = ((), (), s32[]{:S(2)}) async-start(), calls=%async_computation.2 | async-start | bytes 3096576 | tf_op jit(solution)/shard_map/all_gather | solution.py:398
  50.4 20.4 %collective-permute-start.1 = (bf16[36,112,128]{2,1,0:T(8,128)(2,1)}, bf16[36,112,128]{2,1,0:T(8,128)(2,1)S(1)}, u32[]{:S(2)}, u32[]{:S(2)}) collective-permute-start(bf16[36,112,128]{2,1,0:T(8,128)(2,1)} %copy-done.5), channel_id=1, source_target_pairs={{0,16},{1,17},{2,18},{3,19},{4,20},{5,21},{6,22},{7,23},{8,24},{9,... | collective-permute-start | bytes 3096584 | tf_op jit(solution)/shard_map/ppermute | solution.py:364
  70.8 1.0 copy-start.6
  71.8 136.6 %all-gather.29.cloned.1.call-start = ((), (), s32[]{:S(2)}) async-start(), calls=%async_computation.7 | async-start | bytes 3096576 | tf_op jit(solution)/shard_map/all_gather | solution.py:398
  71.9 23.1 %collective-permute-start.4 = (bf16[36,112,128]{2,1,0:T(8,128)(2,1)S(1)}, bf16[36,112,128]{2,1,0:T(8,128)(2,1)S(1)}, u32[]{:S(2)}, u32[]{:S(2)}) collective-permute-start(bf16[36,112,128]{2,1,0:T(8,128)(2,1)S(1)} %copy-done.3), channel_id=1, source_target_pairs={{0,6},{1,14},{2,0},{3,8},{4,2},{5,10},{6,4},{7,12},{8,7},{9,15},{1... | collective-permute-start | bytes 3096584 | tf_op jit(solution)/shard_map/ppermute | solution.py:364
  83.9 4.7 %copy-start = (bf16[112,64,896]{2,1,0:T(8,128)(2,1)}, bf16[112,64,896]{2,1,0:T(8,128)(2,1)S(1)}, u32[]{:S(2)}) copy-start(bf16[112,64,896]{2,1,0:T(8,128)(2,1)S(1)} %relayout.2) | copy-start | bytes 38535172
  95.0 1.0 copy-start.7
  96.0 73.4 %copy-start.8 = (bf16[36,112,128]{2,1,0:T(8,128)(2,1)S(1)}, bf16[36,112,128]{2,1,0:T(8,128)(2,1)}, u32[]{:S(2)}) copy-start(bf16[36,112,128]{2,1,0:T(8,128)(2,1)} %copy-done.7) | copy-start | bytes 3096580
  96.0 112.4 %all-gather.23.cloned.1.call-start = ((), (), s32[]{:S(2)}) async-start(), calls=%async_computation.4 | async-start | bytes 3096576 | tf_op jit(solution)/shard_map/all_gather | solution.py:398
  96.0 23.8 %collective-permute-start.3 = (bf16[36,112,128]{2,1,0:T(8,128)(2,1)}, bf16[36,112,128]{2,1,0:T(8,128)(2,1)S(1)}, u32[]{:S(2)}, u32[]{:S(2)}) collective-permute-start(bf16[36,112,128]{2,1,0:T(8,128)(2,1)} %collective-permute-done.2), channel_id=1, source_target_pairs={{0,16},{1,17},{2,18},{3,19},{4,20},{5,21},{6,22},{7,23},{8,24},{9,... | collective-permute-start | bytes 3096584 | tf_op jit(solution)/shard_map/ppermute | solution.py:364
  119.9 1.0 copy-start.9
  120.9 87.6 %all-gather.25.cloned.1.call-start = ((), (), s32[]{:S(2)}) async-start(), calls=%async_computation.5 | async-start | bytes 3096576 | tf_op jit(solution)/shard_map/all_gather | solution.py:398
  120.9 47.5 %collective-permute-start.5 = (bf16[36,112,128]{2,1,0:T(8,128)(2,1)S(1)}, bf16[36,112,128]{2,1,0:T(8,128)(2,1)S(1)}, u32[]{:S(2)}, u32[]{:S(2)}) collective-permute-start(bf16[36,112,128]{2,1,0:T(8,128)(2,1)S(1)} %dress.7), channel_id=1, source_target_pairs={{0,4},{1,12},{2,6},{3,14},{4,0},{5,8},{6,2},{7,10},{8,5},{9,13},{1... | collective-permute-start | bytes 3096584 | tf_op jit(solution)/shard_map/ppermute | solution.py:364
  168.4 1.0 copy-start.10
  169.4 39.1 %all-gather.31.cloned.1.call-start = ((), (), s32[]{:S(2)}) async-start(), calls=%async_computation.8 | async-start | bytes 3096576 | tf_op jit(solution)/shard_map/all_gather | solution.py:398
  169.4 20.5 %collective-permute-start.7 = (bf16[36,112,128]{2,1,0:T(8,128)(2,1)S(1)}, bf16[36,112,128]{2,1,0:T(8,128)(2,1)S(1)}, u32[]{:S(2)}, u32[]{:S(2)}) collective-permute-start(bf16[36,112,128]{2,1,0:T(8,128)(2,1)S(1)} %copy-done.8), channel_id=1, source_target_pairs={{0,16},{1,17},{2,18},{3,19},{4,20},{5,21},{6,22},{7,23},{8,24},{9,... | collective-permute-start | bytes 3096584 | tf_op jit(solution)/shard_map/ppermute | solution.py:364
  189.9 1.0 copy-start.11
  190.9 16.8 %copy-start.13 = (s32[8,2]{0,1:T(2,128)S(1)}, s32[8,2]{0,1:T(2,128)}, u32[]{:S(2)}) copy-start(s32[8,2]{0,1:T(2,128)} %param.9) | copy-start | bytes 196
  190.9 35.4 %all-gather.27.cloned.1.call-start = ((), (), s32[]{:S(2)}) async-start(), calls=%async_computation.6 | async-start | bytes 3096576 | tf_op jit(solution)/shard_map/all_gather | solution.py:398
  191.0 15.7 %collective-permute-start.6 = (bf16[36,112,128]{2,1,0:T(8,128)(2,1)}, bf16[36,112,128]{2,1,0:T(8,128)(2,1)S(1)}, u32[]{:S(2)}, u32[]{:S(2)}) collective-permute-start(bf16[36,112,128]{2,1,0:T(8,128)(2,1)} %copy-done.10), channel_id=1, source_target_pairs={{0,16},{1,17},{2,18},{3,19},{4,20},{5,21},{6,22},{7,23},{8,24},{9,... | collective-permute-start | bytes 3096584 | tf_op jit(solution)/shard_map/ppermute | solution.py:364
  202.1 4.7 %copy-start.1 = (bf16[112,64,896]{2,1,0:T(8,128)(2,1)}, bf16[112,64,896]{2,1,0:T(8,128)(2,1)S(1)}, u32[]{:S(2)}) copy-start(bf16[112,64,896]{2,1,0:T(8,128)(2,1)S(1)} %relayout.3) | copy-start | bytes 38535172
  206.7 1.0 copy-start.12
Sparse Core Ops, SparseCore 0:
  27.9 19.1 all-gather.16
  50.5 16.6 all-gather.20
  72.0 14.4 all-gather.18
  96.1 15.3 all-gather.28
  121.0 11.7 all-gather.22
  169.5 9.1 all-gather.24
  191.0 10.5 all-gather.30
  207.8 18.4 all-gather.26

commit v5 on v4

--- a/solution.py
+++ b/solution.py
@@ -81,23 +81,28 @@
     ov, vv, out = refs[: p.nm + 1], refs[p.nm + 1 : 2 * p.nm + 2], refs[-1]
     w = p.window
     j = lax.rem(z_ref[0] + offset, p.js)
-    vectors = jnp.concatenate([ref[...].reshape(p.occupied * ROWS, -1) for ref in ov], axis=1)
-    shift = lax.dot_general(a_ref[...], vectors, NN, preferred_element_type=jnp.float32)
-    for m in range(p.nm):
-        here = shift[:, m * LANES : (m + 1) * LANES].reshape(w, ROWS, LANES)
-        out[m * w : (m + 1) * w] = (vv[m][...].astype(jnp.float32) - here).astype(jnp.bfloat16)
-    here = shift[:, p.nm * LANES :].reshape(w, ROWS, p.tail_width)
-    source = vv[p.nm][...].astype(jnp.float32) - here
-    source = source.reshape(p.nt, p.per_row, ROWS, p.tail_width)
     lane = lax.broadcasted_iota(jnp.int32, (p.nt, ROWS, LANES), 2)
-    rest = jnp.zeros((p.nt, ROWS, LANES), jnp.float32)
-    for s in range(p.per_row):
-        turn = lax.rem(s * p.slot - j * p.tail + 2 * p.tail_width, p.tail_width)
-        moved = pltpu.roll(source[:, s].reshape(p.nt * ROWS, p.tail_width), turn, 1)
-        moved = moved[:, :LANES].reshape(p.nt, ROWS, LANES)
-        keep = (lane >= s * p.slot) & (lane < s * p.slot + p.tail)
-        rest = jnp.where(keep, moved, rest)
-    out[p.nm * w :] = rest.astype(jnp.bfloat16)
+    for low in range(0, p.cpad, ROWS):
+        cols = slice(low, low + ROWS)
+        vectors = [ref[:, cols].reshape(p.occupied * ROWS, -1) for ref in ov]
+        shift = lax.dot_general(
+            a_ref[...], jnp.concatenate(vectors, axis=1), NN, preferred_element_type=jnp.float32
+        )
+        for m in range(p.nm):
+            here = shift[:, m * LANES : (m + 1) * LANES].reshape(w, ROWS, LANES)
+            here = vv[m][:, cols].astype(jnp.float32) - here
+            out[m * w : (m + 1) * w, cols] = here.astype(jnp.bfloat16)
+        here = shift[:, p.nm * LANES :].reshape(w, ROWS, p.tail_width)
+        source = vv[p.nm][:, cols].astype(jnp.float32) - here
+        source = source.reshape(p.nt, p.per_row, ROWS, p.tail_width)
+        rest = jnp.zeros((p.nt, ROWS, LANES), jnp.float32)
+        for s in range(p.per_row):
+            turn = lax.rem(s * p.slot - j * p.tail + 2 * p.tail_width, p.tail_width)
+            moved = pltpu.roll(source[:, s].reshape(p.nt * ROWS, p.tail_width), turn, 1)
+            moved = moved[:, :LANES].reshape(p.nt, ROWS, LANES)
+            keep = (lane >= s * p.slot) & (lane < s * p.slot + p.tail)
+            rest = jnp.where(keep, moved, rest)
+        out[p.nm * w :, cols] = rest.astype(jnp.bfloat16)
 
 
 def dress(p, offset, z, spread, chol_vv, chol_ov):
@@ -106,14 +111,14 @@
         for m in range(p.nm):
             found.append(
                 pl.BlockSpec(
-                    (lead, ROWS, LANES),
-                    lambda i, z, m=m: (0, i, lax.rem(z[0] + offset, p.js) * p.nm + m),
+                    (lead, p.cpad, LANES),
+                    lambda i, z, m=m: (0, 0, lax.rem(z[0] + offset, p.js) * p.nm + m),
                 )
             )
         found.append(
             pl.BlockSpec(
-                (lead, ROWS, p.tail_width),
-                lambda i, z: (0, i, p.tail_from // p.tail_width),
+                (lead, p.cpad, p.tail_width),
+                lambda i, z: (0, 0, p.tail_from // p.tail_width),
             )
         )
         return found
@@ -124,11 +129,11 @@
         out_shape=jax.ShapeDtypeStruct((p.planes, p.cpad, LANES), jnp.bfloat16),
         grid_spec=pltpu.PrefetchScalarGridSpec(
             num_scalar_prefetch=1,
-            grid=(p.cpad // ROWS,),
+            grid=(1,),
             in_specs=[pl.BlockSpec((p.window * ROWS, p.occupied * ROWS), lambda i, z: (0, 0))]
             + specs(p.occupied)
             + specs(p.window),
-            out_specs=pl.BlockSpec((p.planes, ROWS, LANES), lambda i, z: (0, i, 0)),
+            out_specs=pl.BlockSpec((p.planes, p.cpad, LANES), lambda i, z: (0, 0, 0)),
         ),
         compiler_params=pltpu.CompilerParams(vmem_limit_bytes=48 * 2**20),
         cost_estimate=pl.CostEstimate(
@@ -171,46 +176,44 @@
 
 
 def ladder_kernel(p, group, place_ref, blocks_ref, *refs):
-    count = p.js * p.xs
+    count = p.js * p.xs * CORES
     pieces, amps, out = refs[:count], refs[count : count + AMPS], refs[count + AMPS]
     scratch = refs[count + AMPS + 1 :]
     vectors, left, strided, tiles, held, total, piece_sem, amp_sem = scratch
-    w, z, chunk = p.window, place_ref[0], place_ref[1]
+    w, z, core, chunk = p.window, place_ref[0], place_ref[1], place_ref[2]
     quads = p.c // QUAD
     width = QUAD * p.ij
     steps = quads // group
-    each = steps // AMPS
     spans = [slice(low, min(low + DEEP, p.d)) for low in range(0, p.d, DEEP)]
 
-    def fetch(span, step, slot, act):
-        for n, amp in enumerate(amps):
-
-            @pl.when(step // each == n)
-            def _():
-                at = pl.multiple_of((step - n * each) * group * width, group * width)
-                copy = pltpu.make_async_copy(
-                    amp.at[pl.ds(at, group * width), span],
-                    held.at[slot, :, : span.stop - span.start],
-                    amp_sem.at[slot],
-                )
-                copy.start() if act == "start" else copy.wait()
+    def fetches(span):
+        rows = p.c * p.ij // AMPS
+        return [
+            pltpu.make_async_copy(
+                amp.at[:, span],
+                held.at[n * rows : (n + 1) * rows, : span.stop - span.start],
+                amp_sem.at[n],
+            )
+            for n, amp in enumerate(amps)
+        ]
 
     copies = []
     for o in range(p.js):
         for r in range(p.xs):
-            for parity in range(CORES):
+            for other in range(CORES):
+                parity = core if other == 0 else 1 - core
                 origin = CORES * lax.rem(z - o + p.js, p.js) + parity
                 row = pl.multiple_of(origin * p.cpad, ROWS)
+                number = (o * p.xs + r) * CORES + other
                 copies.append(
                     pltpu.make_async_copy(
-                        pieces[o * p.xs + r].at[parity],
+                        pieces[number],
                         vectors.at[:, pl.ds(row, p.cpad), r * LANES : (r + 1) * LANES],
-                        piece_sem.at[(o * p.xs + r) * CORES + parity],
+                        piece_sem.at[number],
                     )
                 )
     for copy in copies:
         copy.start()
-    fetch(spans[0], 0, 0, "start")
     total[...] = jnp.zeros_like(total)
     for copy in copies:
         copy.wait()
@@ -239,48 +242,34 @@
 
     slot_of = lax.broadcasted_iota(jnp.int32, (1, p.k), 1) % LANES // p.slot
 
-    for number, span in enumerate(spans):
+    for span in spans:
         size = span.stop - span.start
+        for copy in fetches(span):
+            copy.start()
 
         @pl.loop(0, p.gf)
         def _(gf):
             block = blocks_ref[gf // BLK, 0]
             index = blocks_ref[gf // BLK, 1] * BLK + gf % BLK
             only = (slot_of == index % p.per_row).astype(jnp.float32).astype(jnp.bfloat16)
-            lhs, rhs = [], []
-            for m in range(p.nm):
-                lhs.append(left[block, :, m * p.k : (m + 1) * p.k])
-                rhs.append(vectors[m * w + index, span])
-            lhs.append(left[block, :, p.nm * p.k :] * only)
-            rhs.append(vectors[p.nm * w + index // p.per_row, span])
+            rhs = [vectors[m * w + index, span] for m in range(p.nm)]
+            rhs.append(vectors[p.nm * w + index // p.per_row, span] * only)
             tile = lax.dot_general(
-                jnp.concatenate(lhs, axis=1),
-                jnp.concatenate(rhs, axis=1),
-                NT,
-                preferred_element_type=jnp.float32,
+                left[block], jnp.concatenate(rhs, axis=1), NT, preferred_element_type=jnp.float32
             )
             tiles[:, gf, :, :size] = tile.astype(jnp.bfloat16).reshape(quads, ROWS, size)
 
+        for copy in fetches(span):
+            copy.wait()
+
         @pl.loop(0, steps)
         def _(step):
-            slot = lax.rem(number * steps + step, 2)
-
-            @pl.when(step + 1 < steps)
-            def _():
-                fetch(span, step + 1, 1 - slot, "start")
-
-            if number + 1 < len(spans):
-
-                @pl.when(step + 1 == steps)
-                def _():
-                    fetch(spans[number + 1], 0, 1 - slot, "start")
-
-            fetch(span, step, slot, "wait")
             lhs = [
                 tiles[step * group + n, :, :, :size].reshape(p.gf * ROWS, size)
                 for n in range(group)
             ]
-            rhs = [held[slot, n * width : (n + 1) * width, :size] for n in range(group)]
+            low = pl.multiple_of(step * group * width, width)
+            rhs = [held[pl.ds(low + n * width, width), :size] for n in range(group)]
             total[...] += lax.dot_general(
                 jnp.concatenate(lhs, axis=1),
                 jnp.concatenate(rhs, axis=1),
@@ -304,7 +293,7 @@
 
 def ladder(p, place, blocks, pieces, amps):
     quads = p.c // QUAD
-    group = 4 if quads // AMPS % 4 == 0 else 2
+    group = 4 if quads % 4 == 0 else 2
     width = QUAD * p.ij
     return pl.pallas_call(
         functools.partial(ladder_kernel, p, group),
@@ -317,10 +306,10 @@
             pltpu.VMEM((p.blocks, BLK * p.c, (p.nm + 1) * p.k), jnp.bfloat16),
             pltpu.VMEM((BLK * p.c, LANES), jnp.float32),
             pltpu.VMEM((quads, p.gf, ROWS, DEEP), jnp.bfloat16),
-            pltpu.VMEM((2, group * width, DEEP), jnp.bfloat16),
+            pltpu.VMEM((p.c * p.ij, DEEP), jnp.bfloat16),
             pltpu.VMEM((p.gf * ROWS, width), jnp.float32),
-            pltpu.SemaphoreType.DMA((len(pieces) * CORES,)),
-            pltpu.SemaphoreType.DMA((2,)),
+            pltpu.SemaphoreType.DMA((len(pieces),)),
+            pltpu.SemaphoreType.DMA((AMPS,)),
         ],
         compiler_params=pltpu.CompilerParams(vmem_limit_bytes=60 * 2**20),
         cost_estimate=pl.CostEstimate(
@@ -349,7 +338,7 @@
     p = Plan(window, chol_ov.shape[0], cols, aux_dev, n_aux, n_pair, amplitudes.shape[0])
     me_aux, me_pair = lax.axis_index("aux"), lax.axis_index("pair")
     z = me_pair // CORES
-    place = jnp.stack([z, me_aux]).astype(jnp.int32)
+    place = jnp.stack([z, me_aux % CORES, me_aux]).astype(jnp.int32)
 
     chol_vv = pad_columns(chol_vv, 1, cols, p.cpad)
     chol_ov = pad_columns(chol_ov, 1, cols, p.cpad)
@@ -372,59 +361,51 @@
             ),
         )
 
-    order = sorted(range(p.js), key=lambda o: min(o, p.js - o))
-    messages = {}
-    for place_in_order, o in enumerate(order):
-        messages[o] = dress(p, o, place, spread, chol_vv, chol_ov)
-        if o == 0:
-            turned_here = to_slice(messages[0], 0)
-        if place_in_order == 1:
-            spread, messages[o], turned_here = lax.optimization_barrier(
-                (spread, messages[o], turned_here)
-            )
-        else:
-            spread, messages[o] = lax.optimization_barrier((spread, messages[o]))
-
-    messages[order[-1]], amplitudes = lax.optimization_barrier((messages[order[-1]], amplitudes))
-    amplitudes = pad_columns(pad_columns(amplitudes, 1, cols, p.cpad), 2, cols, p.cpad)
-    amps = [relayout(p, amplitudes, part) for part in range(AMPS)]
-
     def along_x(array, r):
         return permute(array, lambda a, q: (CORES * ((a // CORES + r) % p.xs) + a % CORES, q))
 
-    cores = [list(range(a, a + CORES)) for a in range(0, n_aux, CORES)]
-
-    def share(array):
-        return lax.all_gather(array, "aux", axis_index_groups=cores, axis=0, tiled=False)
-
-    def beside(array, work):
-        return lax.optimization_barrier((array, work))[0]
-
-    late = [messages[o] for o in order[2:]]
-    found = {}
-    before = earlier = swapped = None
-    for place_in_order, o in enumerate(order):
-        if o == 0:
-            own = turned_here
-        else:
-            message, before, earlier = lax.optimization_barrier((messages[o], before, earlier))
-            own = to_slice(message, o)
-        last = p.js - 1 - place_in_order
-        if place_in_order == 1:
-            own = beside(own, late)
-        turned = [own] + [along_x(own, r) for r in range(1, p.xs)]
-        if place_in_order == 0:
-            turned[1:] = beside(turned[1:], late)
-        if last == 2:
-            turned[1:] = beside(turned[1:], amps[0])
-        if last == 1:
-            turned[0] = beside(turned[0], amps[0])
-        if last == 0:
-            turned[1:] = beside(turned[1:], amps[1:])
-        before, earlier, swapped = own, swapped, turned[1:]
-        found[o] = [share(array) for array in turned]
+    def to_core(array):
+        return permute(array, lambda a, q: (a ^ 1, q))
+
+    amplitudes = pad_columns(pad_columns(amplitudes, 1, cols, p.cpad), 2, cols, p.cpad)
+
+    groups = [sorted({n, (p.js - n) % p.js}) for n in range(p.js // 2 + 1)]
+    messages = {0: dress(p, 0, place, spread, chol_vv, chol_ov)}
+    messages, spread = lax.optimization_barrier((messages, spread))
+    own, turned, shared, amps = {}, {}, {}, []
+    for n in range(len(groups) + 2):
+        new_own, new_turned, new_shared, work, new_amps = {}, {}, {}, {}, []
+        if n < len(groups):
+            for o in groups[n]:
+                new_own[o] = to_slice(messages[o], o)
+        if 1 <= n <= len(groups):
+            for o in groups[n - 1]:
+                for r in range(1, p.xs):
+                    new_turned[o, r] = along_x(own[o], r)
+            for o in groups[n - 1]:
+                new_shared[o, 0] = to_core(own[o])
+        if n >= 2:
+            for o in groups[n - 2]:
+                for r in range(1, p.xs):
+                    new_shared[o, r] = to_core(turned[o, r])
+        if n + 1 < len(groups):
+            for o in groups[n + 1]:
+                work[o] = dress(p, o, place, spread, chol_vv, chol_ov)
+        if n == len(groups) - 1:
+            new_amps = [relayout(p, amplitudes, part) for part in range(AMPS)]
+        moved = (new_own, new_turned, new_shared, work, new_amps)
+        everything = (moved, own, turned, shared, amps, spread, amplitudes)
+        moved, own, turned, shared, amps, spread, amplitudes = lax.optimization_barrier(everything)
+        own.update(moved[0])
+        turned.update(moved[1])
+        shared.update(moved[2])
+        messages = moved[3]
+        amps = amps or moved[4]
     amps = [amp.reshape(-1, p.d) for amp in amps]
-    pieces = [piece for o in range(p.js) for piece in found[o]]
+    pieces = []
+    for o in range(p.js):
+        for r in range(p.xs):
+            pieces += [turned[o, r] if r else own[o], shared[o, r]]
 
     partial_terms = ladder(p, place, assignment, pieces, amps)
     share = p.ij // n_aux

time: 368 us -> 269 us (0.73)
  waiting for transfers between devices: 132 us -> 77.4 us
  Pallas kernels: 171 us -> 148 us
  between operations: 13.7 us -> 0.33 us
  local copies, waits for them, and re-layouts: 20.5 us -> 15.9 us
    ppermute x8 -> x16, waiting for transfers between devices: 114 us -> 77.4 us  [permute(): return lax.ppermute(array, ('aux', 'pair'), pairs)]
    all_gather x8 -> x0, waiting for transfers between devices: 17.9 us -> none  [share(): lax.all_gather(array, 'aux', axis_index_groups=cores, axis=0, tiled=False)]
    pallas_call x1, Pallas kernels: 117 us -> 99.5 us  [ladder(): pl.pallas_call(functools.partial(ladder_kernel, p, group), out_shape=jax....]
    pallas_call x4, Pallas kernels: 35 us -> 29.3 us  [dress(): pl.pallas_call(functools.partial(dress_kernel, p, offset), out_shape=jax....]
    unnamed x32 -> x42, local copies, waits for them, and re-layouts: 18 us -> 13.4 us
    ppermute x8 -> x16, starting transfers between devices: 15.3 us -> 16.4 us  [permute(): return lax.ppermute(array, ('aux', 'pair'), pairs)]
  transfers between devices with their start and end apart: 16 -> 16, of which waited for: 7 -> 5; matrix products, arithmetic and copies ran while one was open for 0% -> 0% of each run, Pallas kernels for 12% -> 15%
where the time goes in v5:
time: 269 us; the launch traced here: 268 us
  Pallas kernels  148 us (55%)
  waiting for transfers between devices  77.4 us (29%)
  starting transfers between devices  16.4 us (6%)
  local copies, waits for them, and re-layouts  15.9 us (6%)
  blocking collectives  9.36 us (3%)
    pallas_call x1, Pallas kernels, ladder(): pl.pallas_call(functools.partial(ladder_kernel, p, group), out_shape=jax....  99.5 us
    ppermute x16, waiting for transfers between devices, permute(): return lax.ppermute(array, ('aux', 'pair'), pairs)  77.4 us
    pallas_call x4, Pallas kernels, dress(): pl.pallas_call(functools.partial(dress_kernel, p, offset), out_shape=jax....  29.3 us
    pallas_call x2, Pallas kernels, relayout(): pl.pallas_call(functools.partial(relayout_kernel, p), out_shape=jax.Shape...  18.4 us
    ppermute x16, starting transfers between devices, permute(): return lax.ppermute(array, ('aux', 'pair'), pairs)  16.4 us
    unnamed x42, local copies, waits for them, and re-layouts  13.4 us
    all_to_all x1, blocking collectives, shards(): lax.all_to_all(terms, ('aux', 'pair'), split_axis=0, concat_axis=0, tiled...  9.36 us
  transfers between devices with their start and end apart: 16, of which 5 were waited for; matrix products, arithmetic and copies ran while one was open for 0% of the time, Pallas kernels for 15%

profile of v5, /device:TPU:0, one launch (start us, length us, event | category | flops | bytes accessed | tf_op | source)
XLA Modules:
  0.0 268.1 jit_solution(11993512237824745005)
XLA Ops:
  0.0 0.8 copy.11.t1_ref
  0.8 0.8 spread.1.a_ref
  1.6 0.1 pad_add_fusion.z_ref.place_ref
  1.7 7.4 %dress.4 = bf16[36,112,128]{2,1,0:T(8,128)(2,1)S(1)} custom-call(s32[3]{0:T(128)S(1)} %pad_add_fusion.z_ref.place_ref, bf16[512,1600]{1,0:T(8,128)(2,1)S(1)} %spread.1.a_ref, bf16[100,112,576]{2,1,0:T(8,128)(2,1)} %refs_1_.7, bf16[100,112,576]{2,1,0:T(8,128)(2,1)} %refs_1_.7, bf16[32,112,576]{2,1,0:T(8,128)(2,1)} %refs_3_.7, bf16[32,112,576]{2,1,0:T(8,128)(2,1)} %refs_3_.7), custom_call_target="tpu_custom_call" | custom-call | flops 2936012800 | bytes 9404416 | tf_op jit(solution)/shard_map/dress/pallas_call | solution.py:127
  9.1 0.7 collective-permute-start
  9.8 7.3 %dress.5 = bf16[36,112,128]{2,1,0:T(8,128)(2,1)S(1)} custom-call(s32[3]{0:T(128)S(1)} %pad_add_fusion.z_ref.place_ref, bf16[512,1600]{1,0:T(8,128)(2,1)S(1)} %spread.1.a_ref, bf16[100,112,576]{2,1,0:T(8,128)(2,1)} %refs_1_.7, bf16[100,112,576]{2,1,0:T(8,128)(2,1)} %refs_1_.7, bf16[32,112,576]{2,1,0:T(8,128)(2,1)} %refs_3_.7, bf16[32,112,576]{2,1,0:T(8,128)(2,1)} %refs_3_.7), custom_call_target="tpu_custom_call" | custom-call | flops 2936012800 | bytes 9404416 | tf_op jit(solution)/shard_map/dress/pallas_call | solution.py:127
  17.1 7.3 %dress.6 = bf16[36,112,128]{2,1,0:T(8,128)(2,1)S(1)} custom-call(s32[3]{0:T(128)S(1)} %pad_add_fusion.z_ref.place_ref, bf16[512,1600]{1,0:T(8,128)(2,1)S(1)} %spread.1.a_ref, bf16[100,112,576]{2,1,0:T(8,128)(2,1)} %refs_1_.7, bf16[100,112,576]{2,1,0:T(8,128)(2,1)} %refs_1_.7, bf16[32,112,576]{2,1,0:T(8,128)(2,1)} %refs_3_.7, bf16[32,112,576]{2,1,0:T(8,128)(2,1)} %refs_3_.7), custom_call_target="tpu_custom_call" | custom-call | flops 2936012800 | bytes 9404416 | tf_op jit(solution)/shard_map/dress/pallas_call | solution.py:127
  24.4 3.1 %collective-permute-start.1 = (bf16[36,112,128]{2,1,0:T(8,128)(2,1)S(1)}, bf16[36,112,128]{2,1,0:T(8,128)(2,1)S(1)}, u32[]{:S(2)}, u32[]{:S(2)}) collective-permute-start(bf16[36,112,128]{2,1,0:T(8,128)(2,1)S(1)} %dress.5), channel_id=1, source_target_pairs={{0,2},{1,10},{2,4},{3,12},{4,6},{5,14},{6,0},{7,8},{8,3},{9,11},{1... | collective-permute-start | bytes 3096584 | tf_op jit(solution)/shard_map/ppermute | solution.py:353
  27.5 2.3 collective-permute-start.2
  29.8 1.5 collective-permute-start.3
  31.3 3.1 %collective-permute-start.4 = (bf16[36,112,128]{2,1,0:T(8,128)(2,1)S(1)}, bf16[36,112,128]{2,1,0:T(8,128)(2,1)S(1)}, u32[]{:S(2)}, u32[]{:S(2)}) collective-permute-start(bf16[36,112,128]{2,1,0:T(8,128)(2,1)S(1)} %collective-permute-done.refs_0_), channel_id=1, source_target_pairs={{0,8},{1,9},{2,10},{3,11},{4,12},{5,13},{6,14},{7,15},{8,0},{9,1},... | collective-permute-start | bytes 3096584 | tf_op jit(solution)/shard_map/ppermute | solution.py:353
  34.4 7.3 %dress.7 = bf16[36,112,128]{2,1,0:T(8,128)(2,1)S(1)} custom-call(s32[3]{0:T(128)S(1)} %pad_add_fusion.z_ref.place_ref, bf16[512,1600]{1,0:T(8,128)(2,1)S(1)} %spread.1.a_ref, bf16[100,112,576]{2,1,0:T(8,128)(2,1)} %refs_1_.7, bf16[100,112,576]{2,1,0:T(8,128)(2,1)} %refs_1_.7, bf16[32,112,576]{2,1,0:T(8,128)(2,1)} %refs_3_.7, bf16[32,112,576]{2,1,0:T(8,128)(2,1)} %refs_3_.7), custom_call_target="tpu_custom_call" | custom-call | flops 2936012800 | bytes 9404416 | tf_op jit(solution)/shard_map/dress/pallas_call | solution.py:127
  41.7 9.5 %collective-permute-done.1.refs_4_ = bf16[36,112,128]{2,1,0:T(8,128)(2,1)S(1)} collective-permute-done((bf16[36,112,128]{2,1,0:T(8,128)(2,1)S(1)}, bf16[36,112,128]{2,1,0:T(8,128)(2,1)S(1)}, u32[]{:S(2)}, u32[]{:S(2)}) %collective-permute-start.1) | collective-permute-done | bytes 1032224 | tf_op jit(solution)/shard_map/ppermute | solution.py:353
  51.2 24.0 %collective-permute-done.2.refs_12_ = bf16[36,112,128]{2,1,0:T(8,128)(2,1)S(1)} collective-permute-done((bf16[36,112,128]{2,1,0:T(8,128)(2,1)S(1)}, bf16[36,112,128]{2,1,0:T(8,128)(2,1)S(1)}, u32[]{:S(2)}, u32[]{:S(2)}) %collective-permute-start.2) | collective-permute-done | bytes 1032224 | tf_op jit(solution)/shard_map/ppermute | solution.py:353
  75.2 0.0 collective-permute-done.3.refs_2_
  75.2 0.0 collective-permute-done.4.refs_1_
  75.2 0.1 collective-permute-start.10
  75.3 1.3 collective-permute-start.7
  76.6 0.9 collective-permute-start.5
  77.4 0.5 collective-permute-start.6
  78.0 0.9 collective-permute-start.8
  78.9 0.1 collective-permute-start.9
  79.0 9.3 %relayout.2 = bf16[112,64,896]{2,1,0:T(8,128)(2,1)S(1)} custom-call(bf16[64,224,896]{2,1,0:T(8,128)(2,1)} %in_ref.1), custom_call_target="tpu_custom_call" | custom-call | flops 3288334336 | bytes 25690112 | tf_op jit(solution)/shard_map/relayout/pallas_call | solution.py:162
  88.3 4.6 %copy-done = bf16[112,64,896]{2,1,0:T(8,128)(2,1)} copy-done((bf16[112,64,896]{2,1,0:T(8,128)(2,1)}, bf16[112,64,896]{2,1,0:T(8,128)(2,1)S(1)}, u32[]{:S(2)}) %copy-start) | copy-done | bytes 12845080
  93.0 9.0 %relayout.3 = bf16[112,64,896]{2,1,0:T(8,128)(2,1)S(1)} custom-call(bf16[64,224,896]{2,1,0:T(8,128)(2,1)} %in_ref.1), custom_call_target="tpu_custom_call" | custom-call | flops 3288334336 | bytes 25690112 | tf_op jit(solution)/shard_map/relayout/pallas_call | solution.py:162
  102.0 4.6 %copy-done.1 = bf16[112,64,896]{2,1,0:T(8,128)(2,1)} copy-done((bf16[112,64,896]{2,1,0:T(8,128)(2,1)}, bf16[112,64,896]{2,1,0:T(8,128)(2,1)S(1)}, u32[]{:S(2)}) %copy-start.1) | copy-done | bytes 12845080
  106.6 18.0 %collective-permute-done.5.refs_8_ = bf16[36,112,128]{2,1,0:T(8,128)(2,1)S(1)} collective-permute-done((bf16[36,112,128]{2,1,0:T(8,128)(2,1)S(1)}, bf16[36,112,128]{2,1,0:T(8,128)(2,1)S(1)}, u32[]{:S(2)}, u32[]{:S(2)}) %collective-permute-start.5) | collective-permute-done | bytes 1032224 | tf_op jit(solution)/shard_map/ppermute | solution.py:353
  124.6 0.0 collective-permute-done.6.refs_6_
  124.7 1.3 collective-permute-start.11
  126.0 0.5 collective-permute-start.12
  126.5 0.0 collective-permute-start.14
  126.6 23.9 %collective-permute-done.11.refs_10_ = bf16[36,112,128]{2,1,0:T(8,128)(2,1)S(1)} collective-permute-done((bf16[36,112,128]{2,1,0:T(8,128)(2,1)S(1)}, bf16[36,112,128]{2,1,0:T(8,128)(2,1)S(1)}, u32[]{:S(2)}, u32[]{:S(2)}) %collective-permute-start.11) | collective-permute-done | bytes 1032224 | tf_op jit(solution)/shard_map/ppermute | solution.py:353
  150.5 1.0 copy-done.17
  151.5 0.4 copy-done.16
  151.8 1.0 copy-done.18
  152.8 0.1 collective-permute-start.15
  152.9 0.7 copy.12.blocks_ref
  153.6 2.0 collective-permute-done.15.refs_11_
  155.6 99.5 %ladder.1 = f32[32,4,128]{2,1,0:T(4,128)} custom-call(s32[3]{0:T(128)} %copy-done.2, s32[8,2]{1,0:T(8,128)} %copy.12.blocks_ref, bf16[36,112,128]{2,1,0:T(8,128)(2,1)} %copy-done.4, bf16[36,112,128]{2,1,0:T(8,128)(2,1)} %copy-done.8, bf16[36,112,128]{2,1,0:T(8,128)(2,1)} %copy-done.7, bf16[36,112,128]{2,1,0:T(8,128)(2,1)} %copy-done.13, ...), custom_call_target="tpu_custom_call" | custom-call | flops 13153337344 | bytes 42205184 | tf_op jit(solution)/shard_map/ladder/pallas_call | solution.py:298
  255.1 1.0 reshape.14
  256.2 0.2 copy.13
  256.3 0.2 copy.19
  256.5 0.1 reshape.16
  256.6 9.4 %all_to_all.5 = f32[32,1,256]{2,1,0:T(1,128)S(1)} all-to-all(f32[32,1,256]{2,1,0:T(1,128)S(1)} %reshape.16), channel_id=1, replica_groups=mesh['aux'=4,'pair'=8] {'aux','pair'}, dimensions={0} | all-to-all | bytes 65536 | tf_op jit(solution)/shard_map/all_to_all | solution.py:414
  266.0 0.5 broadcast.2
  266.5 0.7 reduce
  267.3 0.1 reshape.17
  267.4 0.7 copy.16
  (43 shorter events, 0.1 us)
Async XLA Ops:
  1.7 32.7 %copy-start.2 = (s32[3]{0:T(128)}, s32[3]{0:T(128)S(1)}, u32[]{:S(2)}) copy-start(s32[3]{0:T(128)S(1)} %pad_add_fusion.z_ref.place_ref) | copy-start | bytes 40
  9.1 15.3 %collective-permute-start = (bf16[36,112,128]{2,1,0:T(8,128)(2,1)S(1)}, bf16[36,112,128]{2,1,0:T(8,128)(2,1)S(1)}, u32[]{:S(2)}, u32[]{:S(2)}) collective-permute-start(bf16[36,112,128]{2,1,0:T(8,128)(2,1)S(1)} %dress.4), channel_id=1, source_target_pairs={{0,0},{1,8},{2,2},{3,10},{4,4},{5,12},{6,6},{7,14},{8,1},{9,9},{10... | collective-permute-start | bytes 3096584 | tf_op jit(solution)/shard_map/ppermute | solution.py:353
  24.4 17.3 %copy-start.4 = (bf16[36,112,128]{2,1,0:T(8,128)(2,1)}, bf16[36,112,128]{2,1,0:T(8,128)(2,1)S(1)}, u32[]{:S(2)}) copy-start(bf16[36,112,128]{2,1,0:T(8,128)(2,1)S(1)} %collective-permute-done.refs_0_) | copy-start | bytes 3096580
  24.4 26.7 %collective-permute-start.1 = (bf16[36,112,128]{2,1,0:T(8,128)(2,1)S(1)}, bf16[36,112,128]{2,1,0:T(8,128)(2,1)S(1)}, u32[]{:S(2)}, u32[]{:S(2)}) collective-permute-start(bf16[36,112,128]{2,1,0:T(8,128)(2,1)S(1)} %dress.5), channel_id=1, source_target_pairs={{0,2},{1,10},{2,4},{3,12},{4,6},{5,14},{6,0},{7,8},{8,3},{9,11},{1... | collective-permute-start | bytes 3096584 | tf_op jit(solution)/shard_map/ppermute | solution.py:353
  27.5 47.6 %collective-permute-start.2 = (bf16[36,112,128]{2,1,0:T(8,128)(2,1)S(1)}, bf16[36,112,128]{2,1,0:T(8,128)(2,1)S(1)}, u32[]{:S(2)}, u32[]{:S(2)}) collective-permute-start(bf16[36,112,128]{2,1,0:T(8,128)(2,1)S(1)} %dress.6), channel_id=1, source_target_pairs={{0,6},{1,14},{2,0},{3,8},{4,2},{5,10},{6,4},{7,12},{8,7},{9,15},{1... | collective-permute-start | bytes 3096584 | tf_op jit(solution)/shard_map/ppermute | solution.py:353
  29.8 45.4 %collective-permute-start.3 = (bf16[36,112,128]{2,1,0:T(8,128)(2,1)S(1)}, bf16[36,112,128]{2,1,0:T(8,128)(2,1)S(1)}, u32[]{:S(2)}, u32[]{:S(2)}) collective-permute-start(bf16[36,112,128]{2,1,0:T(8,128)(2,1)S(1)} %collective-permute-done.refs_0_), channel_id=1, source_target_pairs={{0,16},{1,17},{2,18},{3,19},{4,20},{5,21},{6,22},{7,23},{8,24},{9,... | collective-permute-start | bytes 3096584 | tf_op jit(solution)/shard_map/ppermute | solution.py:353
  31.3 43.9 %collective-permute-start.4 = (bf16[36,112,128]{2,1,0:T(8,128)(2,1)S(1)}, bf16[36,112,128]{2,1,0:T(8,128)(2,1)S(1)}, u32[]{:S(2)}, u32[]{:S(2)}) collective-permute-start(bf16[36,112,128]{2,1,0:T(8,128)(2,1)S(1)} %collective-permute-done.refs_0_), channel_id=1, source_target_pairs={{0,8},{1,9},{2,10},{3,11},{4,12},{5,13},{6,14},{7,15},{8,0},{9,1},... | collective-permute-start | bytes 3096584 | tf_op jit(solution)/shard_map/ppermute | solution.py:353
  51.2 37.1 %copy-start.5 = (bf16[36,112,128]{2,1,0:T(8,128)(2,1)}, bf16[36,112,128]{2,1,0:T(8,128)(2,1)S(1)}, u32[]{:S(2)}) copy-start(bf16[36,112,128]{2,1,0:T(8,128)(2,1)S(1)} %collective-permute-done.1.refs_4_) | copy-start | bytes 3096580
  75.2 13.1 %copy-start.6 = (bf16[36,112,128]{2,1,0:T(8,128)(2,1)}, bf16[36,112,128]{2,1,0:T(8,128)(2,1)S(1)}, u32[]{:S(2)}) copy-start(bf16[36,112,128]{2,1,0:T(8,128)(2,1)S(1)} %collective-permute-done.2.refs_12_) | copy-start | bytes 3096580
  75.2 13.1 %copy-start.7 = (bf16[36,112,128]{2,1,0:T(8,128)(2,1)}, bf16[36,112,128]{2,1,0:T(8,128)(2,1)S(1)}, u32[]{:S(2)}) copy-start(bf16[36,112,128]{2,1,0:T(8,128)(2,1)S(1)} %collective-permute-done.3.refs_2_) | copy-start | bytes 3096580
  75.2 3.7 %copy-start.8 = (bf16[36,112,128]{2,1,0:T(8,128)(2,1)}, bf16[36,112,128]{2,1,0:T(8,128)(2,1)S(1)}, u32[]{:S(2)}) copy-start(bf16[36,112,128]{2,1,0:T(8,128)(2,1)S(1)} %collective-permute-done.4.refs_1_) | copy-start | bytes 3096580
  75.2 3.7 %collective-permute-start.10 = (bf16[36,112,128]{2,1,0:T(8,128)(2,1)S(1)}, bf16[36,112,128]{2,1,0:T(8,128)(2,1)S(1)}, u32[]{:S(2)}, u32[]{:S(2)}) collective-permute-start(bf16[36,112,128]{2,1,0:T(8,128)(2,1)S(1)} %collective-permute-done.2.refs_12_), channel_id=1, source_target_pairs={{0,8},{1,9},{2,10},{3,11},{4,12},{5,13},{6,14},{7,15},{8,0},{9,1},... | collective-permute-start | bytes 3096584 | tf_op jit(solution)/shard_map/ppermute | solution.py:353
  75.3 49.4 %collective-permute-start.7 = (bf16[36,112,128]{2,1,0:T(8,128)(2,1)S(1)}, bf16[36,112,128]{2,1,0:T(8,128)(2,1)S(1)}, u32[]{:S(2)}, u32[]{:S(2)}) collective-permute-start(bf16[36,112,128]{2,1,0:T(8,128)(2,1)S(1)} %collective-permute-done.2.refs_12_), channel_id=1, source_target_pairs={{0,16},{1,17},{2,18},{3,19},{4,20},{5,21},{6,22},{7,23},{8,24},{9,... | collective-permute-start | bytes 3096584 | tf_op jit(solution)/shard_map/ppermute | solution.py:353
  76.6 48.1 %collective-permute-start.5 = (bf16[36,112,128]{2,1,0:T(8,128)(2,1)S(1)}, bf16[36,112,128]{2,1,0:T(8,128)(2,1)S(1)}, u32[]{:S(2)}, u32[]{:S(2)}) collective-permute-start(bf16[36,112,128]{2,1,0:T(8,128)(2,1)S(1)} %dress.7), channel_id=1, source_target_pairs={{0,4},{1,12},{2,6},{3,14},{4,0},{5,8},{6,2},{7,10},{8,5},{9,13},{1... | collective-permute-start | bytes 3096584 | tf_op jit(solution)/shard_map/ppermute | solution.py:353
  77.4 47.2 %collective-permute-start.6 = (bf16[36,112,128]{2,1,0:T(8,128)(2,1)S(1)}, bf16[36,112,128]{2,1,0:T(8,128)(2,1)S(1)}, u32[]{:S(2)}, u32[]{:S(2)}) collective-permute-start(bf16[36,112,128]{2,1,0:T(8,128)(2,1)S(1)} %collective-permute-done.1.refs_4_), channel_id=1, source_target_pairs={{0,16},{1,17},{2,18},{3,19},{4,20},{5,21},{6,22},{7,23},{8,24},{9,... | collective-permute-start | bytes 3096584 | tf_op jit(solution)/shard_map/ppermute | solution.py:353
  78.0 46.7 %collective-permute-start.8 = (bf16[36,112,128]{2,1,0:T(8,128)(2,1)S(1)}, bf16[36,112,128]{2,1,0:T(8,128)(2,1)S(1)}, u32[]{:S(2)}, u32[]{:S(2)}) collective-permute-start(bf16[36,112,128]{2,1,0:T(8,128)(2,1)S(1)} %collective-permute-done.3.refs_2_), channel_id=1, source_target_pairs={{0,8},{1,9},{2,10},{3,11},{4,12},{5,13},{6,14},{7,15},{8,0},{9,1},... | collective-permute-start | bytes 3096584 | tf_op jit(solution)/shard_map/ppermute | solution.py:353
  78.9 9.5 %copy-start.9 = (bf16[36,112,128]{2,1,0:T(8,128)(2,1)}, bf16[36,112,128]{2,1,0:T(8,128)(2,1)S(1)}, u32[]{:S(2)}) copy-start(bf16[36,112,128]{2,1,0:T(8,128)(2,1)S(1)} %collective-permute-done.10.refs_13_) | copy-start | bytes 3096580
  78.9 45.8 %collective-permute-start.9 = (bf16[36,112,128]{2,1,0:T(8,128)(2,1)S(1)}, bf16[36,112,128]{2,1,0:T(8,128)(2,1)S(1)}, u32[]{:S(2)}, u32[]{:S(2)}) collective-permute-start(bf16[36,112,128]{2,1,0:T(8,128)(2,1)S(1)} %collective-permute-done.1.refs_4_), channel_id=1, source_target_pairs={{0,8},{1,9},{2,10},{3,11},{4,12},{5,13},{6,14},{7,15},{8,0},{9,1},... | collective-permute-start | bytes 3096584 | tf_op jit(solution)/shard_map/ppermute | solution.py:353
  88.3 4.6 %copy-start = (bf16[112,64,896]{2,1,0:T(8,128)(2,1)}, bf16[112,64,896]{2,1,0:T(8,128)(2,1)S(1)}, u32[]{:S(2)}) copy-start(bf16[112,64,896]{2,1,0:T(8,128)(2,1)S(1)} %relayout.2) | copy-start | bytes 38535172
  93.0 60.0 %copy-start.3 = (s32[8,2]{0,1:T(2,128)S(1)}, s32[8,2]{0,1:T(2,128)}, u32[]{:S(2)}) copy-start(s32[8,2]{0,1:T(2,128)} %param.9) | copy-start | bytes 196
  102.0 4.6 %copy-start.1 = (bf16[112,64,896]{2,1,0:T(8,128)(2,1)}, bf16[112,64,896]{2,1,0:T(8,128)(2,1)S(1)}, u32[]{:S(2)}) copy-start(bf16[112,64,896]{2,1,0:T(8,128)(2,1)S(1)} %relayout.3) | copy-start | bytes 38535172
  124.6 31.0 %copy-start.11 = (bf16[36,112,128]{2,1,0:T(8,128)(2,1)}, bf16[36,112,128]{2,1,0:T(8,128)(2,1)S(1)}, u32[]{:S(2)}) copy-start(bf16[36,112,128]{2,1,0:T(8,128)(2,1)S(1)} %collective-permute-done.5.refs_8_) | copy-start | bytes 3096580
  124.6 25.8 %copy-start.12 = (bf16[36,112,128]{2,1,0:T(8,128)(2,1)}, bf16[36,112,128]{2,1,0:T(8,128)(2,1)S(1)}, u32[]{:S(2)}) copy-start(bf16[36,112,128]{2,1,0:T(8,128)(2,1)S(1)} %collective-permute-done.6.refs_6_) | copy-start | bytes 3096580
  124.7 31.0 %copy-start.10 = (bf16[36,112,128]{2,1,0:T(8,128)(2,1)}, bf16[36,112,128]{2,1,0:T(8,128)(2,1)S(1)}, u32[]{:S(2)}) copy-start(bf16[36,112,128]{2,1,0:T(8,128)(2,1)S(1)} %collective-permute-done.7.refs_14_) | copy-start | bytes 3096580
  124.7 25.8 %copy-start.13 = (bf16[36,112,128]{2,1,0:T(8,128)(2,1)}, bf16[36,112,128]{2,1,0:T(8,128)(2,1)S(1)}, u32[]{:S(2)}) copy-start(bf16[36,112,128]{2,1,0:T(8,128)(2,1)S(1)} %collective-permute-done.8.refs_3_) | copy-start | bytes 3096580
  124.7 25.8 %copy-start.14 = (bf16[36,112,128]{2,1,0:T(8,128)(2,1)}, bf16[36,112,128]{2,1,0:T(8,128)(2,1)S(1)}, u32[]{:S(2)}) copy-start(bf16[36,112,128]{2,1,0:T(8,128)(2,1)S(1)} %collective-permute-done.9.refs_5_) | copy-start | bytes 3096580
  124.7 25.7 %collective-permute-start.11 = (bf16[36,112,128]{2,1,0:T(8,128)(2,1)S(1)}, bf16[36,112,128]{2,1,0:T(8,128)(2,1)S(1)}, u32[]{:S(2)}, u32[]{:S(2)}) collective-permute-start(bf16[36,112,128]{2,1,0:T(8,128)(2,1)S(1)} %collective-permute-done.5.refs_8_), channel_id=1, source_target_pairs={{0,16},{1,17},{2,18},{3,19},{4,20},{5,21},{6,22},{7,23},{8,24},{9,... | collective-permute-start | bytes 3096584 | tf_op jit(solution)/shard_map/ppermute | solution.py:353
  126.0 24.4 %collective-permute-start.13 = (bf16[36,112,128]{2,1,0:T(8,128)(2,1)S(1)}, bf16[36,112,128]{2,1,0:T(8,128)(2,1)S(1)}, u32[]{:S(2)}, u32[]{:S(2)}) collective-permute-start(bf16[36,112,128]{2,1,0:T(8,128)(2,1)S(1)} %collective-permute-done.5.refs_8_), channel_id=1, source_target_pairs={{0,8},{1,9},{2,10},{3,11},{4,12},{5,13},{6,14},{7,15},{8,0},{9,1},... | collective-permute-start | bytes 3096584 | tf_op jit(solution)/shard_map/ppermute | solution.py:353
  126.0 24.4 %collective-permute-start.12 = (bf16[36,112,128]{2,1,0:T(8,128)(2,1)S(1)}, bf16[36,112,128]{2,1,0:T(8,128)(2,1)S(1)}, u32[]{:S(2)}, u32[]{:S(2)}) collective-permute-start(bf16[36,112,128]{2,1,0:T(8,128)(2,1)S(1)} %collective-permute-done.6.refs_6_), channel_id=1, source_target_pairs={{0,8},{1,9},{2,10},{3,11},{4,12},{5,13},{6,14},{7,15},{8,0},{9,1},... | collective-permute-start | bytes 3096584 | tf_op jit(solution)/shard_map/ppermute | solution.py:353
  126.5 23.9 %collective-permute-start.14 = (bf16[36,112,128]{2,1,0:T(8,128)(2,1)S(1)}, bf16[36,112,128]{2,1,0:T(8,128)(2,1)S(1)}, u32[]{:S(2)}, u32[]{:S(2)}) collective-permute-start(bf16[36,112,128]{2,1,0:T(8,128)(2,1)S(1)} %collective-permute-done.7.refs_14_), channel_id=1, source_target_pairs={{0,8},{1,9},{2,10},{3,11},{4,12},{5,13},{6,14},{7,15},{8,0},{9,1},... | collective-permute-start | bytes 3096584 | tf_op jit(solution)/shard_map/ppermute | solution.py:353
  150.4 5.2 %copy-start.15 = (bf16[36,112,128]{2,1,0:T(8,128)(2,1)}, bf16[36,112,128]{2,1,0:T(8,128)(2,1)S(1)}, u32[]{:S(2)}) copy-start(bf16[36,112,128]{2,1,0:T(8,128)(2,1)S(1)} %collective-permute-done.11.refs_10_) | copy-start | bytes 3096580
  150.4 1.0 copy-start.17
  150.5 1.4 copy-start.16
  151.8 1.0 copy-start.18
  152.8 2.8 %collective-permute-start.15 = (bf16[36,112,128]{2,1,0:T(8,128)(2,1)S(1)}, bf16[36,112,128]{2,1,0:T(8,128)(2,1)}, u32[]{:S(2)}, u32[]{:S(2)}) collective-permute-start(bf16[36,112,128]{2,1,0:T(8,128)(2,1)S(1)} %collective-permute-done.11.refs_10_), channel_id=1, source_target_pairs={{0,8},{1,9},{2,10},{3,11},{4,12},{5,13},{6,14},{7,15},{8,0},{9,1},... | collective-permute-start | bytes 3096584 | tf_op jit(solution)/shard_map/ppermute | solution.py:353

commit v6 on v3

--- a/solution.py
+++ b/solution.py
@@ -10,6 +10,7 @@
 BLK = 4
 QUAD = 4
 AMPS = 2
+SLOTS = 3
 ROWS = 16
 LANES = 128
 CORES = 2
@@ -80,23 +81,28 @@
     ov, vv, out = refs[: p.nm + 1], refs[p.nm + 1 : 2 * p.nm + 2], refs[-1]
     w = p.window
     j = lax.rem(z_ref[0] + offset, p.js)
-    vectors = jnp.concatenate([ref[...].reshape(p.occupied * ROWS, -1) for ref in ov], axis=1)
-    shift = lax.dot_general(a_ref[...], vectors, NN, preferred_element_type=jnp.float32)
-    for m in range(p.nm):
-        here = shift[:, m * LANES : (m + 1) * LANES].reshape(w, ROWS, LANES)
-        out[m * w : (m + 1) * w] = (vv[m][...].astype(jnp.float32) - here).astype(jnp.bfloat16)
-    here = shift[:, p.nm * LANES :].reshape(w, ROWS, p.tail_width)
-    source = vv[p.nm][...].astype(jnp.float32) - here
-    source = source.reshape(p.nt, p.per_row, ROWS, p.tail_width)
     lane = lax.broadcasted_iota(jnp.int32, (p.nt, ROWS, LANES), 2)
-    rest = jnp.zeros((p.nt, ROWS, LANES), jnp.float32)
-    for s in range(p.per_row):
-        turn = lax.rem(s * p.slot - j * p.tail + 2 * p.tail_width, p.tail_width)
-        moved = pltpu.roll(source[:, s].reshape(p.nt * ROWS, p.tail_width), turn, 1)
-        moved = moved[:, :LANES].reshape(p.nt, ROWS, LANES)
-        keep = (lane >= s * p.slot) & (lane < s * p.slot + p.tail)
-        rest = jnp.where(keep, moved, rest)
-    out[p.nm * w :] = rest.astype(jnp.bfloat16)
+    for low in range(0, p.cpad, ROWS):
+        cols = slice(low, low + ROWS)
+        vectors = [ref[:, cols].reshape(p.occupied * ROWS, -1) for ref in ov]
+        shift = lax.dot_general(
+            a_ref[...], jnp.concatenate(vectors, axis=1), NN, preferred_element_type=jnp.float32
+        )
+        for m in range(p.nm):
+            here = shift[:, m * LANES : (m + 1) * LANES].reshape(w, ROWS, LANES)
+            here = vv[m][:, cols].astype(jnp.float32) - here
+            out[m * w : (m + 1) * w, cols] = here.astype(jnp.bfloat16)
+        here = shift[:, p.nm * LANES :].reshape(w, ROWS, p.tail_width)
+        source = vv[p.nm][:, cols].astype(jnp.float32) - here
+        source = source.reshape(p.nt, p.per_row, ROWS, p.tail_width)
+        rest = jnp.zeros((p.nt, ROWS, LANES), jnp.float32)
+        for s in range(p.per_row):
+            turn = lax.rem(s * p.slot - j * p.tail + 2 * p.tail_width, p.tail_width)
+            moved = pltpu.roll(source[:, s].reshape(p.nt * ROWS, p.tail_width), turn, 1)
+            moved = moved[:, :LANES].reshape(p.nt, ROWS, LANES)
+            keep = (lane >= s * p.slot) & (lane < s * p.slot + p.tail)
+            rest = jnp.where(keep, moved, rest)
+        out[p.nm * w :, cols] = rest.astype(jnp.bfloat16)
 
 
 def dress(p, offset, z, spread, chol_vv, chol_ov):
@@ -105,13 +111,14 @@
         for m in range(p.nm):
             found.append(
                 pl.BlockSpec(
-                    (lead, ROWS, LANES),
-                    lambda i, z, m=m: (0, i, lax.rem(z[0] + offset, p.js) * p.nm + m),
+                    (lead, p.cpad, LANES),
+                    lambda i, z, m=m: (0, 0, lax.rem(z[0] + offset, p.js) * p.nm + m),
                 )
             )
         found.append(
             pl.BlockSpec(
-                (lead, ROWS, p.tail_width), lambda i, z: (0, i, p.tail_from // p.tail_width)
+                (lead, p.cpad, p.tail_width),
+                lambda i, z: (0, 0, p.tail_from // p.tail_width),
             )
         )
         return found
@@ -122,11 +129,11 @@
         out_shape=jax.ShapeDtypeStruct((p.planes, p.cpad, LANES), jnp.bfloat16),
         grid_spec=pltpu.PrefetchScalarGridSpec(
             num_scalar_prefetch=1,
-            grid=(p.cpad // ROWS,),
+            grid=(1,),
             in_specs=[pl.BlockSpec((p.window * ROWS, p.occupied * ROWS), lambda i, z: (0, 0))]
             + specs(p.occupied)
             + specs(p.window),
-            out_specs=pl.BlockSpec((p.planes, ROWS, LANES), lambda i, z: (0, i, 0)),
+            out_specs=pl.BlockSpec((p.planes, p.cpad, LANES), lambda i, z: (0, 0, 0)),
         ),
         compiler_params=pltpu.CompilerParams(vmem_limit_bytes=48 * 2**20),
         cost_estimate=pl.CostEstimate(
@@ -143,10 +150,10 @@
     to = lax.broadcasted_iota(jnp.int32, (rows, rows), 0)
     frm = lax.broadcasted_iota(jnp.int32, (rows, rows), 1)
     turn = (to % ROWS * ROWS + to // ROWS == frm).astype(jnp.float32).astype(jnp.bfloat16)
-    turned = lax.dot_general(
-        turn, in_ref[...].reshape(rows, p.d), NN, preferred_element_type=jnp.float32
-    )
-    out_ref[...] = turned.astype(jnp.bfloat16).reshape(ROWS, ROWS, p.d)
+    for low in range(0, p.ij, ROWS):
+        block = in_ref[low : low + ROWS].reshape(rows, p.d)
+        turned = lax.dot_general(turn, block, NN, preferred_element_type=jnp.float32)
+        out_ref[:, low : low + ROWS] = turned.astype(jnp.bfloat16).reshape(ROWS, ROWS, p.d)
 
 
 def relayout(p, amplitudes, part):
@@ -155,9 +162,10 @@
     return pl.pallas_call(
         functools.partial(relayout_kernel, p),
         out_shape=jax.ShapeDtypeStruct((count, p.ij, p.d), jnp.bfloat16),
-        grid=(blocks, p.ij // ROWS),
-        in_specs=[pl.BlockSpec((ROWS, ROWS, p.d), lambda c, i: (i, part * blocks + c, 0))],
-        out_specs=pl.BlockSpec((ROWS, ROWS, p.d), lambda c, i: (c, i, 0)),
+        grid=(blocks,),
+        in_specs=[pl.BlockSpec((p.ij, ROWS, p.d), lambda c: (0, part * blocks + c, 0))],
+        out_specs=pl.BlockSpec((ROWS, p.ij, p.d), lambda c: (c, 0, 0)),
+        compiler_params=pltpu.CompilerParams(vmem_limit_bytes=40 * 2**20),
         cost_estimate=pl.CostEstimate(
             flops=2 * count * p.ij * p.d * ROWS * ROWS,
             bytes_accessed=4 * count * p.ij * p.d,
@@ -167,11 +175,12 @@
     )(amplitudes)
 
 
-def ladder_kernel(p, parts, group, place_ref, blocks_ref, *refs):
-    pieces, amps, out = refs[: p.js], refs[p.js : p.js + AMPS], refs[p.js + AMPS]
-    scratch = refs[p.js + AMPS + 1 :]
+def ladder_kernel(p, units, parts, group, place_ref, blocks_ref, *refs):
+    count = len(units) * p.xs * CORES
+    pieces, amps, out = refs[:count], refs[count : count + AMPS], refs[count + AMPS]
+    scratch = refs[count + AMPS + 1 :]
     vectors, left_main, left_tail, spread_tail, tiles, held, total, piece_sem, amp_sem = scratch
-    w, z, chunk = p.window, place_ref[0], place_ref[1]
+    w, z, core, chunk = p.window, place_ref[0], place_ref[1], place_ref[2]
     quads = p.c // QUAD
     here = quads // parts
     rows = here * ROWS
@@ -198,21 +207,26 @@
             self.copy(amps[0], 0).wait()
 
     copies = []
-    for o in range(p.js):
-        for source in range(p.n_aux):
-            r, parity = source // CORES, source % CORES
-            origin = CORES * lax.rem(z - o + p.js, p.js) + parity
-            row = pl.multiple_of(origin * p.cpad, ROWS)
-            copies.append(
-                pltpu.make_async_copy(
-                    pieces[o].at[source],
-                    vectors.at[:, pl.ds(row, p.cpad), r * LANES : (r + 1) * LANES],
-                    piece_sem.at[o * p.n_aux + source],
+    for n, (o, low, high) in enumerate(units):
+        for r in range(p.xs):
+            for other in range(CORES):
+                parity = core if other == 0 else 1 - core
+                origin = CORES * lax.rem(z - o + p.js, p.js) + parity
+                row = pl.multiple_of(origin * p.cpad, ROWS)
+                number = (n * p.xs + r) * CORES + other
+                copies.append(
+                    pltpu.make_async_copy(
+                        pieces[number],
+                        vectors.at[
+                            low:high, pl.ds(row, p.cpad), r * LANES : (r + 1) * LANES
+                        ],
+                        piece_sem.at[number],
+                    )
                 )
-            )
     for copy in copies:
         copy.start()
-    Fetch(jnp.int32(0), 0).start()
+    for ahead in range(min(SLOTS - 1, parts * steps)):
+        Fetch(jnp.int32(ahead), ahead).start()
     for copy in copies:
         copy.wait()
 
@@ -266,15 +280,13 @@
             left = blocks_ref[gf // BLK, 0]
             index = blocks_ref[gf // BLK, 1] * BLK + gf % BLK
             only = (slot_of == index % p.per_row).astype(jnp.float32).astype(jnp.bfloat16)
-            lhs = [left_tail[left, part_rows] * only]
-            planes = [p.nm * w + index // p.per_row]
-            for m in range(p.nm):
-                lhs.append(left_main[m, left, part_rows])
-                planes.append(m * w + index)
-            lhs = jnp.concatenate(lhs, axis=1)
+            lhs = [left_main[m, left, part_rows] for m in range(p.nm)]
+            lhs = jnp.concatenate(lhs + [left_tail[left, part_rows]], axis=1)
             for low in range(0, p.d, 256):
                 span = slice(low, min(low + 256, p.d))
-                rhs = jnp.concatenate([vectors[plane, span] for plane in planes], axis=1)
+                rhs = [vectors[m * w + index, span] for m in range(p.nm)]
+                rhs.append(vectors[p.nm * w + index // p.per_row, span] * only)
+                rhs = jnp.concatenate(rhs, axis=1)
                 block = lax.dot_general(lhs, rhs, NT, preferred_element_type=jnp.float32)
                 block = block.astype(jnp.bfloat16).reshape(here, ROWS, span.stop - low)
                 tiles[:, gf, :, span] = block
@@ -282,11 +294,11 @@
         @pl.loop(0, steps)
         def _(step):
             at = part * steps + step
-            slot = lax.rem(at, 2)
-
-            @pl.when(at + 1 < parts * steps)
+            slot = lax.rem(at, SLOTS)
+
+            @pl.when(at + SLOTS - 1 < parts * steps)
             def _():
-                Fetch(at + 1, 1 - slot).start()
+                Fetch(at + SLOTS - 1, lax.rem(at + SLOTS - 1, SLOTS)).start()
 
             Fetch(at, slot).wait()
             width = QUAD * p.ij
@@ -313,7 +325,7 @@
     out[...] = folded[:, :4] + folded[:, 4:]
 
 
-def ladder(p, place, blocks, pieces, amps):
+def ladder(p, units, place, blocks, pieces, amps):
     parts, group = 2, 1
     quads = p.c // QUAD
     for wanted in (4, 2):
@@ -322,7 +334,7 @@
             break
     width = QUAD * p.ij
     return pl.pallas_call(
-        functools.partial(ladder_kernel, p, parts, group),
+        functools.partial(ladder_kernel, p, units, parts, group),
         out_shape=jax.ShapeDtypeStruct((p.gf, BLK, LANES), jnp.float32),
         in_specs=[pl.BlockSpec(memory_space=pltpu.SMEM)] * 2
         + [pl.BlockSpec(memory_space=pl.ANY)] * (len(pieces) + AMPS),
@@ -333,12 +345,12 @@
             pltpu.VMEM((p.blocks, BLK * p.c, p.k), jnp.bfloat16),
             pltpu.VMEM((BLK, p.c, p.k), jnp.bfloat16),
             pltpu.VMEM((quads // parts, p.gf, ROWS, p.d), jnp.bfloat16),
-            pltpu.VMEM((2, group * width, p.d), jnp.bfloat16),
+            pltpu.VMEM((SLOTS, group * width, p.d), jnp.bfloat16),
             pltpu.VMEM((p.gf * ROWS, width), jnp.float32),
-            pltpu.SemaphoreType.DMA((p.js * p.n_aux,)),
-            pltpu.SemaphoreType.DMA((2,)),
+            pltpu.SemaphoreType.DMA((len(pieces),)),
+            pltpu.SemaphoreType.DMA((SLOTS,)),
         ],
-        compiler_params=pltpu.CompilerParams(vmem_limit_bytes=63 * 2**20),
+        compiler_params=pltpu.CompilerParams(vmem_limit_bytes=60 * 2**20),
         cost_estimate=pl.CostEstimate(
             flops=2 * p.gf * BLK * p.c * p.d * p.k,
             bytes_accessed=2 * (p.js * p.n_aux * p.planes * p.cpad * LANES + p.c * p.ij * p.d),
@@ -365,7 +377,7 @@
     p = Plan(window, chol_ov.shape[0], cols, aux_dev, n_aux, n_pair, amplitudes.shape[0])
     me_aux, me_pair = lax.axis_index("aux"), lax.axis_index("pair")
     z = me_pair // CORES
-    place = jnp.stack([z, me_aux]).astype(jnp.int32)
+    place = jnp.stack([z, me_aux % CORES, me_aux]).astype(jnp.int32)
 
     chol_vv = pad_columns(chol_vv, 1, cols, p.cpad)
     chol_ov = pad_columns(chol_ov, 1, cols, p.cpad)
@@ -388,41 +400,76 @@
             ),
         )
 
+    def along_x(array, r):
+        return permute(array, lambda a, q: (CORES * ((a // CORES + r) % p.xs) + a % CORES, q))
+
+    def to_core(array):
+        return permute(array, lambda a, q: (a ^ 1, q))
+
+    amplitudes = pad_columns(pad_columns(amplitudes, 1, cols, p.cpad), 2, cols, p.cpad)
+
     order = sorted(range(p.js), key=lambda o: min(o, p.js - o))
+    units = [(o, 0, p.planes) for o in order]
+    if p.js > 2:
+        half = p.planes // 2
+        units[-1:] = [(order[-1], 0, half), (order[-1], half, p.planes)]
+        rounds = [[units[1], units[0]]] + [[unit] for unit in units[2:]]
+        swaps = [[units[0]], [units[1]]] + [[unit] for unit in units[2:-2]] + [units[-2:]]
+    else:
+        rounds, swaps = [units], [units]
+
+    def make(o, spread):
+        return dress(p, o, place, spread, chol_vv, chol_ov)
+
+    def cut(message, unit):
+        if unit[1:] == (0, p.planes):
+            return message
+        return message[unit[1] : unit[2]]
+
     messages = {}
-    for place_in_order, o in enumerate(order):
-        messages[o] = dress(p, o, place, spread, chol_vv, chol_ov)
-        if o == 0:
-            turned_here = to_slice(messages[0], 0)
-        if place_in_order == 1:
-            spread, messages[o], turned_here = lax.optimization_barrier(
-                (spread, messages[o], turned_here)
-            )
-        else:
-            spread, messages[o] = lax.optimization_barrier((spread, messages[o]))
-
-    messages[order[-1]], amplitudes = lax.optimization_barrier((messages[order[-1]], amplitudes))
-    amplitudes = pad_columns(pad_columns(amplitudes, 1, cols, p.cpad), 2, cols, p.cpad)
-    amps = [relayout(p, amplitudes, part) for part in range(AMPS)]
-
-    found = {}
-    before = turned_here
-    for place_in_order, o in enumerate(order):
-        if o == 0:
-            own = turned_here
-        else:
-            message, before = lax.optimization_barrier((messages[o], before))
-            own = before = to_slice(message, o)
-        if place_in_order == 1:
-            own, messages[order[2]] = lax.optimization_barrier((own, messages[order[2]]))
-        part = place_in_order - (p.js - AMPS)
-        if part >= 0:
-            own, amps[part] = lax.optimization_barrier((own, amps[part]))
-        found[o] = lax.all_gather(own, "aux", axis=0, tiled=False)
+    for o, _, _ in rounds[0]:
+        messages[o] = make(o, spread)
+        messages[o], spread = lax.optimization_barrier((messages[o], spread))
+    amps = [None] * AMPS
+    sources = [amplitudes] * AMPS
+    held = {}
+    share_next = []
+    count = max(len(rounds), len(swaps) + 1) + 1
+    for n in range(count):
+        new, made, laid = {}, {}, {}
+        to_share, share_next = share_next, []
+        if n < len(rounds):
+            for unit in rounds[n]:
+                new[unit, 0, 0] = to_slice(cut(messages[unit[0]], unit), unit[0])
+                share_next.append((unit, 0))
+        if 1 <= n <= len(swaps):
+            for unit in swaps[n - 1]:
+                for r in range(1, p.xs):
+                    new[unit, r, 0] = along_x(held[unit, 0, 0], r)
+                    share_next.append((unit, r))
+        for unit, r in to_share:
+            new[unit, r, 1] = to_core(held[unit, r, 0])
+        if n + 1 < len(rounds):
+            for o, _, _ in rounds[n + 1]:
+                if o not in messages:
+                    made[o] = make(o, spread)
+        part = n - (len(swaps) - AMPS)
+        if 0 <= part < AMPS:
+            laid[part] = relayout(p, sources[part], part)
+        moved = (list(new.values()), list(made.values()), list(laid.values()))
+        kept = (list(held.values()), spread, sources)
+        moved, (old, spread, sources) = lax.optimization_barrier((moved, kept))
+        held = dict(zip(held, old))
+        held.update(zip(new, moved[0]))
+        messages.update(zip(made, moved[1]))
+        for part, amp in zip(laid, moved[2]):
+            amps[part] = amp
     amps = [amp.reshape(-1, p.d) for amp in amps]
-    pieces = [found[o] for o in range(p.js)]
-
-    partial_terms = ladder(p, place, assignment, pieces, amps)
+    pieces = [
+        held[unit, r, other] for unit in units for r in range(p.xs) for other in range(CORES)
+    ]
+
+    partial_terms = ladder(p, units, place, assignment, pieces, amps)
     share = p.ij // n_aux
     terms = partial_terms[:, :, : p.ij].reshape(n_pair, BLK, BLK, n_aux, share)
     terms = terms.transpose(3, 0, 4, 2, 1).reshape(n_aux * n_pair, share, BLK * BLK)

time: 277 us -> 242 us (0.87)
  Pallas kernels: 157 us -> 122 us
  starting transfers between devices: 6.28 us -> 19.9 us
  between operations: 13.3 us -> 0.37 us
  local copies, waits for them, and re-layouts: 7.18 us -> 14.7 us
  waiting for transfers between devices: 78.8 us -> 74.3 us
    all_gather x4 -> x0, waiting for transfers between devices: 47.5 us -> none  [shards(): found[o] = lax.all_gather(own, 'aux', axis=0, tiled=False)]
    ppermute x4 -> x20, waiting for transfers between devices: 31.2 us -> 74.3 us  [permute(): return lax.ppermute(array, ('aux', 'pair'), pairs)]
    pallas_call x2, Pallas kernels: 45.8 us -> 18.1 us  [relayout(): pl.pallas_call(functools.partial(relayout_kernel, p), out_shape=jax.Shape...]
    ppermute x4 -> x20, starting transfers between devices: 6.16 us -> 19.9 us  [permute(): return lax.ppermute(array, ('aux', 'pair'), pairs)]
    unnamed x14 -> x50, local copies, waits for them, and re-layouts: 4.67 us -> 12.1 us
    pallas_call x4, Pallas kernels: 34.8 us -> 29.2 us  [dress(): pl.pallas_call(functools.partial(dress_kernel, p, offset), out_shape=jax....]
  transfers between devices with their start and end apart: 8 -> 20, of which waited for: 4 -> 9; matrix products, arithmetic and copies ran while one was open for 0% -> 0% of each run, Pallas kernels for 26% -> 13%
where the time goes in v6:
time: 242 us
  Pallas kernels  122 us (50%)
  waiting for transfers between devices  74.3 us (31%)
  starting transfers between devices  19.9 us (8%)
  local copies, waits for them, and re-layouts  14.7 us (6%)
  blocking collectives  9.83 us (4%)
    ppermute x20, waiting for transfers between devices, permute(): return lax.ppermute(array, ('aux', 'pair'), pairs)  74.3 us
    pallas_call x1, Pallas kernels, ladder(): pl.pallas_call(functools.partial(ladder_kernel, p, units, parts, group),...  73.7 us
    pallas_call x4, Pallas kernels, dress(): pl.pallas_call(functools.partial(dress_kernel, p, offset), out_shape=jax....  29.2 us
    ppermute x20, starting transfers between devices, permute(): return lax.ppermute(array, ('aux', 'pair'), pairs)  19.9 us
    pallas_call x2, Pallas kernels, relayout(): pl.pallas_call(functools.partial(relayout_kernel, p), out_shape=jax.Shape...  18.1 us
    unnamed x50, local copies, waits for them, and re-layouts  12.1 us
    all_to_all x1, blocking collectives, shards(): lax.all_to_all(terms, ('aux', 'pair'), split_axis=0, concat_axis=0, tiled...  9.83 us
  transfers between devices with their start and end apart: 20, of which 9 were waited for; matrix products, arithmetic and copies ran while one was open for 0% of the time, Pallas kernels for 13%

profile of v6, /device:TPU:0, one launch (start us, length us, event | category | flops | bytes accessed | tf_op | source)
XLA Modules:
  0.0 241.8 jit_solution(12598723015576847689)
XLA Ops:
  0.0 0.8 copy.11.t1_ref
  0.8 0.8 spread.1.a_ref
  1.6 0.1 pad_add_fusion.z_ref.place_ref
  1.7 7.3 %dress.4 = bf16[36,112,128]{2,1,0:T(8,128)(2,1)S(1)} custom-call(s32[3]{0:T(128)S(1)} %pad_add_fusion.z_ref.place_ref, bf16[512,1600]{1,0:T(8,128)(2,1)S(1)} %spread.1.a_ref, bf16[100,112,576]{2,1,0:T(8,128)(2,1)} %refs_1_.7, bf16[100,112,576]{2,1,0:T(8,128)(2,1)} %refs_1_.7, bf16[32,112,576]{2,1,0:T(8,128)(2,1)} %refs_3_.7, bf16[32,112,576]{2,1,0:T(8,128)(2,1)} %refs_3_.7), custom_call_target="tpu_custom_call" | custom-call | flops 2936012800 | bytes 9404416 | tf_op jit(solution)/shard_map/dress/pallas_call | solution.py:127
  9.0 7.4 %dress.5 = bf16[36,112,128]{2,1,0:T(8,128)(2,1)S(1)} custom-call(s32[3]{0:T(128)S(1)} %pad_add_fusion.z_ref.place_ref, bf16[512,1600]{1,0:T(8,128)(2,1)S(1)} %spread.1.a_ref, bf16[100,112,576]{2,1,0:T(8,128)(2,1)} %refs_1_.7, bf16[100,112,576]{2,1,0:T(8,128)(2,1)} %refs_1_.7, bf16[32,112,576]{2,1,0:T(8,128)(2,1)} %refs_3_.7, bf16[32,112,576]{2,1,0:T(8,128)(2,1)} %refs_3_.7), custom_call_target="tpu_custom_call" | custom-call | flops 2936012800 | bytes 9404416 | tf_op jit(solution)/shard_map/dress/pallas_call | solution.py:127
  16.4 0.7 collective-permute-start.1
  17.1 3.0 %collective-permute-start = (bf16[36,112,128]{2,1,0:T(8,128)(2,1)S(1)}, bf16[36,112,128]{2,1,0:T(8,128)(2,1)S(1)}, u32[]{:S(2)}, u32[]{:S(2)}) collective-permute-start(bf16[36,112,128]{2,1,0:T(8,128)(2,1)S(1)} %dress.4), channel_id=1, source_target_pairs={{0,2},{1,10},{2,4},{3,12},{4,6},{5,14},{6,0},{7,8},{8,3},{9,11},{1... | collective-permute-start | bytes 3096584 | tf_op jit(solution)/shard_map/ppermute | solution.py:392
  20.1 7.3 %dress.6 = bf16[36,112,128]{2,1,0:T(8,128)(2,1)S(1)} custom-call(s32[3]{0:T(128)S(1)} %pad_add_fusion.z_ref.place_ref, bf16[512,1600]{1,0:T(8,128)(2,1)S(1)} %spread.1.a_ref, bf16[100,112,576]{2,1,0:T(8,128)(2,1)} %refs_1_.7, bf16[100,112,576]{2,1,0:T(8,128)(2,1)} %refs_1_.7, bf16[32,112,576]{2,1,0:T(8,128)(2,1)} %refs_3_.7, bf16[32,112,576]{2,1,0:T(8,128)(2,1)} %refs_3_.7), custom_call_target="tpu_custom_call" | custom-call | flops 2936012800 | bytes 9404416 | tf_op jit(solution)/shard_map/dress/pallas_call | solution.py:127
  27.4 16.3 %collective-permute-done.refs_4_ = bf16[36,112,128]{2,1,0:T(8,128)(2,1)S(1)} collective-permute-done((bf16[36,112,128]{2,1,0:T(8,128)(2,1)S(1)}, bf16[36,112,128]{2,1,0:T(8,128)(2,1)S(1)}, u32[]{:S(2)}, u32[]{:S(2)}) %collective-permute-start) | collective-permute-done | bytes 1032224 | tf_op jit(solution)/shard_map/ppermute | solution.py:392
  43.7 2.6 %collective-permute-start.2 = (bf16[36,112,128]{2,1,0:T(8,128)(2,1)S(1)}, bf16[36,112,128]{2,1,0:T(8,128)(2,1)S(1)}, u32[]{:S(2)}, u32[]{:S(2)}) collective-permute-start(bf16[36,112,128]{2,1,0:T(8,128)(2,1)S(1)} %dress.6), channel_id=1, source_target_pairs={{0,6},{1,14},{2,0},{3,8},{4,2},{5,10},{6,4},{7,12},{8,7},{9,15},{1... | collective-permute-start | bytes 3096584 | tf_op jit(solution)/shard_map/ppermute | solution.py:392
  46.3 1.5 collective-permute-start.3
  47.8 3.2 %collective-permute-start.4 = (bf16[36,112,128]{2,1,0:T(8,128)(2,1)S(1)}, bf16[36,112,128]{2,1,0:T(8,128)(2,1)S(1)}, u32[]{:S(2)}, u32[]{:S(2)}) collective-permute-start(bf16[36,112,128]{2,1,0:T(8,128)(2,1)S(1)} %collective-permute-done.refs_4_), channel_id=1, source_target_pairs={{0,8},{1,9},{2,10},{3,11},{4,12},{5,13},{6,14},{7,15},{8,0},{9,1},... | collective-permute-start | bytes 3096584 | tf_op jit(solution)/shard_map/ppermute | solution.py:392
  51.0 7.3 %dress.7 = bf16[36,112,128]{2,1,0:T(8,128)(2,1)S(1)} custom-call(s32[3]{0:T(128)S(1)} %pad_add_fusion.z_ref.place_ref, bf16[512,1600]{1,0:T(8,128)(2,1)S(1)} %spread.1.a_ref, bf16[100,112,576]{2,1,0:T(8,128)(2,1)} %refs_1_.7, bf16[100,112,576]{2,1,0:T(8,128)(2,1)} %refs_1_.7, bf16[32,112,576]{2,1,0:T(8,128)(2,1)} %refs_3_.7, bf16[32,112,576]{2,1,0:T(8,128)(2,1)} %refs_3_.7), custom_call_target="tpu_custom_call" | custom-call | flops 2936012800 | bytes 9404416 | tf_op jit(solution)/shard_map/dress/pallas_call | solution.py:127
  58.3 8.5 %collective-permute-done.2.refs_8_ = bf16[36,112,128]{2,1,0:T(8,128)(2,1)S(1)} collective-permute-done((bf16[36,112,128]{2,1,0:T(8,128)(2,1)S(1)}, bf16[36,112,128]{2,1,0:T(8,128)(2,1)S(1)}, u32[]{:S(2)}, u32[]{:S(2)}) %collective-permute-start.2) | collective-permute-done | bytes 1032224 | tf_op jit(solution)/shard_map/ppermute | solution.py:392
  66.8 2.6 %collective-permute-done.3.refs_2_ = bf16[36,112,128]{2,1,0:T(8,128)(2,1)S(1)} collective-permute-done((bf16[36,112,128]{2,1,0:T(8,128)(2,1)S(1)}, bf16[36,112,128]{2,1,0:T(8,128)(2,1)S(1)}, u32[]{:S(2)}, u32[]{:S(2)}) %collective-permute-start.3) | collective-permute-done | bytes 1032224 | tf_op jit(solution)/shard_map/ppermute | solution.py:392
  69.4 2.5 %collective-permute-start.10 = (bf16[36,112,128]{2,1,0:T(8,128)(2,1)S(1)}, bf16[36,112,128]{2,1,0:T(8,128)(2,1)S(1)}, u32[]{:S(2)}, u32[]{:S(2)}) collective-permute-start(bf16[36,112,128]{2,1,0:T(8,128)(2,1)S(1)} %collective-permute-done.3.refs_2_), channel_id=1, source_target_pairs={{0,8},{1,9},{2,10},{3,11},{4,12},{5,13},{6,14},{7,15},{8,0},{9,1},... | collective-permute-start | bytes 3096584 | tf_op jit(solution)/shard_map/ppermute | solution.py:392
  71.9 1.5 collective-permute-start.8
  73.5 0.1 collective-permute-start.7
  73.5 9.0 %relayout.2 = bf16[112,64,896]{2,1,0:T(8,128)(2,1)S(1)} custom-call(bf16[64,224,896]{2,1,0:T(8,128)(2,1)} %in_ref.1), custom_call_target="tpu_custom_call" | custom-call | flops 3288334336 | bytes 25690112 | tf_op jit(solution)/shard_map/relayout/pallas_call | solution.py:162
  82.6 4.6 %copy-done = bf16[112,64,896]{2,1,0:T(8,128)(2,1)} copy-done((bf16[112,64,896]{2,1,0:T(8,128)(2,1)}, bf16[112,64,896]{2,1,0:T(8,128)(2,1)S(1)}, u32[]{:S(2)}) %copy-start) | copy-done | bytes 12845080
  87.2 10.9 %collective-permute-done.7.refs_12_ = bf16[18,112,128]{2,1,0:T(8,128)(2,1)S(1)} collective-permute-done((bf16[18,112,128]{2,1,0:T(8,128)(2,1)S(1)}, bf16[18,112,128]{2,1,0:T(8,128)(2,1)S(1)}, u32[]{:S(2)}, u32[]{:S(2)}) %collective-permute-start.7) | collective-permute-done | bytes 516128 | tf_op jit(solution)/shard_map/ppermute | solution.py:392
  98.2 1.0 collective-permute-start.11
  99.2 0.2 collective-permute-start.13
  99.4 0.3 collective-permute-start.12
  99.8 9.0 %relayout.3 = bf16[112,64,896]{2,1,0:T(8,128)(2,1)S(1)} custom-call(bf16[64,224,896]{2,1,0:T(8,128)(2,1)} %in_ref.1), custom_call_target="tpu_custom_call" | custom-call | flops 3288334336 | bytes 25690112 | tf_op jit(solution)/shard_map/relayout/pallas_call | solution.py:162
  108.8 4.6 %copy-done.1 = bf16[112,64,896]{2,1,0:T(8,128)(2,1)} copy-done((bf16[112,64,896]{2,1,0:T(8,128)(2,1)}, bf16[112,64,896]{2,1,0:T(8,128)(2,1)S(1)}, u32[]{:S(2)}) %copy-start.1) | copy-done | bytes 12845080
  113.5 11.6 %collective-permute-done.6.refs_16_ = bf16[18,112,128]{2,1,0:T(8,128)(2,1)S(1)} collective-permute-done((bf16[18,112,128]{2,1,0:T(8,128)(2,1)S(1)}, bf16[18,112,128]{2,1,0:T(8,128)(2,1)S(1)}, u32[]{:S(2)}, u32[]{:S(2)}) %collective-permute-start.6) | collective-permute-done | bytes 516128 | tf_op jit(solution)/shard_map/ppermute | solution.py:392
  125.1 1.0 copy-done.13
  126.2 0.8 collective-permute-start.17
  127.0 0.9 collective-permute-start.14
  127.8 1.2 collective-permute-start.15
  129.0 12.6 %collective-permute-done.14.refs_14_ = bf16[18,112,128]{2,1,0:T(8,128)(2,1)S(1)} collective-permute-done((bf16[18,112,128]{2,1,0:T(8,128)(2,1)S(1)}, bf16[18,112,128]{2,1,0:T(8,128)(2,1)S(1)}, u32[]{:S(2)}, u32[]{:S(2)}) %collective-permute-start.14) | collective-permute-done | bytes 516128 | tf_op jit(solution)/shard_map/ppermute | solution.py:392
  141.6 10.2 %collective-permute-done.15.refs_18_ = bf16[18,112,128]{2,1,0:T(8,128)(2,1)S(1)} collective-permute-done((bf16[18,112,128]{2,1,0:T(8,128)(2,1)S(1)}, bf16[18,112,128]{2,1,0:T(8,128)(2,1)S(1)}, u32[]{:S(2)}, u32[]{:S(2)}) %collective-permute-start.15) | collective-permute-done | bytes 516128 | tf_op jit(solution)/shard_map/ppermute | solution.py:392
  151.8 0.1 collective-permute-start.18
  151.9 0.5 collective-permute-start.19
  152.4 0.7 copy.12.blocks_ref
  153.1 0.7 collective-permute-done.18.refs_15_
  153.8 0.9 collective-permute-done.19.refs_19_
  154.7 73.7 %ladder.1 = f32[32,4,128]{2,1,0:T(4,128)} custom-call(s32[3]{0:T(128)} %copy-done.2, s32[8,2]{1,0:T(8,128)} %copy.12.blocks_ref, bf16[36,112,128]{2,1,0:T(8,128)(2,1)} %copy-done.4, bf16[36,112,128]{2,1,0:T(8,128)(2,1)} %copy-done.9, bf16[36,112,128]{2,1,0:T(8,128)(2,1)} %copy-done.7, bf16[36,112,128]{2,1,0:T(8,128)(2,1)} %copy-done.10, ...), custom_call_target="tpu_custom_call" | custom-call | flops 13153337344 | bytes 42205184 | tf_op jit(solution)/shard_map/ladder/pallas_call | solution.py:336
  228.4 1.0 reshape.14
  229.4 0.2 copy.13
  229.6 0.2 copy.19
  229.7 0.1 reshape.16
  229.9 9.8 %all_to_all.5 = f32[32,1,256]{2,1,0:T(1,128)S(1)} all-to-all(f32[32,1,256]{2,1,0:T(1,128)S(1)} %reshape.16), channel_id=1, replica_groups=mesh['aux'=4,'pair'=8] {'aux','pair'}, dimensions={0} | all-to-all | bytes 65536 | tf_op jit(solution)/shard_map/all_to_all | solution.py:476
  239.7 0.5 broadcast.2
  240.2 0.7 reduce
  240.9 0.1 reshape.17
  241.1 0.7 copy.16
  (60 shorter events, 0.2 us)
Async XLA Ops:
  1.7 49.3 %copy-start.2 = (s32[3]{0:T(128)}, s32[3]{0:T(128)S(1)}, u32[]{:S(2)}) copy-start(s32[3]{0:T(128)S(1)} %pad_add_fusion.z_ref.place_ref) | copy-start | bytes 40
  16.4 11.0 %collective-permute-start.1 = (bf16[36,112,128]{2,1,0:T(8,128)(2,1)S(1)}, bf16[36,112,128]{2,1,0:T(8,128)(2,1)S(1)}, u32[]{:S(2)}, u32[]{:S(2)}) collective-permute-start(bf16[36,112,128]{2,1,0:T(8,128)(2,1)S(1)} %dress.5), channel_id=1, source_target_pairs={{0,0},{1,8},{2,2},{3,10},{4,4},{5,12},{6,6},{7,14},{8,1},{9,9},{10... | collective-permute-start | bytes 3096584 | tf_op jit(solution)/shard_map/ppermute | solution.py:392
  17.1 26.6 %collective-permute-start = (bf16[36,112,128]{2,1,0:T(8,128)(2,1)S(1)}, bf16[36,112,128]{2,1,0:T(8,128)(2,1)S(1)}, u32[]{:S(2)}, u32[]{:S(2)}) collective-permute-start(bf16[36,112,128]{2,1,0:T(8,128)(2,1)S(1)} %dress.4), channel_id=1, source_target_pairs={{0,2},{1,10},{2,4},{3,12},{4,6},{5,14},{6,0},{7,8},{8,3},{9,11},{1... | collective-permute-start | bytes 3096584 | tf_op jit(solution)/shard_map/ppermute | solution.py:392
  27.4 30.9 %copy-start.4 = (bf16[36,112,128]{2,1,0:T(8,128)(2,1)}, bf16[36,112,128]{2,1,0:T(8,128)(2,1)S(1)}, u32[]{:S(2)}) copy-start(bf16[36,112,128]{2,1,0:T(8,128)(2,1)S(1)} %collective-permute-done.1.refs_0_) | copy-start | bytes 3096580
  43.7 28.2 %copy-start.5 = (bf16[36,112,128]{2,1,0:T(8,128)(2,1)}, bf16[36,112,128]{2,1,0:T(8,128)(2,1)S(1)}, u32[]{:S(2)}) copy-start(bf16[36,112,128]{2,1,0:T(8,128)(2,1)S(1)} %collective-permute-done.refs_4_) | copy-start | bytes 3096580
  43.7 23.1 %collective-permute-start.2 = (bf16[36,112,128]{2,1,0:T(8,128)(2,1)S(1)}, bf16[36,112,128]{2,1,0:T(8,128)(2,1)S(1)}, u32[]{:S(2)}, u32[]{:S(2)}) collective-permute-start(bf16[36,112,128]{2,1,0:T(8,128)(2,1)S(1)} %dress.6), channel_id=1, source_target_pairs={{0,6},{1,14},{2,0},{3,8},{4,2},{5,10},{6,4},{7,12},{8,7},{9,15},{1... | collective-permute-start | bytes 3096584 | tf_op jit(solution)/shard_map/ppermute | solution.py:392
  46.3 23.1 %collective-permute-start.3 = (bf16[36,112,128]{2,1,0:T(8,128)(2,1)S(1)}, bf16[36,112,128]{2,1,0:T(8,128)(2,1)S(1)}, u32[]{:S(2)}, u32[]{:S(2)}) collective-permute-start(bf16[36,112,128]{2,1,0:T(8,128)(2,1)S(1)} %collective-permute-done.1.refs_0_), channel_id=1, source_target_pairs={{0,16},{1,17},{2,18},{3,19},{4,20},{5,21},{6,22},{7,23},{8,24},{9,... | collective-permute-start | bytes 3096584 | tf_op jit(solution)/shard_map/ppermute | solution.py:392
  47.8 21.6 %collective-permute-start.4 = (bf16[36,112,128]{2,1,0:T(8,128)(2,1)S(1)}, bf16[36,112,128]{2,1,0:T(8,128)(2,1)S(1)}, u32[]{:S(2)}, u32[]{:S(2)}) collective-permute-start(bf16[36,112,128]{2,1,0:T(8,128)(2,1)S(1)} %collective-permute-done.refs_4_), channel_id=1, source_target_pairs={{0,8},{1,9},{2,10},{3,11},{4,12},{5,13},{6,14},{7,15},{8,0},{9,1},... | collective-permute-start | bytes 3096584 | tf_op jit(solution)/shard_map/ppermute | solution.py:392
  51.0 18.4 %collective-permute-start.5 = (bf16[36,112,128]{2,1,0:T(8,128)(2,1)S(1)}, bf16[36,112,128]{2,1,0:T(8,128)(2,1)S(1)}, u32[]{:S(2)}, u32[]{:S(2)}) collective-permute-start(bf16[36,112,128]{2,1,0:T(8,128)(2,1)S(1)} %collective-permute-done.1.refs_0_), channel_id=1, source_target_pairs={{0,8},{1,9},{2,10},{3,11},{4,12},{5,13},{6,14},{7,15},{8,0},{9,1},... | collective-permute-start | bytes 3096584 | tf_op jit(solution)/shard_map/ppermute | solution.py:392
  66.8 31.4 %copy-start.6 = (bf16[36,112,128]{2,1,0:T(8,128)(2,1)}, bf16[36,112,128]{2,1,0:T(8,128)(2,1)S(1)}, u32[]{:S(2)}) copy-start(bf16[36,112,128]{2,1,0:T(8,128)(2,1)S(1)} %collective-permute-done.2.refs_8_) | copy-start | bytes 3096580
  69.4 13.2 %copy-start.7 = (bf16[36,112,128]{2,1,0:T(8,128)(2,1)}, bf16[36,112,128]{2,1,0:T(8,128)(2,1)S(1)}, u32[]{:S(2)}) copy-start(bf16[36,112,128]{2,1,0:T(8,128)(2,1)S(1)} %collective-permute-done.3.refs_2_) | copy-start | bytes 3096580
  69.4 4.1 %copy-start.8 = (bf16[36,112,128]{2,1,0:T(8,128)(2,1)}, bf16[36,112,128]{2,1,0:T(8,128)(2,1)S(1)}, u32[]{:S(2)}) copy-start(bf16[36,112,128]{2,1,0:T(8,128)(2,1)S(1)} %collective-permute-done.4.refs_5_) | copy-start | bytes 3096580
  69.4 4.0 %copy-start.9 = (bf16[36,112,128]{2,1,0:T(8,128)(2,1)}, bf16[36,112,128]{2,1,0:T(8,128)(2,1)S(1)}, u32[]{:S(2)}) copy-start(bf16[36,112,128]{2,1,0:T(8,128)(2,1)S(1)} %collective-permute-done.5.refs_1_) | copy-start | bytes 3096580
  69.4 28.8 %collective-permute-start.10 = (bf16[36,112,128]{2,1,0:T(8,128)(2,1)S(1)}, bf16[36,112,128]{2,1,0:T(8,128)(2,1)S(1)}, u32[]{:S(2)}, u32[]{:S(2)}) collective-permute-start(bf16[36,112,128]{2,1,0:T(8,128)(2,1)S(1)} %collective-permute-done.3.refs_2_), channel_id=1, source_target_pairs={{0,8},{1,9},{2,10},{3,11},{4,12},{5,13},{6,14},{7,15},{8,0},{9,1},... | collective-permute-start | bytes 3096584 | tf_op jit(solution)/shard_map/ppermute | solution.py:392
  71.9 26.3 %collective-permute-start.8 = (bf16[36,112,128]{2,1,0:T(8,128)(2,1)S(1)}, bf16[36,112,128]{2,1,0:T(8,128)(2,1)S(1)}, u32[]{:S(2)}, u32[]{:S(2)}) collective-permute-start(bf16[36,112,128]{2,1,0:T(8,128)(2,1)S(1)} %collective-permute-done.refs_4_), channel_id=1, source_target_pairs={{0,16},{1,17},{2,18},{3,19},{4,20},{5,21},{6,22},{7,23},{8,24},{9,... | collective-permute-start | bytes 3096584 | tf_op jit(solution)/shard_map/ppermute | solution.py:392
  73.4 24.8 %collective-permute-start.9 = (bf16[36,112,128]{2,1,0:T(8,128)(2,1)S(1)}, bf16[36,112,128]{2,1,0:T(8,128)(2,1)S(1)}, u32[]{:S(2)}, u32[]{:S(2)}) collective-permute-start(bf16[36,112,128]{2,1,0:T(8,128)(2,1)S(1)} %collective-permute-done.2.refs_8_), channel_id=1, source_target_pairs={{0,8},{1,9},{2,10},{3,11},{4,12},{5,13},{6,14},{7,15},{8,0},{9,1},... | collective-permute-start | bytes 3096584 | tf_op jit(solution)/shard_map/ppermute | solution.py:392
  73.5 24.7 %collective-permute-start.7 = (bf16[18,112,128]{2,1,0:T(8,128)(2,1)S(1)}, bf16[18,112,128]{2,1,0:T(8,128)(2,1)S(1)}, u32[]{:S(2)}, u32[]{:S(2)}) collective-permute-start(bf16[18,112,128]{2,1,0:T(8,128)(2,1)S(1)} %get-tuple-element.173), channel_id=1, source_target_pairs={{0,4},{1,12},{2,6},{3,14},{4,0},{5,8},{6,2},{7,10},{8,5},{9,13},{1... | collective-permute-start | bytes 1548296 | tf_op jit(solution)/shard_map/ppermute | solution.py:392
  82.6 4.6 %copy-start = (bf16[112,64,896]{2,1,0:T(8,128)(2,1)}, bf16[112,64,896]{2,1,0:T(8,128)(2,1)S(1)}, u32[]{:S(2)}) copy-start(bf16[112,64,896]{2,1,0:T(8,128)(2,1)S(1)} %relayout.2) | copy-start | bytes 38535172
  98.2 28.8 %copy-start.16 = (bf16[18,112,128]{2,1,0:T(8,128)(2,1)}, bf16[18,112,128]{2,1,0:T(8,128)(2,1)S(1)}, u32[]{:S(2)}) copy-start(bf16[18,112,128]{2,1,0:T(8,128)(2,1)S(1)} %collective-permute-done.7.refs_12_) | copy-start | bytes 1548292
  98.2 10.6 %copy-start.10 = (bf16[36,112,128]{2,1,0:T(8,128)(2,1)}, bf16[36,112,128]{2,1,0:T(8,128)(2,1)S(1)}, u32[]{:S(2)}) copy-start(bf16[36,112,128]{2,1,0:T(8,128)(2,1)S(1)} %collective-permute-done.10.refs_3_) | copy-start | bytes 3096580
  98.2 10.6 %copy-start.11 = (bf16[36,112,128]{2,1,0:T(8,128)(2,1)}, bf16[36,112,128]{2,1,0:T(8,128)(2,1)S(1)}, u32[]{:S(2)}) copy-start(bf16[36,112,128]{2,1,0:T(8,128)(2,1)S(1)} %collective-permute-done.8.refs_6_) | copy-start | bytes 3096580
  98.2 10.6 %copy-start.12 = (bf16[36,112,128]{2,1,0:T(8,128)(2,1)}, bf16[36,112,128]{2,1,0:T(8,128)(2,1)S(1)}, u32[]{:S(2)}) copy-start(bf16[36,112,128]{2,1,0:T(8,128)(2,1)S(1)} %collective-permute-done.9.refs_9_) | copy-start | bytes 3096580
  98.2 26.9 %collective-permute-start.11 = (bf16[36,112,128]{2,1,0:T(8,128)(2,1)S(1)}, bf16[36,112,128]{2,1,0:T(8,128)(2,1)S(1)}, u32[]{:S(2)}, u32[]{:S(2)}) collective-permute-start(bf16[36,112,128]{2,1,0:T(8,128)(2,1)S(1)} %collective-permute-done.2.refs_8_), channel_id=1, source_target_pairs={{0,16},{1,17},{2,18},{3,19},{4,20},{5,21},{6,22},{7,23},{8,24},{9,... | collective-permute-start | bytes 3096584 | tf_op jit(solution)/shard_map/ppermute | solution.py:392
  99.2 25.9 %collective-permute-start.13 = (bf16[36,112,128]{2,1,0:T(8,128)(2,1)S(1)}, bf16[36,112,128]{2,1,0:T(8,128)(2,1)S(1)}, u32[]{:S(2)}, u32[]{:S(2)}) collective-permute-start(bf16[36,112,128]{2,1,0:T(8,128)(2,1)S(1)} %collective-permute-done.8.refs_6_), channel_id=1, source_target_pairs={{0,8},{1,9},{2,10},{3,11},{4,12},{5,13},{6,14},{7,15},{8,0},{9,1},... | collective-permute-start | bytes 3096584 | tf_op jit(solution)/shard_map/ppermute | solution.py:392
  99.4 52.9 %copy-start.3 = (s32[8,2]{0,1:T(2,128)S(1)}, s32[8,2]{0,1:T(2,128)}, u32[]{:S(2)}) copy-start(s32[8,2]{0,1:T(2,128)} %param.9) | copy-start | bytes 196
  99.4 25.7 %collective-permute-start.6 = (bf16[18,112,128]{2,1,0:T(8,128)(2,1)S(1)}, bf16[18,112,128]{2,1,0:T(8,128)(2,1)S(1)}, u32[]{:S(2)}, u32[]{:S(2)}) collective-permute-start(bf16[18,112,128]{2,1,0:T(8,128)(2,1)S(1)} %get-tuple-element.174), channel_id=1, source_target_pairs={{0,4},{1,12},{2,6},{3,14},{4,0},{5,8},{6,2},{7,10},{8,5},{9,13},{1... | collective-permute-start | bytes 1548296 | tf_op jit(solution)/shard_map/ppermute | solution.py:392
  99.4 25.7 %collective-permute-start.12 = (bf16[18,112,128]{2,1,0:T(8,128)(2,1)S(1)}, bf16[18,112,128]{2,1,0:T(8,128)(2,1)S(1)}, u32[]{:S(2)}, u32[]{:S(2)}) collective-permute-start(bf16[18,112,128]{2,1,0:T(8,128)(2,1)S(1)} %collective-permute-done.7.refs_12_), channel_id=1, source_target_pairs={{0,8},{1,9},{2,10},{3,11},{4,12},{5,13},{6,14},{7,15},{8,0},{9,1},... | collective-permute-start | bytes 1548296 | tf_op jit(solution)/shard_map/ppermute | solution.py:392
  108.8 4.6 %copy-start.1 = (bf16[112,64,896]{2,1,0:T(8,128)(2,1)}, bf16[112,64,896]{2,1,0:T(8,128)(2,1)S(1)}, u32[]{:S(2)}) copy-start(bf16[112,64,896]{2,1,0:T(8,128)(2,1)S(1)} %relayout.3) | copy-start | bytes 38535172
  125.1 26.8 %copy-start.17 = (bf16[18,112,128]{2,1,0:T(8,128)(2,1)}, bf16[18,112,128]{2,1,0:T(8,128)(2,1)S(1)}, u32[]{:S(2)}) copy-start(bf16[18,112,128]{2,1,0:T(8,128)(2,1)S(1)} %collective-permute-done.6.refs_16_) | copy-start | bytes 1548292
  125.1 26.8 %copy-start.18 = (bf16[18,112,128]{2,1,0:T(8,128)(2,1)}, bf16[18,112,128]{2,1,0:T(8,128)(2,1)S(1)}, u32[]{:S(2)}) copy-start(bf16[18,112,128]{2,1,0:T(8,128)(2,1)S(1)} %collective-permute-done.12.refs_13_) | copy-start | bytes 1548292
  125.1 1.0 copy-start.13
  126.2 25.6 %copy-start.14 = (bf16[36,112,128]{2,1,0:T(8,128)(2,1)}, bf16[36,112,128]{2,1,0:T(8,128)(2,1)S(1)}, u32[]{:S(2)}) copy-start(bf16[36,112,128]{2,1,0:T(8,128)(2,1)S(1)} %collective-permute-done.13.refs_7_) | copy-start | bytes 3096580
  126.2 25.6 %collective-permute-start.17 = (bf16[36,112,128]{2,1,0:T(8,128)(2,1)S(1)}, bf16[36,112,128]{2,1,0:T(8,128)(2,1)S(1)}, u32[]{:S(2)}, u32[]{:S(2)}) collective-permute-start(bf16[36,112,128]{2,1,0:T(8,128)(2,1)S(1)} %collective-permute-done.11.refs_10_), channel_id=1, source_target_pairs={{0,8},{1,9},{2,10},{3,11},{4,12},{5,13},{6,14},{7,15},{8,0},{9,1},... | collective-permute-start | bytes 3096584 | tf_op jit(solution)/shard_map/ppermute | solution.py:392
  127.0 14.6 %collective-permute-start.14 = (bf16[18,112,128]{2,1,0:T(8,128)(2,1)S(1)}, bf16[18,112,128]{2,1,0:T(8,128)(2,1)S(1)}, u32[]{:S(2)}, u32[]{:S(2)}) collective-permute-start(bf16[18,112,128]{2,1,0:T(8,128)(2,1)S(1)} %collective-permute-done.7.refs_12_), channel_id=1, source_target_pairs={{0,16},{1,17},{2,18},{3,19},{4,20},{5,21},{6,22},{7,23},{8,24},{9,... | collective-permute-start | bytes 1548296 | tf_op jit(solution)/shard_map/ppermute | solution.py:392
  127.8 23.9 %collective-permute-start.15 = (bf16[18,112,128]{2,1,0:T(8,128)(2,1)S(1)}, bf16[18,112,128]{2,1,0:T(8,128)(2,1)S(1)}, u32[]{:S(2)}, u32[]{:S(2)}) collective-permute-start(bf16[18,112,128]{2,1,0:T(8,128)(2,1)S(1)} %collective-permute-done.6.refs_16_), channel_id=1, source_target_pairs={{0,16},{1,17},{2,18},{3,19},{4,20},{5,21},{6,22},{7,23},{8,24},{9,... | collective-permute-start | bytes 1548296 | tf_op jit(solution)/shard_map/ppermute | solution.py:392
  129.0 22.8 %collective-permute-start.16 = (bf16[18,112,128]{2,1,0:T(8,128)(2,1)S(1)}, bf16[18,112,128]{2,1,0:T(8,128)(2,1)S(1)}, u32[]{:S(2)}, u32[]{:S(2)}) collective-permute-start(bf16[18,112,128]{2,1,0:T(8,128)(2,1)S(1)} %collective-permute-done.6.refs_16_), channel_id=1, source_target_pairs={{0,8},{1,9},{2,10},{3,11},{4,12},{5,13},{6,14},{7,15},{8,0},{9,1},... | collective-permute-start | bytes 1548296 | tf_op jit(solution)/shard_map/ppermute | solution.py:392
  141.6 13.0 %copy-start.19 = (bf16[18,112,128]{2,1,0:T(8,128)(2,1)}, bf16[18,112,128]{2,1,0:T(8,128)(2,1)S(1)}, u32[]{:S(2)}) copy-start(bf16[18,112,128]{2,1,0:T(8,128)(2,1)S(1)} %collective-permute-done.14.refs_14_) | copy-start | bytes 1548292
  151.8 2.9 %copy-start.20 = (bf16[18,112,128]{2,1,0:T(8,128)(2,1)}, bf16[18,112,128]{2,1,0:T(8,128)(2,1)S(1)}, u32[]{:S(2)}) copy-start(bf16[18,112,128]{2,1,0:T(8,128)(2,1)S(1)} %collective-permute-done.15.refs_18_) | copy-start | bytes 1548292
  151.8 2.9 %copy-start.21 = (bf16[18,112,128]{2,1,0:T(8,128)(2,1)}, bf16[18,112,128]{2,1,0:T(8,128)(2,1)S(1)}, u32[]{:S(2)}) copy-start(bf16[18,112,128]{2,1,0:T(8,128)(2,1)S(1)} %collective-permute-done.16.refs_17_) | copy-start | bytes 1548292
  151.8 2.9 %copy-start.15 = (bf16[36,112,128]{2,1,0:T(8,128)(2,1)}, bf16[36,112,128]{2,1,0:T(8,128)(2,1)S(1)}, u32[]{:S(2)}) copy-start(bf16[36,112,128]{2,1,0:T(8,128)(2,1)S(1)} %collective-permute-done.17.refs_11_) | copy-start | bytes 3096580
  151.8 2.0 collective-permute-start.18
  151.9 2.7 %collective-permute-start.19 = (bf16[18,112,128]{2,1,0:T(8,128)(2,1)S(1)}, bf16[18,112,128]{2,1,0:T(8,128)(2,1)}, u32[]{:S(2)}, u32[]{:S(2)}) collective-permute-start(bf16[18,112,128]{2,1,0:T(8,128)(2,1)S(1)} %collective-permute-done.15.refs_18_), channel_id=1, source_target_pairs={{0,8},{1,9},{2,10},{3,11},{4,12},{5,13},{6,14},{7,15},{8,0},{9,1},... | collective-permute-start | bytes 1548296 | tf_op jit(solution)/shard_map/ppermute | solution.py:392
  153.8 0.9 copy-start.22

commit v7 on v6

--- a/solution.py
+++ b/solution.py
@@ -179,7 +179,7 @@
     count = len(units) * p.xs * CORES
     pieces, amps, out = refs[:count], refs[count : count + AMPS], refs[count + AMPS]
     scratch = refs[count + AMPS + 1 :]
-    vectors, left_main, left_tail, spread_tail, tiles, held, total, piece_sem, amp_sem = scratch
+    vectors, left, tiles, held, total, sums, piece_sem, amp_sem = scratch
     w, z, core, chunk = p.window, place_ref[0], place_ref[1], place_ref[2]
     quads = p.c // QUAD
     here = quads // parts
@@ -230,43 +230,38 @@
     for copy in copies:
         copy.wait()
 
-    mixed = QUAD * ROWS
-    to = lax.broadcasted_iota(jnp.int32, (mixed, mixed), 0)
-    frm = lax.broadcasted_iota(jnp.int32, (mixed, mixed), 1)
-    weave = ((to % BLK) * ROWS + to // BLK == frm).astype(jnp.float32).astype(jnp.bfloat16)
-    lane_in = lax.broadcasted_iota(jnp.int32, (LANES, LANES), 0)
-    lane_out = lax.broadcasted_iota(jnp.int32, (LANES, LANES), 1)
-    same = lane_in % p.slot == lane_out % p.slot
     first = pl.multiple_of(chunk * p.c, ROWS)
+    lane = lax.broadcasted_iota(jnp.int32, (p.c, LANES), 1)
+    upper = lax.broadcasted_iota(jnp.int32, (p.c // 8, 8, LANES), 1) < QUAD
 
     def woven(stack):
-        return lax.dot_general(weave, stack, NN, preferred_element_type=jnp.float32).astype(
-            jnp.bfloat16
-        )
+        stack = [rows.reshape(p.c // 8, 8, LANES) for rows in stack]
+        even, odd = [], []
+        for one, two in (stack[:2], stack[2:]):
+            even.append(jnp.where(upper, one, pltpu.roll(two, QUAD, 1)))
+            odd.append(jnp.where(upper, pltpu.roll(one, QUAD, 1), two))
+        rows = jnp.stack(even + odd, axis=1)
+        return rows.reshape(BLK * p.c, LANES).astype(jnp.bfloat16)
 
     @pl.loop(0, p.blocks)
     def _(b):
-        for e in range(BLK):
-            index = b * BLK + e
-            plane = p.nm * w + index // p.per_row
-            copier = (same & (lane_in // p.slot == index % p.per_row)).astype(jnp.float32)
-            copier = copier.astype(jnp.bfloat16)
-            for r in range(p.xs):
-                span = slice(r * LANES, (r + 1) * LANES)
-                spread_tail[e, :, span] = lax.dot_general(
-                    vectors[plane, pl.ds(first, p.c), span],
-                    copier,
-                    NN,
-                    preferred_element_type=jnp.float32,
-                ).astype(jnp.bfloat16)
-        for i in range(p.c // ROWS):
-            span = slice(i * mixed, (i + 1) * mixed)
-            tail = [spread_tail[e, i * ROWS : (i + 1) * ROWS, :] for e in range(BLK)]
-            left_tail[b, span] = woven(jnp.concatenate(tail, axis=0))
-            for m in range(p.nm):
-                at = pl.ds(pl.multiple_of(first + i * ROWS, ROWS), ROWS)
-                stack = [vectors[m * w + b * BLK + e, at] for e in range(BLK)]
-                left_main[m, b, span] = woven(jnp.concatenate(stack, axis=0))
+        for r in range(p.xs):
+            span = slice(r * LANES, (r + 1) * LANES)
+            for m in range(p.nm + 1):
+                stack = []
+                for e in range(BLK):
+                    index = b * BLK + e
+                    plane = m * w + index if m < p.nm else m * w + index // p.per_row
+                    rows = vectors[plane, pl.ds(first, p.c), span].astype(jnp.float32)
+                    if m == p.nm:
+                        rows = jnp.where(lane // p.slot == index % p.per_row, rows, 0.0)
+                        turn = p.slot
+                        while turn < LANES:
+                            rows += pltpu.roll(rows, turn, 1)
+                            turn *= 2
+                    stack.append(rows)
+                at = slice((m * p.xs + r) * LANES, (m * p.xs + r + 1) * LANES)
+                left[b, :, at] = woven(stack)
 
     total[...] = jnp.zeros_like(total)
     slot_of = lax.broadcasted_iota(jnp.int32, (1, p.k), 1) % LANES // p.slot
@@ -277,19 +272,18 @@
 
         @pl.loop(0, p.gf)
         def _(gf):
-            left = blocks_ref[gf // BLK, 0]
+            block = blocks_ref[gf // BLK, 0]
             index = blocks_ref[gf // BLK, 1] * BLK + gf % BLK
             only = (slot_of == index % p.per_row).astype(jnp.float32).astype(jnp.bfloat16)
-            lhs = [left_main[m, left, part_rows] for m in range(p.nm)]
-            lhs = jnp.concatenate(lhs + [left_tail[left, part_rows]], axis=1)
+            lhs = left[block, part_rows]
             for low in range(0, p.d, 256):
                 span = slice(low, min(low + 256, p.d))
                 rhs = [vectors[m * w + index, span] for m in range(p.nm)]
                 rhs.append(vectors[p.nm * w + index // p.per_row, span] * only)
                 rhs = jnp.concatenate(rhs, axis=1)
-                block = lax.dot_general(lhs, rhs, NT, preferred_element_type=jnp.float32)
-                block = block.astype(jnp.bfloat16).reshape(here, ROWS, span.stop - low)
-                tiles[:, gf, :, span] = block
+                tile = lax.dot_general(lhs, rhs, NT, preferred_element_type=jnp.float32)
+                tile = tile.astype(jnp.bfloat16).reshape(here, ROWS, span.stop - low)
+                tiles[:, gf, :, span] = tile
 
         @pl.loop(0, steps)
         def _(step):
@@ -311,7 +305,7 @@
                 )
 
     width = QUAD * p.ij
-    row = lax.broadcasted_iota(jnp.int32, (p.gf * ROWS, width), 0) % ROWS // BLK
+    row = lax.broadcasted_iota(jnp.int32, (p.gf * ROWS, width), 0) % QUAD
     col = lax.broadcasted_iota(jnp.int32, (p.gf * ROWS, width), 1) // p.ij
     kept = jnp.where(row == col, total[...], 0.0)
     folded = kept[:, :LANES]
@@ -321,8 +315,11 @@
     while shift > p.ij:
         shift //= 2
         folded += pltpu.roll(folded, shift, 1)
-    folded = folded.reshape(p.gf, 2, 8, LANES).sum(axis=1)
-    out[...] = folded[:, :4] + folded[:, 4:]
+    folded = folded.reshape(-1, 8, LANES)
+    folded += pltpu.roll(folded, 1, 1)
+    folded += pltpu.roll(folded, 2, 1)
+    sums[...] = folded.reshape(p.gf * ROWS, LANES)
+    out[...] = sums[pl.ds(QUAD - 1, p.gf * BLK, stride=QUAD), :]
 
 
 def ladder(p, units, place, blocks, pieces, amps):
@@ -335,18 +332,17 @@
     width = QUAD * p.ij
     return pl.pallas_call(
         functools.partial(ladder_kernel, p, units, parts, group),
-        out_shape=jax.ShapeDtypeStruct((p.gf, BLK, LANES), jnp.float32),
+        out_shape=jax.ShapeDtypeStruct((p.gf * BLK, LANES), jnp.float32),
         in_specs=[pl.BlockSpec(memory_space=pltpu.SMEM)] * 2
         + [pl.BlockSpec(memory_space=pl.ANY)] * (len(pieces) + AMPS),
         out_specs=pl.BlockSpec(memory_space=pltpu.VMEM),
         scratch_shapes=[
             pltpu.VMEM((p.planes, p.d, p.k), jnp.bfloat16),
-            pltpu.VMEM((max(p.nm, 1), p.blocks, BLK * p.c if p.nm else ROWS, p.k), jnp.bfloat16),
-            pltpu.VMEM((p.blocks, BLK * p.c, p.k), jnp.bfloat16),
-            pltpu.VMEM((BLK, p.c, p.k), jnp.bfloat16),
+            pltpu.VMEM((p.blocks, BLK * p.c, (p.nm + 1) * p.k), jnp.bfloat16),
             pltpu.VMEM((quads // parts, p.gf, ROWS, p.d), jnp.bfloat16),
             pltpu.VMEM((SLOTS, group * width, p.d), jnp.bfloat16),
             pltpu.VMEM((p.gf * ROWS, width), jnp.float32),
+            pltpu.VMEM((p.gf * ROWS, LANES), jnp.float32),
             pltpu.SemaphoreType.DMA((len(pieces),)),
             pltpu.SemaphoreType.DMA((SLOTS,)),
         ],
@@ -413,10 +409,7 @@
     if p.js > 2:
         half = p.planes // 2
         units[-1:] = [(order[-1], 0, half), (order[-1], half, p.planes)]
-        rounds = [[units[1], units[0]]] + [[unit] for unit in units[2:]]
-        swaps = [[units[0]], [units[1]]] + [[unit] for unit in units[2:-2]] + [units[-2:]]
-    else:
-        rounds, swaps = [units], [units]
+    rounds = swaps = [[unit] for unit in units]
 
     def make(o, spread):
         return dress(p, o, place, spread, chol_vv, chol_ov)
@@ -434,7 +427,7 @@
     sources = [amplitudes] * AMPS
     held = {}
     share_next = []
-    count = max(len(rounds), len(swaps) + 1) + 1
+    count = len(rounds) + 2
     for n in range(count):
         new, made, laid = {}, {}, {}
         to_share, share_next = share_next, []
@@ -453,7 +446,7 @@
             for o, _, _ in rounds[n + 1]:
                 if o not in messages:
                     made[o] = make(o, spread)
-        part = n - (len(swaps) - AMPS)
+        part = n - (len(rounds) - AMPS)
         if 0 <= part < AMPS:
             laid[part] = relayout(p, sources[part], part)
         moved = (list(new.values()), list(made.values()), list(laid.values()))
@@ -471,7 +464,7 @@
 
     partial_terms = ladder(p, units, place, assignment, pieces, amps)
     share = p.ij // n_aux
-    terms = partial_terms[:, :, : p.ij].reshape(n_pair, BLK, BLK, n_aux, share)
+    terms = partial_terms[:, : p.ij].reshape(n_pair, BLK, BLK, n_aux, share)
     terms = terms.transpose(3, 0, 4, 2, 1).reshape(n_aux * n_pair, share, BLK * BLK)
     terms = lax.all_to_all(terms, ("aux", "pair"), split_axis=0, concat_axis=0, tiled=True)
     return terms.sum(axis=0)

time: 242 us -> 238 us (0.983)
  waiting for transfers between devices: 74.3 us -> 35.9 us
  starting transfers between devices: 19.9 us -> 49.3 us
  Pallas kernels: 122 us -> 128 us
    ppermute x20, waiting for transfers between devices: 74.3 us -> 35.9 us  [permute(): return lax.ppermute(array, ('aux', 'pair'), pairs)]
    ppermute x20, starting transfers between devices: 19.9 us -> 49.3 us  [permute(): return lax.ppermute(array, ('aux', 'pair'), pairs)]
    pallas_call x1, Pallas kernels: 73.7 us -> 80.1 us  [ladder(): pl.pallas_call(functools.partial(ladder_kernel, p, units, parts, group),...]
  transfers between devices with their start and end apart: 20 -> 20, of which waited for: 9 -> 5; matrix products, arithmetic and copies ran while one was open for 0% -> 0% of each run, Pallas kernels for 13% -> 17%
where the time goes in v7:
time: 238 us; the launch traced here: 237 us
  Pallas kernels  128 us (54%)
  starting transfers between devices  49.3 us (21%)
  waiting for transfers between devices  35.9 us (15%)
  local copies, waits for them, and re-layouts  13.9 us (6%)
  blocking collectives  8.88 us (4%)
    pallas_call x1, Pallas kernels, ladder(): pl.pallas_call(functools.partial(ladder_kernel, p, units, parts, group),...  80.1 us
    ppermute x20, starting transfers between devices, permute(): return lax.ppermute(array, ('aux', 'pair'), pairs)  49.3 us
    ppermute x20, waiting for transfers between devices, permute(): return lax.ppermute(array, ('aux', 'pair'), pairs)  35.9 us
    pallas_call x4, Pallas kernels, dress(): pl.pallas_call(functools.partial(dress_kernel, p, offset), out_shape=jax....  29.2 us
    pallas_call x2, Pallas kernels, relayout(): pl.pallas_call(functools.partial(relayout_kernel, p), out_shape=jax.Shape...  18.1 us
    unnamed x50, local copies, waits for them, and re-layouts  11.3 us
    all_to_all x1, blocking collectives, shards(): lax.all_to_all(terms, ('aux', 'pair'), split_axis=0, concat_axis=0, tiled...  8.88 us
  transfers between devices with their start and end apart: 20, of which 5 were waited for; matrix products, arithmetic and copies ran while one was open for 0% of the time, Pallas kernels for 17%

profile of v7, /device:TPU:0, one launch (start us, length us, event | category | flops | bytes accessed | tf_op | source)
XLA Modules:
  0.0 237.5 jit_solution(2288467364054295919)
XLA Ops:
  0.0 0.8 copy.11.t1_ref
  0.8 0.8 spread.1.a_ref
  1.6 0.1 pad_add_fusion.z_ref.place_ref
  1.7 7.4 %dress.4 = bf16[36,112,128]{2,1,0:T(8,128)(2,1)S(1)} custom-call(s32[3]{0:T(128)S(1)} %pad_add_fusion.z_ref.place_ref, bf16[512,1600]{1,0:T(8,128)(2,1)S(1)} %spread.1.a_ref, bf16[100,112,576]{2,1,0:T(8,128)(2,1)} %refs_1_.7, bf16[100,112,576]{2,1,0:T(8,128)(2,1)} %refs_1_.7, bf16[32,112,576]{2,1,0:T(8,128)(2,1)} %refs_3_.7, bf16[32,112,576]{2,1,0:T(8,128)(2,1)} %refs_3_.7), custom_call_target="tpu_custom_call" | custom-call | flops 2936012800 | bytes 9404416 | tf_op jit(solution)/shard_map/dress/pallas_call | solution.py:127
  9.1 0.7 collective-permute-start
  9.8 7.3 %dress.5 = bf16[36,112,128]{2,1,0:T(8,128)(2,1)S(1)} custom-call(s32[3]{0:T(128)S(1)} %pad_add_fusion.z_ref.place_ref, bf16[512,1600]{1,0:T(8,128)(2,1)S(1)} %spread.1.a_ref, bf16[100,112,576]{2,1,0:T(8,128)(2,1)} %refs_1_.7, bf16[100,112,576]{2,1,0:T(8,128)(2,1)} %refs_1_.7, bf16[32,112,576]{2,1,0:T(8,128)(2,1)} %refs_3_.7, bf16[32,112,576]{2,1,0:T(8,128)(2,1)} %refs_3_.7), custom_call_target="tpu_custom_call" | custom-call | flops 2936012800 | bytes 9404416 | tf_op jit(solution)/shard_map/dress/pallas_call | solution.py:127
  17.1 0.0 collective-permute-done.refs_0_
  17.1 3.0 %collective-permute-start.1 = (bf16[36,112,128]{2,1,0:T(8,128)(2,1)S(1)}, bf16[36,112,128]{2,1,0:T(8,128)(2,1)S(1)}, u32[]{:S(2)}, u32[]{:S(2)}) collective-permute-start(bf16[36,112,128]{2,1,0:T(8,128)(2,1)S(1)} %dress.5), channel_id=1, source_target_pairs={{0,2},{1,10},{2,4},{3,12},{4,6},{5,14},{6,0},{7,8},{8,3},{9,11},{1... | collective-permute-start | bytes 3096584 | tf_op jit(solution)/shard_map/ppermute | solution.py:388
  20.1 1.5 collective-permute-start.2
  21.6 8.6 %collective-permute-start.3 = (bf16[36,112,128]{2,1,0:T(8,128)(2,1)S(1)}, bf16[36,112,128]{2,1,0:T(8,128)(2,1)S(1)}, u32[]{:S(2)}, u32[]{:S(2)}) collective-permute-start(bf16[36,112,128]{2,1,0:T(8,128)(2,1)S(1)} %collective-permute-done.refs_0_), channel_id=1, source_target_pairs={{0,8},{1,9},{2,10},{3,11},{4,12},{5,13},{6,14},{7,15},{8,0},{9,1},... | collective-permute-start | bytes 3096584 | tf_op jit(solution)/shard_map/ppermute | solution.py:388
  30.2 7.3 %dress.6 = bf16[36,112,128]{2,1,0:T(8,128)(2,1)S(1)} custom-call(s32[3]{0:T(128)S(1)} %pad_add_fusion.z_ref.place_ref, bf16[512,1600]{1,0:T(8,128)(2,1)S(1)} %spread.1.a_ref, bf16[100,112,576]{2,1,0:T(8,128)(2,1)} %refs_1_.7, bf16[100,112,576]{2,1,0:T(8,128)(2,1)} %refs_1_.7, bf16[32,112,576]{2,1,0:T(8,128)(2,1)} %refs_3_.7, bf16[32,112,576]{2,1,0:T(8,128)(2,1)} %refs_3_.7), custom_call_target="tpu_custom_call" | custom-call | flops 2936012800 | bytes 9404416 | tf_op jit(solution)/shard_map/dress/pallas_call | solution.py:127
  37.6 0.2 collective-permute-done.2.refs_2_
  37.8 2.4 %collective-permute-start.4 = (bf16[36,112,128]{2,1,0:T(8,128)(2,1)S(1)}, bf16[36,112,128]{2,1,0:T(8,128)(2,1)S(1)}, u32[]{:S(2)}, u32[]{:S(2)}) collective-permute-start(bf16[36,112,128]{2,1,0:T(8,128)(2,1)S(1)} %dress.6), channel_id=1, source_target_pairs={{0,6},{1,14},{2,0},{3,8},{4,2},{5,10},{6,4},{7,12},{8,7},{9,15},{1... | collective-permute-start | bytes 3096584 | tf_op jit(solution)/shard_map/ppermute | solution.py:388
  40.2 1.7 collective-permute-start.5
  41.9 19.6 %collective-permute-start.6 = (bf16[36,112,128]{2,1,0:T(8,128)(2,1)S(1)}, bf16[36,112,128]{2,1,0:T(8,128)(2,1)S(1)}, u32[]{:S(2)}, u32[]{:S(2)}) collective-permute-start(bf16[36,112,128]{2,1,0:T(8,128)(2,1)S(1)} %collective-permute-done.1.refs_4_), channel_id=1, source_target_pairs={{0,8},{1,9},{2,10},{3,11},{4,12},{5,13},{6,14},{7,15},{8,0},{9,1},... | collective-permute-start | bytes 3096584 | tf_op jit(solution)/shard_map/ppermute | solution.py:388
  61.5 7.3 %dress.7 = bf16[36,112,128]{2,1,0:T(8,128)(2,1)S(1)} custom-call(s32[3]{0:T(128)S(1)} %pad_add_fusion.z_ref.place_ref, bf16[512,1600]{1,0:T(8,128)(2,1)S(1)} %spread.1.a_ref, bf16[100,112,576]{2,1,0:T(8,128)(2,1)} %refs_1_.7, bf16[100,112,576]{2,1,0:T(8,128)(2,1)} %refs_1_.7, bf16[32,112,576]{2,1,0:T(8,128)(2,1)} %refs_3_.7, bf16[32,112,576]{2,1,0:T(8,128)(2,1)} %refs_3_.7), custom_call_target="tpu_custom_call" | custom-call | flops 2936012800 | bytes 9404416 | tf_op jit(solution)/shard_map/dress/pallas_call | solution.py:127
  68.8 0.0 collective-permute-done.5.refs_6_
  68.8 0.0 collective-permute-done.6.refs_5_
  68.9 0.6 collective-permute-start.10
  69.5 8.1 %collective-permute-start.11 = (bf16[36,112,128]{2,1,0:T(8,128)(2,1)S(1)}, bf16[36,112,128]{2,1,0:T(8,128)(2,1)S(1)}, u32[]{:S(2)}, u32[]{:S(2)}) collective-permute-start(bf16[36,112,128]{2,1,0:T(8,128)(2,1)S(1)} %collective-permute-done.4.refs_8_), channel_id=1, source_target_pairs={{0,8},{1,9},{2,10},{3,11},{4,12},{5,13},{6,14},{7,15},{8,0},{9,1},... | collective-permute-start | bytes 3096584 | tf_op jit(solution)/shard_map/ppermute | solution.py:388
  77.6 0.1 fusion
  77.7 0.1 collective-permute-start.9
  77.8 9.0 %relayout.2 = bf16[112,64,896]{2,1,0:T(8,128)(2,1)S(1)} custom-call(bf16[64,224,896]{2,1,0:T(8,128)(2,1)} %in_ref.1), custom_call_target="tpu_custom_call" | custom-call | flops 3288334336 | bytes 25690112 | tf_op jit(solution)/shard_map/relayout/pallas_call | solution.py:162
  86.9 4.6 %copy-done = bf16[112,64,896]{2,1,0:T(8,128)(2,1)} copy-done((bf16[112,64,896]{2,1,0:T(8,128)(2,1)}, bf16[112,64,896]{2,1,0:T(8,128)(2,1)S(1)}, u32[]{:S(2)}) %copy-start) | copy-done | bytes 12845080
  91.5 10.2 %collective-permute-done.9.refs_12_ = bf16[18,112,128]{2,1,0:T(8,128)(2,1)S(1)} collective-permute-done((bf16[18,112,128]{2,1,0:T(8,128)(2,1)S(1)}, bf16[18,112,128]{2,1,0:T(8,128)(2,1)S(1)}, u32[]{:S(2)}, u32[]{:S(2)}) %collective-permute-start.9) | collective-permute-done | bytes 516128 | tf_op jit(solution)/shard_map/ppermute | solution.py:388
  101.7 1.7 collective-permute-start.15
  103.4 0.2 collective-permute-start.13
  103.6 0.1 collective-permute-start.14
  103.7 9.0 %relayout.3 = bf16[112,64,896]{2,1,0:T(8,128)(2,1)S(1)} custom-call(bf16[64,224,896]{2,1,0:T(8,128)(2,1)} %in_ref.1), custom_call_target="tpu_custom_call" | custom-call | flops 3288334336 | bytes 25690112 | tf_op jit(solution)/shard_map/relayout/pallas_call | solution.py:162
  112.8 4.6 %copy-done.1 = bf16[112,64,896]{2,1,0:T(8,128)(2,1)} copy-done((bf16[112,64,896]{2,1,0:T(8,128)(2,1)}, bf16[112,64,896]{2,1,0:T(8,128)(2,1)S(1)}, u32[]{:S(2)}) %copy-start.1) | copy-done | bytes 12845080
  117.4 11.2 %collective-permute-done.8.refs_16_ = bf16[18,112,128]{2,1,0:T(8,128)(2,1)S(1)} collective-permute-done((bf16[18,112,128]{2,1,0:T(8,128)(2,1)S(1)}, bf16[18,112,128]{2,1,0:T(8,128)(2,1)S(1)}, u32[]{:S(2)}, u32[]{:S(2)}) %collective-permute-start.8) | collective-permute-done | bytes 516128 | tf_op jit(solution)/shard_map/ppermute | solution.py:388
  128.6 0.4 collective-permute-start.16
  129.0 0.1 collective-permute-start.17
  129.1 0.4 collective-permute-start.18
  129.5 13.2 %collective-permute-done.16.refs_18_ = bf16[18,112,128]{2,1,0:T(8,128)(2,1)S(1)} collective-permute-done((bf16[18,112,128]{2,1,0:T(8,128)(2,1)S(1)}, bf16[18,112,128]{2,1,0:T(8,128)(2,1)S(1)}, u32[]{:S(2)}, u32[]{:S(2)}) %collective-permute-start.16) | collective-permute-done | bytes 516128 | tf_op jit(solution)/shard_map/ppermute | solution.py:388
  142.8 0.1 collective-permute-start.19
  142.9 0.9 copy.12.blocks_ref
  143.7 1.1 collective-permute-done.19.refs_19_
  144.9 80.1 %ladder.1 = f32[128,128]{1,0:T(8,128)} custom-call(s32[3]{0:T(128)} %copy-done.2, s32[8,2]{1,0:T(8,128)} %copy.12.blocks_ref, bf16[36,112,128]{2,1,0:T(8,128)(2,1)} %copy-done.4, bf16[36,112,128]{2,1,0:T(8,128)(2,1)} %copy-done.7, bf16[36,112,128]{2,1,0:T(8,128)(2,1)} %copy-done.6, bf16[36,112,128]{2,1,0:T(8,128)(2,1)} %copy-done.11, ...), custom_call_target="tpu_custom_call" | custom-call | flops 13153337344 | bytes 42205184 | tf_op jit(solution)/shard_map/ladder/pallas_call | solution.py:333
  225.0 1.0 reshape.14
  226.1 0.2 copy.13
  226.2 0.2 copy.19
  226.4 0.1 reshape.16
  226.5 8.9 %all_to_all.5 = f32[32,1,256]{2,1,0:T(1,128)S(1)} all-to-all(f32[32,1,256]{2,1,0:T(1,128)S(1)} %reshape.16), channel_id=1, replica_groups=mesh['aux'=4,'pair'=8] {'aux','pair'}, dimensions={0} | all-to-all | bytes 65536 | tf_op jit(solution)/shard_map/all_to_all | solution.py:469
  235.4 0.5 broadcast.2
  235.9 0.7 reduce
  236.7 0.1 reshape.17
  236.8 0.7 copy.16
  (60 shorter events, 0.2 us)
Async XLA Ops:
  1.7 59.8 %copy-start.2 = (s32[3]{0:T(128)}, s32[3]{0:T(128)S(1)}, u32[]{:S(2)}) copy-start(s32[3]{0:T(128)S(1)} %pad_add_fusion.z_ref.place_ref) | copy-start | bytes 40
  9.1 8.0 %collective-permute-start = (bf16[36,112,128]{2,1,0:T(8,128)(2,1)S(1)}, bf16[36,112,128]{2,1,0:T(8,128)(2,1)S(1)}, u32[]{:S(2)}, u32[]{:S(2)}) collective-permute-start(bf16[36,112,128]{2,1,0:T(8,128)(2,1)S(1)} %dress.4), channel_id=1, source_target_pairs={{0,0},{1,8},{2,2},{3,10},{4,4},{5,12},{6,6},{7,14},{8,1},{9,9},{10... | collective-permute-start | bytes 3096584 | tf_op jit(solution)/shard_map/ppermute | solution.py:388
  17.1 20.4 %copy-start.4 = (bf16[36,112,128]{2,1,0:T(8,128)(2,1)}, bf16[36,112,128]{2,1,0:T(8,128)(2,1)S(1)}, u32[]{:S(2)}) copy-start(bf16[36,112,128]{2,1,0:T(8,128)(2,1)S(1)} %collective-permute-done.refs_0_) | copy-start | bytes 3096580
  17.1 20.4 %collective-permute-start.1 = (bf16[36,112,128]{2,1,0:T(8,128)(2,1)S(1)}, bf16[36,112,128]{2,1,0:T(8,128)(2,1)S(1)}, u32[]{:S(2)}, u32[]{:S(2)}) collective-permute-start(bf16[36,112,128]{2,1,0:T(8,128)(2,1)S(1)} %dress.5), channel_id=1, source_target_pairs={{0,2},{1,10},{2,4},{3,12},{4,6},{5,14},{6,0},{7,8},{8,3},{9,11},{1... | collective-permute-start | bytes 3096584 | tf_op jit(solution)/shard_map/ppermute | solution.py:388
  20.1 17.7 %collective-permute-start.2 = (bf16[36,112,128]{2,1,0:T(8,128)(2,1)S(1)}, bf16[36,112,128]{2,1,0:T(8,128)(2,1)S(1)}, u32[]{:S(2)}, u32[]{:S(2)}) collective-permute-start(bf16[36,112,128]{2,1,0:T(8,128)(2,1)S(1)} %collective-permute-done.refs_0_), channel_id=1, source_target_pairs={{0,16},{1,17},{2,18},{3,19},{4,20},{5,21},{6,22},{7,23},{8,24},{9,... | collective-permute-start | bytes 3096584 | tf_op jit(solution)/shard_map/ppermute | solution.py:388
  21.6 16.2 %collective-permute-start.3 = (bf16[36,112,128]{2,1,0:T(8,128)(2,1)S(1)}, bf16[36,112,128]{2,1,0:T(8,128)(2,1)S(1)}, u32[]{:S(2)}, u32[]{:S(2)}) collective-permute-start(bf16[36,112,128]{2,1,0:T(8,128)(2,1)S(1)} %collective-permute-done.refs_0_), channel_id=1, source_target_pairs={{0,8},{1,9},{2,10},{3,11},{4,12},{5,13},{6,14},{7,15},{8,0},{9,1},... | collective-permute-start | bytes 3096584 | tf_op jit(solution)/shard_map/ppermute | solution.py:388
  37.5 31.2 %copy-start.5 = (bf16[36,112,128]{2,1,0:T(8,128)(2,1)}, bf16[36,112,128]{2,1,0:T(8,128)(2,1)S(1)}, u32[]{:S(2)}) copy-start(bf16[36,112,128]{2,1,0:T(8,128)(2,1)S(1)} %collective-permute-done.1.refs_4_) | copy-start | bytes 3096580
  37.8 31.0 %copy-start.6 = (bf16[36,112,128]{2,1,0:T(8,128)(2,1)}, bf16[36,112,128]{2,1,0:T(8,128)(2,1)S(1)}, u32[]{:S(2)}) copy-start(bf16[36,112,128]{2,1,0:T(8,128)(2,1)S(1)} %collective-permute-done.2.refs_2_) | copy-start | bytes 3096580
  37.8 31.0 %copy-start.7 = (bf16[36,112,128]{2,1,0:T(8,128)(2,1)}, bf16[36,112,128]{2,1,0:T(8,128)(2,1)S(1)}, u32[]{:S(2)}) copy-start(bf16[36,112,128]{2,1,0:T(8,128)(2,1)S(1)} %collective-permute-done.3.refs_1_) | copy-start | bytes 3096580
  37.8 31.0 %collective-permute-start.4 = (bf16[36,112,128]{2,1,0:T(8,128)(2,1)S(1)}, bf16[36,112,128]{2,1,0:T(8,128)(2,1)S(1)}, u32[]{:S(2)}, u32[]{:S(2)}) collective-permute-start(bf16[36,112,128]{2,1,0:T(8,128)(2,1)S(1)} %dress.6), channel_id=1, source_target_pairs={{0,6},{1,14},{2,0},{3,8},{4,2},{5,10},{6,4},{7,12},{8,7},{9,15},{1... | collective-permute-start | bytes 3096584 | tf_op jit(solution)/shard_map/ppermute | solution.py:388
  40.2 28.6 %collective-permute-start.5 = (bf16[36,112,128]{2,1,0:T(8,128)(2,1)S(1)}, bf16[36,112,128]{2,1,0:T(8,128)(2,1)S(1)}, u32[]{:S(2)}, u32[]{:S(2)}) collective-permute-start(bf16[36,112,128]{2,1,0:T(8,128)(2,1)S(1)} %collective-permute-done.1.refs_4_), channel_id=1, source_target_pairs={{0,16},{1,17},{2,18},{3,19},{4,20},{5,21},{6,22},{7,23},{8,24},{9,... | collective-permute-start | bytes 3096584 | tf_op jit(solution)/shard_map/ppermute | solution.py:388
  41.9 27.0 %collective-permute-start.6 = (bf16[36,112,128]{2,1,0:T(8,128)(2,1)S(1)}, bf16[36,112,128]{2,1,0:T(8,128)(2,1)S(1)}, u32[]{:S(2)}, u32[]{:S(2)}) collective-permute-start(bf16[36,112,128]{2,1,0:T(8,128)(2,1)S(1)} %collective-permute-done.1.refs_4_), channel_id=1, source_target_pairs={{0,8},{1,9},{2,10},{3,11},{4,12},{5,13},{6,14},{7,15},{8,0},{9,1},... | collective-permute-start | bytes 3096584 | tf_op jit(solution)/shard_map/ppermute | solution.py:388
  61.5 7.4 %collective-permute-start.7 = (bf16[36,112,128]{2,1,0:T(8,128)(2,1)S(1)}, bf16[36,112,128]{2,1,0:T(8,128)(2,1)S(1)}, u32[]{:S(2)}, u32[]{:S(2)}) collective-permute-start(bf16[36,112,128]{2,1,0:T(8,128)(2,1)S(1)} %collective-permute-done.2.refs_2_), channel_id=1, source_target_pairs={{0,8},{1,9},{2,10},{3,11},{4,12},{5,13},{6,14},{7,15},{8,0},{9,1},... | collective-permute-start | bytes 3096584 | tf_op jit(solution)/shard_map/ppermute | solution.py:388
  68.8 18.0 %copy-start.8 = (bf16[36,112,128]{2,1,0:T(8,128)(2,1)}, bf16[36,112,128]{2,1,0:T(8,128)(2,1)S(1)}, u32[]{:S(2)}) copy-start(bf16[36,112,128]{2,1,0:T(8,128)(2,1)S(1)} %collective-permute-done.4.refs_8_) | copy-start | bytes 3096580
  68.8 18.0 %copy-start.9 = (bf16[36,112,128]{2,1,0:T(8,128)(2,1)}, bf16[36,112,128]{2,1,0:T(8,128)(2,1)S(1)}, u32[]{:S(2)}) copy-start(bf16[36,112,128]{2,1,0:T(8,128)(2,1)S(1)} %collective-permute-done.5.refs_6_) | copy-start | bytes 3096580
  68.9 18.0 %copy-start.10 = (bf16[36,112,128]{2,1,0:T(8,128)(2,1)}, bf16[36,112,128]{2,1,0:T(8,128)(2,1)S(1)}, u32[]{:S(2)}) copy-start(bf16[36,112,128]{2,1,0:T(8,128)(2,1)S(1)} %collective-permute-done.6.refs_5_) | copy-start | bytes 3096580
  68.9 18.0 %copy-start.11 = (bf16[36,112,128]{2,1,0:T(8,128)(2,1)}, bf16[36,112,128]{2,1,0:T(8,128)(2,1)S(1)}, u32[]{:S(2)}) copy-start(bf16[36,112,128]{2,1,0:T(8,128)(2,1)S(1)} %collective-permute-done.7.refs_3_) | copy-start | bytes 3096580
  68.9 32.8 %collective-permute-start.10 = (bf16[36,112,128]{2,1,0:T(8,128)(2,1)S(1)}, bf16[36,112,128]{2,1,0:T(8,128)(2,1)S(1)}, u32[]{:S(2)}, u32[]{:S(2)}) collective-permute-start(bf16[36,112,128]{2,1,0:T(8,128)(2,1)S(1)} %collective-permute-done.4.refs_8_), channel_id=1, source_target_pairs={{0,16},{1,17},{2,18},{3,19},{4,20},{5,21},{6,22},{7,23},{8,24},{9,... | collective-permute-start | bytes 3096584 | tf_op jit(solution)/shard_map/ppermute | solution.py:388
  69.5 32.2 %collective-permute-start.11 = (bf16[36,112,128]{2,1,0:T(8,128)(2,1)S(1)}, bf16[36,112,128]{2,1,0:T(8,128)(2,1)S(1)}, u32[]{:S(2)}, u32[]{:S(2)}) collective-permute-start(bf16[36,112,128]{2,1,0:T(8,128)(2,1)S(1)} %collective-permute-done.4.refs_8_), channel_id=1, source_target_pairs={{0,8},{1,9},{2,10},{3,11},{4,12},{5,13},{6,14},{7,15},{8,0},{9,1},... | collective-permute-start | bytes 3096584 | tf_op jit(solution)/shard_map/ppermute | solution.py:388
  77.6 24.1 %collective-permute-start.12 = (bf16[36,112,128]{2,1,0:T(8,128)(2,1)S(1)}, bf16[36,112,128]{2,1,0:T(8,128)(2,1)S(1)}, u32[]{:S(2)}, u32[]{:S(2)}) collective-permute-start(bf16[36,112,128]{2,1,0:T(8,128)(2,1)S(1)} %collective-permute-done.5.refs_6_), channel_id=1, source_target_pairs={{0,8},{1,9},{2,10},{3,11},{4,12},{5,13},{6,14},{7,15},{8,0},{9,1},... | collective-permute-start | bytes 3096584 | tf_op jit(solution)/shard_map/ppermute | solution.py:388
  77.7 24.0 %collective-permute-start.9 = (bf16[18,112,128]{2,1,0:T(8,128)(2,1)S(1)}, bf16[18,112,128]{2,1,0:T(8,128)(2,1)S(1)}, u32[]{:S(2)}, u32[]{:S(2)}) collective-permute-start(bf16[18,112,128]{2,1,0:T(8,128)(2,1)S(1)} %get-tuple-element.197), channel_id=1, source_target_pairs={{0,4},{1,12},{2,6},{3,14},{4,0},{5,8},{6,2},{7,10},{8,5},{9,13},{1... | collective-permute-start | bytes 1548296 | tf_op jit(solution)/shard_map/ppermute | solution.py:388
  86.9 4.6 %copy-start = (bf16[112,64,896]{2,1,0:T(8,128)(2,1)}, bf16[112,64,896]{2,1,0:T(8,128)(2,1)S(1)}, u32[]{:S(2)}) copy-start(bf16[112,64,896]{2,1,0:T(8,128)(2,1)S(1)} %relayout.2) | copy-start | bytes 38535172
  101.7 11.0 %copy-start.16 = (bf16[18,112,128]{2,1,0:T(8,128)(2,1)}, bf16[18,112,128]{2,1,0:T(8,128)(2,1)S(1)}, u32[]{:S(2)}) copy-start(bf16[18,112,128]{2,1,0:T(8,128)(2,1)S(1)} %collective-permute-done.9.refs_12_) | copy-start | bytes 1548292
  101.7 11.0 %copy-start.12 = (bf16[36,112,128]{2,1,0:T(8,128)(2,1)}, bf16[36,112,128]{2,1,0:T(8,128)(2,1)S(1)}, u32[]{:S(2)}) copy-start(bf16[36,112,128]{2,1,0:T(8,128)(2,1)S(1)} %collective-permute-done.10.refs_10_) | copy-start | bytes 3096580
  101.7 11.0 %copy-start.13 = (bf16[36,112,128]{2,1,0:T(8,128)(2,1)}, bf16[36,112,128]{2,1,0:T(8,128)(2,1)S(1)}, u32[]{:S(2)}) copy-start(bf16[36,112,128]{2,1,0:T(8,128)(2,1)S(1)} %collective-permute-done.11.refs_9_) | copy-start | bytes 3096580
  101.7 11.0 %copy-start.14 = (bf16[36,112,128]{2,1,0:T(8,128)(2,1)}, bf16[36,112,128]{2,1,0:T(8,128)(2,1)S(1)}, u32[]{:S(2)}) copy-start(bf16[36,112,128]{2,1,0:T(8,128)(2,1)S(1)} %collective-permute-done.12.refs_7_) | copy-start | bytes 3096580
  101.7 26.9 %collective-permute-start.15 = (bf16[36,112,128]{2,1,0:T(8,128)(2,1)S(1)}, bf16[36,112,128]{2,1,0:T(8,128)(2,1)S(1)}, u32[]{:S(2)}, u32[]{:S(2)}) collective-permute-start(bf16[36,112,128]{2,1,0:T(8,128)(2,1)S(1)} %collective-permute-done.10.refs_10_), channel_id=1, source_target_pairs={{0,8},{1,9},{2,10},{3,11},{4,12},{5,13},{6,14},{7,15},{8,0},{9,1},... | collective-permute-start | bytes 3096584 | tf_op jit(solution)/shard_map/ppermute | solution.py:388
  103.4 39.4 %copy-start.3 = (s32[8,2]{0,1:T(2,128)S(1)}, s32[8,2]{0,1:T(2,128)}, u32[]{:S(2)}) copy-start(s32[8,2]{0,1:T(2,128)} %param.9) | copy-start | bytes 196
  103.4 25.1 %collective-permute-start.8 = (bf16[18,112,128]{2,1,0:T(8,128)(2,1)S(1)}, bf16[18,112,128]{2,1,0:T(8,128)(2,1)S(1)}, u32[]{:S(2)}, u32[]{:S(2)}) collective-permute-start(bf16[18,112,128]{2,1,0:T(8,128)(2,1)S(1)} %get-tuple-element.198), channel_id=1, source_target_pairs={{0,4},{1,12},{2,6},{3,14},{4,0},{5,8},{6,2},{7,10},{8,5},{9,13},{1... | collective-permute-start | bytes 1548296 | tf_op jit(solution)/shard_map/ppermute | solution.py:388
  103.4 25.1 %collective-permute-start.13 = (bf16[18,112,128]{2,1,0:T(8,128)(2,1)S(1)}, bf16[18,112,128]{2,1,0:T(8,128)(2,1)S(1)}, u32[]{:S(2)}, u32[]{:S(2)}) collective-permute-start(bf16[18,112,128]{2,1,0:T(8,128)(2,1)S(1)} %collective-permute-done.9.refs_12_), channel_id=1, source_target_pairs={{0,16},{1,17},{2,18},{3,19},{4,20},{5,21},{6,22},{7,23},{8,24},{9,... | collective-permute-start | bytes 1548296 | tf_op jit(solution)/shard_map/ppermute | solution.py:388
  103.6 25.0 %collective-permute-start.14 = (bf16[18,112,128]{2,1,0:T(8,128)(2,1)S(1)}, bf16[18,112,128]{2,1,0:T(8,128)(2,1)S(1)}, u32[]{:S(2)}, u32[]{:S(2)}) collective-permute-start(bf16[18,112,128]{2,1,0:T(8,128)(2,1)S(1)} %collective-permute-done.9.refs_12_), channel_id=1, source_target_pairs={{0,8},{1,9},{2,10},{3,11},{4,12},{5,13},{6,14},{7,15},{8,0},{9,1},... | collective-permute-start | bytes 1548296 | tf_op jit(solution)/shard_map/ppermute | solution.py:388
  112.7 4.6 %copy-start.1 = (bf16[112,64,896]{2,1,0:T(8,128)(2,1)}, bf16[112,64,896]{2,1,0:T(8,128)(2,1)S(1)}, u32[]{:S(2)}) copy-start(bf16[112,64,896]{2,1,0:T(8,128)(2,1)S(1)} %relayout.3) | copy-start | bytes 38535172
  128.6 16.3 %copy-start.17 = (bf16[18,112,128]{2,1,0:T(8,128)(2,1)}, bf16[18,112,128]{2,1,0:T(8,128)(2,1)S(1)}, u32[]{:S(2)}) copy-start(bf16[18,112,128]{2,1,0:T(8,128)(2,1)S(1)} %collective-permute-done.8.refs_16_) | copy-start | bytes 1548292
  128.6 14.2 %copy-start.18 = (bf16[18,112,128]{2,1,0:T(8,128)(2,1)}, bf16[18,112,128]{2,1,0:T(8,128)(2,1)S(1)}, u32[]{:S(2)}) copy-start(bf16[18,112,128]{2,1,0:T(8,128)(2,1)S(1)} %collective-permute-done.13.refs_14_) | copy-start | bytes 1548292
  128.6 14.2 %copy-start.19 = (bf16[18,112,128]{2,1,0:T(8,128)(2,1)}, bf16[18,112,128]{2,1,0:T(8,128)(2,1)S(1)}, u32[]{:S(2)}) copy-start(bf16[18,112,128]{2,1,0:T(8,128)(2,1)S(1)} %collective-permute-done.14.refs_13_) | copy-start | bytes 1548292
  128.6 16.3 %copy-start.15 = (bf16[36,112,128]{2,1,0:T(8,128)(2,1)}, bf16[36,112,128]{2,1,0:T(8,128)(2,1)S(1)}, u32[]{:S(2)}) copy-start(bf16[36,112,128]{2,1,0:T(8,128)(2,1)S(1)} %collective-permute-done.15.refs_11_) | copy-start | bytes 3096580
  128.6 14.1 %collective-permute-start.16 = (bf16[18,112,128]{2,1,0:T(8,128)(2,1)S(1)}, bf16[18,112,128]{2,1,0:T(8,128)(2,1)S(1)}, u32[]{:S(2)}, u32[]{:S(2)}) collective-permute-start(bf16[18,112,128]{2,1,0:T(8,128)(2,1)S(1)} %collective-permute-done.8.refs_16_), channel_id=1, source_target_pairs={{0,16},{1,17},{2,18},{3,19},{4,20},{5,21},{6,22},{7,23},{8,24},{9,... | collective-permute-start | bytes 1548296 | tf_op jit(solution)/shard_map/ppermute | solution.py:388
  129.0 13.7 %collective-permute-start.17 = (bf16[18,112,128]{2,1,0:T(8,128)(2,1)S(1)}, bf16[18,112,128]{2,1,0:T(8,128)(2,1)S(1)}, u32[]{:S(2)}, u32[]{:S(2)}) collective-permute-start(bf16[18,112,128]{2,1,0:T(8,128)(2,1)S(1)} %collective-permute-done.8.refs_16_), channel_id=1, source_target_pairs={{0,8},{1,9},{2,10},{3,11},{4,12},{5,13},{6,14},{7,15},{8,0},{9,1},... | collective-permute-start | bytes 1548296 | tf_op jit(solution)/shard_map/ppermute | solution.py:388
  129.1 13.6 %collective-permute-start.18 = (bf16[18,112,128]{2,1,0:T(8,128)(2,1)S(1)}, bf16[18,112,128]{2,1,0:T(8,128)(2,1)S(1)}, u32[]{:S(2)}, u32[]{:S(2)}) collective-permute-start(bf16[18,112,128]{2,1,0:T(8,128)(2,1)S(1)} %collective-permute-done.13.refs_14_), channel_id=1, source_target_pairs={{0,8},{1,9},{2,10},{3,11},{4,12},{5,13},{6,14},{7,15},{8,0},{9,1},... | collective-permute-start | bytes 1548296 | tf_op jit(solution)/shard_map/ppermute | solution.py:388
  142.7 2.2 copy-start.20
  142.7 2.1 copy-start.21
  142.8 2.1 copy-start.22
  142.8 2.1 collective-permute-start.19

commit v8 on v6

--- a/solution.py
+++ b/solution.py
@@ -10,7 +10,7 @@
 BLK = 4
 QUAD = 4
 AMPS = 2
-SLOTS = 3
+DEEP = 256
 ROWS = 16
 LANES = 128
 CORES = 2
@@ -77,8 +77,15 @@
     )(t1_window)
 
 
-def dress_kernel(p, offset, z_ref, a_ref, *refs):
-    ov, vv, out = refs[: p.nm + 1], refs[p.nm + 1 : 2 * p.nm + 2], refs[-1]
+def dress_kernel(p, offset, bounds, z_ref, a_ref, *refs):
+    ov, vv, outs = refs[: p.nm + 1], refs[p.nm + 1 : 2 * p.nm + 2], refs[2 * p.nm + 2 :]
+
+    def put(start, cols, planes):
+        for out, (low, high) in zip(outs, bounds):
+            first, last = max(low, start), min(high, start + planes.shape[0])
+            if first < last:
+                out[first - low : last - low, cols] = planes[first - start : last - start]
+
     w = p.window
     j = lax.rem(z_ref[0] + offset, p.js)
     lane = lax.broadcasted_iota(jnp.int32, (p.nt, ROWS, LANES), 2)
@@ -91,7 +98,7 @@
         for m in range(p.nm):
             here = shift[:, m * LANES : (m + 1) * LANES].reshape(w, ROWS, LANES)
             here = vv[m][:, cols].astype(jnp.float32) - here
-            out[m * w : (m + 1) * w, cols] = here.astype(jnp.bfloat16)
+            put(m * w, cols, here.astype(jnp.bfloat16))
         here = shift[:, p.nm * LANES :].reshape(w, ROWS, p.tail_width)
         source = vv[p.nm][:, cols].astype(jnp.float32) - here
         source = source.reshape(p.nt, p.per_row, ROWS, p.tail_width)
@@ -102,10 +109,10 @@
             moved = moved[:, :LANES].reshape(p.nt, ROWS, LANES)
             keep = (lane >= s * p.slot) & (lane < s * p.slot + p.tail)
             rest = jnp.where(keep, moved, rest)
-        out[p.nm * w :, cols] = rest.astype(jnp.bfloat16)
-
-
-def dress(p, offset, z, spread, chol_vv, chol_ov):
+        put(p.nm * w, cols, rest.astype(jnp.bfloat16))
+
+
+def dress(p, offset, bounds, z, spread, chol_vv, chol_ov):
     def specs(lead):
         found = []
         for m in range(p.nm):
@@ -125,15 +132,20 @@
 
     count = p.nm + 1
     return pl.pallas_call(
-        functools.partial(dress_kernel, p, offset),
-        out_shape=jax.ShapeDtypeStruct((p.planes, p.cpad, LANES), jnp.bfloat16),
+        functools.partial(dress_kernel, p, offset, bounds),
+        out_shape=[
+            jax.ShapeDtypeStruct((high - low, p.cpad, LANES), jnp.bfloat16) for low, high in bounds
+        ],
         grid_spec=pltpu.PrefetchScalarGridSpec(
             num_scalar_prefetch=1,
             grid=(1,),
             in_specs=[pl.BlockSpec((p.window * ROWS, p.occupied * ROWS), lambda i, z: (0, 0))]
             + specs(p.occupied)
             + specs(p.window),
-            out_specs=pl.BlockSpec((p.planes, p.cpad, LANES), lambda i, z: (0, 0, 0)),
+            out_specs=[
+                pl.BlockSpec((high - low, p.cpad, LANES), lambda i, z: (0, 0, 0))
+                for low, high in bounds
+            ],
         ),
         compiler_params=pltpu.CompilerParams(vmem_limit_bytes=48 * 2**20),
         cost_estimate=pl.CostEstimate(
@@ -146,25 +158,40 @@
 
 
 def relayout_kernel(p, in_ref, out_ref):
-    rows = ROWS * ROWS
-    to = lax.broadcasted_iota(jnp.int32, (rows, rows), 0)
-    frm = lax.broadcasted_iota(jnp.int32, (rows, rows), 1)
+    rows, half = ROWS * ROWS, LANES // 2
+    to = lax.broadcasted_iota(jnp.int32, (rows, rows), 1)
+    frm = lax.broadcasted_iota(jnp.int32, (rows, rows), 0)
     turn = (to % ROWS * ROWS + to // ROWS == frm).astype(jnp.float32).astype(jnp.bfloat16)
-    for low in range(0, p.ij, ROWS):
-        block = in_ref[low : low + ROWS].reshape(rows, p.d)
-        turned = lax.dot_general(turn, block, NN, preferred_element_type=jnp.float32)
-        out_ref[:, low : low + ROWS] = turned.astype(jnp.bfloat16).reshape(ROWS, ROWS, p.d)
+    lane = lax.broadcasted_iota(jnp.int32, (p.d, LANES), 1)
+    for pair in range(p.ij // ROWS // 2):
+        one, two = [
+            lax.dot_general(
+                in_ref[low : low + ROWS].reshape(rows, p.d),
+                turn,
+                (((0,), (0,)), ((), ())),
+                preferred_element_type=jnp.float32,
+            )
+            for low in (2 * pair * ROWS, (2 * pair + 1) * ROWS)
+        ]
+        at = slice(pair * LANES, (pair + 1) * LANES)
+        for tile in range(rows // LANES):
+            span = slice(tile * LANES, (tile + 1) * LANES)
+            even = jnp.where(lane < half, one[:, span], pltpu.roll(two[:, span], half, 1))
+            odd = jnp.where(lane < half, pltpu.roll(one[:, span], half, 1), two[:, span])
+            out_ref[2 * tile, :, at] = even.astype(jnp.bfloat16)
+            out_ref[2 * tile + 1, :, at] = odd.astype(jnp.bfloat16)
 
 
 def relayout(p, amplitudes, part):
     count = p.c // AMPS
     blocks = count // ROWS
+    width = QUAD * p.ij
     return pl.pallas_call(
         functools.partial(relayout_kernel, p),
-        out_shape=jax.ShapeDtypeStruct((count, p.ij, p.d), jnp.bfloat16),
+        out_shape=jax.ShapeDtypeStruct((count // QUAD, p.d, width), jnp.bfloat16),
         grid=(blocks,),
         in_specs=[pl.BlockSpec((p.ij, ROWS, p.d), lambda c: (0, part * blocks + c, 0))],
-        out_specs=pl.BlockSpec((ROWS, p.ij, p.d), lambda c: (c, 0, 0)),
+        out_specs=pl.BlockSpec((ROWS // QUAD, p.d, width), lambda c: (c, 0, 0)),
         compiler_params=pltpu.CompilerParams(vmem_limit_bytes=40 * 2**20),
         cost_estimate=pl.CostEstimate(
             flops=2 * count * p.ij * p.d * ROWS * ROWS,
@@ -175,36 +202,27 @@
     )(amplitudes)
 
 
-def ladder_kernel(p, units, parts, group, place_ref, blocks_ref, *refs):
+def ladder_kernel(p, units, group, place_ref, blocks_ref, *refs):
     count = len(units) * p.xs * CORES
     pieces, amps, out = refs[:count], refs[count : count + AMPS], refs[count + AMPS]
     scratch = refs[count + AMPS + 1 :]
-    vectors, left_main, left_tail, spread_tail, tiles, held, total, piece_sem, amp_sem = scratch
+    vectors, left, spread_tail, tiles, held, total, piece_sem, amp_sem = scratch
     w, z, core, chunk = p.window, place_ref[0], place_ref[1], place_ref[2]
     quads = p.c // QUAD
-    here = quads // parts
-    rows = here * ROWS
-    steps = here // group
-    wide = group * QUAD * p.ij
-    each = parts * steps // AMPS
-
-    class Fetch:
-        def __init__(self, step, slot):
-            self.step, self.slot = step, slot
-
-        def copy(self, amp, step):
-            at = pl.ds(pl.multiple_of(step * wide, wide), wide)
-            return pltpu.make_async_copy(amp.at[at], held.at[self.slot], amp_sem.at[self.slot])
-
-        def start(self):
-            for n, amp in enumerate(amps):
-
-                @pl.when(self.step // each == n)
-                def _():
-                    self.copy(amp, self.step - n * each).start()
-
-        def wait(self):
-            self.copy(amps[0], 0).wait()
+    width = QUAD * p.ij
+    steps = quads // group
+    spans = [slice(low, min(low + DEEP, p.d)) for low in range(0, p.d, DEEP)]
+
+    def fetches(span):
+        each = quads // AMPS
+        return [
+            pltpu.make_async_copy(
+                amp.at[:, span],
+                held.at[n * each : (n + 1) * each, : span.stop - span.start],
+                amp_sem.at[n],
+            )
+            for n, amp in enumerate(amps)
+        ]
 
     copies = []
     for n, (o, low, high) in enumerate(units):
@@ -225,8 +243,7 @@
                 )
     for copy in copies:
         copy.start()
-    for ahead in range(min(SLOTS - 1, parts * steps)):
-        Fetch(jnp.int32(ahead), ahead).start()
+    total[...] = jnp.zeros_like(total)
     for copy in copies:
         copy.wait()
 
@@ -262,98 +279,81 @@
         for i in range(p.c // ROWS):
             span = slice(i * mixed, (i + 1) * mixed)
             tail = [spread_tail[e, i * ROWS : (i + 1) * ROWS, :] for e in range(BLK)]
-            left_tail[b, span] = woven(jnp.concatenate(tail, axis=0))
+            left[b, span, p.nm * p.k :] = woven(jnp.concatenate(tail, axis=0))
             for m in range(p.nm):
                 at = pl.ds(pl.multiple_of(first + i * ROWS, ROWS), ROWS)
                 stack = [vectors[m * w + b * BLK + e, at] for e in range(BLK)]
-                left_main[m, b, span] = woven(jnp.concatenate(stack, axis=0))
-
-    total[...] = jnp.zeros_like(total)
+                left[b, span, m * p.k : (m + 1) * p.k] = woven(jnp.concatenate(stack, axis=0))
+
     slot_of = lax.broadcasted_iota(jnp.int32, (1, p.k), 1) % LANES // p.slot
 
-    @pl.loop(0, parts)
-    def _(part):
-        part_rows = pl.ds(pl.multiple_of(part * rows, rows), rows)
+    for span in spans:
+        size = span.stop - span.start
+        for copy in fetches(span):
+            copy.start()
 
         @pl.loop(0, p.gf)
         def _(gf):
-            left = blocks_ref[gf // BLK, 0]
+            block = blocks_ref[gf // BLK, 0]
             index = blocks_ref[gf // BLK, 1] * BLK + gf % BLK
             only = (slot_of == index % p.per_row).astype(jnp.float32).astype(jnp.bfloat16)
-            lhs = [left_main[m, left, part_rows] for m in range(p.nm)]
-            lhs = jnp.concatenate(lhs + [left_tail[left, part_rows]], axis=1)
-            for low in range(0, p.d, 256):
-                span = slice(low, min(low + 256, p.d))
-                rhs = [vectors[m * w + index, span] for m in range(p.nm)]
-                rhs.append(vectors[p.nm * w + index // p.per_row, span] * only)
-                rhs = jnp.concatenate(rhs, axis=1)
-                block = lax.dot_general(lhs, rhs, NT, preferred_element_type=jnp.float32)
-                block = block.astype(jnp.bfloat16).reshape(here, ROWS, span.stop - low)
-                tiles[:, gf, :, span] = block
+            rhs = [vectors[m * w + index, span] for m in range(p.nm)]
+            rhs.append(vectors[p.nm * w + index // p.per_row, span] * only)
+            tile = lax.dot_general(
+                left[block], jnp.concatenate(rhs, axis=1), NT, preferred_element_type=jnp.float32
+            )
+            tiles[:, gf, :, :size] = tile.astype(jnp.bfloat16).reshape(quads, ROWS, size)
+
+        for copy in fetches(span):
+            copy.wait()
 
         @pl.loop(0, steps)
         def _(step):
-            at = part * steps + step
-            slot = lax.rem(at, SLOTS)
-
-            @pl.when(at + SLOTS - 1 < parts * steps)
-            def _():
-                Fetch(at + SLOTS - 1, lax.rem(at + SLOTS - 1, SLOTS)).start()
-
-            Fetch(at, slot).wait()
-            width = QUAD * p.ij
-            for n in range(group):
-                total[...] += lax.dot_general(
-                    tiles[step * group + n].reshape(p.gf * ROWS, p.d),
-                    held[slot, n * width : (n + 1) * width],
-                    NT,
-                    preferred_element_type=jnp.float32,
-                )
-
-    width = QUAD * p.ij
+            lhs = [
+                tiles[step * group + n, :, :, :size].reshape(p.gf * ROWS, size)
+                for n in range(group)
+            ]
+            rhs = [held[step * group + n, :size] for n in range(group)]
+            total[...] += lax.dot_general(
+                jnp.concatenate(lhs, axis=1),
+                jnp.concatenate(rhs, axis=0),
+                NN,
+                preferred_element_type=jnp.float32,
+            )
+
     row = lax.broadcasted_iota(jnp.int32, (p.gf * ROWS, width), 0) % ROWS // BLK
-    col = lax.broadcasted_iota(jnp.int32, (p.gf * ROWS, width), 1) // p.ij
+    col = lax.broadcasted_iota(jnp.int32, (p.gf * ROWS, width), 1) // ROWS % QUAD
     kept = jnp.where(row == col, total[...], 0.0)
-    folded = kept[:, :LANES]
-    for low in range(LANES, width, LANES):
-        folded += kept[:, low : low + LANES]
-    shift = LANES
-    while shift > p.ij:
-        shift //= 2
-        folded += pltpu.roll(folded, shift, 1)
-    folded = folded.reshape(p.gf, 2, 8, LANES).sum(axis=1)
-    out[...] = folded[:, :4] + folded[:, 4:]
+    kept += pltpu.roll(kept, width - ROWS, 1)
+    kept += pltpu.roll(kept, width - 2 * ROWS, 1)
+    kept = kept.reshape(p.gf, 2, 8, width).sum(axis=1)
+    out[...] = kept[:, :4] + kept[:, 4:]
 
 
 def ladder(p, units, place, blocks, pieces, amps):
-    parts, group = 2, 1
     quads = p.c // QUAD
-    for wanted in (4, 2):
-        if quads // parts % wanted == 0:
-            group = wanted
-            break
+    group = 4 if quads % 4 == 0 else 2
     width = QUAD * p.ij
     return pl.pallas_call(
-        functools.partial(ladder_kernel, p, units, parts, group),
-        out_shape=jax.ShapeDtypeStruct((p.gf, BLK, LANES), jnp.float32),
+        functools.partial(ladder_kernel, p, units, group),
+        out_shape=jax.ShapeDtypeStruct((p.gf, BLK, width), jnp.float32),
         in_specs=[pl.BlockSpec(memory_space=pltpu.SMEM)] * 2
         + [pl.BlockSpec(memory_space=pl.ANY)] * (len(pieces) + AMPS),
         out_specs=pl.BlockSpec(memory_space=pltpu.VMEM),
         scratch_shapes=[
             pltpu.VMEM((p.planes, p.d, p.k), jnp.bfloat16),
-            pltpu.VMEM((max(p.nm, 1), p.blocks, BLK * p.c if p.nm else ROWS, p.k), jnp.bfloat16),
-            pltpu.VMEM((p.blocks, BLK * p.c, p.k), jnp.bfloat16),
+            pltpu.VMEM((p.blocks, BLK * p.c, (p.nm + 1) * p.k), jnp.bfloat16),
             pltpu.VMEM((BLK, p.c, p.k), jnp.bfloat16),
-            pltpu.VMEM((quads // parts, p.gf, ROWS, p.d), jnp.bfloat16),
-            pltpu.VMEM((SLOTS, group * width, p.d), jnp.bfloat16),
+            pltpu.VMEM((quads, p.gf, ROWS, DEEP), jnp.bfloat16),
+            pltpu.VMEM((quads, DEEP, width), jnp.bfloat16),
             pltpu.VMEM((p.gf * ROWS, width), jnp.float32),
             pltpu.SemaphoreType.DMA((len(pieces),)),
-            pltpu.SemaphoreType.DMA((SLOTS,)),
+            pltpu.SemaphoreType.DMA((AMPS,)),
         ],
         compiler_params=pltpu.CompilerParams(vmem_limit_bytes=60 * 2**20),
         cost_estimate=pl.CostEstimate(
             flops=2 * p.gf * BLK * p.c * p.d * p.k,
-            bytes_accessed=2 * (p.js * p.n_aux * p.planes * p.cpad * LANES + p.c * p.ij * p.d),
+            bytes_accessed=2 * (p.planes * p.d * p.k + p.c * p.ij * p.d),
             transcendentals=0,
         ),
         name="ladder",
@@ -409,69 +409,72 @@
     amplitudes = pad_columns(pad_columns(amplitudes, 1, cols, p.cpad), 2, cols, p.cpad)
 
     order = sorted(range(p.js), key=lambda o: min(o, p.js - o))
-    units = [(o, 0, p.planes) for o in order]
+    whole = (0, p.planes)
+    bounds = {o: [whole] for o in order}
     if p.js > 2:
         half = p.planes // 2
-        units[-1:] = [(order[-1], 0, half), (order[-1], half, p.planes)]
-        rounds = [[units[1], units[0]]] + [[unit] for unit in units[2:]]
-        swaps = [[units[0]], [units[1]]] + [[unit] for unit in units[2:-2]] + [units[-2:]]
-    else:
-        rounds, swaps = [units], [units]
+        bounds[order[-1]] = [(0, half), (half, p.planes)]
+    units = [(o, *bound) for o in order for bound in bounds[o]]
+    rounds = [units[:2]] + [[unit] for unit in units[2:]]
+    swaps = [[], units[1:2]] + [[unit] for unit in units[2:]]
+
+    messages = {}
 
     def make(o, spread):
-        return dress(p, o, place, spread, chol_vv, chol_ov)
-
-    def cut(message, unit):
-        if unit[1:] == (0, p.planes):
-            return message
-        return message[unit[1] : unit[2]]
-
-    messages = {}
-    for o, _, _ in rounds[0]:
-        messages[o] = make(o, spread)
-        messages[o], spread = lax.optimization_barrier((messages[o], spread))
+        made = dress(p, o, bounds[o], place, spread, chol_vv, chol_ov)
+        return dict(zip([(o, *bound) for bound in bounds[o]], made))
+
+    for o in order[:2]:
+        made, spread = lax.optimization_barrier((make(o, spread), spread))
+        messages.update(made)
     amps = [None] * AMPS
     sources = [amplitudes] * AMPS
-    held = {}
+    held, raw = {}, {}
     share_next = []
-    count = max(len(rounds), len(swaps) + 1) + 1
-    for n in range(count):
-        new, made, laid = {}, {}, {}
+    for n in range(len(swaps) + 1):
+        new, made, laid, crossed = {}, {}, {}, {}
         to_share, share_next = share_next, []
         if n < len(rounds):
             for unit in rounds[n]:
-                new[unit, 0, 0] = to_slice(cut(messages[unit[0]], unit), unit[0])
+                new[unit, 0, 0] = to_slice(messages[unit], unit[0])
                 share_next.append((unit, 0))
-        if 1 <= n <= len(swaps):
-            for unit in swaps[n - 1]:
+        if n < len(swaps):
+            for unit in swaps[n]:
                 for r in range(1, p.xs):
                     new[unit, r, 0] = along_x(held[unit, 0, 0], r)
                     share_next.append((unit, r))
+        for r in range(1, p.xs):
+            if n == 0:
+                crossed[r] = along_x(messages[units[0]], r)
+            if n == 1:
+                new[units[0], r, 0] = to_slice(raw[r], 0)
+                share_next.append((units[0], r))
         for unit, r in to_share:
             new[unit, r, 1] = to_core(held[unit, r, 0])
         if n + 1 < len(rounds):
-            for o, _, _ in rounds[n + 1]:
-                if o not in messages:
-                    made[o] = make(o, spread)
-        part = n - (len(swaps) - AMPS)
+            for unit in rounds[n + 1]:
+                if unit not in messages:
+                    made.update(make(unit[0], spread))
+        part = n - (len(rounds) - AMPS)
         if 0 <= part < AMPS:
             laid[part] = relayout(p, sources[part], part)
-        moved = (list(new.values()), list(made.values()), list(laid.values()))
+        moved = (list(new.values()), list(made.values()), list(laid.values()), crossed)
         kept = (list(held.values()), spread, sources)
         moved, (old, spread, sources) = lax.optimization_barrier((moved, kept))
         held = dict(zip(held, old))
         held.update(zip(new, moved[0]))
         messages.update(zip(made, moved[1]))
+        raw = moved[3]
         for part, amp in zip(laid, moved[2]):
             amps[part] = amp
-    amps = [amp.reshape(-1, p.d) for amp in amps]
     pieces = [
         held[unit, r, other] for unit in units for r in range(p.xs) for other in range(CORES)
     ]
 
     partial_terms = ladder(p, units, place, assignment, pieces, amps)
     share = p.ij // n_aux
-    terms = partial_terms[:, :, : p.ij].reshape(n_pair, BLK, BLK, n_aux, share)
+    terms = partial_terms.reshape(n_pair, BLK, BLK, p.ij // ROWS, QUAD * ROWS)[..., :ROWS]
+    terms = terms.reshape(n_pair, BLK, BLK, n_aux, share)
     terms = terms.transpose(3, 0, 4, 2, 1).reshape(n_aux * n_pair, share, BLK * BLK)
     terms = lax.all_to_all(terms, ("aux", "pair"), split_axis=0, concat_axis=0, tiled=True)
     return terms.sum(axis=0)

time: 242 us -> 252 us (1.041)
  Pallas kernels: 122 us -> 143 us
  waiting for transfers between devices: 74.3 us -> 59.6 us
  starting transfers between devices: 19.9 us -> 22.5 us
    pallas_call x5, Pallas kernels: 103 us -> 121 us  [the longest x1 91.7 us: ladder(): pl.pallas_call(functools.partial(ladder_kernel, p, units, group), out_sha...]
    ppermute x20 -> x21, waiting for transfers between devices: 74.3 us -> 59.6 us  [permute(): return lax.ppermute(array, ('aux', 'pair'), pairs)]
    pallas_call x2, Pallas kernels: 18.1 us -> 21.2 us  [relayout(): pl.pallas_call(functools.partial(relayout_kernel, p), out_shape=jax.Shape...]
    ppermute x20 -> x21, starting transfers between devices: 19.9 us -> 22.5 us  [permute(): return lax.ppermute(array, ('aux', 'pair'), pairs)]
    unnamed x50 -> x47, local copies, waits for them, and re-layouts: 12.1 us -> 13.2 us
  transfers between devices with their start and end apart: 20 -> 21, of which waited for: 9 -> 7; matrix products, arithmetic and copies ran while one was open for 0% -> 0% of each run, Pallas kernels for 13% -> 14%
where the time goes in v8:
time: 252 us
  Pallas kernels  143 us (57%)
  waiting for transfers between devices  59.6 us (24%)
  starting transfers between devices  22.5 us (9%)
  local copies, waits for them, and re-layouts  15.6 us (6%)
  blocking collectives  9.81 us (4%)
    pallas_call x1, Pallas kernels, ladder(): pl.pallas_call(functools.partial(ladder_kernel, p, units, group), out_sha...  91.7 us
    ppermute x21, waiting for transfers between devices, permute(): return lax.ppermute(array, ('aux', 'pair'), pairs)  59.6 us
    pallas_call x4, Pallas kernels, dress(): pl.pallas_call(functools.partial(dress_kernel, p, offset, bounds), out_sh...  29.2 us
    ppermute x21, starting transfers between devices, permute(): return lax.ppermute(array, ('aux', 'pair'), pairs)  22.5 us
    pallas_call x2, Pallas kernels, relayout(): pl.pallas_call(functools.partial(relayout_kernel, p), out_shape=jax.Shape...  21.2 us
    unnamed x47, local copies, waits for them, and re-layouts  13.2 us
    all_to_all x1, blocking collectives, shards(): lax.all_to_all(terms, ('aux', 'pair'), split_axis=0, concat_axis=0, tiled...  9.81 us
  transfers between devices with their start and end apart: 21, of which 7 were waited for; matrix products, arithmetic and copies ran while one was open for 0% of the time, Pallas kernels for 14%

profile of v8, /device:TPU:0, one launch (start us, length us, event | category | flops | bytes accessed | tf_op | source)
XLA Modules:
  0.0 251.7 jit_solution(7034083622716996393)
XLA Ops:
  0.0 0.8 copy.11.t1_ref
  0.8 0.8 spread.1.a_ref
  1.6 0.1 pad_add_fusion.z_ref.place_ref
  1.7 7.4 %dress.4 = bf16[36,112,128]{2,1,0:T(8,128)(2,1)S(1)} custom-call(s32[3]{0:T(128)S(1)} %pad_add_fusion.z_ref.place_ref, bf16[512,1600]{1,0:T(8,128)(2,1)S(1)} %spread.1.a_ref, bf16[100,112,576]{2,1,0:T(8,128)(2,1)} %refs_1_.7, bf16[100,112,576]{2,1,0:T(8,128)(2,1)} %refs_1_.7, bf16[32,112,576]{2,1,0:T(8,128)(2,1)} %refs_3_.7, bf16[32,112,576]{2,1,0:T(8,128)(2,1)} %refs_3_.7), custom_call_target="tpu_custom_call" | custom-call | flops 2936012800 | bytes 9404416 | tf_op jit(solution)/shard_map/dress/pallas_call | solution.py:134
  9.1 7.3 %dress.5 = bf16[36,112,128]{2,1,0:T(8,128)(2,1)S(1)} custom-call(s32[3]{0:T(128)S(1)} %pad_add_fusion.z_ref.place_ref, bf16[512,1600]{1,0:T(8,128)(2,1)S(1)} %spread.1.a_ref, bf16[100,112,576]{2,1,0:T(8,128)(2,1)} %refs_1_.7, bf16[100,112,576]{2,1,0:T(8,128)(2,1)} %refs_1_.7, bf16[32,112,576]{2,1,0:T(8,128)(2,1)} %refs_3_.7, bf16[32,112,576]{2,1,0:T(8,128)(2,1)} %refs_3_.7), custom_call_target="tpu_custom_call" | custom-call | flops 2936012800 | bytes 9404416 | tf_op jit(solution)/shard_map/dress/pallas_call | solution.py:134
  16.4 3.0 %collective-permute-start.1 = (bf16[36,112,128]{2,1,0:T(8,128)(2,1)S(1)}, bf16[36,112,128]{2,1,0:T(8,128)(2,1)S(1)}, u32[]{:S(2)}, u32[]{:S(2)}) collective-permute-start(bf16[36,112,128]{2,1,0:T(8,128)(2,1)S(1)} %dress.5), channel_id=1, source_target_pairs={{0,2},{1,10},{2,4},{3,12},{4,6},{5,14},{6,0},{7,8},{8,3},{9,11},{1... | collective-permute-start | bytes 3096584 | tf_op jit(solution)/shard_map/ppermute | solution.py:392
  19.4 0.7 collective-permute-start
  20.1 1.6 collective-permute-start.2
  21.6 7.3 %dress.6 = bf16[36,112,128]{2,1,0:T(8,128)(2,1)S(1)} custom-call(s32[3]{0:T(128)S(1)} %pad_add_fusion.z_ref.place_ref, bf16[512,1600]{1,0:T(8,128)(2,1)S(1)} %spread.1.a_ref, bf16[100,112,576]{2,1,0:T(8,128)(2,1)} %refs_1_.7, bf16[100,112,576]{2,1,0:T(8,128)(2,1)} %refs_1_.7, bf16[32,112,576]{2,1,0:T(8,128)(2,1)} %refs_3_.7, bf16[32,112,576]{2,1,0:T(8,128)(2,1)} %refs_3_.7), custom_call_target="tpu_custom_call" | custom-call | flops 2936012800 | bytes 9404416 | tf_op jit(solution)/shard_map/dress/pallas_call | solution.py:134
  28.9 15.7 %collective-permute-done.1.refs_4_ = bf16[36,112,128]{2,1,0:T(8,128)(2,1)S(1)} collective-permute-done((bf16[36,112,128]{2,1,0:T(8,128)(2,1)S(1)}, bf16[36,112,128]{2,1,0:T(8,128)(2,1)S(1)}, u32[]{:S(2)}, u32[]{:S(2)}) %collective-permute-start.1) | collective-permute-done | bytes 1032224 | tf_op jit(solution)/shard_map/ppermute | solution.py:392
  44.6 2.3 collective-permute-start.3
  46.9 1.5 collective-permute-start.4
  48.4 1.6 collective-permute-start.5
  50.1 3.3 %collective-permute-start.6 = (bf16[36,112,128]{2,1,0:T(8,128)(2,1)S(1)}, bf16[36,112,128]{2,1,0:T(8,128)(2,1)S(1)}, u32[]{:S(2)}, u32[]{:S(2)}) collective-permute-start(bf16[36,112,128]{2,1,0:T(8,128)(2,1)S(1)} %collective-permute-done.refs_0_), channel_id=1, source_target_pairs={{0,8},{1,9},{2,10},{3,11},{4,12},{5,13},{6,14},{7,15},{8,0},{9,1},... | collective-permute-start | bytes 3096584 | tf_op jit(solution)/shard_map/ppermute | solution.py:392
  53.4 0.1 collective-permute-start.7
  53.4 7.3 %dress.7 = (bf16[18,112,128]{2,1,0:T(8,128)(2,1)S(1)}, bf16[18,112,128]{2,1,0:T(8,128)(2,1)S(1)}) custom-call(s32[3]{0:T(128)S(1)} %pad_add_fusion.z_ref.place_ref, bf16[512,1600]{1,0:T(8,128)(2,1)S(1)} %spread.1.a_ref, bf16[100,112,576]{2,1,0:T(8,128)(2,1)} %refs_1_.7, bf16[100,112,576]{2,1,0:T(8,128)(2,1)} %refs_1_.7, bf16[32,112,576]{2,1,0:T(8,128)(2,1)} %refs_3_.7, ...), custom_call_target="tpu_custom_call" | custom-call | flops 2936012800 | bytes 9404416 | tf_op jit(solution)/shard_map/dress/pallas_call | solution.py:134
  60.7 8.3 %collective-permute-done.3.refs_8_ = bf16[36,112,128]{2,1,0:T(8,128)(2,1)} collective-permute-done((bf16[36,112,128]{2,1,0:T(8,128)(2,1)S(1)}, bf16[36,112,128]{2,1,0:T(8,128)(2,1)}, u32[]{:S(2)}, u32[]{:S(2)}) %collective-permute-start.3) | collective-permute-done | bytes 1032224 | tf_op jit(solution)/shard_map/ppermute | solution.py:392
  69.0 2.6 %collective-permute-done.4.refs_6_ = bf16[36,112,128]{2,1,0:T(8,128)(2,1)} collective-permute-done((bf16[36,112,128]{2,1,0:T(8,128)(2,1)S(1)}, bf16[36,112,128]{2,1,0:T(8,128)(2,1)}, u32[]{:S(2)}, u32[]{:S(2)}) %collective-permute-start.4) | collective-permute-done | bytes 1032224 | tf_op jit(solution)/shard_map/ppermute | solution.py:392
  71.6 1.6 collective-permute-start.10
  73.2 2.7 %collective-permute-start.11 = (bf16[36,112,128]{2,1,0:T(8,128)(2,1)}, bf16[36,112,128]{2,1,0:T(8,128)(2,1)S(1)}, u32[]{:S(2)}, u32[]{:S(2)}) collective-permute-start(bf16[36,112,128]{2,1,0:T(8,128)(2,1)} %collective-permute-done.3.refs_8_), channel_id=1, source_target_pairs={{0,8},{1,9},{2,10},{3,11},{4,12},{5,13},{6,14},{7,15},{8,0},{9,1},... | collective-permute-start | bytes 3096584 | tf_op jit(solution)/shard_map/ppermute | solution.py:392
  75.9 0.5 collective-permute-start.13
  76.4 0.8 collective-permute-start.9
  77.2 10.5 %relayout.2.refs_20_ = bf16[28,896,256]{2,1,0:T(8,128)(2,1)S(1)} custom-call(bf16[64,224,896]{2,1,0:T(8,128)(2,1)} %in_ref.1), custom_call_target="tpu_custom_call" | custom-call | flops 3288334336 | bytes 25690112 | tf_op jit(solution)/shard_map/relayout/pallas_call | solution.py:189
  87.7 4.6 %copy-done = bf16[28,896,256]{2,1,0:T(8,128)(2,1)} copy-done((bf16[28,896,256]{2,1,0:T(8,128)(2,1)}, bf16[28,896,256]{2,1,0:T(8,128)(2,1)S(1)}, u32[]{:S(2)}) %copy-start) | copy-done | bytes 12845080
  92.4 10.3 %collective-permute-done.9.refs_12_ = bf16[18,112,128]{2,1,0:T(8,128)(2,1)S(1)} collective-permute-done((bf16[18,112,128]{2,1,0:T(8,128)(2,1)S(1)}, bf16[18,112,128]{2,1,0:T(8,128)(2,1)S(1)}, u32[]{:S(2)}, u32[]{:S(2)}) %collective-permute-start.9) | collective-permute-done | bytes 516128 | tf_op jit(solution)/shard_map/ppermute | solution.py:392
  102.7 0.2 collective-permute-start.16
  102.9 1.1 collective-permute-start.14
  104.0 10.7 %relayout.3.refs_21_ = bf16[28,896,256]{2,1,0:T(8,128)(2,1)S(1)} custom-call(bf16[64,224,896]{2,1,0:T(8,128)(2,1)} %in_ref.1), custom_call_target="tpu_custom_call" | custom-call | flops 3288334336 | bytes 25690112 | tf_op jit(solution)/shard_map/relayout/pallas_call | solution.py:189
  114.8 4.6 %copy-done.1 = bf16[28,896,256]{2,1,0:T(8,128)(2,1)} copy-done((bf16[28,896,256]{2,1,0:T(8,128)(2,1)}, bf16[28,896,256]{2,1,0:T(8,128)(2,1)S(1)}, u32[]{:S(2)}) %copy-start.1) | copy-done | bytes 12845080
  119.4 8.8 %collective-permute-done.8.refs_16_ = bf16[18,112,128]{2,1,0:T(8,128)(2,1)S(1)} collective-permute-done((bf16[18,112,128]{2,1,0:T(8,128)(2,1)S(1)}, bf16[18,112,128]{2,1,0:T(8,128)(2,1)S(1)}, u32[]{:S(2)}, u32[]{:S(2)}) %collective-permute-start.8) | collective-permute-done | bytes 516128 | tf_op jit(solution)/shard_map/ppermute | solution.py:392
  128.3 1.0 copy-done.12
  129.3 1.0 collective-permute-start.17
  130.3 0.5 collective-permute-start.18
  130.8 12.9 %collective-permute-done.17.refs_18_ = bf16[18,112,128]{2,1,0:T(8,128)(2,1)S(1)} collective-permute-done((bf16[18,112,128]{2,1,0:T(8,128)(2,1)S(1)}, bf16[18,112,128]{2,1,0:T(8,128)(2,1)S(1)}, u32[]{:S(2)}, u32[]{:S(2)}) %collective-permute-start.17) | collective-permute-done | bytes 516128 | tf_op jit(solution)/shard_map/ppermute | solution.py:392
  143.8 0.1 collective-permute-start.20
  143.9 0.9 copy.12.blocks_ref
  144.7 1.0 collective-permute-done.20.refs_19_
  145.8 0.8 copy-done.20
  146.5 91.7 %ladder.1 = f32[32,4,256]{2,1,0:T(4,128)} custom-call(s32[3]{0:T(128)} %copy-done.2, s32[8,2]{1,0:T(8,128)} %copy.12.blocks_ref, bf16[36,112,128]{2,1,0:T(8,128)(2,1)} %copy-done.5, bf16[36,112,128]{2,1,0:T(8,128)(2,1)} %copy-done.6, bf16[36,112,128]{2,1,0:T(8,128)(2,1)} %collective-permute-done.5.refs_2_, bf16[36,112,128]{2,1,0:T(8,128)(2,1)} %copy-done.11, ...), custom_call_target="tpu_custom_call" | custom-call | flops 13153337344 | bytes 42205184 | tf_op jit(solution)/shard_map/ladder/pallas_call | solution.py:337
  238.3 1.1 reshape.6
  239.4 0.2 copy.18
  239.5 0.2 copy.20
  239.7 0.1 reshape.8
  239.8 9.8 %all_to_all.5 = f32[32,1,256]{2,1,0:T(1,128)S(1)} all-to-all(f32[32,1,256]{2,1,0:T(1,128)S(1)} %reshape.8), channel_id=1, replica_groups=mesh['aux'=4,'pair'=8] {'aux','pair'}, dimensions={0} | all-to-all | bytes 65536 | tf_op jit(solution)/shard_map/all_to_all | solution.py:479
  249.7 0.5 broadcast.2
  250.2 0.7 reduce
  250.9 0.1 reshape.9
  251.1 0.7 copy.16
  (57 shorter events, 0.2 us)
Async XLA Ops:
  1.7 51.7 %copy-start.2 = (s32[3]{0:T(128)}, s32[3]{0:T(128)S(1)}, u32[]{:S(2)}) copy-start(s32[3]{0:T(128)S(1)} %pad_add_fusion.z_ref.place_ref) | copy-start | bytes 40
  16.4 28.2 %collective-permute-start.1 = (bf16[36,112,128]{2,1,0:T(8,128)(2,1)S(1)}, bf16[36,112,128]{2,1,0:T(8,128)(2,1)S(1)}, u32[]{:S(2)}, u32[]{:S(2)}) collective-permute-start(bf16[36,112,128]{2,1,0:T(8,128)(2,1)S(1)} %dress.5), channel_id=1, source_target_pairs={{0,2},{1,10},{2,4},{3,12},{4,6},{5,14},{6,0},{7,8},{8,3},{9,11},{1... | collective-permute-start | bytes 3096584 | tf_op jit(solution)/shard_map/ppermute | solution.py:392
  19.4 25.3 %collective-permute-start = (bf16[36,112,128]{2,1,0:T(8,128)(2,1)S(1)}, bf16[36,112,128]{2,1,0:T(8,128)(2,1)S(1)}, u32[]{:S(2)}, u32[]{:S(2)}) collective-permute-start(bf16[36,112,128]{2,1,0:T(8,128)(2,1)S(1)} %dress.4), channel_id=1, source_target_pairs={{0,0},{1,8},{2,2},{3,10},{4,4},{5,12},{6,6},{7,14},{8,1},{9,9},{10... | collective-permute-start | bytes 3096584 | tf_op jit(solution)/shard_map/ppermute | solution.py:392
  20.1 24.6 %collective-permute-start.2 = (bf16[36,112,128]{2,1,0:T(8,128)(2,1)S(1)}, bf16[36,112,128]{2,1,0:T(8,128)(2,1)S(1)}, u32[]{:S(2)}, u32[]{:S(2)}) collective-permute-start(bf16[36,112,128]{2,1,0:T(8,128)(2,1)S(1)} %dress.4), channel_id=1, source_target_pairs={{0,16},{1,17},{2,18},{3,19},{4,20},{5,21},{6,22},{7,23},{8,24},{9,... | collective-permute-start | bytes 3096584 | tf_op jit(solution)/shard_map/ppermute | solution.py:392
  44.6 16.1 %copy-start.4 = (bf16[36,112,128]{2,1,0:T(8,128)(2,1)}, bf16[36,112,128]{2,1,0:T(8,128)(2,1)S(1)}, u32[]{:S(2)}) copy-start(bf16[36,112,128]{2,1,0:T(8,128)(2,1)S(1)} %collective-permute-done.1.refs_4_) | copy-start | bytes 3096580
  44.6 16.1 %copy-start.5 = (bf16[36,112,128]{2,1,0:T(8,128)(2,1)}, bf16[36,112,128]{2,1,0:T(8,128)(2,1)S(1)}, u32[]{:S(2)}) copy-start(bf16[36,112,128]{2,1,0:T(8,128)(2,1)S(1)} %collective-permute-done.refs_0_) | copy-start | bytes 3096580
  44.6 24.4 %collective-permute-start.3 = (bf16[36,112,128]{2,1,0:T(8,128)(2,1)S(1)}, bf16[36,112,128]{2,1,0:T(8,128)(2,1)}, u32[]{:S(2)}, u32[]{:S(2)}) collective-permute-start(bf16[36,112,128]{2,1,0:T(8,128)(2,1)S(1)} %dress.6), channel_id=1, source_target_pairs={{0,6},{1,14},{2,0},{3,8},{4,2},{5,10},{6,4},{7,12},{8,7},{9,15},{1... | collective-permute-start | bytes 3096584 | tf_op jit(solution)/shard_map/ppermute | solution.py:392
  46.9 24.6 %collective-permute-start.4 = (bf16[36,112,128]{2,1,0:T(8,128)(2,1)S(1)}, bf16[36,112,128]{2,1,0:T(8,128)(2,1)}, u32[]{:S(2)}, u32[]{:S(2)}) collective-permute-start(bf16[36,112,128]{2,1,0:T(8,128)(2,1)S(1)} %collective-permute-done.1.refs_4_), channel_id=1, source_target_pairs={{0,16},{1,17},{2,18},{3,19},{4,20},{5,21},{6,22},{7,23},{8,24},{9,... | collective-permute-start | bytes 3096584 | tf_op jit(solution)/shard_map/ppermute | solution.py:392
  48.4 23.2 %collective-permute-start.5 = (bf16[36,112,128]{2,1,0:T(8,128)(2,1)S(1)}, bf16[36,112,128]{2,1,0:T(8,128)(2,1)}, u32[]{:S(2)}, u32[]{:S(2)}) collective-permute-start(bf16[36,112,128]{2,1,0:T(8,128)(2,1)S(1)} %collective-permute-done.2), channel_id=1, source_target_pairs={{0,0},{1,8},{2,2},{3,10},{4,4},{5,12},{6,6},{7,14},{8,1},{9,9},{10... | collective-permute-start | bytes 3096584 | tf_op jit(solution)/shard_map/ppermute | solution.py:392
  50.1 21.6 %collective-permute-start.6 = (bf16[36,112,128]{2,1,0:T(8,128)(2,1)S(1)}, bf16[36,112,128]{2,1,0:T(8,128)(2,1)S(1)}, u32[]{:S(2)}, u32[]{:S(2)}) collective-permute-start(bf16[36,112,128]{2,1,0:T(8,128)(2,1)S(1)} %collective-permute-done.refs_0_), channel_id=1, source_target_pairs={{0,8},{1,9},{2,10},{3,11},{4,12},{5,13},{6,14},{7,15},{8,0},{9,1},... | collective-permute-start | bytes 3096584 | tf_op jit(solution)/shard_map/ppermute | solution.py:392
  53.4 18.3 %collective-permute-start.7 = (bf16[36,112,128]{2,1,0:T(8,128)(2,1)S(1)}, bf16[36,112,128]{2,1,0:T(8,128)(2,1)S(1)}, u32[]{:S(2)}, u32[]{:S(2)}) collective-permute-start(bf16[36,112,128]{2,1,0:T(8,128)(2,1)S(1)} %collective-permute-done.1.refs_4_), channel_id=1, source_target_pairs={{0,8},{1,9},{2,10},{3,11},{4,12},{5,13},{6,14},{7,15},{8,0},{9,1},... | collective-permute-start | bytes 3096584 | tf_op jit(solution)/shard_map/ppermute | solution.py:392
  71.6 4.8 %copy-start.6 = (bf16[36,112,128]{2,1,0:T(8,128)(2,1)}, bf16[36,112,128]{2,1,0:T(8,128)(2,1)S(1)}, u32[]{:S(2)}) copy-start(bf16[36,112,128]{2,1,0:T(8,128)(2,1)S(1)} %collective-permute-done.6.refs_1_) | copy-start | bytes 3096580
  71.6 4.8 %copy-start.7 = (bf16[36,112,128]{2,1,0:T(8,128)(2,1)}, bf16[36,112,128]{2,1,0:T(8,128)(2,1)S(1)}, u32[]{:S(2)}) copy-start(bf16[36,112,128]{2,1,0:T(8,128)(2,1)S(1)} %collective-permute-done.7.refs_5_) | copy-start | bytes 3096580
  71.6 31.0 %collective-permute-start.10 = (bf16[36,112,128]{2,1,0:T(8,128)(2,1)}, bf16[36,112,128]{2,1,0:T(8,128)(2,1)S(1)}, u32[]{:S(2)}, u32[]{:S(2)}) collective-permute-start(bf16[36,112,128]{2,1,0:T(8,128)(2,1)} %collective-permute-done.3.refs_8_), channel_id=1, source_target_pairs={{0,16},{1,17},{2,18},{3,19},{4,20},{5,21},{6,22},{7,23},{8,24},{9,... | collective-permute-start | bytes 3096584 | tf_op jit(solution)/shard_map/ppermute | solution.py:392
  73.2 29.4 %collective-permute-start.11 = (bf16[36,112,128]{2,1,0:T(8,128)(2,1)}, bf16[36,112,128]{2,1,0:T(8,128)(2,1)S(1)}, u32[]{:S(2)}, u32[]{:S(2)}) collective-permute-start(bf16[36,112,128]{2,1,0:T(8,128)(2,1)} %collective-permute-done.3.refs_8_), channel_id=1, source_target_pairs={{0,8},{1,9},{2,10},{3,11},{4,12},{5,13},{6,14},{7,15},{8,0},{9,1},... | collective-permute-start | bytes 3096584 | tf_op jit(solution)/shard_map/ppermute | solution.py:392
  75.9 26.7 %collective-permute-start.12 = (bf16[36,112,128]{2,1,0:T(8,128)(2,1)}, bf16[36,112,128]{2,1,0:T(8,128)(2,1)S(1)}, u32[]{:S(2)}, u32[]{:S(2)}) collective-permute-start(bf16[36,112,128]{2,1,0:T(8,128)(2,1)} %collective-permute-done.4.refs_6_), channel_id=1, source_target_pairs={{0,8},{1,9},{2,10},{3,11},{4,12},{5,13},{6,14},{7,15},{8,0},{9,1},... | collective-permute-start | bytes 3096584 | tf_op jit(solution)/shard_map/ppermute | solution.py:392
  75.9 26.7 %collective-permute-start.13 = (bf16[36,112,128]{2,1,0:T(8,128)(2,1)}, bf16[36,112,128]{2,1,0:T(8,128)(2,1)S(1)}, u32[]{:S(2)}, u32[]{:S(2)}) collective-permute-start(bf16[36,112,128]{2,1,0:T(8,128)(2,1)} %collective-permute-done.5.refs_2_), channel_id=1, source_target_pairs={{0,8},{1,9},{2,10},{3,11},{4,12},{5,13},{6,14},{7,15},{8,0},{9,1},... | collective-permute-start | bytes 3096584 | tf_op jit(solution)/shard_map/ppermute | solution.py:392
  76.4 26.2 %collective-permute-start.9 = (bf16[18,112,128]{2,1,0:T(8,128)(2,1)S(1)}, bf16[18,112,128]{2,1,0:T(8,128)(2,1)S(1)}, u32[]{:S(2)}, u32[]{:S(2)}) collective-permute-start(bf16[18,112,128]{2,1,0:T(8,128)(2,1)S(1)} %get-tuple-element.113), channel_id=1, source_target_pairs={{0,4},{1,12},{2,6},{3,14},{4,0},{5,8},{6,2},{7,10},{8,5},{9,13},{1... | collective-permute-start | bytes 1548296 | tf_op jit(solution)/shard_map/ppermute | solution.py:392
  87.7 4.6 %copy-start = (bf16[28,896,256]{2,1,0:T(8,128)(2,1)}, bf16[28,896,256]{2,1,0:T(8,128)(2,1)S(1)}, u32[]{:S(2)}) copy-start(bf16[28,896,256]{2,1,0:T(8,128)(2,1)S(1)} %relayout.2.refs_20_) | copy-start | bytes 38535172
  92.4 51.5 %copy-start.3 = (s32[8,2]{0,1:T(2,128)S(1)}, s32[8,2]{0,1:T(2,128)}, u32[]{:S(2)}) copy-start(s32[8,2]{0,1:T(2,128)} %param.9) | copy-start | bytes 196
  102.6 12.1 %copy-start.13 = (bf16[18,112,128]{2,1,0:T(8,128)(2,1)}, bf16[18,112,128]{2,1,0:T(8,128)(2,1)S(1)}, u32[]{:S(2)}) copy-start(bf16[18,112,128]{2,1,0:T(8,128)(2,1)S(1)} %collective-permute-done.9.refs_12_) | copy-start | bytes 1548292
  102.6 12.1 %copy-start.8 = (bf16[36,112,128]{2,1,0:T(8,128)(2,1)}, bf16[36,112,128]{2,1,0:T(8,128)(2,1)S(1)}, u32[]{:S(2)}) copy-start(bf16[36,112,128]{2,1,0:T(8,128)(2,1)S(1)} %collective-permute-done.10.refs_10_) | copy-start | bytes 3096580
  102.6 12.1 %copy-start.9 = (bf16[36,112,128]{2,1,0:T(8,128)(2,1)}, bf16[36,112,128]{2,1,0:T(8,128)(2,1)S(1)}, u32[]{:S(2)}) copy-start(bf16[36,112,128]{2,1,0:T(8,128)(2,1)S(1)} %collective-permute-done.11.refs_9_) | copy-start | bytes 3096580
  102.7 12.1 %copy-start.10 = (bf16[36,112,128]{2,1,0:T(8,128)(2,1)}, bf16[36,112,128]{2,1,0:T(8,128)(2,1)S(1)}, u32[]{:S(2)}) copy-start(bf16[36,112,128]{2,1,0:T(8,128)(2,1)S(1)} %collective-permute-done.12.refs_7_) | copy-start | bytes 3096580
  102.7 12.1 %copy-start.11 = (bf16[36,112,128]{2,1,0:T(8,128)(2,1)}, bf16[36,112,128]{2,1,0:T(8,128)(2,1)S(1)}, u32[]{:S(2)}) copy-start(bf16[36,112,128]{2,1,0:T(8,128)(2,1)S(1)} %collective-permute-done.13.refs_3_) | copy-start | bytes 3096580
  102.7 25.6 %collective-permute-start.16 = (bf16[36,112,128]{2,1,0:T(8,128)(2,1)S(1)}, bf16[36,112,128]{2,1,0:T(8,128)(2,1)S(1)}, u32[]{:S(2)}, u32[]{:S(2)}) collective-permute-start(bf16[36,112,128]{2,1,0:T(8,128)(2,1)S(1)} %collective-permute-done.10.refs_10_), channel_id=1, source_target_pairs={{0,8},{1,9},{2,10},{3,11},{4,12},{5,13},{6,14},{7,15},{8,0},{9,1},... | collective-permute-start | bytes 3096584 | tf_op jit(solution)/shard_map/ppermute | solution.py:392
  102.9 25.3 %collective-permute-start.8 = (bf16[18,112,128]{2,1,0:T(8,128)(2,1)S(1)}, bf16[18,112,128]{2,1,0:T(8,128)(2,1)S(1)}, u32[]{:S(2)}, u32[]{:S(2)}) collective-permute-start(bf16[18,112,128]{2,1,0:T(8,128)(2,1)S(1)} %get-tuple-element.112), channel_id=1, source_target_pairs={{0,4},{1,12},{2,6},{3,14},{4,0},{5,8},{6,2},{7,10},{8,5},{9,13},{1... | collective-permute-start | bytes 1548296 | tf_op jit(solution)/shard_map/ppermute | solution.py:392
  102.9 25.4 %collective-permute-start.14 = (bf16[18,112,128]{2,1,0:T(8,128)(2,1)S(1)}, bf16[18,112,128]{2,1,0:T(8,128)(2,1)S(1)}, u32[]{:S(2)}, u32[]{:S(2)}) collective-permute-start(bf16[18,112,128]{2,1,0:T(8,128)(2,1)S(1)} %collective-permute-done.9.refs_12_), channel_id=1, source_target_pairs={{0,16},{1,17},{2,18},{3,19},{4,20},{5,21},{6,22},{7,23},{8,24},{9,... | collective-permute-start | bytes 1548296 | tf_op jit(solution)/shard_map/ppermute | solution.py:392
  103.9 24.3 %collective-permute-start.15 = (bf16[18,112,128]{2,1,0:T(8,128)(2,1)S(1)}, bf16[18,112,128]{2,1,0:T(8,128)(2,1)S(1)}, u32[]{:S(2)}, u32[]{:S(2)}) collective-permute-start(bf16[18,112,128]{2,1,0:T(8,128)(2,1)S(1)} %collective-permute-done.9.refs_12_), channel_id=1, source_target_pairs={{0,8},{1,9},{2,10},{3,11},{4,12},{5,13},{6,14},{7,15},{8,0},{9,1},... | collective-permute-start | bytes 1548296 | tf_op jit(solution)/shard_map/ppermute | solution.py:392
  114.8 4.6 %copy-start.1 = (bf16[28,896,256]{2,1,0:T(8,128)(2,1)}, bf16[28,896,256]{2,1,0:T(8,128)(2,1)S(1)}, u32[]{:S(2)}) copy-start(bf16[28,896,256]{2,1,0:T(8,128)(2,1)S(1)} %relayout.3.refs_21_) | copy-start | bytes 38535172
  128.2 17.5 %copy-start.14 = (bf16[18,112,128]{2,1,0:T(8,128)(2,1)}, bf16[18,112,128]{2,1,0:T(8,128)(2,1)S(1)}, u32[]{:S(2)}) copy-start(bf16[18,112,128]{2,1,0:T(8,128)(2,1)S(1)} %collective-permute-done.8.refs_16_) | copy-start | bytes 1548292
  128.2 15.5 %copy-start.15 = (bf16[18,112,128]{2,1,0:T(8,128)(2,1)}, bf16[18,112,128]{2,1,0:T(8,128)(2,1)S(1)}, u32[]{:S(2)}) copy-start(bf16[18,112,128]{2,1,0:T(8,128)(2,1)S(1)} %collective-permute-done.14.refs_14_) | copy-start | bytes 1548292
  128.2 15.5 %copy-start.16 = (bf16[18,112,128]{2,1,0:T(8,128)(2,1)}, bf16[18,112,128]{2,1,0:T(8,128)(2,1)S(1)}, u32[]{:S(2)}) copy-start(bf16[18,112,128]{2,1,0:T(8,128)(2,1)S(1)} %collective-permute-done.15.refs_13_) | copy-start | bytes 1548292
  128.3 1.0 copy-start.12
  129.3 14.4 %collective-permute-start.17 = (bf16[18,112,128]{2,1,0:T(8,128)(2,1)S(1)}, bf16[18,112,128]{2,1,0:T(8,128)(2,1)S(1)}, u32[]{:S(2)}, u32[]{:S(2)}) collective-permute-start(bf16[18,112,128]{2,1,0:T(8,128)(2,1)S(1)} %collective-permute-done.8.refs_16_), channel_id=1, source_target_pairs={{0,16},{1,17},{2,18},{3,19},{4,20},{5,21},{6,22},{7,23},{8,24},{9,... | collective-permute-start | bytes 1548296 | tf_op jit(solution)/shard_map/ppermute | solution.py:392
  130.3 13.4 %collective-permute-start.18 = (bf16[18,112,128]{2,1,0:T(8,128)(2,1)S(1)}, bf16[18,112,128]{2,1,0:T(8,128)(2,1)S(1)}, u32[]{:S(2)}, u32[]{:S(2)}) collective-permute-start(bf16[18,112,128]{2,1,0:T(8,128)(2,1)S(1)} %collective-permute-done.8.refs_16_), channel_id=1, source_target_pairs={{0,8},{1,9},{2,10},{3,11},{4,12},{5,13},{6,14},{7,15},{8,0},{9,1},... | collective-permute-start | bytes 1548296 | tf_op jit(solution)/shard_map/ppermute | solution.py:392
  130.8 12.9 %collective-permute-start.19 = (bf16[18,112,128]{2,1,0:T(8,128)(2,1)S(1)}, bf16[18,112,128]{2,1,0:T(8,128)(2,1)S(1)}, u32[]{:S(2)}, u32[]{:S(2)}) collective-permute-start(bf16[18,112,128]{2,1,0:T(8,128)(2,1)S(1)} %collective-permute-done.14.refs_14_), channel_id=1, source_target_pairs={{0,8},{1,9},{2,10},{3,11},{4,12},{5,13},{6,14},{7,15},{8,0},{9,1},... | collective-permute-start | bytes 1548296 | tf_op jit(solution)/shard_map/ppermute | solution.py:392
  143.7 2.0 copy-start.17
  143.7 2.0 copy-start.18
  143.8 2.0 copy-start.19
  143.8 2.0 collective-permute-start.20
  145.7 0.8 copy-start.20

commit v9 on v8

--- a/solution.py
+++ b/solution.py
@@ -10,7 +10,8 @@
 BLK = 4
 QUAD = 4
 AMPS = 2
-DEEP = 256
+PARTS = 4
+SLOTS = 4
 ROWS = 16
 LANES = 128
 CORES = 2
@@ -202,27 +203,35 @@
     )(amplitudes)
 
 
-def ladder_kernel(p, units, group, place_ref, blocks_ref, *refs):
+def ladder_kernel(p, units, parts, group, place_ref, blocks_ref, *refs):
     count = len(units) * p.xs * CORES
     pieces, amps, out = refs[:count], refs[count : count + AMPS], refs[count + AMPS]
     scratch = refs[count + AMPS + 1 :]
     vectors, left, spread_tail, tiles, held, total, piece_sem, amp_sem = scratch
     w, z, core, chunk = p.window, place_ref[0], place_ref[1], place_ref[2]
     quads = p.c // QUAD
-    width = QUAD * p.ij
-    steps = quads // group
-    spans = [slice(low, min(low + DEEP, p.d)) for low in range(0, p.d, DEEP)]
-
-    def fetches(span):
-        each = quads // AMPS
-        return [
-            pltpu.make_async_copy(
-                amp.at[:, span],
-                held.at[n * each : (n + 1) * each, : span.stop - span.start],
-                amp_sem.at[n],
-            )
-            for n, amp in enumerate(amps)
-        ]
+    here = quads // parts
+    rows = here * ROWS
+    steps = here // group
+    each = parts * steps // AMPS
+
+    class Fetch:
+        def __init__(self, step, slot):
+            self.step, self.slot = step, slot
+
+        def copy(self, amp, step):
+            at = pl.ds(step * group, group)
+            return pltpu.make_async_copy(amp.at[at], held.at[self.slot], amp_sem.at[self.slot])
+
+        def start(self):
+            for n, amp in enumerate(amps):
+
+                @pl.when(self.step // each == n)
+                def _():
+                    self.copy(amp, self.step - n * each).start()
+
+        def wait(self):
+            self.copy(amps[0], 0).wait()
 
     copies = []
     for n, (o, low, high) in enumerate(units):
@@ -243,7 +252,8 @@
                 )
     for copy in copies:
         copy.start()
-    total[...] = jnp.zeros_like(total)
+    for ahead in range(min(SLOTS - 1, parts * steps)):
+        Fetch(jnp.int32(ahead), ahead).start()
     for copy in copies:
         copy.wait()
 
@@ -285,42 +295,47 @@
                 stack = [vectors[m * w + b * BLK + e, at] for e in range(BLK)]
                 left[b, span, m * p.k : (m + 1) * p.k] = woven(jnp.concatenate(stack, axis=0))
 
+    total[...] = jnp.zeros_like(total)
     slot_of = lax.broadcasted_iota(jnp.int32, (1, p.k), 1) % LANES // p.slot
 
-    for span in spans:
-        size = span.stop - span.start
-        for copy in fetches(span):
-            copy.start()
+    @pl.loop(0, parts)
+    def _(part):
+        part_rows = pl.ds(pl.multiple_of(part * rows, rows), rows)
 
         @pl.loop(0, p.gf)
         def _(gf):
-            block = blocks_ref[gf // BLK, 0]
+            first_block = blocks_ref[gf // BLK, 0]
             index = blocks_ref[gf // BLK, 1] * BLK + gf % BLK
             only = (slot_of == index % p.per_row).astype(jnp.float32).astype(jnp.bfloat16)
-            rhs = [vectors[m * w + index, span] for m in range(p.nm)]
-            rhs.append(vectors[p.nm * w + index // p.per_row, span] * only)
-            tile = lax.dot_general(
-                left[block], jnp.concatenate(rhs, axis=1), NT, preferred_element_type=jnp.float32
-            )
-            tiles[:, gf, :, :size] = tile.astype(jnp.bfloat16).reshape(quads, ROWS, size)
-
-        for copy in fetches(span):
-            copy.wait()
+            lhs = left[first_block, part_rows]
+            for low in range(0, p.d, 256):
+                span = slice(low, min(low + 256, p.d))
+                rhs = [vectors[m * w + index, span] for m in range(p.nm)]
+                rhs.append(vectors[p.nm * w + index // p.per_row, span] * only)
+                rhs = jnp.concatenate(rhs, axis=1)
+                block = lax.dot_general(lhs, rhs, NT, preferred_element_type=jnp.float32)
+                block = block.astype(jnp.bfloat16).reshape(here, ROWS, span.stop - low)
+                tiles[:, gf, :, span] = block
 
         @pl.loop(0, steps)
         def _(step):
-            lhs = [
-                tiles[step * group + n, :, :, :size].reshape(p.gf * ROWS, size)
-                for n in range(group)
-            ]
-            rhs = [held[step * group + n, :size] for n in range(group)]
-            total[...] += lax.dot_general(
-                jnp.concatenate(lhs, axis=1),
-                jnp.concatenate(rhs, axis=0),
-                NN,
-                preferred_element_type=jnp.float32,
-            )
-
+            at = part * steps + step
+            slot = lax.rem(at, SLOTS)
+
+            @pl.when(at + SLOTS - 1 < parts * steps)
+            def _():
+                Fetch(at + SLOTS - 1, lax.rem(at + SLOTS - 1, SLOTS)).start()
+
+            Fetch(at, slot).wait()
+            for n in range(group):
+                total[...] += lax.dot_general(
+                    tiles[step * group + n].reshape(p.gf * ROWS, p.d),
+                    held[slot, n],
+                    NN,
+                    preferred_element_type=jnp.float32,
+                )
+
+    width = QUAD * p.ij
     row = lax.broadcasted_iota(jnp.int32, (p.gf * ROWS, width), 0) % ROWS // BLK
     col = lax.broadcasted_iota(jnp.int32, (p.gf * ROWS, width), 1) // ROWS % QUAD
     kept = jnp.where(row == col, total[...], 0.0)
@@ -331,11 +346,11 @@
 
 
 def ladder(p, units, place, blocks, pieces, amps):
+    parts, group = PARTS, 2
     quads = p.c // QUAD
-    group = 4 if quads % 4 == 0 else 2
     width = QUAD * p.ij
     return pl.pallas_call(
-        functools.partial(ladder_kernel, p, units, group),
+        functools.partial(ladder_kernel, p, units, parts, group),
         out_shape=jax.ShapeDtypeStruct((p.gf, BLK, width), jnp.float32),
         in_specs=[pl.BlockSpec(memory_space=pltpu.SMEM)] * 2
         + [pl.BlockSpec(memory_space=pl.ANY)] * (len(pieces) + AMPS),
@@ -344,16 +359,16 @@
             pltpu.VMEM((p.planes, p.d, p.k), jnp.bfloat16),
             pltpu.VMEM((p.blocks, BLK * p.c, (p.nm + 1) * p.k), jnp.bfloat16),
             pltpu.VMEM((BLK, p.c, p.k), jnp.bfloat16),
-            pltpu.VMEM((quads, p.gf, ROWS, DEEP), jnp.bfloat16),
-            pltpu.VMEM((quads, DEEP, width), jnp.bfloat16),
+            pltpu.VMEM((quads // parts, p.gf, ROWS, p.d), jnp.bfloat16),
+            pltpu.VMEM((SLOTS, group, p.d, width), jnp.bfloat16),
             pltpu.VMEM((p.gf * ROWS, width), jnp.float32),
             pltpu.SemaphoreType.DMA((len(pieces),)),
-            pltpu.SemaphoreType.DMA((AMPS,)),
+            pltpu.SemaphoreType.DMA((SLOTS,)),
         ],
         compiler_params=pltpu.CompilerParams(vmem_limit_bytes=60 * 2**20),
         cost_estimate=pl.CostEstimate(
             flops=2 * p.gf * BLK * p.c * p.d * p.k,
-            bytes_accessed=2 * (p.planes * p.d * p.k + p.c * p.ij * p.d),
+            bytes_accessed=2 * (p.js * p.n_aux * p.planes * p.cpad * LANES + p.c * p.ij * p.d),
             transcendentals=0,
         ),
         name="ladder",

time: 252 us -> 254 us (level)
  no operation moved by 1% of the time
where the time goes in v9:
time: 254 us; the launch traced here: 253 us
  Pallas kernels  145 us (57%)
  waiting for transfers between devices  59.6 us (23%)
  starting transfers between devices  22.5 us (9%)
  local copies, waits for them, and re-layouts  15.6 us (6%)
  blocking collectives  9.82 us (4%)
    pallas_call x1, Pallas kernels, ladder(): pl.pallas_call(functools.partial(ladder_kernel, p, units, parts, group),...  93.4 us
    ppermute x21, waiting for transfers between devices, permute(): return lax.ppermute(array, ('aux', 'pair'), pairs)  59.6 us
    pallas_call x4, Pallas kernels, dress(): pl.pallas_call(functools.partial(dress_kernel, p, offset, bounds), out_sh...  29.2 us
    ppermute x21, starting transfers between devices, permute(): return lax.ppermute(array, ('aux', 'pair'), pairs)  22.5 us
    pallas_call x2, Pallas kernels, relayout(): pl.pallas_call(functools.partial(relayout_kernel, p), out_shape=jax.Shape...  21.2 us
    unnamed x47, local copies, waits for them, and re-layouts  13.2 us
    all_to_all x1, blocking collectives, shards(): lax.all_to_all(terms, ('aux', 'pair'), split_axis=0, concat_axis=0, tiled...  9.82 us
  transfers between devices with their start and end apart: 21, of which 7 were waited for; matrix products, arithmetic and copies ran while one was open for 0% of the time, Pallas kernels for 14%

profile of v9, /device:TPU:0, one launch (start us, length us, event | category | flops | bytes accessed | tf_op | source)
XLA Modules:
  0.0 253.4 jit_solution(9614833490068563409)
XLA Ops:
  0.0 0.8 copy.11.t1_ref
  0.8 0.8 spread.1.a_ref
  1.6 0.1 pad_add_fusion.z_ref.place_ref
  1.7 7.4 %dress.4 = bf16[36,112,128]{2,1,0:T(8,128)(2,1)S(1)} custom-call(s32[3]{0:T(128)S(1)} %pad_add_fusion.z_ref.place_ref, bf16[512,1600]{1,0:T(8,128)(2,1)S(1)} %spread.1.a_ref, bf16[100,112,576]{2,1,0:T(8,128)(2,1)} %refs_1_.7, bf16[100,112,576]{2,1,0:T(8,128)(2,1)} %refs_1_.7, bf16[32,112,576]{2,1,0:T(8,128)(2,1)} %refs_3_.7, bf16[32,112,576]{2,1,0:T(8,128)(2,1)} %refs_3_.7), custom_call_target="tpu_custom_call" | custom-call | flops 2936012800 | bytes 9404416 | tf_op jit(solution)/shard_map/dress/pallas_call | solution.py:135
  9.1 7.3 %dress.5 = bf16[36,112,128]{2,1,0:T(8,128)(2,1)S(1)} custom-call(s32[3]{0:T(128)S(1)} %pad_add_fusion.z_ref.place_ref, bf16[512,1600]{1,0:T(8,128)(2,1)S(1)} %spread.1.a_ref, bf16[100,112,576]{2,1,0:T(8,128)(2,1)} %refs_1_.7, bf16[100,112,576]{2,1,0:T(8,128)(2,1)} %refs_1_.7, bf16[32,112,576]{2,1,0:T(8,128)(2,1)} %refs_3_.7, bf16[32,112,576]{2,1,0:T(8,128)(2,1)} %refs_3_.7), custom_call_target="tpu_custom_call" | custom-call | flops 2936012800 | bytes 9404416 | tf_op jit(solution)/shard_map/dress/pallas_call | solution.py:135
  16.4 3.0 %collective-permute-start.1 = (bf16[36,112,128]{2,1,0:T(8,128)(2,1)S(1)}, bf16[36,112,128]{2,1,0:T(8,128)(2,1)S(1)}, u32[]{:S(2)}, u32[]{:S(2)}) collective-permute-start(bf16[36,112,128]{2,1,0:T(8,128)(2,1)S(1)} %dress.5), channel_id=1, source_target_pairs={{0,2},{1,10},{2,4},{3,12},{4,6},{5,14},{6,0},{7,8},{8,3},{9,11},{1... | collective-permute-start | bytes 3096584 | tf_op jit(solution)/shard_map/ppermute | solution.py:407
  19.4 0.7 collective-permute-start
  20.1 1.6 collective-permute-start.2
  21.6 7.3 %dress.6 = bf16[36,112,128]{2,1,0:T(8,128)(2,1)S(1)} custom-call(s32[3]{0:T(128)S(1)} %pad_add_fusion.z_ref.place_ref, bf16[512,1600]{1,0:T(8,128)(2,1)S(1)} %spread.1.a_ref, bf16[100,112,576]{2,1,0:T(8,128)(2,1)} %refs_1_.7, bf16[100,112,576]{2,1,0:T(8,128)(2,1)} %refs_1_.7, bf16[32,112,576]{2,1,0:T(8,128)(2,1)} %refs_3_.7, bf16[32,112,576]{2,1,0:T(8,128)(2,1)} %refs_3_.7), custom_call_target="tpu_custom_call" | custom-call | flops 2936012800 | bytes 9404416 | tf_op jit(solution)/shard_map/dress/pallas_call | solution.py:135
  28.9 15.7 %collective-permute-done.1.refs_4_ = bf16[36,112,128]{2,1,0:T(8,128)(2,1)S(1)} collective-permute-done((bf16[36,112,128]{2,1,0:T(8,128)(2,1)S(1)}, bf16[36,112,128]{2,1,0:T(8,128)(2,1)S(1)}, u32[]{:S(2)}, u32[]{:S(2)}) %collective-permute-start.1) | collective-permute-done | bytes 1032224 | tf_op jit(solution)/shard_map/ppermute | solution.py:407
  44.6 2.3 collective-permute-start.3
  46.9 1.5 collective-permute-start.4
  48.4 1.6 collective-permute-start.5
  50.1 3.3 %collective-permute-start.6 = (bf16[36,112,128]{2,1,0:T(8,128)(2,1)S(1)}, bf16[36,112,128]{2,1,0:T(8,128)(2,1)S(1)}, u32[]{:S(2)}, u32[]{:S(2)}) collective-permute-start(bf16[36,112,128]{2,1,0:T(8,128)(2,1)S(1)} %collective-permute-done.refs_0_), channel_id=1, source_target_pairs={{0,8},{1,9},{2,10},{3,11},{4,12},{5,13},{6,14},{7,15},{8,0},{9,1},... | collective-permute-start | bytes 3096584 | tf_op jit(solution)/shard_map/ppermute | solution.py:407
  53.4 0.1 collective-permute-start.7
  53.4 7.3 %dress.7 = (bf16[18,112,128]{2,1,0:T(8,128)(2,1)S(1)}, bf16[18,112,128]{2,1,0:T(8,128)(2,1)S(1)}) custom-call(s32[3]{0:T(128)S(1)} %pad_add_fusion.z_ref.place_ref, bf16[512,1600]{1,0:T(8,128)(2,1)S(1)} %spread.1.a_ref, bf16[100,112,576]{2,1,0:T(8,128)(2,1)} %refs_1_.7, bf16[100,112,576]{2,1,0:T(8,128)(2,1)} %refs_1_.7, bf16[32,112,576]{2,1,0:T(8,128)(2,1)} %refs_3_.7, ...), custom_call_target="tpu_custom_call" | custom-call | flops 2936012800 | bytes 9404416 | tf_op jit(solution)/shard_map/dress/pallas_call | solution.py:135
  60.7 8.3 %collective-permute-done.3.refs_8_ = bf16[36,112,128]{2,1,0:T(8,128)(2,1)} collective-permute-done((bf16[36,112,128]{2,1,0:T(8,128)(2,1)S(1)}, bf16[36,112,128]{2,1,0:T(8,128)(2,1)}, u32[]{:S(2)}, u32[]{:S(2)}) %collective-permute-start.3) | collective-permute-done | bytes 1032224 | tf_op jit(solution)/shard_map/ppermute | solution.py:407
  69.0 2.6 %collective-permute-done.4.refs_6_ = bf16[36,112,128]{2,1,0:T(8,128)(2,1)} collective-permute-done((bf16[36,112,128]{2,1,0:T(8,128)(2,1)S(1)}, bf16[36,112,128]{2,1,0:T(8,128)(2,1)}, u32[]{:S(2)}, u32[]{:S(2)}) %collective-permute-start.4) | collective-permute-done | bytes 1032224 | tf_op jit(solution)/shard_map/ppermute | solution.py:407
  71.6 1.6 collective-permute-start.10
  73.2 2.7 %collective-permute-start.11 = (bf16[36,112,128]{2,1,0:T(8,128)(2,1)}, bf16[36,112,128]{2,1,0:T(8,128)(2,1)S(1)}, u32[]{:S(2)}, u32[]{:S(2)}) collective-permute-start(bf16[36,112,128]{2,1,0:T(8,128)(2,1)} %collective-permute-done.3.refs_8_), channel_id=1, source_target_pairs={{0,8},{1,9},{2,10},{3,11},{4,12},{5,13},{6,14},{7,15},{8,0},{9,1},... | collective-permute-start | bytes 3096584 | tf_op jit(solution)/shard_map/ppermute | solution.py:407
  75.9 0.5 collective-permute-start.13
  76.4 0.8 collective-permute-start.9
  77.2 10.5 %relayout.2.refs_20_ = bf16[28,896,256]{2,1,0:T(8,128)(2,1)S(1)} custom-call(bf16[64,224,896]{2,1,0:T(8,128)(2,1)} %in_ref.1), custom_call_target="tpu_custom_call" | custom-call | flops 3288334336 | bytes 25690112 | tf_op jit(solution)/shard_map/relayout/pallas_call | solution.py:190
  87.7 4.6 %copy-done = bf16[28,896,256]{2,1,0:T(8,128)(2,1)} copy-done((bf16[28,896,256]{2,1,0:T(8,128)(2,1)}, bf16[28,896,256]{2,1,0:T(8,128)(2,1)S(1)}, u32[]{:S(2)}) %copy-start) | copy-done | bytes 12845080
  92.4 10.3 %collective-permute-done.9.refs_12_ = bf16[18,112,128]{2,1,0:T(8,128)(2,1)S(1)} collective-permute-done((bf16[18,112,128]{2,1,0:T(8,128)(2,1)S(1)}, bf16[18,112,128]{2,1,0:T(8,128)(2,1)S(1)}, u32[]{:S(2)}, u32[]{:S(2)}) %collective-permute-start.9) | collective-permute-done | bytes 516128 | tf_op jit(solution)/shard_map/ppermute | solution.py:407
  102.7 0.2 collective-permute-start.16
  102.9 1.1 collective-permute-start.14
  104.0 10.7 %relayout.3.refs_21_ = bf16[28,896,256]{2,1,0:T(8,128)(2,1)S(1)} custom-call(bf16[64,224,896]{2,1,0:T(8,128)(2,1)} %in_ref.1), custom_call_target="tpu_custom_call" | custom-call | flops 3288334336 | bytes 25690112 | tf_op jit(solution)/shard_map/relayout/pallas_call | solution.py:190
  114.8 4.6 %copy-done.1 = bf16[28,896,256]{2,1,0:T(8,128)(2,1)} copy-done((bf16[28,896,256]{2,1,0:T(8,128)(2,1)}, bf16[28,896,256]{2,1,0:T(8,128)(2,1)S(1)}, u32[]{:S(2)}) %copy-start.1) | copy-done | bytes 12845080
  119.4 8.8 %collective-permute-done.8.refs_16_ = bf16[18,112,128]{2,1,0:T(8,128)(2,1)S(1)} collective-permute-done((bf16[18,112,128]{2,1,0:T(8,128)(2,1)S(1)}, bf16[18,112,128]{2,1,0:T(8,128)(2,1)S(1)}, u32[]{:S(2)}, u32[]{:S(2)}) %collective-permute-start.8) | collective-permute-done | bytes 516128 | tf_op jit(solution)/shard_map/ppermute | solution.py:407
  128.3 1.0 copy-done.12
  129.3 1.0 collective-permute-start.17
  130.3 0.5 collective-permute-start.18
  130.8 12.9 %collective-permute-done.17.refs_18_ = bf16[18,112,128]{2,1,0:T(8,128)(2,1)S(1)} collective-permute-done((bf16[18,112,128]{2,1,0:T(8,128)(2,1)S(1)}, bf16[18,112,128]{2,1,0:T(8,128)(2,1)S(1)}, u32[]{:S(2)}, u32[]{:S(2)}) %collective-permute-start.17) | collective-permute-done | bytes 516128 | tf_op jit(solution)/shard_map/ppermute | solution.py:407
  143.8 0.1 collective-permute-start.20
  143.9 0.9 copy.12.blocks_ref
  144.7 1.0 collective-permute-done.20.refs_19_
  145.8 0.8 copy-done.20
  146.5 93.4 %ladder.1 = f32[32,4,256]{2,1,0:T(4,128)} custom-call(s32[3]{0:T(128)} %copy-done.2, s32[8,2]{1,0:T(8,128)} %copy.12.blocks_ref, bf16[36,112,128]{2,1,0:T(8,128)(2,1)} %copy-done.5, bf16[36,112,128]{2,1,0:T(8,128)(2,1)} %copy-done.6, bf16[36,112,128]{2,1,0:T(8,128)(2,1)} %collective-permute-done.5.refs_2_, bf16[36,112,128]{2,1,0:T(8,128)(2,1)} %copy-done.11, ...), custom_call_target="tpu_custom_call" | custom-call | flops 13153337344 | bytes 42205184 | tf_op jit(solution)/shard_map/ladder/pallas_call | solution.py:352
  239.9 1.1 reshape.6
  241.0 0.2 copy.18
  241.2 0.2 copy.20
  241.3 0.1 reshape.8
  241.5 9.8 %all_to_all.5 = f32[32,1,256]{2,1,0:T(1,128)S(1)} all-to-all(f32[32,1,256]{2,1,0:T(1,128)S(1)} %reshape.8), channel_id=1, replica_groups=mesh['aux'=4,'pair'=8] {'aux','pair'}, dimensions={0} | all-to-all | bytes 65536 | tf_op jit(solution)/shard_map/all_to_all | solution.py:494
  251.3 0.5 broadcast.2
  251.8 0.7 reduce
  252.5 0.1 reshape.9
  252.7 0.7 copy.16
  (57 shorter events, 0.2 us)
Async XLA Ops:
  1.7 51.7 %copy-start.2 = (s32[3]{0:T(128)}, s32[3]{0:T(128)S(1)}, u32[]{:S(2)}) copy-start(s32[3]{0:T(128)S(1)} %pad_add_fusion.z_ref.place_ref) | copy-start | bytes 40
  16.4 28.2 %collective-permute-start.1 = (bf16[36,112,128]{2,1,0:T(8,128)(2,1)S(1)}, bf16[36,112,128]{2,1,0:T(8,128)(2,1)S(1)}, u32[]{:S(2)}, u32[]{:S(2)}) collective-permute-start(bf16[36,112,128]{2,1,0:T(8,128)(2,1)S(1)} %dress.5), channel_id=1, source_target_pairs={{0,2},{1,10},{2,4},{3,12},{4,6},{5,14},{6,0},{7,8},{8,3},{9,11},{1... | collective-permute-start | bytes 3096584 | tf_op jit(solution)/shard_map/ppermute | solution.py:407
  19.4 25.3 %collective-permute-start = (bf16[36,112,128]{2,1,0:T(8,128)(2,1)S(1)}, bf16[36,112,128]{2,1,0:T(8,128)(2,1)S(1)}, u32[]{:S(2)}, u32[]{:S(2)}) collective-permute-start(bf16[36,112,128]{2,1,0:T(8,128)(2,1)S(1)} %dress.4), channel_id=1, source_target_pairs={{0,0},{1,8},{2,2},{3,10},{4,4},{5,12},{6,6},{7,14},{8,1},{9,9},{10... | collective-permute-start | bytes 3096584 | tf_op jit(solution)/shard_map/ppermute | solution.py:407
  20.1 24.6 %collective-permute-start.2 = (bf16[36,112,128]{2,1,0:T(8,128)(2,1)S(1)}, bf16[36,112,128]{2,1,0:T(8,128)(2,1)S(1)}, u32[]{:S(2)}, u32[]{:S(2)}) collective-permute-start(bf16[36,112,128]{2,1,0:T(8,128)(2,1)S(1)} %dress.4), channel_id=1, source_target_pairs={{0,16},{1,17},{2,18},{3,19},{4,20},{5,21},{6,22},{7,23},{8,24},{9,... | collective-permute-start | bytes 3096584 | tf_op jit(solution)/shard_map/ppermute | solution.py:407
  44.6 16.1 %copy-start.4 = (bf16[36,112,128]{2,1,0:T(8,128)(2,1)}, bf16[36,112,128]{2,1,0:T(8,128)(2,1)S(1)}, u32[]{:S(2)}) copy-start(bf16[36,112,128]{2,1,0:T(8,128)(2,1)S(1)} %collective-permute-done.1.refs_4_) | copy-start | bytes 3096580
  44.6 16.1 %copy-start.5 = (bf16[36,112,128]{2,1,0:T(8,128)(2,1)}, bf16[36,112,128]{2,1,0:T(8,128)(2,1)S(1)}, u32[]{:S(2)}) copy-start(bf16[36,112,128]{2,1,0:T(8,128)(2,1)S(1)} %collective-permute-done.refs_0_) | copy-start | bytes 3096580
  44.6 24.4 %collective-permute-start.3 = (bf16[36,112,128]{2,1,0:T(8,128)(2,1)S(1)}, bf16[36,112,128]{2,1,0:T(8,128)(2,1)}, u32[]{:S(2)}, u32[]{:S(2)}) collective-permute-start(bf16[36,112,128]{2,1,0:T(8,128)(2,1)S(1)} %dress.6), channel_id=1, source_target_pairs={{0,6},{1,14},{2,0},{3,8},{4,2},{5,10},{6,4},{7,12},{8,7},{9,15},{1... | collective-permute-start | bytes 3096584 | tf_op jit(solution)/shard_map/ppermute | solution.py:407
  46.9 24.6 %collective-permute-start.4 = (bf16[36,112,128]{2,1,0:T(8,128)(2,1)S(1)}, bf16[36,112,128]{2,1,0:T(8,128)(2,1)}, u32[]{:S(2)}, u32[]{:S(2)}) collective-permute-start(bf16[36,112,128]{2,1,0:T(8,128)(2,1)S(1)} %collective-permute-done.1.refs_4_), channel_id=1, source_target_pairs={{0,16},{1,17},{2,18},{3,19},{4,20},{5,21},{6,22},{7,23},{8,24},{9,... | collective-permute-start | bytes 3096584 | tf_op jit(solution)/shard_map/ppermute | solution.py:407
  48.4 23.2 %collective-permute-start.5 = (bf16[36,112,128]{2,1,0:T(8,128)(2,1)S(1)}, bf16[36,112,128]{2,1,0:T(8,128)(2,1)}, u32[]{:S(2)}, u32[]{:S(2)}) collective-permute-start(bf16[36,112,128]{2,1,0:T(8,128)(2,1)S(1)} %collective-permute-done.2), channel_id=1, source_target_pairs={{0,0},{1,8},{2,2},{3,10},{4,4},{5,12},{6,6},{7,14},{8,1},{9,9},{10... | collective-permute-start | bytes 3096584 | tf_op jit(solution)/shard_map/ppermute | solution.py:407
  50.1 21.6 %collective-permute-start.6 = (bf16[36,112,128]{2,1,0:T(8,128)(2,1)S(1)}, bf16[36,112,128]{2,1,0:T(8,128)(2,1)S(1)}, u32[]{:S(2)}, u32[]{:S(2)}) collective-permute-start(bf16[36,112,128]{2,1,0:T(8,128)(2,1)S(1)} %collective-permute-done.refs_0_), channel_id=1, source_target_pairs={{0,8},{1,9},{2,10},{3,11},{4,12},{5,13},{6,14},{7,15},{8,0},{9,1},... | collective-permute-start | bytes 3096584 | tf_op jit(solution)/shard_map/ppermute | solution.py:407
  53.4 18.3 %collective-permute-start.7 = (bf16[36,112,128]{2,1,0:T(8,128)(2,1)S(1)}, bf16[36,112,128]{2,1,0:T(8,128)(2,1)S(1)}, u32[]{:S(2)}, u32[]{:S(2)}) collective-permute-start(bf16[36,112,128]{2,1,0:T(8,128)(2,1)S(1)} %collective-permute-done.1.refs_4_), channel_id=1, source_target_pairs={{0,8},{1,9},{2,10},{3,11},{4,12},{5,13},{6,14},{7,15},{8,0},{9,1},... | collective-permute-start | bytes 3096584 | tf_op jit(solution)/shard_map/ppermute | solution.py:407
  71.6 4.8 %copy-start.6 = (bf16[36,112,128]{2,1,0:T(8,128)(2,1)}, bf16[36,112,128]{2,1,0:T(8,128)(2,1)S(1)}, u32[]{:S(2)}) copy-start(bf16[36,112,128]{2,1,0:T(8,128)(2,1)S(1)} %collective-permute-done.6.refs_1_) | copy-start | bytes 3096580
  71.6 4.8 %copy-start.7 = (bf16[36,112,128]{2,1,0:T(8,128)(2,1)}, bf16[36,112,128]{2,1,0:T(8,128)(2,1)S(1)}, u32[]{:S(2)}) copy-start(bf16[36,112,128]{2,1,0:T(8,128)(2,1)S(1)} %collective-permute-done.7.refs_5_) | copy-start | bytes 3096580
  71.6 31.0 %collective-permute-start.10 = (bf16[36,112,128]{2,1,0:T(8,128)(2,1)}, bf16[36,112,128]{2,1,0:T(8,128)(2,1)S(1)}, u32[]{:S(2)}, u32[]{:S(2)}) collective-permute-start(bf16[36,112,128]{2,1,0:T(8,128)(2,1)} %collective-permute-done.3.refs_8_), channel_id=1, source_target_pairs={{0,16},{1,17},{2,18},{3,19},{4,20},{5,21},{6,22},{7,23},{8,24},{9,... | collective-permute-start | bytes 3096584 | tf_op jit(solution)/shard_map/ppermute | solution.py:407
  73.2 29.4 %collective-permute-start.11 = (bf16[36,112,128]{2,1,0:T(8,128)(2,1)}, bf16[36,112,128]{2,1,0:T(8,128)(2,1)S(1)}, u32[]{:S(2)}, u32[]{:S(2)}) collective-permute-start(bf16[36,112,128]{2,1,0:T(8,128)(2,1)} %collective-permute-done.3.refs_8_), channel_id=1, source_target_pairs={{0,8},{1,9},{2,10},{3,11},{4,12},{5,13},{6,14},{7,15},{8,0},{9,1},... | collective-permute-start | bytes 3096584 | tf_op jit(solution)/shard_map/ppermute | solution.py:407
  75.9 26.7 %collective-permute-start.12 = (bf16[36,112,128]{2,1,0:T(8,128)(2,1)}, bf16[36,112,128]{2,1,0:T(8,128)(2,1)S(1)}, u32[]{:S(2)}, u32[]{:S(2)}) collective-permute-start(bf16[36,112,128]{2,1,0:T(8,128)(2,1)} %collective-permute-done.4.refs_6_), channel_id=1, source_target_pairs={{0,8},{1,9},{2,10},{3,11},{4,12},{5,13},{6,14},{7,15},{8,0},{9,1},... | collective-permute-start | bytes 3096584 | tf_op jit(solution)/shard_map/ppermute | solution.py:407
  75.9 26.7 %collective-permute-start.13 = (bf16[36,112,128]{2,1,0:T(8,128)(2,1)}, bf16[36,112,128]{2,1,0:T(8,128)(2,1)S(1)}, u32[]{:S(2)}, u32[]{:S(2)}) collective-permute-start(bf16[36,112,128]{2,1,0:T(8,128)(2,1)} %collective-permute-done.5.refs_2_), channel_id=1, source_target_pairs={{0,8},{1,9},{2,10},{3,11},{4,12},{5,13},{6,14},{7,15},{8,0},{9,1},... | collective-permute-start | bytes 3096584 | tf_op jit(solution)/shard_map/ppermute | solution.py:407
  76.4 26.2 %collective-permute-start.9 = (bf16[18,112,128]{2,1,0:T(8,128)(2,1)S(1)}, bf16[18,112,128]{2,1,0:T(8,128)(2,1)S(1)}, u32[]{:S(2)}, u32[]{:S(2)}) collective-permute-start(bf16[18,112,128]{2,1,0:T(8,128)(2,1)S(1)} %get-tuple-element.113), channel_id=1, source_target_pairs={{0,4},{1,12},{2,6},{3,14},{4,0},{5,8},{6,2},{7,10},{8,5},{9,13},{1... | collective-permute-start | bytes 1548296 | tf_op jit(solution)/shard_map/ppermute | solution.py:407
  87.7 4.6 %copy-start = (bf16[28,896,256]{2,1,0:T(8,128)(2,1)}, bf16[28,896,256]{2,1,0:T(8,128)(2,1)S(1)}, u32[]{:S(2)}) copy-start(bf16[28,896,256]{2,1,0:T(8,128)(2,1)S(1)} %relayout.2.refs_20_) | copy-start | bytes 38535172
  92.4 51.5 %copy-start.3 = (s32[8,2]{0,1:T(2,128)S(1)}, s32[8,2]{0,1:T(2,128)}, u32[]{:S(2)}) copy-start(s32[8,2]{0,1:T(2,128)} %param.9) | copy-start | bytes 196
  102.6 12.1 %copy-start.13 = (bf16[18,112,128]{2,1,0:T(8,128)(2,1)}, bf16[18,112,128]{2,1,0:T(8,128)(2,1)S(1)}, u32[]{:S(2)}) copy-start(bf16[18,112,128]{2,1,0:T(8,128)(2,1)S(1)} %collective-permute-done.9.refs_12_) | copy-start | bytes 1548292
  102.6 12.1 %copy-start.8 = (bf16[36,112,128]{2,1,0:T(8,128)(2,1)}, bf16[36,112,128]{2,1,0:T(8,128)(2,1)S(1)}, u32[]{:S(2)}) copy-start(bf16[36,112,128]{2,1,0:T(8,128)(2,1)S(1)} %collective-permute-done.10.refs_10_) | copy-start | bytes 3096580
  102.6 12.1 %copy-start.9 = (bf16[36,112,128]{2,1,0:T(8,128)(2,1)}, bf16[36,112,128]{2,1,0:T(8,128)(2,1)S(1)}, u32[]{:S(2)}) copy-start(bf16[36,112,128]{2,1,0:T(8,128)(2,1)S(1)} %collective-permute-done.11.refs_9_) | copy-start | bytes 3096580
  102.7 12.1 %copy-start.10 = (bf16[36,112,128]{2,1,0:T(8,128)(2,1)}, bf16[36,112,128]{2,1,0:T(8,128)(2,1)S(1)}, u32[]{:S(2)}) copy-start(bf16[36,112,128]{2,1,0:T(8,128)(2,1)S(1)} %collective-permute-done.12.refs_7_) | copy-start | bytes 3096580
  102.7 12.1 %copy-start.11 = (bf16[36,112,128]{2,1,0:T(8,128)(2,1)}, bf16[36,112,128]{2,1,0:T(8,128)(2,1)S(1)}, u32[]{:S(2)}) copy-start(bf16[36,112,128]{2,1,0:T(8,128)(2,1)S(1)} %collective-permute-done.13.refs_3_) | copy-start | bytes 3096580
  102.7 25.6 %collective-permute-start.16 = (bf16[36,112,128]{2,1,0:T(8,128)(2,1)S(1)}, bf16[36,112,128]{2,1,0:T(8,128)(2,1)S(1)}, u32[]{:S(2)}, u32[]{:S(2)}) collective-permute-start(bf16[36,112,128]{2,1,0:T(8,128)(2,1)S(1)} %collective-permute-done.10.refs_10_), channel_id=1, source_target_pairs={{0,8},{1,9},{2,10},{3,11},{4,12},{5,13},{6,14},{7,15},{8,0},{9,1},... | collective-permute-start | bytes 3096584 | tf_op jit(solution)/shard_map/ppermute | solution.py:407
  102.9 25.3 %collective-permute-start.8 = (bf16[18,112,128]{2,1,0:T(8,128)(2,1)S(1)}, bf16[18,112,128]{2,1,0:T(8,128)(2,1)S(1)}, u32[]{:S(2)}, u32[]{:S(2)}) collective-permute-start(bf16[18,112,128]{2,1,0:T(8,128)(2,1)S(1)} %get-tuple-element.112), channel_id=1, source_target_pairs={{0,4},{1,12},{2,6},{3,14},{4,0},{5,8},{6,2},{7,10},{8,5},{9,13},{1... | collective-permute-start | bytes 1548296 | tf_op jit(solution)/shard_map/ppermute | solution.py:407
  102.9 25.4 %collective-permute-start.14 = (bf16[18,112,128]{2,1,0:T(8,128)(2,1)S(1)}, bf16[18,112,128]{2,1,0:T(8,128)(2,1)S(1)}, u32[]{:S(2)}, u32[]{:S(2)}) collective-permute-start(bf16[18,112,128]{2,1,0:T(8,128)(2,1)S(1)} %collective-permute-done.9.refs_12_), channel_id=1, source_target_pairs={{0,16},{1,17},{2,18},{3,19},{4,20},{5,21},{6,22},{7,23},{8,24},{9,... | collective-permute-start | bytes 1548296 | tf_op jit(solution)/shard_map/ppermute | solution.py:407
  103.9 24.3 %collective-permute-start.15 = (bf16[18,112,128]{2,1,0:T(8,128)(2,1)S(1)}, bf16[18,112,128]{2,1,0:T(8,128)(2,1)S(1)}, u32[]{:S(2)}, u32[]{:S(2)}) collective-permute-start(bf16[18,112,128]{2,1,0:T(8,128)(2,1)S(1)} %collective-permute-done.9.refs_12_), channel_id=1, source_target_pairs={{0,8},{1,9},{2,10},{3,11},{4,12},{5,13},{6,14},{7,15},{8,0},{9,1},... | collective-permute-start | bytes 1548296 | tf_op jit(solution)/shard_map/ppermute | solution.py:407
  114.8 4.6 %copy-start.1 = (bf16[28,896,256]{2,1,0:T(8,128)(2,1)}, bf16[28,896,256]{2,1,0:T(8,128)(2,1)S(1)}, u32[]{:S(2)}) copy-start(bf16[28,896,256]{2,1,0:T(8,128)(2,1)S(1)} %relayout.3.refs_21_) | copy-start | bytes 38535172
  128.2 17.5 %copy-start.14 = (bf16[18,112,128]{2,1,0:T(8,128)(2,1)}, bf16[18,112,128]{2,1,0:T(8,128)(2,1)S(1)}, u32[]{:S(2)}) copy-start(bf16[18,112,128]{2,1,0:T(8,128)(2,1)S(1)} %collective-permute-done.8.refs_16_) | copy-start | bytes 1548292
  128.2 15.5 %copy-start.15 = (bf16[18,112,128]{2,1,0:T(8,128)(2,1)}, bf16[18,112,128]{2,1,0:T(8,128)(2,1)S(1)}, u32[]{:S(2)}) copy-start(bf16[18,112,128]{2,1,0:T(8,128)(2,1)S(1)} %collective-permute-done.14.refs_14_) | copy-start | bytes 1548292
  128.2 15.5 %copy-start.16 = (bf16[18,112,128]{2,1,0:T(8,128)(2,1)}, bf16[18,112,128]{2,1,0:T(8,128)(2,1)S(1)}, u32[]{:S(2)}) copy-start(bf16[18,112,128]{2,1,0:T(8,128)(2,1)S(1)} %collective-permute-done.15.refs_13_) | copy-start | bytes 1548292
  128.3 1.0 copy-start.12
  129.3 14.4 %collective-permute-start.17 = (bf16[18,112,128]{2,1,0:T(8,128)(2,1)S(1)}, bf16[18,112,128]{2,1,0:T(8,128)(2,1)S(1)}, u32[]{:S(2)}, u32[]{:S(2)}) collective-permute-start(bf16[18,112,128]{2,1,0:T(8,128)(2,1)S(1)} %collective-permute-done.8.refs_16_), channel_id=1, source_target_pairs={{0,16},{1,17},{2,18},{3,19},{4,20},{5,21},{6,22},{7,23},{8,24},{9,... | collective-permute-start | bytes 1548296 | tf_op jit(solution)/shard_map/ppermute | solution.py:407
  130.3 13.4 %collective-permute-start.18 = (bf16[18,112,128]{2,1,0:T(8,128)(2,1)S(1)}, bf16[18,112,128]{2,1,0:T(8,128)(2,1)S(1)}, u32[]{:S(2)}, u32[]{:S(2)}) collective-permute-start(bf16[18,112,128]{2,1,0:T(8,128)(2,1)S(1)} %collective-permute-done.8.refs_16_), channel_id=1, source_target_pairs={{0,8},{1,9},{2,10},{3,11},{4,12},{5,13},{6,14},{7,15},{8,0},{9,1},... | collective-permute-start | bytes 1548296 | tf_op jit(solution)/shard_map/ppermute | solution.py:407
  130.8 12.9 %collective-permute-start.19 = (bf16[18,112,128]{2,1,0:T(8,128)(2,1)S(1)}, bf16[18,112,128]{2,1,0:T(8,128)(2,1)S(1)}, u32[]{:S(2)}, u32[]{:S(2)}) collective-permute-start(bf16[18,112,128]{2,1,0:T(8,128)(2,1)S(1)} %collective-permute-done.14.refs_14_), channel_id=1, source_target_pairs={{0,8},{1,9},{2,10},{3,11},{4,12},{5,13},{6,14},{7,15},{8,0},{9,1},... | collective-permute-start | bytes 1548296 | tf_op jit(solution)/shard_map/ppermute | solution.py:407
  143.7 2.0 copy-start.17
  143.7 2.0 copy-start.18
  143.8 2.0 copy-start.19
  143.8 2.0 collective-permute-start.20
  145.7 0.8 copy-start.20

commit v10 on v8

--- a/solution.py
+++ b/solution.py
@@ -158,40 +158,25 @@
 
 
 def relayout_kernel(p, in_ref, out_ref):
-    rows, half = ROWS * ROWS, LANES // 2
-    to = lax.broadcasted_iota(jnp.int32, (rows, rows), 1)
-    frm = lax.broadcasted_iota(jnp.int32, (rows, rows), 0)
+    rows = ROWS * ROWS
+    to = lax.broadcasted_iota(jnp.int32, (rows, rows), 0)
+    frm = lax.broadcasted_iota(jnp.int32, (rows, rows), 1)
     turn = (to % ROWS * ROWS + to // ROWS == frm).astype(jnp.float32).astype(jnp.bfloat16)
-    lane = lax.broadcasted_iota(jnp.int32, (p.d, LANES), 1)
-    for pair in range(p.ij // ROWS // 2):
-        one, two = [
-            lax.dot_general(
-                in_ref[low : low + ROWS].reshape(rows, p.d),
-                turn,
-                (((0,), (0,)), ((), ())),
-                preferred_element_type=jnp.float32,
-            )
-            for low in (2 * pair * ROWS, (2 * pair + 1) * ROWS)
-        ]
-        at = slice(pair * LANES, (pair + 1) * LANES)
-        for tile in range(rows // LANES):
-            span = slice(tile * LANES, (tile + 1) * LANES)
-            even = jnp.where(lane < half, one[:, span], pltpu.roll(two[:, span], half, 1))
-            odd = jnp.where(lane < half, pltpu.roll(one[:, span], half, 1), two[:, span])
-            out_ref[2 * tile, :, at] = even.astype(jnp.bfloat16)
-            out_ref[2 * tile + 1, :, at] = odd.astype(jnp.bfloat16)
+    for low in range(0, p.ij, ROWS):
+        block = in_ref[low : low + ROWS].reshape(rows, p.d)
+        turned = lax.dot_general(turn, block, NN, preferred_element_type=jnp.float32)
+        out_ref[:, low : low + ROWS] = turned.astype(jnp.bfloat16).reshape(ROWS, ROWS, p.d)
 
 
 def relayout(p, amplitudes, part):
     count = p.c // AMPS
     blocks = count // ROWS
-    width = QUAD * p.ij
     return pl.pallas_call(
         functools.partial(relayout_kernel, p),
-        out_shape=jax.ShapeDtypeStruct((count // QUAD, p.d, width), jnp.bfloat16),
+        out_shape=jax.ShapeDtypeStruct((count, p.ij, p.d), jnp.bfloat16),
         grid=(blocks,),
         in_specs=[pl.BlockSpec((p.ij, ROWS, p.d), lambda c: (0, part * blocks + c, 0))],
-        out_specs=pl.BlockSpec((ROWS // QUAD, p.d, width), lambda c: (c, 0, 0)),
+        out_specs=pl.BlockSpec((ROWS, p.ij, p.d), lambda c: (c, 0, 0)),
         compiler_params=pltpu.CompilerParams(vmem_limit_bytes=40 * 2**20),
         cost_estimate=pl.CostEstimate(
             flops=2 * count * p.ij * p.d * ROWS * ROWS,
@@ -214,11 +199,11 @@
     spans = [slice(low, min(low + DEEP, p.d)) for low in range(0, p.d, DEEP)]
 
     def fetches(span):
-        each = quads // AMPS
+        rows = p.c * p.ij // AMPS
         return [
             pltpu.make_async_copy(
                 amp.at[:, span],
-                held.at[n * each : (n + 1) * each, : span.stop - span.start],
+                held.at[n * rows : (n + 1) * rows, : span.stop - span.start],
                 amp_sem.at[n],
             )
             for n, amp in enumerate(amps)
@@ -313,21 +298,27 @@
                 tiles[step * group + n, :, :, :size].reshape(p.gf * ROWS, size)
                 for n in range(group)
             ]
-            rhs = [held[step * group + n, :size] for n in range(group)]
+            low = pl.multiple_of(step * group * width, width)
+            rhs = [held[pl.ds(low + n * width, width), :size] for n in range(group)]
             total[...] += lax.dot_general(
                 jnp.concatenate(lhs, axis=1),
-                jnp.concatenate(rhs, axis=0),
-                NN,
+                jnp.concatenate(rhs, axis=1),
+                NT,
                 preferred_element_type=jnp.float32,
             )
 
     row = lax.broadcasted_iota(jnp.int32, (p.gf * ROWS, width), 0) % ROWS // BLK
-    col = lax.broadcasted_iota(jnp.int32, (p.gf * ROWS, width), 1) // ROWS % QUAD
+    col = lax.broadcasted_iota(jnp.int32, (p.gf * ROWS, width), 1) // p.ij
     kept = jnp.where(row == col, total[...], 0.0)
-    kept += pltpu.roll(kept, width - ROWS, 1)
-    kept += pltpu.roll(kept, width - 2 * ROWS, 1)
-    kept = kept.reshape(p.gf, 2, 8, width).sum(axis=1)
-    out[...] = kept[:, :4] + kept[:, 4:]
+    folded = kept[:, :LANES]
+    for low in range(LANES, width, LANES):
+        folded += kept[:, low : low + LANES]
+    shift = LANES
+    while shift > p.ij:
+        shift //= 2
+        folded += pltpu.roll(folded, shift, 1)
+    folded = folded.reshape(p.gf, 2, 8, LANES).sum(axis=1)
+    out[...] = folded[:, :4] + folded[:, 4:]
 
 
 def ladder(p, units, place, blocks, pieces, amps):
@@ -336,7 +327,7 @@
     width = QUAD * p.ij
     return pl.pallas_call(
         functools.partial(ladder_kernel, p, units, group),
-        out_shape=jax.ShapeDtypeStruct((p.gf, BLK, width), jnp.float32),
+        out_shape=jax.ShapeDtypeStruct((p.gf, BLK, LANES), jnp.float32),
         in_specs=[pl.BlockSpec(memory_space=pltpu.SMEM)] * 2
         + [pl.BlockSpec(memory_space=pl.ANY)] * (len(pieces) + AMPS),
         out_specs=pl.BlockSpec(memory_space=pltpu.VMEM),
@@ -345,7 +336,7 @@
             pltpu.VMEM((p.blocks, BLK * p.c, (p.nm + 1) * p.k), jnp.bfloat16),
             pltpu.VMEM((BLK, p.c, p.k), jnp.bfloat16),
             pltpu.VMEM((quads, p.gf, ROWS, DEEP), jnp.bfloat16),
-            pltpu.VMEM((quads, DEEP, width), jnp.bfloat16),
+            pltpu.VMEM((p.c * p.ij, DEEP), jnp.bfloat16),
             pltpu.VMEM((p.gf * ROWS, width), jnp.float32),
             pltpu.SemaphoreType.DMA((len(pieces),)),
             pltpu.SemaphoreType.DMA((AMPS,)),
@@ -411,9 +402,6 @@
     order = sorted(range(p.js), key=lambda o: min(o, p.js - o))
     whole = (0, p.planes)
     bounds = {o: [whole] for o in order}
-    if p.js > 2:
-        half = p.planes // 2
-        bounds[order[-1]] = [(0, half), (half, p.planes)]
     units = [(o, *bound) for o in order for bound in bounds[o]]
     rounds = [units[:2]] + [[unit] for unit in units[2:]]
     swaps = [[], units[1:2]] + [[unit] for unit in units[2:]]
@@ -433,7 +421,9 @@
     share_next = []
     for n in range(len(swaps) + 1):
         new, made, laid, crossed = {}, {}, {}, {}
-        to_share, share_next = share_next, []
+        to_share = []
+        if n != len(rounds) - 1:
+            to_share, share_next = share_next, []
         if n < len(rounds):
             for unit in rounds[n]:
                 new[unit, 0, 0] = to_slice(messages[unit], unit[0])
@@ -449,15 +439,14 @@
             if n == 1:
                 new[units[0], r, 0] = to_slice(raw[r], 0)
                 share_next.append((units[0], r))
-        for unit, r in to_share:
-            new[unit, r, 1] = to_core(held[unit, r, 0])
         if n + 1 < len(rounds):
             for unit in rounds[n + 1]:
                 if unit not in messages:
                     made.update(make(unit[0], spread))
-        part = n - (len(rounds) - AMPS)
-        if 0 <= part < AMPS:
-            laid[part] = relayout(p, sources[part], part)
+        if n == len(rounds) - 1:
+            laid = {part: relayout(p, sources[part], part) for part in range(AMPS)}
+        for unit, r in to_share:
+            new[unit, r, 1] = to_core(held[unit, r, 0])
         moved = (list(new.values()), list(made.values()), list(laid.values()), crossed)
         kept = (list(held.values()), spread, sources)
         moved, (old, spread, sources) = lax.optimization_barrier((moved, kept))
@@ -467,14 +456,14 @@
         raw = moved[3]
         for part, amp in zip(laid, moved[2]):
             amps[part] = amp
+    amps = [amp.reshape(-1, p.d) for amp in amps]
     pieces = [
         held[unit, r, other] for unit in units for r in range(p.xs) for other in range(CORES)
     ]
 
     partial_terms = ladder(p, units, place, assignment, pieces, amps)
     share = p.ij // n_aux
-    terms = partial_terms.reshape(n_pair, BLK, BLK, p.ij // ROWS, QUAD * ROWS)[..., :ROWS]
-    terms = terms.reshape(n_pair, BLK, BLK, n_aux, share)
+    terms = partial_terms[:, :, : p.ij].reshape(n_pair, BLK, BLK, n_aux, share)
     terms = terms.transpose(3, 0, 4, 2, 1).reshape(n_aux * n_pair, share, BLK * BLK)
     terms = lax.all_to_all(terms, ("aux", "pair"), split_axis=0, concat_axis=0, tiled=True)
     return terms.sum(axis=0)

time: 252 us -> 257 us (1.020)
  waiting for transfers between devices: 59.6 us -> 66.1 us
  blocking collectives: 9.81 us -> 13.2 us
  starting transfers between devices: 22.5 us -> 19.9 us
    ppermute x21 -> x17, waiting for transfers between devices: 59.6 us -> 66.1 us  [permute(): return lax.ppermute(array, ('aux', 'pair'), pairs)]
    all_to_all x1, blocking collectives: 9.81 us -> 13.2 us  [shards(): lax.all_to_all(terms, ('aux', 'pair'), split_axis=0, concat_axis=0, tiled...]
    pallas_call x2, Pallas kernels: 21.2 us -> 18.1 us  [relayout(): pl.pallas_call(functools.partial(relayout_kernel, p), out_shape=jax.Shape...]
    ppermute x21 -> x17, starting transfers between devices: 22.5 us -> 19.9 us  [permute(): return lax.ppermute(array, ('aux', 'pair'), pairs)]
    unnamed x47 -> x42, local copies, waits for them, and re-layouts: 13.2 us -> 12 us
  transfers between devices with their start and end apart: 21 -> 17, of which waited for: 7 -> 7; matrix products, arithmetic and copies ran while one was open for 0% -> 0% of each run, Pallas kernels for 14% -> 13%
where the time goes in v10:
time: 257 us; the launch traced here: 256 us
  Pallas kernels  142 us (55%)
  waiting for transfers between devices  66.1 us (26%)
  starting transfers between devices  19.9 us (8%)
  local copies, waits for them, and re-layouts  14.5 us (6%)
  blocking collectives  13.2 us (5%)
    pallas_call x1, Pallas kernels, ladder(): pl.pallas_call(functools.partial(ladder_kernel, p, units, group), out_sha...  93.4 us
    ppermute x17, waiting for transfers between devices, permute(): return lax.ppermute(array, ('aux', 'pair'), pairs)  66.1 us
    pallas_call x4, Pallas kernels, dress(): pl.pallas_call(functools.partial(dress_kernel, p, offset, bounds), out_sh...  29.2 us
    ppermute x17, starting transfers between devices, permute(): return lax.ppermute(array, ('aux', 'pair'), pairs)  19.9 us
    pallas_call x2, Pallas kernels, relayout(): pl.pallas_call(functools.partial(relayout_kernel, p), out_shape=jax.Shape...  18.1 us
    all_to_all x1, blocking collectives, shards(): lax.all_to_all(terms, ('aux', 'pair'), split_axis=0, concat_axis=0, tiled...  13.2 us
    unnamed x42, local copies, waits for them, and re-layouts  12 us
  transfers between devices with their start and end apart: 17, of which 7 were waited for; matrix products, arithmetic and copies ran while one was open for 0% of the time, Pallas kernels for 13%

profile of v10, /device:TPU:0, one launch (start us, length us, event | category | flops | bytes accessed | tf_op | source)
XLA Modules:
  0.0 256.5 jit_solution(4784890970060817493)
XLA Ops:
  0.0 0.8 copy.11.t1_ref
  0.8 0.8 spread.1.a_ref
  1.6 0.1 pad_add_fusion.z_ref.place_ref
  1.7 7.4 %dress.4 = bf16[36,112,128]{2,1,0:T(8,128)(2,1)S(1)} custom-call(s32[3]{0:T(128)S(1)} %pad_add_fusion.z_ref.place_ref, bf16[512,1600]{1,0:T(8,128)(2,1)S(1)} %spread.1.a_ref, bf16[100,112,576]{2,1,0:T(8,128)(2,1)} %refs_1_.7, bf16[100,112,576]{2,1,0:T(8,128)(2,1)} %refs_1_.7, bf16[32,112,576]{2,1,0:T(8,128)(2,1)} %refs_3_.7, bf16[32,112,576]{2,1,0:T(8,128)(2,1)} %refs_3_.7), custom_call_target="tpu_custom_call" | custom-call | flops 2936012800 | bytes 9404416 | tf_op jit(solution)/shard_map/dress/pallas_call | solution.py:134
  9.1 7.3 %dress.5 = bf16[36,112,128]{2,1,0:T(8,128)(2,1)S(1)} custom-call(s32[3]{0:T(128)S(1)} %pad_add_fusion.z_ref.place_ref, bf16[512,1600]{1,0:T(8,128)(2,1)S(1)} %spread.1.a_ref, bf16[100,112,576]{2,1,0:T(8,128)(2,1)} %refs_1_.7, bf16[100,112,576]{2,1,0:T(8,128)(2,1)} %refs_1_.7, bf16[32,112,576]{2,1,0:T(8,128)(2,1)} %refs_3_.7, bf16[32,112,576]{2,1,0:T(8,128)(2,1)} %refs_3_.7), custom_call_target="tpu_custom_call" | custom-call | flops 2936012800 | bytes 9404416 | tf_op jit(solution)/shard_map/dress/pallas_call | solution.py:134
  16.4 3.0 %collective-permute-start.1 = (bf16[36,112,128]{2,1,0:T(8,128)(2,1)S(1)}, bf16[36,112,128]{2,1,0:T(8,128)(2,1)S(1)}, u32[]{:S(2)}, u32[]{:S(2)}) collective-permute-start(bf16[36,112,128]{2,1,0:T(8,128)(2,1)S(1)} %dress.5), channel_id=1, source_target_pairs={{0,2},{1,10},{2,4},{3,12},{4,6},{5,14},{6,0},{7,8},{8,3},{9,11},{1... | collective-permute-start | bytes 3096584 | tf_op jit(solution)/shard_map/ppermute | solution.py:383
  19.4 0.7 collective-permute-start
  20.1 1.6 collective-permute-start.2
  21.6 7.3 %dress.6 = bf16[36,112,128]{2,1,0:T(8,128)(2,1)S(1)} custom-call(s32[3]{0:T(128)S(1)} %pad_add_fusion.z_ref.place_ref, bf16[512,1600]{1,0:T(8,128)(2,1)S(1)} %spread.1.a_ref, bf16[100,112,576]{2,1,0:T(8,128)(2,1)} %refs_1_.7, bf16[100,112,576]{2,1,0:T(8,128)(2,1)} %refs_1_.7, bf16[32,112,576]{2,1,0:T(8,128)(2,1)} %refs_3_.7, bf16[32,112,576]{2,1,0:T(8,128)(2,1)} %refs_3_.7), custom_call_target="tpu_custom_call" | custom-call | flops 2936012800 | bytes 9404416 | tf_op jit(solution)/shard_map/dress/pallas_call | solution.py:134
  28.9 15.7 %collective-permute-done.1.refs_4_ = bf16[36,112,128]{2,1,0:T(8,128)(2,1)S(1)} collective-permute-done((bf16[36,112,128]{2,1,0:T(8,128)(2,1)S(1)}, bf16[36,112,128]{2,1,0:T(8,128)(2,1)S(1)}, u32[]{:S(2)}, u32[]{:S(2)}) %collective-permute-start.1) | collective-permute-done | bytes 1032224 | tf_op jit(solution)/shard_map/ppermute | solution.py:383
  44.6 0.0 collective-permute-done.refs_0_
  44.6 0.0 collective-permute-done.2
  44.6 2.3 collective-permute-start.3
  46.9 1.5 collective-permute-start.4
  48.4 0.9 collective-permute-start.5
  49.3 4.0 %collective-permute-start.6 = (bf16[36,112,128]{2,1,0:T(8,128)(2,1)S(1)}, bf16[36,112,128]{2,1,0:T(8,128)(2,1)S(1)}, u32[]{:S(2)}, u32[]{:S(2)}) collective-permute-start(bf16[36,112,128]{2,1,0:T(8,128)(2,1)S(1)} %collective-permute-done.refs_0_), channel_id=1, source_target_pairs={{0,8},{1,9},{2,10},{3,11},{4,12},{5,13},{6,14},{7,15},{8,0},{9,1},... | collective-permute-start | bytes 3096584 | tf_op jit(solution)/shard_map/ppermute | solution.py:383
  53.4 0.1 collective-permute-start.7
  53.4 7.3 %dress.7 = bf16[36,112,128]{2,1,0:T(8,128)(2,1)S(1)} custom-call(s32[3]{0:T(128)S(1)} %pad_add_fusion.z_ref.place_ref, bf16[512,1600]{1,0:T(8,128)(2,1)S(1)} %spread.1.a_ref, bf16[100,112,576]{2,1,0:T(8,128)(2,1)} %refs_1_.7, bf16[100,112,576]{2,1,0:T(8,128)(2,1)} %refs_1_.7, bf16[32,112,576]{2,1,0:T(8,128)(2,1)} %refs_3_.7, bf16[32,112,576]{2,1,0:T(8,128)(2,1)} %refs_3_.7), custom_call_target="tpu_custom_call" | custom-call | flops 2936012800 | bytes 9404416 | tf_op jit(solution)/shard_map/dress/pallas_call | solution.py:134
  60.7 8.2 %collective-permute-done.3.refs_8_ = bf16[36,112,128]{2,1,0:T(8,128)(2,1)S(1)} collective-permute-done((bf16[36,112,128]{2,1,0:T(8,128)(2,1)S(1)}, bf16[36,112,128]{2,1,0:T(8,128)(2,1)S(1)}, u32[]{:S(2)}, u32[]{:S(2)}) %collective-permute-start.3) | collective-permute-done | bytes 1032224 | tf_op jit(solution)/shard_map/ppermute | solution.py:383
  68.9 2.6 %collective-permute-done.4.refs_6_ = bf16[36,112,128]{2,1,0:T(8,128)(2,1)S(1)} collective-permute-done((bf16[36,112,128]{2,1,0:T(8,128)(2,1)S(1)}, bf16[36,112,128]{2,1,0:T(8,128)(2,1)S(1)}, u32[]{:S(2)}, u32[]{:S(2)}) %collective-permute-start.4) | collective-permute-done | bytes 1032224 | tf_op jit(solution)/shard_map/ppermute | solution.py:383
  71.5 0.0 collective-permute-done.5.refs_2_
  71.5 1.5 collective-permute-start.8
  73.1 1.5 collective-permute-start.9
  74.6 9.0 %relayout.2 = bf16[112,64,896]{2,1,0:T(8,128)(2,1)S(1)} custom-call(bf16[64,224,896]{2,1,0:T(8,128)(2,1)} %in_ref.1), custom_call_target="tpu_custom_call" | custom-call | flops 3288334336 | bytes 25690112 | tf_op jit(solution)/shard_map/relayout/pallas_call | solution.py:174
  83.6 4.6 %copy-done = bf16[112,64,896]{2,1,0:T(8,128)(2,1)} copy-done((bf16[112,64,896]{2,1,0:T(8,128)(2,1)}, bf16[112,64,896]{2,1,0:T(8,128)(2,1)S(1)}, u32[]{:S(2)}) %copy-start) | copy-done | bytes 12845080
  88.2 9.0 %relayout.3 = bf16[112,64,896]{2,1,0:T(8,128)(2,1)S(1)} custom-call(bf16[64,224,896]{2,1,0:T(8,128)(2,1)} %in_ref.1), custom_call_target="tpu_custom_call" | custom-call | flops 3288334336 | bytes 25690112 | tf_op jit(solution)/shard_map/relayout/pallas_call | solution.py:174
  97.3 4.6 %copy-done.1 = bf16[112,64,896]{2,1,0:T(8,128)(2,1)} copy-done((bf16[112,64,896]{2,1,0:T(8,128)(2,1)}, bf16[112,64,896]{2,1,0:T(8,128)(2,1)S(1)}, u32[]{:S(2)}) %copy-start.1) | copy-done | bytes 12845080
  101.9 17.9 %collective-permute-done.8.refs_12_ = bf16[36,112,128]{2,1,0:T(8,128)(2,1)S(1)} collective-permute-done((bf16[36,112,128]{2,1,0:T(8,128)(2,1)S(1)}, bf16[36,112,128]{2,1,0:T(8,128)(2,1)S(1)}, u32[]{:S(2)}, u32[]{:S(2)}) %collective-permute-start.8) | collective-permute-done | bytes 1032224 | tf_op jit(solution)/shard_map/ppermute | solution.py:383
  119.8 1.8 collective-permute-start.10
  121.6 0.5 collective-permute-start.11
  122.1 0.1 collective-permute-start.12
  122.2 0.4 collective-permute-start.13
  122.6 17.2 %collective-permute-done.10.refs_14_ = bf16[36,112,128]{2,1,0:T(8,128)(2,1)S(1)} collective-permute-done((bf16[36,112,128]{2,1,0:T(8,128)(2,1)S(1)}, bf16[36,112,128]{2,1,0:T(8,128)(2,1)S(1)}, u32[]{:S(2)}, u32[]{:S(2)}) %collective-permute-start.10) | collective-permute-done | bytes 1032224 | tf_op jit(solution)/shard_map/ppermute | solution.py:383
  139.9 2.6 collective-permute-done.15.refs_11_
  142.5 0.9 copy-done.18
  143.5 0.1 collective-permute-start.16
  143.6 0.7 copy.12.blocks_ref
  144.3 2.0 collective-permute-done.16.refs_15_
  146.2 93.4 %ladder.1 = f32[32,4,128]{2,1,0:T(4,128)} custom-call(s32[3]{0:T(128)} %copy-done.2, s32[8,2]{1,0:T(8,128)} %copy.12.blocks_ref, bf16[36,112,128]{2,1,0:T(8,128)(2,1)} %copy-done.5, bf16[36,112,128]{2,1,0:T(8,128)(2,1)} %copy-done.9, bf16[36,112,128]{2,1,0:T(8,128)(2,1)} %copy-done.8, bf16[36,112,128]{2,1,0:T(8,128)(2,1)} %copy-done.17, ...), custom_call_target="tpu_custom_call" | custom-call | flops 13153337344 | bytes 42205184 | tf_op jit(solution)/shard_map/ladder/pallas_call | solution.py:328
  239.7 1.0 reshape.14
  240.7 0.2 copy.13
  240.9 0.2 copy.19
  241.0 0.1 reshape.16
  241.2 13.2 %all_to_all.5 = f32[32,1,256]{2,1,0:T(1,128)S(1)} all-to-all(f32[32,1,256]{2,1,0:T(1,128)S(1)} %reshape.16), channel_id=1, replica_groups=mesh['aux'=4,'pair'=8] {'aux','pair'}, dimensions={0} | all-to-all | bytes 65536 | tf_op jit(solution)/shard_map/all_to_all | solution.py:468
  254.4 0.5 broadcast.2
  254.9 0.7 reduce
  255.6 0.1 reshape.17
  255.8 0.7 copy.16
  (45 shorter events, 0.1 us)
Async XLA Ops:
  1.7 51.7 %copy-start.2 = (s32[3]{0:T(128)}, s32[3]{0:T(128)S(1)}, u32[]{:S(2)}) copy-start(s32[3]{0:T(128)S(1)} %pad_add_fusion.z_ref.place_ref) | copy-start | bytes 40
  16.4 28.2 %collective-permute-start.1 = (bf16[36,112,128]{2,1,0:T(8,128)(2,1)S(1)}, bf16[36,112,128]{2,1,0:T(8,128)(2,1)S(1)}, u32[]{:S(2)}, u32[]{:S(2)}) collective-permute-start(bf16[36,112,128]{2,1,0:T(8,128)(2,1)S(1)} %dress.5), channel_id=1, source_target_pairs={{0,2},{1,10},{2,4},{3,12},{4,6},{5,14},{6,0},{7,8},{8,3},{9,11},{1... | collective-permute-start | bytes 3096584 | tf_op jit(solution)/shard_map/ppermute | solution.py:383
  19.4 25.3 %collective-permute-start = (bf16[36,112,128]{2,1,0:T(8,128)(2,1)S(1)}, bf16[36,112,128]{2,1,0:T(8,128)(2,1)S(1)}, u32[]{:S(2)}, u32[]{:S(2)}) collective-permute-start(bf16[36,112,128]{2,1,0:T(8,128)(2,1)S(1)} %dress.4), channel_id=1, source_target_pairs={{0,0},{1,8},{2,2},{3,10},{4,4},{5,12},{6,6},{7,14},{8,1},{9,9},{10... | collective-permute-start | bytes 3096584 | tf_op jit(solution)/shard_map/ppermute | solution.py:383
  20.1 24.6 %collective-permute-start.2 = (bf16[36,112,128]{2,1,0:T(8,128)(2,1)S(1)}, bf16[36,112,128]{2,1,0:T(8,128)(2,1)S(1)}, u32[]{:S(2)}, u32[]{:S(2)}) collective-permute-start(bf16[36,112,128]{2,1,0:T(8,128)(2,1)S(1)} %dress.4), channel_id=1, source_target_pairs={{0,16},{1,17},{2,18},{3,19},{4,20},{5,21},{6,22},{7,23},{8,24},{9,... | collective-permute-start | bytes 3096584 | tf_op jit(solution)/shard_map/ppermute | solution.py:383
  44.6 16.1 %copy-start.4 = (bf16[36,112,128]{2,1,0:T(8,128)(2,1)}, bf16[36,112,128]{2,1,0:T(8,128)(2,1)S(1)}, u32[]{:S(2)}) copy-start(bf16[36,112,128]{2,1,0:T(8,128)(2,1)S(1)} %collective-permute-done.1.refs_4_) | copy-start | bytes 3096580
  44.6 16.1 %copy-start.5 = (bf16[36,112,128]{2,1,0:T(8,128)(2,1)}, bf16[36,112,128]{2,1,0:T(8,128)(2,1)S(1)}, u32[]{:S(2)}) copy-start(bf16[36,112,128]{2,1,0:T(8,128)(2,1)S(1)} %collective-permute-done.refs_0_) | copy-start | bytes 3096580
  44.6 24.3 %collective-permute-start.3 = (bf16[36,112,128]{2,1,0:T(8,128)(2,1)S(1)}, bf16[36,112,128]{2,1,0:T(8,128)(2,1)S(1)}, u32[]{:S(2)}, u32[]{:S(2)}) collective-permute-start(bf16[36,112,128]{2,1,0:T(8,128)(2,1)S(1)} %dress.6), channel_id=1, source_target_pairs={{0,6},{1,14},{2,0},{3,8},{4,2},{5,10},{6,4},{7,12},{8,7},{9,15},{1... | collective-permute-start | bytes 3096584 | tf_op jit(solution)/shard_map/ppermute | solution.py:383
  46.9 24.5 %collective-permute-start.4 = (bf16[36,112,128]{2,1,0:T(8,128)(2,1)S(1)}, bf16[36,112,128]{2,1,0:T(8,128)(2,1)S(1)}, u32[]{:S(2)}, u32[]{:S(2)}) collective-permute-start(bf16[36,112,128]{2,1,0:T(8,128)(2,1)S(1)} %collective-permute-done.1.refs_4_), channel_id=1, source_target_pairs={{0,16},{1,17},{2,18},{3,19},{4,20},{5,21},{6,22},{7,23},{8,24},{9,... | collective-permute-start | bytes 3096584 | tf_op jit(solution)/shard_map/ppermute | solution.py:383
  48.4 23.1 %collective-permute-start.5 = (bf16[36,112,128]{2,1,0:T(8,128)(2,1)S(1)}, bf16[36,112,128]{2,1,0:T(8,128)(2,1)S(1)}, u32[]{:S(2)}, u32[]{:S(2)}) collective-permute-start(bf16[36,112,128]{2,1,0:T(8,128)(2,1)S(1)} %collective-permute-done.2), channel_id=1, source_target_pairs={{0,0},{1,8},{2,2},{3,10},{4,4},{5,12},{6,6},{7,14},{8,1},{9,9},{10... | collective-permute-start | bytes 3096584 | tf_op jit(solution)/shard_map/ppermute | solution.py:383
  49.3 22.2 %collective-permute-start.6 = (bf16[36,112,128]{2,1,0:T(8,128)(2,1)S(1)}, bf16[36,112,128]{2,1,0:T(8,128)(2,1)S(1)}, u32[]{:S(2)}, u32[]{:S(2)}) collective-permute-start(bf16[36,112,128]{2,1,0:T(8,128)(2,1)S(1)} %collective-permute-done.refs_0_), channel_id=1, source_target_pairs={{0,8},{1,9},{2,10},{3,11},{4,12},{5,13},{6,14},{7,15},{8,0},{9,1},... | collective-permute-start | bytes 3096584 | tf_op jit(solution)/shard_map/ppermute | solution.py:383
  53.4 18.2 %collective-permute-start.7 = (bf16[36,112,128]{2,1,0:T(8,128)(2,1)S(1)}, bf16[36,112,128]{2,1,0:T(8,128)(2,1)S(1)}, u32[]{:S(2)}, u32[]{:S(2)}) collective-permute-start(bf16[36,112,128]{2,1,0:T(8,128)(2,1)S(1)} %collective-permute-done.1.refs_4_), channel_id=1, source_target_pairs={{0,8},{1,9},{2,10},{3,11},{4,12},{5,13},{6,14},{7,15},{8,0},{9,1},... | collective-permute-start | bytes 3096584 | tf_op jit(solution)/shard_map/ppermute | solution.py:383
  68.9 52.7 %copy-start.6 = (bf16[36,112,128]{2,1,0:T(8,128)(2,1)}, bf16[36,112,128]{2,1,0:T(8,128)(2,1)S(1)}, u32[]{:S(2)}) copy-start(bf16[36,112,128]{2,1,0:T(8,128)(2,1)S(1)} %collective-permute-done.3.refs_8_) | copy-start | bytes 3096580
  71.5 50.6 %copy-start.7 = (bf16[36,112,128]{2,1,0:T(8,128)(2,1)}, bf16[36,112,128]{2,1,0:T(8,128)(2,1)S(1)}, u32[]{:S(2)}) copy-start(bf16[36,112,128]{2,1,0:T(8,128)(2,1)S(1)} %collective-permute-done.4.refs_6_) | copy-start | bytes 3096580
  71.5 50.7 %copy-start.8 = (bf16[36,112,128]{2,1,0:T(8,128)(2,1)}, bf16[36,112,128]{2,1,0:T(8,128)(2,1)S(1)}, u32[]{:S(2)}) copy-start(bf16[36,112,128]{2,1,0:T(8,128)(2,1)S(1)} %collective-permute-done.5.refs_2_) | copy-start | bytes 3096580
  71.5 1.5 copy-start.9
  71.5 1.5 copy-start.10
  71.5 48.3 %collective-permute-start.8 = (bf16[36,112,128]{2,1,0:T(8,128)(2,1)S(1)}, bf16[36,112,128]{2,1,0:T(8,128)(2,1)S(1)}, u32[]{:S(2)}, u32[]{:S(2)}) collective-permute-start(bf16[36,112,128]{2,1,0:T(8,128)(2,1)S(1)} %dress.7), channel_id=1, source_target_pairs={{0,4},{1,12},{2,6},{3,14},{4,0},{5,8},{6,2},{7,10},{8,5},{9,13},{1... | collective-permute-start | bytes 3096584 | tf_op jit(solution)/shard_map/ppermute | solution.py:383
  73.1 46.8 %collective-permute-start.9 = (bf16[36,112,128]{2,1,0:T(8,128)(2,1)S(1)}, bf16[36,112,128]{2,1,0:T(8,128)(2,1)S(1)}, u32[]{:S(2)}, u32[]{:S(2)}) collective-permute-start(bf16[36,112,128]{2,1,0:T(8,128)(2,1)S(1)} %collective-permute-done.3.refs_8_), channel_id=1, source_target_pairs={{0,16},{1,17},{2,18},{3,19},{4,20},{5,21},{6,22},{7,23},{8,24},{9,... | collective-permute-start | bytes 3096584 | tf_op jit(solution)/shard_map/ppermute | solution.py:383
  83.6 4.6 %copy-start = (bf16[112,64,896]{2,1,0:T(8,128)(2,1)}, bf16[112,64,896]{2,1,0:T(8,128)(2,1)S(1)}, u32[]{:S(2)}) copy-start(bf16[112,64,896]{2,1,0:T(8,128)(2,1)S(1)} %relayout.2) | copy-start | bytes 38535172
  88.2 55.4 %copy-start.3 = (s32[8,2]{0,1:T(2,128)S(1)}, s32[8,2]{0,1:T(2,128)}, u32[]{:S(2)}) copy-start(s32[8,2]{0,1:T(2,128)} %param.9) | copy-start | bytes 196
  97.3 4.6 %copy-start.1 = (bf16[112,64,896]{2,1,0:T(8,128)(2,1)}, bf16[112,64,896]{2,1,0:T(8,128)(2,1)S(1)}, u32[]{:S(2)}) copy-start(bf16[112,64,896]{2,1,0:T(8,128)(2,1)S(1)} %relayout.3) | copy-start | bytes 38535172
  119.8 26.4 %copy-start.11 = (bf16[36,112,128]{2,1,0:T(8,128)(2,1)}, bf16[36,112,128]{2,1,0:T(8,128)(2,1)S(1)}, u32[]{:S(2)}) copy-start(bf16[36,112,128]{2,1,0:T(8,128)(2,1)S(1)} %collective-permute-done.8.refs_12_) | copy-start | bytes 3096580
  119.8 26.4 %copy-start.12 = (bf16[36,112,128]{2,1,0:T(8,128)(2,1)}, bf16[36,112,128]{2,1,0:T(8,128)(2,1)S(1)}, u32[]{:S(2)}) copy-start(bf16[36,112,128]{2,1,0:T(8,128)(2,1)S(1)} %collective-permute-done.9.refs_10_) | copy-start | bytes 3096580
  119.8 20.0 %collective-permute-start.10 = (bf16[36,112,128]{2,1,0:T(8,128)(2,1)S(1)}, bf16[36,112,128]{2,1,0:T(8,128)(2,1)S(1)}, u32[]{:S(2)}, u32[]{:S(2)}) collective-permute-start(bf16[36,112,128]{2,1,0:T(8,128)(2,1)S(1)} %collective-permute-done.8.refs_12_), channel_id=1, source_target_pairs={{0,16},{1,17},{2,18},{3,19},{4,20},{5,21},{6,22},{7,23},{8,24},{9,... | collective-permute-start | bytes 3096584 | tf_op jit(solution)/shard_map/ppermute | solution.py:383
  121.6 18.3 %collective-permute-start.14 = (bf16[36,112,128]{2,1,0:T(8,128)(2,1)S(1)}, bf16[36,112,128]{2,1,0:T(8,128)(2,1)S(1)}, u32[]{:S(2)}, u32[]{:S(2)}) collective-permute-start(bf16[36,112,128]{2,1,0:T(8,128)(2,1)S(1)} %collective-permute-done.8.refs_12_), channel_id=1, source_target_pairs={{0,8},{1,9},{2,10},{3,11},{4,12},{5,13},{6,14},{7,15},{8,0},{9,1},... | collective-permute-start | bytes 3096584 | tf_op jit(solution)/shard_map/ppermute | solution.py:383
  121.6 18.2 %collective-permute-start.11 = (bf16[36,112,128]{2,1,0:T(8,128)(2,1)S(1)}, bf16[36,112,128]{2,1,0:T(8,128)(2,1)S(1)}, u32[]{:S(2)}, u32[]{:S(2)}) collective-permute-start(bf16[36,112,128]{2,1,0:T(8,128)(2,1)S(1)} %collective-permute-done.3.refs_8_), channel_id=1, source_target_pairs={{0,8},{1,9},{2,10},{3,11},{4,12},{5,13},{6,14},{7,15},{8,0},{9,1},... | collective-permute-start | bytes 3096584 | tf_op jit(solution)/shard_map/ppermute | solution.py:383
  122.1 17.8 %collective-permute-start.12 = (bf16[36,112,128]{2,1,0:T(8,128)(2,1)S(1)}, bf16[36,112,128]{2,1,0:T(8,128)(2,1)S(1)}, u32[]{:S(2)}, u32[]{:S(2)}) collective-permute-start(bf16[36,112,128]{2,1,0:T(8,128)(2,1)S(1)} %collective-permute-done.4.refs_6_), channel_id=1, source_target_pairs={{0,8},{1,9},{2,10},{3,11},{4,12},{5,13},{6,14},{7,15},{8,0},{9,1},... | collective-permute-start | bytes 3096584 | tf_op jit(solution)/shard_map/ppermute | solution.py:383
  122.2 17.7 %collective-permute-start.13 = (bf16[36,112,128]{2,1,0:T(8,128)(2,1)S(1)}, bf16[36,112,128]{2,1,0:T(8,128)(2,1)S(1)}, u32[]{:S(2)}, u32[]{:S(2)}) collective-permute-start(bf16[36,112,128]{2,1,0:T(8,128)(2,1)S(1)} %collective-permute-done.5.refs_2_), channel_id=1, source_target_pairs={{0,8},{1,9},{2,10},{3,11},{4,12},{5,13},{6,14},{7,15},{8,0},{9,1},... | collective-permute-start | bytes 3096584 | tf_op jit(solution)/shard_map/ppermute | solution.py:383
  139.8 6.4 %copy-start.13 = (bf16[36,112,128]{2,1,0:T(8,128)(2,1)}, bf16[36,112,128]{2,1,0:T(8,128)(2,1)S(1)}, u32[]{:S(2)}) copy-start(bf16[36,112,128]{2,1,0:T(8,128)(2,1)S(1)} %collective-permute-done.10.refs_14_) | copy-start | bytes 3096580
  139.8 2.6 %collective-permute-start.15 = (bf16[36,112,128]{2,1,0:T(8,128)(2,1)S(1)}, bf16[36,112,128]{2,1,0:T(8,128)(2,1)S(1)}, u32[]{:S(2)}, u32[]{:S(2)}) collective-permute-start(bf16[36,112,128]{2,1,0:T(8,128)(2,1)S(1)} %collective-permute-done.9.refs_10_), channel_id=1, source_target_pairs={{0,8},{1,9},{2,10},{3,11},{4,12},{5,13},{6,14},{7,15},{8,0},{9,1},... | collective-permute-start | bytes 3096584 | tf_op jit(solution)/shard_map/ppermute | solution.py:383
  139.9 2.6 %copy-start.15 = (bf16[36,112,128]{2,1,0:T(8,128)(2,1)}, bf16[36,112,128]{2,1,0:T(8,128)(2,1)S(1)}, u32[]{:S(2)}) copy-start(bf16[36,112,128]{2,1,0:T(8,128)(2,1)S(1)} %collective-permute-done.11.refs_9_) | copy-start | bytes 3096580
  139.9 2.6 %copy-start.16 = (bf16[36,112,128]{2,1,0:T(8,128)(2,1)}, bf16[36,112,128]{2,1,0:T(8,128)(2,1)S(1)}, u32[]{:S(2)}) copy-start(bf16[36,112,128]{2,1,0:T(8,128)(2,1)S(1)} %collective-permute-done.12.refs_7_) | copy-start | bytes 3096580
  139.9 2.6 %copy-start.17 = (bf16[36,112,128]{2,1,0:T(8,128)(2,1)}, bf16[36,112,128]{2,1,0:T(8,128)(2,1)S(1)}, u32[]{:S(2)}) copy-start(bf16[36,112,128]{2,1,0:T(8,128)(2,1)S(1)} %collective-permute-done.13.refs_3_) | copy-start | bytes 3096580
  139.9 2.6 %copy-start.14 = (bf16[36,112,128]{2,1,0:T(8,128)(2,1)}, bf16[36,112,128]{2,1,0:T(8,128)(2,1)S(1)}, u32[]{:S(2)}) copy-start(bf16[36,112,128]{2,1,0:T(8,128)(2,1)S(1)} %collective-permute-done.14.refs_13_) | copy-start | bytes 3096580
  142.5 1.0 copy-start.18
  143.5 2.8 %collective-permute-start.16 = (bf16[36,112,128]{2,1,0:T(8,128)(2,1)S(1)}, bf16[36,112,128]{2,1,0:T(8,128)(2,1)}, u32[]{:S(2)}, u32[]{:S(2)}) collective-permute-start(bf16[36,112,128]{2,1,0:T(8,128)(2,1)S(1)} %collective-permute-done.10.refs_14_), channel_id=1, source_target_pairs={{0,8},{1,9},{2,10},{3,11},{4,12},{5,13},{6,14},{7,15},{8,0},{9,1},... | collective-permute-start | bytes 3096584 | tf_op jit(solution)/shard_map/ppermute | solution.py:383

commit v11 on v6

--- a/solution.py
+++ b/solution.py
@@ -77,8 +77,15 @@
     )(t1_window)
 
 
-def dress_kernel(p, offset, z_ref, a_ref, *refs):
-    ov, vv, out = refs[: p.nm + 1], refs[p.nm + 1 : 2 * p.nm + 2], refs[-1]
+def dress_kernel(p, offset, bounds, z_ref, a_ref, *refs):
+    ov, vv, outs = refs[: p.nm + 1], refs[p.nm + 1 : 2 * p.nm + 2], refs[2 * p.nm + 2 :]
+
+    def put(start, cols, planes):
+        for out, (low, high) in zip(outs, bounds):
+            first, last = max(low, start), min(high, start + planes.shape[0])
+            if first < last:
+                out[first - low : last - low, cols] = planes[first - start : last - start]
+
     w = p.window
     j = lax.rem(z_ref[0] + offset, p.js)
     lane = lax.broadcasted_iota(jnp.int32, (p.nt, ROWS, LANES), 2)
@@ -91,7 +98,7 @@
         for m in range(p.nm):
             here = shift[:, m * LANES : (m + 1) * LANES].reshape(w, ROWS, LANES)
             here = vv[m][:, cols].astype(jnp.float32) - here
-            out[m * w : (m + 1) * w, cols] = here.astype(jnp.bfloat16)
+            put(m * w, cols, here.astype(jnp.bfloat16))
         here = shift[:, p.nm * LANES :].reshape(w, ROWS, p.tail_width)
         source = vv[p.nm][:, cols].astype(jnp.float32) - here
         source = source.reshape(p.nt, p.per_row, ROWS, p.tail_width)
@@ -102,10 +109,10 @@
             moved = moved[:, :LANES].reshape(p.nt, ROWS, LANES)
             keep = (lane >= s * p.slot) & (lane < s * p.slot + p.tail)
             rest = jnp.where(keep, moved, rest)
-        out[p.nm * w :, cols] = rest.astype(jnp.bfloat16)
-
-
-def dress(p, offset, z, spread, chol_vv, chol_ov):
+        put(p.nm * w, cols, rest.astype(jnp.bfloat16))
+
+
+def dress(p, offset, bounds, z, spread, chol_vv, chol_ov):
     def specs(lead):
         found = []
         for m in range(p.nm):
@@ -125,15 +132,20 @@
 
     count = p.nm + 1
     return pl.pallas_call(
-        functools.partial(dress_kernel, p, offset),
-        out_shape=jax.ShapeDtypeStruct((p.planes, p.cpad, LANES), jnp.bfloat16),
+        functools.partial(dress_kernel, p, offset, bounds),
+        out_shape=[
+            jax.ShapeDtypeStruct((high - low, p.cpad, LANES), jnp.bfloat16) for low, high in bounds
+        ],
         grid_spec=pltpu.PrefetchScalarGridSpec(
             num_scalar_prefetch=1,
             grid=(1,),
             in_specs=[pl.BlockSpec((p.window * ROWS, p.occupied * ROWS), lambda i, z: (0, 0))]
             + specs(p.occupied)
             + specs(p.window),
-            out_specs=pl.BlockSpec((p.planes, p.cpad, LANES), lambda i, z: (0, 0, 0)),
+            out_specs=[
+                pl.BlockSpec((high - low, p.cpad, LANES), lambda i, z: (0, 0, 0))
+                for low, high in bounds
+            ],
         ),
         compiler_params=pltpu.CompilerParams(vmem_limit_bytes=48 * 2**20),
         cost_estimate=pl.CostEstimate(
@@ -410,52 +422,39 @@
 
     order = sorted(range(p.js), key=lambda o: min(o, p.js - o))
     units = [(o, 0, p.planes) for o in order]
-    if p.js > 2:
-        half = p.planes // 2
-        units[-1:] = [(order[-1], 0, half), (order[-1], half, p.planes)]
-        rounds = [[units[1], units[0]]] + [[unit] for unit in units[2:]]
-        swaps = [[units[0]], [units[1]]] + [[unit] for unit in units[2:-2]] + [units[-2:]]
-    else:
-        rounds, swaps = [units], [units]
-
-    def make(o, spread):
-        return dress(p, o, place, spread, chol_vv, chol_ov)
-
-    def cut(message, unit):
-        if unit[1:] == (0, p.planes):
-            return message
-        return message[unit[1] : unit[2]]
+    rounds = [units[1:2], units[2:3] + units[:1]] + [[unit] for unit in units[3:]]
+    rounds = [members for members in rounds if members]
+
+    def make(unit, spread):
+        return dress(p, unit[0], [unit[1:]], place, spread, chol_vv, chol_ov)[0]
 
     messages = {}
-    for o, _, _ in rounds[0]:
-        messages[o] = make(o, spread)
-        messages[o], spread = lax.optimization_barrier((messages[o], spread))
+    for unit in rounds[0]:
+        messages[unit], spread = lax.optimization_barrier((make(unit, spread), spread))
     amps = [None] * AMPS
     sources = [amplitudes] * AMPS
     held = {}
     share_next = []
-    count = max(len(rounds), len(swaps) + 1) + 1
-    for n in range(count):
+    for n in range(len(rounds) + 2):
         new, made, laid = {}, {}, {}
-        to_share, share_next = share_next, []
+        to_share = []
+        if n != len(rounds) - 1:
+            to_share, share_next = share_next, []
         if n < len(rounds):
             for unit in rounds[n]:
-                new[unit, 0, 0] = to_slice(cut(messages[unit[0]], unit), unit[0])
+                new[unit, 0, 0] = to_slice(messages[unit], unit[0])
                 share_next.append((unit, 0))
-        if 1 <= n <= len(swaps):
-            for unit in swaps[n - 1]:
+        if 1 <= n <= len(rounds):
+            for unit in rounds[n - 1]:
                 for r in range(1, p.xs):
                     new[unit, r, 0] = along_x(held[unit, 0, 0], r)
                     share_next.append((unit, r))
         for unit, r in to_share:
             new[unit, r, 1] = to_core(held[unit, r, 0])
         if n + 1 < len(rounds):
-            for o, _, _ in rounds[n + 1]:
-                if o not in messages:
-                    made[o] = make(o, spread)
-        part = n - (len(swaps) - AMPS)
-        if 0 <= part < AMPS:
-            laid[part] = relayout(p, sources[part], part)
+            made = {unit: make(unit, spread) for unit in rounds[n + 1]}
+        if n == len(rounds) - 1:
+            laid = {part: relayout(p, sources[part], part) for part in range(AMPS)}
         moved = (list(new.values()), list(made.values()), list(laid.values()))
         kept = (list(held.values()), spread, sources)
         moved, (old, spread, sources) = lax.optimization_barrier((moved, kept))

time: 242 us -> 231 us (0.955)
  waiting for transfers between devices: 74.3 us -> 66.9 us
  starting transfers between devices: 19.9 us -> 15.6 us
    ppermute x20 -> x16, waiting for transfers between devices: 74.3 us -> 66.9 us  [permute(): return lax.ppermute(array, ('aux', 'pair'), pairs)]
    ppermute x20 -> x16, starting transfers between devices: 19.9 us -> 15.6 us  [permute(): return lax.ppermute(array, ('aux', 'pair'), pairs)]
    unnamed x50 -> x40, local copies, waits for them, and re-layouts: 12.1 us -> 12 us
  transfers between devices with their start and end apart: 20 -> 16, of which waited for: 9 -> 10; matrix products, arithmetic and copies ran while one was open for 0% -> 0% of each run, Pallas kernels for 13% -> 17%
where the time goes in v11:
time: 231 us
  Pallas kernels  122 us (53%)
  waiting for transfers between devices  66.9 us (29%)
  starting transfers between devices  15.6 us (7%)
  local copies, waits for them, and re-layouts  14.5 us (6%)
  blocking collectives  10.9 us (5%)
    pallas_call x1, Pallas kernels, ladder(): pl.pallas_call(functools.partial(ladder_kernel, p, units, parts, group),...  73.7 us
    ppermute x16, waiting for transfers between devices, permute(): return lax.ppermute(array, ('aux', 'pair'), pairs)  66.9 us
    pallas_call x4, Pallas kernels, dress(): pl.pallas_call(functools.partial(dress_kernel, p, offset, bounds), out_sh...  29.2 us
    pallas_call x2, Pallas kernels, relayout(): pl.pallas_call(functools.partial(relayout_kernel, p), out_shape=jax.Shape...  18.1 us
    ppermute x16, starting transfers between devices, permute(): return lax.ppermute(array, ('aux', 'pair'), pairs)  15.6 us
    unnamed x40, local copies, waits for them, and re-layouts  12 us
    all_to_all x1, blocking collectives, shards(): lax.all_to_all(terms, ('aux', 'pair'), split_axis=0, concat_axis=0, tiled...  10.9 us
  transfers between devices with their start and end apart: 16, of which 10 were waited for; matrix products, arithmetic and copies ran while one was open for 0% of the time, Pallas kernels for 17%

profile of v11, /device:TPU:0, one launch (start us, length us, event | category | flops | bytes accessed | tf_op | source)
XLA Modules:
  0.0 230.7 jit_solution(11519529036742716520)
XLA Ops:
  0.0 0.8 copy.11.t1_ref
  0.8 0.8 spread.1.a_ref
  1.6 0.1 pad_add_fusion.z_ref.place_ref
  1.7 7.3 %dress.4 = bf16[36,112,128]{2,1,0:T(8,128)(2,1)S(1)} custom-call(s32[3]{0:T(128)S(1)} %pad_add_fusion.z_ref.place_ref, bf16[512,1600]{1,0:T(8,128)(2,1)S(1)} %spread.1.a_ref, bf16[100,112,576]{2,1,0:T(8,128)(2,1)} %refs_1_.7, bf16[100,112,576]{2,1,0:T(8,128)(2,1)} %refs_1_.7, bf16[32,112,576]{2,1,0:T(8,128)(2,1)} %refs_3_.7, bf16[32,112,576]{2,1,0:T(8,128)(2,1)} %refs_3_.7), custom_call_target="tpu_custom_call" | custom-call | flops 2936012800 | bytes 9404416 | tf_op jit(solution)/shard_map/dress/pallas_call | solution.py:134
  9.0 3.1 %collective-permute-start = (bf16[36,112,128]{2,1,0:T(8,128)(2,1)S(1)}, bf16[36,112,128]{2,1,0:T(8,128)(2,1)S(1)}, u32[]{:S(2)}, u32[]{:S(2)}) collective-permute-start(bf16[36,112,128]{2,1,0:T(8,128)(2,1)S(1)} %dress.4), channel_id=1, source_target_pairs={{0,2},{1,10},{2,4},{3,12},{4,6},{5,14},{6,0},{7,8},{8,3},{9,11},{1... | collective-permute-start | bytes 3096584 | tf_op jit(solution)/shard_map/ppermute | solution.py:404
  12.1 7.3 %dress.5 = bf16[36,112,128]{2,1,0:T(8,128)(2,1)S(1)} custom-call(s32[3]{0:T(128)S(1)} %pad_add_fusion.z_ref.place_ref, bf16[512,1600]{1,0:T(8,128)(2,1)S(1)} %spread.1.a_ref, bf16[100,112,576]{2,1,0:T(8,128)(2,1)} %refs_1_.7, bf16[100,112,576]{2,1,0:T(8,128)(2,1)} %refs_1_.7, bf16[32,112,576]{2,1,0:T(8,128)(2,1)} %refs_3_.7, bf16[32,112,576]{2,1,0:T(8,128)(2,1)} %refs_3_.7), custom_call_target="tpu_custom_call" | custom-call | flops 2936012800 | bytes 9404416 | tf_op jit(solution)/shard_map/dress/pallas_call | solution.py:134
  19.3 7.4 %dress.6 = bf16[36,112,128]{2,1,0:T(8,128)(2,1)S(1)} custom-call(s32[3]{0:T(128)S(1)} %pad_add_fusion.z_ref.place_ref, bf16[512,1600]{1,0:T(8,128)(2,1)S(1)} %spread.1.a_ref, bf16[100,112,576]{2,1,0:T(8,128)(2,1)} %refs_1_.7, bf16[100,112,576]{2,1,0:T(8,128)(2,1)} %refs_1_.7, bf16[32,112,576]{2,1,0:T(8,128)(2,1)} %refs_3_.7, bf16[32,112,576]{2,1,0:T(8,128)(2,1)} %refs_3_.7), custom_call_target="tpu_custom_call" | custom-call | flops 2936012800 | bytes 9404416 | tf_op jit(solution)/shard_map/dress/pallas_call | solution.py:134
  26.8 10.7 %collective-permute-done.refs_4_ = bf16[36,112,128]{2,1,0:T(8,128)(2,1)S(1)} collective-permute-done((bf16[36,112,128]{2,1,0:T(8,128)(2,1)S(1)}, bf16[36,112,128]{2,1,0:T(8,128)(2,1)S(1)}, u32[]{:S(2)}, u32[]{:S(2)}) %collective-permute-start) | collective-permute-done | bytes 1032224 | tf_op jit(solution)/shard_map/ppermute | solution.py:404
  37.4 2.1 collective-permute-start.1
  39.6 0.9 collective-permute-start.2
  40.5 1.6 collective-permute-start.3
  42.0 2.2 collective-permute-start.4
  44.3 7.3 %dress.7 = bf16[36,112,128]{2,1,0:T(8,128)(2,1)S(1)} custom-call(s32[3]{0:T(128)S(1)} %pad_add_fusion.z_ref.place_ref, bf16[512,1600]{1,0:T(8,128)(2,1)S(1)} %spread.1.a_ref, bf16[100,112,576]{2,1,0:T(8,128)(2,1)} %refs_1_.7, bf16[100,112,576]{2,1,0:T(8,128)(2,1)} %refs_1_.7, bf16[32,112,576]{2,1,0:T(8,128)(2,1)} %refs_3_.7, bf16[32,112,576]{2,1,0:T(8,128)(2,1)} %refs_3_.7), custom_call_target="tpu_custom_call" | custom-call | flops 2936012800 | bytes 9404416 | tf_op jit(solution)/shard_map/dress/pallas_call | solution.py:134
  51.6 10.9 %collective-permute-done.1.refs_8_ = bf16[36,112,128]{2,1,0:T(8,128)(2,1)S(1)} collective-permute-done((bf16[36,112,128]{2,1,0:T(8,128)(2,1)S(1)}, bf16[36,112,128]{2,1,0:T(8,128)(2,1)S(1)}, u32[]{:S(2)}, u32[]{:S(2)}) %collective-permute-start.1) | collective-permute-done | bytes 1032224 | tf_op jit(solution)/shard_map/ppermute | solution.py:404
  62.4 2.2 collective-permute-done.3.refs_6_
  64.6 0.1 collective-permute-start.5
  64.7 1.6 collective-permute-start.6
  66.3 0.8 collective-permute-start.7
  67.1 9.0 %relayout.2 = bf16[112,64,896]{2,1,0:T(8,128)(2,1)S(1)} custom-call(bf16[64,224,896]{2,1,0:T(8,128)(2,1)} %in_ref.1), custom_call_target="tpu_custom_call" | custom-call | flops 3288334336 | bytes 25690112 | tf_op jit(solution)/shard_map/relayout/pallas_call | solution.py:174
  76.2 4.6 %copy-done = bf16[112,64,896]{2,1,0:T(8,128)(2,1)} copy-done((bf16[112,64,896]{2,1,0:T(8,128)(2,1)}, bf16[112,64,896]{2,1,0:T(8,128)(2,1)S(1)}, u32[]{:S(2)}) %copy-start) | copy-done | bytes 12845080
  80.8 9.0 %relayout.3 = bf16[112,64,896]{2,1,0:T(8,128)(2,1)S(1)} custom-call(bf16[64,224,896]{2,1,0:T(8,128)(2,1)} %in_ref.1), custom_call_target="tpu_custom_call" | custom-call | flops 3288334336 | bytes 25690112 | tf_op jit(solution)/shard_map/relayout/pallas_call | solution.py:174
  89.8 4.6 %copy-done.1 = bf16[112,64,896]{2,1,0:T(8,128)(2,1)} copy-done((bf16[112,64,896]{2,1,0:T(8,128)(2,1)}, bf16[112,64,896]{2,1,0:T(8,128)(2,1)S(1)}, u32[]{:S(2)}) %copy-start.1) | copy-done | bytes 12845080
  94.4 18.0 %collective-permute-done.5.refs_12_ = bf16[36,112,128]{2,1,0:T(8,128)(2,1)S(1)} collective-permute-done((bf16[36,112,128]{2,1,0:T(8,128)(2,1)S(1)}, bf16[36,112,128]{2,1,0:T(8,128)(2,1)S(1)}, u32[]{:S(2)}, u32[]{:S(2)}) %collective-permute-start.5) | collective-permute-done | bytes 1032224 | tf_op jit(solution)/shard_map/ppermute | solution.py:404
  112.5 0.1 collective-permute-start.10
  112.6 0.5 collective-permute-start.11
  113.1 0.1 collective-permute-start.12
  113.1 1.9 collective-permute-start.8
  115.1 0.2 collective-permute-start.13
  115.2 0.4 collective-permute-start.14
  115.6 1.1 collective-permute-done.11.refs_7_
  116.7 0.1 collective-permute-start.9
  116.8 1.3 collective-permute-done.12.refs_13_
  118.1 1.5 collective-permute-done.13.refs_11_
  119.6 1.5 collective-permute-done.14.refs_3_
  121.1 17.5 %collective-permute-done.8.refs_14_ = bf16[36,112,128]{2,1,0:T(8,128)(2,1)} collective-permute-done((bf16[36,112,128]{2,1,0:T(8,128)(2,1)S(1)}, bf16[36,112,128]{2,1,0:T(8,128)(2,1)}, u32[]{:S(2)}, u32[]{:S(2)}) %collective-permute-start.8) | collective-permute-done | bytes 1032224 | tf_op jit(solution)/shard_map/ppermute | solution.py:404
  138.6 1.0 copy-done.17
  139.6 0.7 copy.12.blocks_ref
  140.2 2.3 collective-permute-done.15.refs_15_
  142.6 73.7 %ladder.1 = f32[32,4,128]{2,1,0:T(4,128)} custom-call(s32[3]{0:T(128)} %copy-done.2, s32[8,2]{1,0:T(8,128)} %copy.12.blocks_ref, bf16[36,112,128]{2,1,0:T(8,128)(2,1)} %copy-done.6, bf16[36,112,128]{2,1,0:T(8,128)(2,1)} %copy-done.12, bf16[36,112,128]{2,1,0:T(8,128)(2,1)} %copy-done.11, bf16[36,112,128]{2,1,0:T(8,128)(2,1)} %copy-done.16, ...), custom_call_target="tpu_custom_call" | custom-call | flops 13153337344 | bytes 42205184 | tf_op jit(solution)/shard_map/ladder/pallas_call | solution.py:348
  216.3 1.0 reshape.14
  217.3 0.2 copy.13
  217.5 0.2 copy.19
  217.6 0.1 reshape.16
  217.8 10.9 %all_to_all.5 = f32[32,1,256]{2,1,0:T(1,128)S(1)} all-to-all(f32[32,1,256]{2,1,0:T(1,128)S(1)} %reshape.16), channel_id=1, replica_groups=mesh['aux'=4,'pair'=8] {'aux','pair'}, dimensions={0} | all-to-all | bytes 65536 | tf_op jit(solution)/shard_map/all_to_all | solution.py:475
  228.7 0.5 broadcast.2
  229.2 0.7 reduce
  229.9 0.1 reshape.17
  230.1 0.7 copy.16
  (41 shorter events, 0.1 us)
Async XLA Ops:
  1.7 42.6 %copy-start.2 = (s32[3]{0:T(128)}, s32[3]{0:T(128)S(1)}, u32[]{:S(2)}) copy-start(s32[3]{0:T(128)S(1)} %pad_add_fusion.z_ref.place_ref) | copy-start | bytes 40
  9.0 28.5 %collective-permute-start = (bf16[36,112,128]{2,1,0:T(8,128)(2,1)S(1)}, bf16[36,112,128]{2,1,0:T(8,128)(2,1)S(1)}, u32[]{:S(2)}, u32[]{:S(2)}) collective-permute-start(bf16[36,112,128]{2,1,0:T(8,128)(2,1)S(1)} %dress.4), channel_id=1, source_target_pairs={{0,2},{1,10},{2,4},{3,12},{4,6},{5,14},{6,0},{7,8},{8,3},{9,11},{1... | collective-permute-start | bytes 3096584 | tf_op jit(solution)/shard_map/ppermute | solution.py:404
  37.4 14.1 %copy-start.4 = (bf16[36,112,128]{2,1,0:T(8,128)(2,1)}, bf16[36,112,128]{2,1,0:T(8,128)(2,1)S(1)}, u32[]{:S(2)}) copy-start(bf16[36,112,128]{2,1,0:T(8,128)(2,1)S(1)} %collective-permute-done.refs_4_) | copy-start | bytes 3096580
  37.4 25.0 %collective-permute-start.1 = (bf16[36,112,128]{2,1,0:T(8,128)(2,1)S(1)}, bf16[36,112,128]{2,1,0:T(8,128)(2,1)S(1)}, u32[]{:S(2)}, u32[]{:S(2)}) collective-permute-start(bf16[36,112,128]{2,1,0:T(8,128)(2,1)S(1)} %dress.5), channel_id=1, source_target_pairs={{0,6},{1,14},{2,0},{3,8},{4,2},{5,10},{6,4},{7,12},{8,7},{9,15},{1... | collective-permute-start | bytes 3096584 | tf_op jit(solution)/shard_map/ppermute | solution.py:404
  39.6 22.9 %collective-permute-start.2 = (bf16[36,112,128]{2,1,0:T(8,128)(2,1)S(1)}, bf16[36,112,128]{2,1,0:T(8,128)(2,1)S(1)}, u32[]{:S(2)}, u32[]{:S(2)}) collective-permute-start(bf16[36,112,128]{2,1,0:T(8,128)(2,1)S(1)} %dress.6), channel_id=1, source_target_pairs={{0,0},{1,8},{2,2},{3,10},{4,4},{5,12},{6,6},{7,14},{8,1},{9,9},{10... | collective-permute-start | bytes 3096584 | tf_op jit(solution)/shard_map/ppermute | solution.py:404
  40.5 24.1 %collective-permute-start.3 = (bf16[36,112,128]{2,1,0:T(8,128)(2,1)S(1)}, bf16[36,112,128]{2,1,0:T(8,128)(2,1)S(1)}, u32[]{:S(2)}, u32[]{:S(2)}) collective-permute-start(bf16[36,112,128]{2,1,0:T(8,128)(2,1)S(1)} %collective-permute-done.refs_4_), channel_id=1, source_target_pairs={{0,16},{1,17},{2,18},{3,19},{4,20},{5,21},{6,22},{7,23},{8,24},{9,... | collective-permute-start | bytes 3096584 | tf_op jit(solution)/shard_map/ppermute | solution.py:404
  42.0 22.6 %collective-permute-start.4 = (bf16[36,112,128]{2,1,0:T(8,128)(2,1)S(1)}, bf16[36,112,128]{2,1,0:T(8,128)(2,1)S(1)}, u32[]{:S(2)}, u32[]{:S(2)}) collective-permute-start(bf16[36,112,128]{2,1,0:T(8,128)(2,1)S(1)} %collective-permute-done.refs_4_), channel_id=1, source_target_pairs={{0,8},{1,9},{2,10},{3,11},{4,12},{5,13},{6,14},{7,15},{8,0},{9,1},... | collective-permute-start | bytes 3096584 | tf_op jit(solution)/shard_map/ppermute | solution.py:404
  62.4 54.2 %copy-start.5 = (bf16[36,112,128]{2,1,0:T(8,128)(2,1)}, bf16[36,112,128]{2,1,0:T(8,128)(2,1)S(1)}, u32[]{:S(2)}) copy-start(bf16[36,112,128]{2,1,0:T(8,128)(2,1)S(1)} %collective-permute-done.1.refs_8_) | copy-start | bytes 3096580
  62.4 50.0 %copy-start.6 = (bf16[36,112,128]{2,1,0:T(8,128)(2,1)}, bf16[36,112,128]{2,1,0:T(8,128)(2,1)S(1)}, u32[]{:S(2)}) copy-start(bf16[36,112,128]{2,1,0:T(8,128)(2,1)S(1)} %collective-permute-done.2.refs_0_) | copy-start | bytes 3096580
  64.6 47.9 %copy-start.7 = (bf16[36,112,128]{2,1,0:T(8,128)(2,1)}, bf16[36,112,128]{2,1,0:T(8,128)(2,1)S(1)}, u32[]{:S(2)}) copy-start(bf16[36,112,128]{2,1,0:T(8,128)(2,1)S(1)} %collective-permute-done.3.refs_6_) | copy-start | bytes 3096580
  64.6 1.6 copy-start.8
  64.6 47.8 %collective-permute-start.5 = (bf16[36,112,128]{2,1,0:T(8,128)(2,1)S(1)}, bf16[36,112,128]{2,1,0:T(8,128)(2,1)S(1)}, u32[]{:S(2)}, u32[]{:S(2)}) collective-permute-start(bf16[36,112,128]{2,1,0:T(8,128)(2,1)S(1)} %dress.7), channel_id=1, source_target_pairs={{0,4},{1,12},{2,6},{3,14},{4,0},{5,8},{6,2},{7,10},{8,5},{9,13},{1... | collective-permute-start | bytes 3096584 | tf_op jit(solution)/shard_map/ppermute | solution.py:404
  64.7 47.7 %collective-permute-start.6 = (bf16[36,112,128]{2,1,0:T(8,128)(2,1)S(1)}, bf16[36,112,128]{2,1,0:T(8,128)(2,1)S(1)}, u32[]{:S(2)}, u32[]{:S(2)}) collective-permute-start(bf16[36,112,128]{2,1,0:T(8,128)(2,1)S(1)} %collective-permute-done.1.refs_8_), channel_id=1, source_target_pairs={{0,16},{1,17},{2,18},{3,19},{4,20},{5,21},{6,22},{7,23},{8,24},{9,... | collective-permute-start | bytes 3096584 | tf_op jit(solution)/shard_map/ppermute | solution.py:404
  66.3 46.2 %collective-permute-start.7 = (bf16[36,112,128]{2,1,0:T(8,128)(2,1)S(1)}, bf16[36,112,128]{2,1,0:T(8,128)(2,1)S(1)}, u32[]{:S(2)}, u32[]{:S(2)}) collective-permute-start(bf16[36,112,128]{2,1,0:T(8,128)(2,1)S(1)} %collective-permute-done.2.refs_0_), channel_id=1, source_target_pairs={{0,16},{1,17},{2,18},{3,19},{4,20},{5,21},{6,22},{7,23},{8,24},{9,... | collective-permute-start | bytes 3096584 | tf_op jit(solution)/shard_map/ppermute | solution.py:404
  76.2 4.6 %copy-start = (bf16[112,64,896]{2,1,0:T(8,128)(2,1)}, bf16[112,64,896]{2,1,0:T(8,128)(2,1)S(1)}, u32[]{:S(2)}) copy-start(bf16[112,64,896]{2,1,0:T(8,128)(2,1)S(1)} %relayout.2) | copy-start | bytes 38535172
  80.8 58.8 %copy-start.3 = (s32[8,2]{0,1:T(2,128)S(1)}, s32[8,2]{0,1:T(2,128)}, u32[]{:S(2)}) copy-start(s32[8,2]{0,1:T(2,128)} %param.9) | copy-start | bytes 196
  89.8 4.6 %copy-start.1 = (bf16[112,64,896]{2,1,0:T(8,128)(2,1)}, bf16[112,64,896]{2,1,0:T(8,128)(2,1)S(1)}, u32[]{:S(2)}) copy-start(bf16[112,64,896]{2,1,0:T(8,128)(2,1)S(1)} %relayout.3) | copy-start | bytes 38535172
  112.4 30.1 %copy-start.9 = (bf16[36,112,128]{2,1,0:T(8,128)(2,1)}, bf16[36,112,128]{2,1,0:T(8,128)(2,1)S(1)}, u32[]{:S(2)}) copy-start(bf16[36,112,128]{2,1,0:T(8,128)(2,1)S(1)} %collective-permute-done.5.refs_12_) | copy-start | bytes 3096580
  112.5 30.1 %copy-start.10 = (bf16[36,112,128]{2,1,0:T(8,128)(2,1)}, bf16[36,112,128]{2,1,0:T(8,128)(2,1)S(1)}, u32[]{:S(2)}) copy-start(bf16[36,112,128]{2,1,0:T(8,128)(2,1)S(1)} %collective-permute-done.6.refs_10_) | copy-start | bytes 3096580
  112.5 30.1 %copy-start.11 = (bf16[36,112,128]{2,1,0:T(8,128)(2,1)}, bf16[36,112,128]{2,1,0:T(8,128)(2,1)S(1)}, u32[]{:S(2)}) copy-start(bf16[36,112,128]{2,1,0:T(8,128)(2,1)S(1)} %collective-permute-done.7.refs_2_) | copy-start | bytes 3096580
  112.5 2.7 %collective-permute-start.10 = (bf16[36,112,128]{2,1,0:T(8,128)(2,1)S(1)}, bf16[36,112,128]{2,1,0:T(8,128)(2,1)S(1)}, u32[]{:S(2)}, u32[]{:S(2)}) collective-permute-start(bf16[36,112,128]{2,1,0:T(8,128)(2,1)S(1)} %collective-permute-done.2.refs_0_), channel_id=1, source_target_pairs={{0,8},{1,9},{2,10},{3,11},{4,12},{5,13},{6,14},{7,15},{8,0},{9,1},... | collective-permute-start | bytes 3096584 | tf_op jit(solution)/shard_map/ppermute | solution.py:404
  112.6 4.1 %collective-permute-start.11 = (bf16[36,112,128]{2,1,0:T(8,128)(2,1)S(1)}, bf16[36,112,128]{2,1,0:T(8,128)(2,1)S(1)}, u32[]{:S(2)}, u32[]{:S(2)}) collective-permute-start(bf16[36,112,128]{2,1,0:T(8,128)(2,1)S(1)} %collective-permute-done.3.refs_6_), channel_id=1, source_target_pairs={{0,8},{1,9},{2,10},{3,11},{4,12},{5,13},{6,14},{7,15},{8,0},{9,1},... | collective-permute-start | bytes 3096584 | tf_op jit(solution)/shard_map/ppermute | solution.py:404
  113.1 5.1 %collective-permute-start.12 = (bf16[36,112,128]{2,1,0:T(8,128)(2,1)S(1)}, bf16[36,112,128]{2,1,0:T(8,128)(2,1)S(1)}, u32[]{:S(2)}, u32[]{:S(2)}) collective-permute-start(bf16[36,112,128]{2,1,0:T(8,128)(2,1)S(1)} %collective-permute-done.5.refs_12_), channel_id=1, source_target_pairs={{0,8},{1,9},{2,10},{3,11},{4,12},{5,13},{6,14},{7,15},{8,0},{9,1},... | collective-permute-start | bytes 3096584 | tf_op jit(solution)/shard_map/ppermute | solution.py:404
  113.1 25.4 %collective-permute-start.8 = (bf16[36,112,128]{2,1,0:T(8,128)(2,1)S(1)}, bf16[36,112,128]{2,1,0:T(8,128)(2,1)}, u32[]{:S(2)}, u32[]{:S(2)}) collective-permute-start(bf16[36,112,128]{2,1,0:T(8,128)(2,1)S(1)} %collective-permute-done.5.refs_12_), channel_id=1, source_target_pairs={{0,16},{1,17},{2,18},{3,19},{4,20},{5,21},{6,22},{7,23},{8,24},{9,... | collective-permute-start | bytes 3096584 | tf_op jit(solution)/shard_map/ppermute | solution.py:404
  115.1 4.6 %collective-permute-start.13 = (bf16[36,112,128]{2,1,0:T(8,128)(2,1)S(1)}, bf16[36,112,128]{2,1,0:T(8,128)(2,1)S(1)}, u32[]{:S(2)}, u32[]{:S(2)}) collective-permute-start(bf16[36,112,128]{2,1,0:T(8,128)(2,1)S(1)} %collective-permute-done.6.refs_10_), channel_id=1, source_target_pairs={{0,8},{1,9},{2,10},{3,11},{4,12},{5,13},{6,14},{7,15},{8,0},{9,1},... | collective-permute-start | bytes 3096584 | tf_op jit(solution)/shard_map/ppermute | solution.py:404
  115.2 23.3 %copy-start.12 = (bf16[36,112,128]{2,1,0:T(8,128)(2,1)}, bf16[36,112,128]{2,1,0:T(8,128)(2,1)S(1)}, u32[]{:S(2)}) copy-start(bf16[36,112,128]{2,1,0:T(8,128)(2,1)S(1)} %collective-permute-done.10.refs_1_) | copy-start | bytes 3096580
  115.2 5.9 %collective-permute-start.14 = (bf16[36,112,128]{2,1,0:T(8,128)(2,1)S(1)}, bf16[36,112,128]{2,1,0:T(8,128)(2,1)S(1)}, u32[]{:S(2)}, u32[]{:S(2)}) collective-permute-start(bf16[36,112,128]{2,1,0:T(8,128)(2,1)S(1)} %collective-permute-done.7.refs_2_), channel_id=1, source_target_pairs={{0,8},{1,9},{2,10},{3,11},{4,12},{5,13},{6,14},{7,15},{8,0},{9,1},... | collective-permute-start | bytes 3096584 | tf_op jit(solution)/shard_map/ppermute | solution.py:404
  116.7 21.9 %copy-start.13 = (bf16[36,112,128]{2,1,0:T(8,128)(2,1)}, bf16[36,112,128]{2,1,0:T(8,128)(2,1)S(1)}, u32[]{:S(2)}) copy-start(bf16[36,112,128]{2,1,0:T(8,128)(2,1)S(1)} %collective-permute-done.11.refs_7_) | copy-start | bytes 3096580
  116.7 21.9 %collective-permute-start.9 = (bf16[36,112,128]{2,1,0:T(8,128)(2,1)S(1)}, bf16[36,112,128]{2,1,0:T(8,128)(2,1)S(1)}, u32[]{:S(2)}, u32[]{:S(2)}) collective-permute-start(bf16[36,112,128]{2,1,0:T(8,128)(2,1)S(1)} %collective-permute-done.1.refs_8_), channel_id=1, source_target_pairs={{0,8},{1,9},{2,10},{3,11},{4,12},{5,13},{6,14},{7,15},{8,0},{9,1},... | collective-permute-start | bytes 3096584 | tf_op jit(solution)/shard_map/ppermute | solution.py:404
  118.1 20.4 %copy-start.14 = (bf16[36,112,128]{2,1,0:T(8,128)(2,1)}, bf16[36,112,128]{2,1,0:T(8,128)(2,1)S(1)}, u32[]{:S(2)}) copy-start(bf16[36,112,128]{2,1,0:T(8,128)(2,1)S(1)} %collective-permute-done.12.refs_13_) | copy-start | bytes 3096580
  119.6 19.0 %copy-start.15 = (bf16[36,112,128]{2,1,0:T(8,128)(2,1)}, bf16[36,112,128]{2,1,0:T(8,128)(2,1)S(1)}, u32[]{:S(2)}) copy-start(bf16[36,112,128]{2,1,0:T(8,128)(2,1)S(1)} %collective-permute-done.13.refs_11_) | copy-start | bytes 3096580
  121.1 17.5 %copy-start.16 = (bf16[36,112,128]{2,1,0:T(8,128)(2,1)}, bf16[36,112,128]{2,1,0:T(8,128)(2,1)S(1)}, u32[]{:S(2)}) copy-start(bf16[36,112,128]{2,1,0:T(8,128)(2,1)S(1)} %collective-permute-done.14.refs_3_) | copy-start | bytes 3096580
  138.6 1.0 copy-start.17
  139.6 3.0 %collective-permute-start.15 = (bf16[36,112,128]{2,1,0:T(8,128)(2,1)}, bf16[36,112,128]{2,1,0:T(8,128)(2,1)}, u32[]{:S(2)}, u32[]{:S(2)}) collective-permute-start(bf16[36,112,128]{2,1,0:T(8,128)(2,1)} %collective-permute-done.8.refs_14_), channel_id=1, source_target_pairs={{0,8},{1,9},{2,10},{3,11},{4,12},{5,13},{6,14},{7,15},{8,0},{9,1},... | collective-permute-start | bytes 3096584 | tf_op jit(solution)/shard_map/ppermute | solution.py:404

commit v12 on v11

--- a/solution.py
+++ b/solution.py
@@ -314,13 +314,16 @@
 
             Fetch(at, slot).wait()
             width = QUAD * p.ij
-            for n in range(group):
-                total[...] += lax.dot_general(
+            terms = [
+                lax.dot_general(
                     tiles[step * group + n].reshape(p.gf * ROWS, p.d),
                     held[slot, n * width : (n + 1) * width],
                     NT,
                     preferred_element_type=jnp.float32,
                 )
+                for n in range(group)
+            ]
+            total[...] += functools.reduce(jnp.add, terms)
 
     width = QUAD * p.ij
     row = lax.broadcasted_iota(jnp.int32, (p.gf * ROWS, width), 0) % ROWS // BLK

time: 231 us -> 231 us (level)
  no operation moved by 1% of the time
where the time goes in v12:
time: 231 us
  Pallas kernels  122 us (53%)
  waiting for transfers between devices  66.9 us (29%)
  starting transfers between devices  15.6 us (7%)
  local copies, waits for them, and re-layouts  14.5 us (6%)
  blocking collectives  10.9 us (5%)
    pallas_call x1, Pallas kernels, ladder(): pl.pallas_call(functools.partial(ladder_kernel, p, units, parts, group),...  73.8 us
    ppermute x16, waiting for transfers between devices, permute(): return lax.ppermute(array, ('aux', 'pair'), pairs)  66.9 us
    pallas_call x4, Pallas kernels, dress(): pl.pallas_call(functools.partial(dress_kernel, p, offset, bounds), out_sh...  29.2 us
    pallas_call x2, Pallas kernels, relayout(): pl.pallas_call(functools.partial(relayout_kernel, p), out_shape=jax.Shape...  18.1 us
    ppermute x16, starting transfers between devices, permute(): return lax.ppermute(array, ('aux', 'pair'), pairs)  15.6 us
    unnamed x40, local copies, waits for them, and re-layouts  12 us
    all_to_all x1, blocking collectives, shards(): lax.all_to_all(terms, ('aux', 'pair'), split_axis=0, concat_axis=0, tiled...  10.9 us
  transfers between devices with their start and end apart: 16, of which 10 were waited for; matrix products, arithmetic and copies ran while one was open for 0% of the time, Pallas kernels for 17%

profile of v12, /device:TPU:0, one launch (start us, length us, event | category | flops | bytes accessed | tf_op | source)
XLA Modules:
  0.0 230.8 jit_solution(17260592368573855017)
XLA Ops:
  0.0 0.8 copy.11.t1_ref
  0.8 0.8 spread.1.a_ref
  1.6 0.1 pad_add_fusion.z_ref.place_ref
  1.7 7.3 %dress.4 = bf16[36,112,128]{2,1,0:T(8,128)(2,1)S(1)} custom-call(s32[3]{0:T(128)S(1)} %pad_add_fusion.z_ref.place_ref, bf16[512,1600]{1,0:T(8,128)(2,1)S(1)} %spread.1.a_ref, bf16[100,112,576]{2,1,0:T(8,128)(2,1)} %refs_1_.7, bf16[100,112,576]{2,1,0:T(8,128)(2,1)} %refs_1_.7, bf16[32,112,576]{2,1,0:T(8,128)(2,1)} %refs_3_.7, bf16[32,112,576]{2,1,0:T(8,128)(2,1)} %refs_3_.7), custom_call_target="tpu_custom_call" | custom-call | flops 2936012800 | bytes 9404416 | tf_op jit(solution)/shard_map/dress/pallas_call | solution.py:134
  9.0 3.1 %collective-permute-start = (bf16[36,112,128]{2,1,0:T(8,128)(2,1)S(1)}, bf16[36,112,128]{2,1,0:T(8,128)(2,1)S(1)}, u32[]{:S(2)}, u32[]{:S(2)}) collective-permute-start(bf16[36,112,128]{2,1,0:T(8,128)(2,1)S(1)} %dress.4), channel_id=1, source_target_pairs={{0,2},{1,10},{2,4},{3,12},{4,6},{5,14},{6,0},{7,8},{8,3},{9,11},{1... | collective-permute-start | bytes 3096584 | tf_op jit(solution)/shard_map/ppermute | solution.py:407
  12.1 7.3 %dress.5 = bf16[36,112,128]{2,1,0:T(8,128)(2,1)S(1)} custom-call(s32[3]{0:T(128)S(1)} %pad_add_fusion.z_ref.place_ref, bf16[512,1600]{1,0:T(8,128)(2,1)S(1)} %spread.1.a_ref, bf16[100,112,576]{2,1,0:T(8,128)(2,1)} %refs_1_.7, bf16[100,112,576]{2,1,0:T(8,128)(2,1)} %refs_1_.7, bf16[32,112,576]{2,1,0:T(8,128)(2,1)} %refs_3_.7, bf16[32,112,576]{2,1,0:T(8,128)(2,1)} %refs_3_.7), custom_call_target="tpu_custom_call" | custom-call | flops 2936012800 | bytes 9404416 | tf_op jit(solution)/shard_map/dress/pallas_call | solution.py:134
  19.3 7.4 %dress.6 = bf16[36,112,128]{2,1,0:T(8,128)(2,1)S(1)} custom-call(s32[3]{0:T(128)S(1)} %pad_add_fusion.z_ref.place_ref, bf16[512,1600]{1,0:T(8,128)(2,1)S(1)} %spread.1.a_ref, bf16[100,112,576]{2,1,0:T(8,128)(2,1)} %refs_1_.7, bf16[100,112,576]{2,1,0:T(8,128)(2,1)} %refs_1_.7, bf16[32,112,576]{2,1,0:T(8,128)(2,1)} %refs_3_.7, bf16[32,112,576]{2,1,0:T(8,128)(2,1)} %refs_3_.7), custom_call_target="tpu_custom_call" | custom-call | flops 2936012800 | bytes 9404416 | tf_op jit(solution)/shard_map/dress/pallas_call | solution.py:134
  26.8 10.7 %collective-permute-done.refs_4_ = bf16[36,112,128]{2,1,0:T(8,128)(2,1)S(1)} collective-permute-done((bf16[36,112,128]{2,1,0:T(8,128)(2,1)S(1)}, bf16[36,112,128]{2,1,0:T(8,128)(2,1)S(1)}, u32[]{:S(2)}, u32[]{:S(2)}) %collective-permute-start) | collective-permute-done | bytes 1032224 | tf_op jit(solution)/shard_map/ppermute | solution.py:407
  37.4 2.1 collective-permute-start.1
  39.6 0.9 collective-permute-start.2
  40.5 1.6 collective-permute-start.3
  42.0 2.2 collective-permute-start.4
  44.3 7.3 %dress.7 = bf16[36,112,128]{2,1,0:T(8,128)(2,1)S(1)} custom-call(s32[3]{0:T(128)S(1)} %pad_add_fusion.z_ref.place_ref, bf16[512,1600]{1,0:T(8,128)(2,1)S(1)} %spread.1.a_ref, bf16[100,112,576]{2,1,0:T(8,128)(2,1)} %refs_1_.7, bf16[100,112,576]{2,1,0:T(8,128)(2,1)} %refs_1_.7, bf16[32,112,576]{2,1,0:T(8,128)(2,1)} %refs_3_.7, bf16[32,112,576]{2,1,0:T(8,128)(2,1)} %refs_3_.7), custom_call_target="tpu_custom_call" | custom-call | flops 2936012800 | bytes 9404416 | tf_op jit(solution)/shard_map/dress/pallas_call | solution.py:134
  51.6 10.9 %collective-permute-done.1.refs_8_ = bf16[36,112,128]{2,1,0:T(8,128)(2,1)S(1)} collective-permute-done((bf16[36,112,128]{2,1,0:T(8,128)(2,1)S(1)}, bf16[36,112,128]{2,1,0:T(8,128)(2,1)S(1)}, u32[]{:S(2)}, u32[]{:S(2)}) %collective-permute-start.1) | collective-permute-done | bytes 1032224 | tf_op jit(solution)/shard_map/ppermute | solution.py:407
  62.4 2.2 collective-permute-done.3.refs_6_
  64.6 0.1 collective-permute-start.5
  64.7 1.6 collective-permute-start.6
  66.3 0.8 collective-permute-start.7
  67.1 9.0 %relayout.2 = bf16[112,64,896]{2,1,0:T(8,128)(2,1)S(1)} custom-call(bf16[64,224,896]{2,1,0:T(8,128)(2,1)} %in_ref.1), custom_call_target="tpu_custom_call" | custom-call | flops 3288334336 | bytes 25690112 | tf_op jit(solution)/shard_map/relayout/pallas_call | solution.py:174
  76.2 4.6 %copy-done = bf16[112,64,896]{2,1,0:T(8,128)(2,1)} copy-done((bf16[112,64,896]{2,1,0:T(8,128)(2,1)}, bf16[112,64,896]{2,1,0:T(8,128)(2,1)S(1)}, u32[]{:S(2)}) %copy-start) | copy-done | bytes 12845080
  80.8 9.0 %relayout.3 = bf16[112,64,896]{2,1,0:T(8,128)(2,1)S(1)} custom-call(bf16[64,224,896]{2,1,0:T(8,128)(2,1)} %in_ref.1), custom_call_target="tpu_custom_call" | custom-call | flops 3288334336 | bytes 25690112 | tf_op jit(solution)/shard_map/relayout/pallas_call | solution.py:174
  89.8 4.6 %copy-done.1 = bf16[112,64,896]{2,1,0:T(8,128)(2,1)} copy-done((bf16[112,64,896]{2,1,0:T(8,128)(2,1)}, bf16[112,64,896]{2,1,0:T(8,128)(2,1)S(1)}, u32[]{:S(2)}) %copy-start.1) | copy-done | bytes 12845080
  94.4 18.0 %collective-permute-done.5.refs_12_ = bf16[36,112,128]{2,1,0:T(8,128)(2,1)S(1)} collective-permute-done((bf16[36,112,128]{2,1,0:T(8,128)(2,1)S(1)}, bf16[36,112,128]{2,1,0:T(8,128)(2,1)S(1)}, u32[]{:S(2)}, u32[]{:S(2)}) %collective-permute-start.5) | collective-permute-done | bytes 1032224 | tf_op jit(solution)/shard_map/ppermute | solution.py:407
  112.5 0.1 collective-permute-start.10
  112.6 0.5 collective-permute-start.11
  113.1 0.1 collective-permute-start.12
  113.1 1.9 collective-permute-start.8
  115.1 0.2 collective-permute-start.13
  115.2 0.4 collective-permute-start.14
  115.6 1.1 collective-permute-done.11.refs_7_
  116.7 0.1 collective-permute-start.9
  116.8 1.3 collective-permute-done.12.refs_13_
  118.1 1.5 collective-permute-done.13.refs_11_
  119.6 1.5 collective-permute-done.14.refs_3_
  121.1 17.5 %collective-permute-done.8.refs_14_ = bf16[36,112,128]{2,1,0:T(8,128)(2,1)} collective-permute-done((bf16[36,112,128]{2,1,0:T(8,128)(2,1)S(1)}, bf16[36,112,128]{2,1,0:T(8,128)(2,1)}, u32[]{:S(2)}, u32[]{:S(2)}) %collective-permute-start.8) | collective-permute-done | bytes 1032224 | tf_op jit(solution)/shard_map/ppermute | solution.py:407
  138.6 1.0 copy-done.17
  139.6 0.7 copy.12.blocks_ref
  140.2 2.3 collective-permute-done.15.refs_15_
  142.6 73.8 %ladder.1 = f32[32,4,128]{2,1,0:T(4,128)} custom-call(s32[3]{0:T(128)} %copy-done.2, s32[8,2]{1,0:T(8,128)} %copy.12.blocks_ref, bf16[36,112,128]{2,1,0:T(8,128)(2,1)} %copy-done.6, bf16[36,112,128]{2,1,0:T(8,128)(2,1)} %copy-done.12, bf16[36,112,128]{2,1,0:T(8,128)(2,1)} %copy-done.11, bf16[36,112,128]{2,1,0:T(8,128)(2,1)} %copy-done.16, ...), custom_call_target="tpu_custom_call" | custom-call | flops 13153337344 | bytes 42205184 | tf_op jit(solution)/shard_map/ladder/pallas_call | solution.py:351
  216.3 1.0 reshape.14
  217.3 0.2 copy.13
  217.5 0.2 copy.19
  217.7 0.1 reshape.16
  217.8 10.9 %all_to_all.5 = f32[32,1,256]{2,1,0:T(1,128)S(1)} all-to-all(f32[32,1,256]{2,1,0:T(1,128)S(1)} %reshape.16), channel_id=1, replica_groups=mesh['aux'=4,'pair'=8] {'aux','pair'}, dimensions={0} | all-to-all | bytes 65536 | tf_op jit(solution)/shard_map/all_to_all | solution.py:478
  228.7 0.5 broadcast.2
  229.2 0.7 reduce
  230.0 0.1 reshape.17
  230.1 0.7 copy.16
  (41 shorter events, 0.1 us)
Async XLA Ops:
  1.7 42.6 %copy-start.2 = (s32[3]{0:T(128)}, s32[3]{0:T(128)S(1)}, u32[]{:S(2)}) copy-start(s32[3]{0:T(128)S(1)} %pad_add_fusion.z_ref.place_ref) | copy-start | bytes 40
  9.0 28.5 %collective-permute-start = (bf16[36,112,128]{2,1,0:T(8,128)(2,1)S(1)}, bf16[36,112,128]{2,1,0:T(8,128)(2,1)S(1)}, u32[]{:S(2)}, u32[]{:S(2)}) collective-permute-start(bf16[36,112,128]{2,1,0:T(8,128)(2,1)S(1)} %dress.4), channel_id=1, source_target_pairs={{0,2},{1,10},{2,4},{3,12},{4,6},{5,14},{6,0},{7,8},{8,3},{9,11},{1... | collective-permute-start | bytes 3096584 | tf_op jit(solution)/shard_map/ppermute | solution.py:407
  37.4 14.1 %copy-start.4 = (bf16[36,112,128]{2,1,0:T(8,128)(2,1)}, bf16[36,112,128]{2,1,0:T(8,128)(2,1)S(1)}, u32[]{:S(2)}) copy-start(bf16[36,112,128]{2,1,0:T(8,128)(2,1)S(1)} %collective-permute-done.refs_4_) | copy-start | bytes 3096580
  37.4 25.0 %collective-permute-start.1 = (bf16[36,112,128]{2,1,0:T(8,128)(2,1)S(1)}, bf16[36,112,128]{2,1,0:T(8,128)(2,1)S(1)}, u32[]{:S(2)}, u32[]{:S(2)}) collective-permute-start(bf16[36,112,128]{2,1,0:T(8,128)(2,1)S(1)} %dress.5), channel_id=1, source_target_pairs={{0,6},{1,14},{2,0},{3,8},{4,2},{5,10},{6,4},{7,12},{8,7},{9,15},{1... | collective-permute-start | bytes 3096584 | tf_op jit(solution)/shard_map/ppermute | solution.py:407
  39.6 22.9 %collective-permute-start.2 = (bf16[36,112,128]{2,1,0:T(8,128)(2,1)S(1)}, bf16[36,112,128]{2,1,0:T(8,128)(2,1)S(1)}, u32[]{:S(2)}, u32[]{:S(2)}) collective-permute-start(bf16[36,112,128]{2,1,0:T(8,128)(2,1)S(1)} %dress.6), channel_id=1, source_target_pairs={{0,0},{1,8},{2,2},{3,10},{4,4},{5,12},{6,6},{7,14},{8,1},{9,9},{10... | collective-permute-start | bytes 3096584 | tf_op jit(solution)/shard_map/ppermute | solution.py:407
  40.5 24.1 %collective-permute-start.3 = (bf16[36,112,128]{2,1,0:T(8,128)(2,1)S(1)}, bf16[36,112,128]{2,1,0:T(8,128)(2,1)S(1)}, u32[]{:S(2)}, u32[]{:S(2)}) collective-permute-start(bf16[36,112,128]{2,1,0:T(8,128)(2,1)S(1)} %collective-permute-done.refs_4_), channel_id=1, source_target_pairs={{0,16},{1,17},{2,18},{3,19},{4,20},{5,21},{6,22},{7,23},{8,24},{9,... | collective-permute-start | bytes 3096584 | tf_op jit(solution)/shard_map/ppermute | solution.py:407
  42.0 22.6 %collective-permute-start.4 = (bf16[36,112,128]{2,1,0:T(8,128)(2,1)S(1)}, bf16[36,112,128]{2,1,0:T(8,128)(2,1)S(1)}, u32[]{:S(2)}, u32[]{:S(2)}) collective-permute-start(bf16[36,112,128]{2,1,0:T(8,128)(2,1)S(1)} %collective-permute-done.refs_4_), channel_id=1, source_target_pairs={{0,8},{1,9},{2,10},{3,11},{4,12},{5,13},{6,14},{7,15},{8,0},{9,1},... | collective-permute-start | bytes 3096584 | tf_op jit(solution)/shard_map/ppermute | solution.py:407
  62.4 54.2 %copy-start.5 = (bf16[36,112,128]{2,1,0:T(8,128)(2,1)}, bf16[36,112,128]{2,1,0:T(8,128)(2,1)S(1)}, u32[]{:S(2)}) copy-start(bf16[36,112,128]{2,1,0:T(8,128)(2,1)S(1)} %collective-permute-done.1.refs_8_) | copy-start | bytes 3096580
  62.4 50.0 %copy-start.6 = (bf16[36,112,128]{2,1,0:T(8,128)(2,1)}, bf16[36,112,128]{2,1,0:T(8,128)(2,1)S(1)}, u32[]{:S(2)}) copy-start(bf16[36,112,128]{2,1,0:T(8,128)(2,1)S(1)} %collective-permute-done.2.refs_0_) | copy-start | bytes 3096580
  64.6 47.9 %copy-start.7 = (bf16[36,112,128]{2,1,0:T(8,128)(2,1)}, bf16[36,112,128]{2,1,0:T(8,128)(2,1)S(1)}, u32[]{:S(2)}) copy-start(bf16[36,112,128]{2,1,0:T(8,128)(2,1)S(1)} %collective-permute-done.3.refs_6_) | copy-start | bytes 3096580
  64.6 1.6 copy-start.8
  64.6 47.8 %collective-permute-start.5 = (bf16[36,112,128]{2,1,0:T(8,128)(2,1)S(1)}, bf16[36,112,128]{2,1,0:T(8,128)(2,1)S(1)}, u32[]{:S(2)}, u32[]{:S(2)}) collective-permute-start(bf16[36,112,128]{2,1,0:T(8,128)(2,1)S(1)} %dress.7), channel_id=1, source_target_pairs={{0,4},{1,12},{2,6},{3,14},{4,0},{5,8},{6,2},{7,10},{8,5},{9,13},{1... | collective-permute-start | bytes 3096584 | tf_op jit(solution)/shard_map/ppermute | solution.py:407
  64.7 47.7 %collective-permute-start.6 = (bf16[36,112,128]{2,1,0:T(8,128)(2,1)S(1)}, bf16[36,112,128]{2,1,0:T(8,128)(2,1)S(1)}, u32[]{:S(2)}, u32[]{:S(2)}) collective-permute-start(bf16[36,112,128]{2,1,0:T(8,128)(2,1)S(1)} %collective-permute-done.1.refs_8_), channel_id=1, source_target_pairs={{0,16},{1,17},{2,18},{3,19},{4,20},{5,21},{6,22},{7,23},{8,24},{9,... | collective-permute-start | bytes 3096584 | tf_op jit(solution)/shard_map/ppermute | solution.py:407
  66.3 46.2 %collective-permute-start.7 = (bf16[36,112,128]{2,1,0:T(8,128)(2,1)S(1)}, bf16[36,112,128]{2,1,0:T(8,128)(2,1)S(1)}, u32[]{:S(2)}, u32[]{:S(2)}) collective-permute-start(bf16[36,112,128]{2,1,0:T(8,128)(2,1)S(1)} %collective-permute-done.2.refs_0_), channel_id=1, source_target_pairs={{0,16},{1,17},{2,18},{3,19},{4,20},{5,21},{6,22},{7,23},{8,24},{9,... | collective-permute-start | bytes 3096584 | tf_op jit(solution)/shard_map/ppermute | solution.py:407
  76.2 4.6 %copy-start = (bf16[112,64,896]{2,1,0:T(8,128)(2,1)}, bf16[112,64,896]{2,1,0:T(8,128)(2,1)S(1)}, u32[]{:S(2)}) copy-start(bf16[112,64,896]{2,1,0:T(8,128)(2,1)S(1)} %relayout.2) | copy-start | bytes 38535172
  80.8 58.8 %copy-start.3 = (s32[8,2]{0,1:T(2,128)S(1)}, s32[8,2]{0,1:T(2,128)}, u32[]{:S(2)}) copy-start(s32[8,2]{0,1:T(2,128)} %param.9) | copy-start | bytes 196
  89.8 4.6 %copy-start.1 = (bf16[112,64,896]{2,1,0:T(8,128)(2,1)}, bf16[112,64,896]{2,1,0:T(8,128)(2,1)S(1)}, u32[]{:S(2)}) copy-start(bf16[112,64,896]{2,1,0:T(8,128)(2,1)S(1)} %relayout.3) | copy-start | bytes 38535172
  112.4 30.1 %copy-start.9 = (bf16[36,112,128]{2,1,0:T(8,128)(2,1)}, bf16[36,112,128]{2,1,0:T(8,128)(2,1)S(1)}, u32[]{:S(2)}) copy-start(bf16[36,112,128]{2,1,0:T(8,128)(2,1)S(1)} %collective-permute-done.5.refs_12_) | copy-start | bytes 3096580
  112.5 30.1 %copy-start.10 = (bf16[36,112,128]{2,1,0:T(8,128)(2,1)}, bf16[36,112,128]{2,1,0:T(8,128)(2,1)S(1)}, u32[]{:S(2)}) copy-start(bf16[36,112,128]{2,1,0:T(8,128)(2,1)S(1)} %collective-permute-done.6.refs_10_) | copy-start | bytes 3096580
  112.5 30.1 %copy-start.11 = (bf16[36,112,128]{2,1,0:T(8,128)(2,1)}, bf16[36,112,128]{2,1,0:T(8,128)(2,1)S(1)}, u32[]{:S(2)}) copy-start(bf16[36,112,128]{2,1,0:T(8,128)(2,1)S(1)} %collective-permute-done.7.refs_2_) | copy-start | bytes 3096580
  112.5 2.7 %collective-permute-start.10 = (bf16[36,112,128]{2,1,0:T(8,128)(2,1)S(1)}, bf16[36,112,128]{2,1,0:T(8,128)(2,1)S(1)}, u32[]{:S(2)}, u32[]{:S(2)}) collective-permute-start(bf16[36,112,128]{2,1,0:T(8,128)(2,1)S(1)} %collective-permute-done.2.refs_0_), channel_id=1, source_target_pairs={{0,8},{1,9},{2,10},{3,11},{4,12},{5,13},{6,14},{7,15},{8,0},{9,1},... | collective-permute-start | bytes 3096584 | tf_op jit(solution)/shard_map/ppermute | solution.py:407
  112.6 4.1 %collective-permute-start.11 = (bf16[36,112,128]{2,1,0:T(8,128)(2,1)S(1)}, bf16[36,112,128]{2,1,0:T(8,128)(2,1)S(1)}, u32[]{:S(2)}, u32[]{:S(2)}) collective-permute-start(bf16[36,112,128]{2,1,0:T(8,128)(2,1)S(1)} %collective-permute-done.3.refs_6_), channel_id=1, source_target_pairs={{0,8},{1,9},{2,10},{3,11},{4,12},{5,13},{6,14},{7,15},{8,0},{9,1},... | collective-permute-start | bytes 3096584 | tf_op jit(solution)/shard_map/ppermute | solution.py:407
  113.1 5.1 %collective-permute-start.12 = (bf16[36,112,128]{2,1,0:T(8,128)(2,1)S(1)}, bf16[36,112,128]{2,1,0:T(8,128)(2,1)S(1)}, u32[]{:S(2)}, u32[]{:S(2)}) collective-permute-start(bf16[36,112,128]{2,1,0:T(8,128)(2,1)S(1)} %collective-permute-done.5.refs_12_), channel_id=1, source_target_pairs={{0,8},{1,9},{2,10},{3,11},{4,12},{5,13},{6,14},{7,15},{8,0},{9,1},... | collective-permute-start | bytes 3096584 | tf_op jit(solution)/shard_map/ppermute | solution.py:407
  113.1 25.4 %collective-permute-start.8 = (bf16[36,112,128]{2,1,0:T(8,128)(2,1)S(1)}, bf16[36,112,128]{2,1,0:T(8,128)(2,1)}, u32[]{:S(2)}, u32[]{:S(2)}) collective-permute-start(bf16[36,112,128]{2,1,0:T(8,128)(2,1)S(1)} %collective-permute-done.5.refs_12_), channel_id=1, source_target_pairs={{0,16},{1,17},{2,18},{3,19},{4,20},{5,21},{6,22},{7,23},{8,24},{9,... | collective-permute-start | bytes 3096584 | tf_op jit(solution)/shard_map/ppermute | solution.py:407
  115.1 4.6 %collective-permute-start.13 = (bf16[36,112,128]{2,1,0:T(8,128)(2,1)S(1)}, bf16[36,112,128]{2,1,0:T(8,128)(2,1)S(1)}, u32[]{:S(2)}, u32[]{:S(2)}) collective-permute-start(bf16[36,112,128]{2,1,0:T(8,128)(2,1)S(1)} %collective-permute-done.6.refs_10_), channel_id=1, source_target_pairs={{0,8},{1,9},{2,10},{3,11},{4,12},{5,13},{6,14},{7,15},{8,0},{9,1},... | collective-permute-start | bytes 3096584 | tf_op jit(solution)/shard_map/ppermute | solution.py:407
  115.2 23.3 %copy-start.12 = (bf16[36,112,128]{2,1,0:T(8,128)(2,1)}, bf16[36,112,128]{2,1,0:T(8,128)(2,1)S(1)}, u32[]{:S(2)}) copy-start(bf16[36,112,128]{2,1,0:T(8,128)(2,1)S(1)} %collective-permute-done.10.refs_1_) | copy-start | bytes 3096580
  115.2 5.9 %collective-permute-start.14 = (bf16[36,112,128]{2,1,0:T(8,128)(2,1)S(1)}, bf16[36,112,128]{2,1,0:T(8,128)(2,1)S(1)}, u32[]{:S(2)}, u32[]{:S(2)}) collective-permute-start(bf16[36,112,128]{2,1,0:T(8,128)(2,1)S(1)} %collective-permute-done.7.refs_2_), channel_id=1, source_target_pairs={{0,8},{1,9},{2,10},{3,11},{4,12},{5,13},{6,14},{7,15},{8,0},{9,1},... | collective-permute-start | bytes 3096584 | tf_op jit(solution)/shard_map/ppermute | solution.py:407
  116.7 21.9 %copy-start.13 = (bf16[36,112,128]{2,1,0:T(8,128)(2,1)}, bf16[36,112,128]{2,1,0:T(8,128)(2,1)S(1)}, u32[]{:S(2)}) copy-start(bf16[36,112,128]{2,1,0:T(8,128)(2,1)S(1)} %collective-permute-done.11.refs_7_) | copy-start | bytes 3096580
  116.7 21.9 %collective-permute-start.9 = (bf16[36,112,128]{2,1,0:T(8,128)(2,1)S(1)}, bf16[36,112,128]{2,1,0:T(8,128)(2,1)S(1)}, u32[]{:S(2)}, u32[]{:S(2)}) collective-permute-start(bf16[36,112,128]{2,1,0:T(8,128)(2,1)S(1)} %collective-permute-done.1.refs_8_), channel_id=1, source_target_pairs={{0,8},{1,9},{2,10},{3,11},{4,12},{5,13},{6,14},{7,15},{8,0},{9,1},... | collective-permute-start | bytes 3096584 | tf_op jit(solution)/shard_map/ppermute | solution.py:407
  118.1 20.4 %copy-start.14 = (bf16[36,112,128]{2,1,0:T(8,128)(2,1)}, bf16[36,112,128]{2,1,0:T(8,128)(2,1)S(1)}, u32[]{:S(2)}) copy-start(bf16[36,112,128]{2,1,0:T(8,128)(2,1)S(1)} %collective-permute-done.12.refs_13_) | copy-start | bytes 3096580
  119.6 19.0 %copy-start.15 = (bf16[36,112,128]{2,1,0:T(8,128)(2,1)}, bf16[36,112,128]{2,1,0:T(8,128)(2,1)S(1)}, u32[]{:S(2)}) copy-start(bf16[36,112,128]{2,1,0:T(8,128)(2,1)S(1)} %collective-permute-done.13.refs_11_) | copy-start | bytes 3096580
  121.1 17.5 %copy-start.16 = (bf16[36,112,128]{2,1,0:T(8,128)(2,1)}, bf16[36,112,128]{2,1,0:T(8,128)(2,1)S(1)}, u32[]{:S(2)}) copy-start(bf16[36,112,128]{2,1,0:T(8,128)(2,1)S(1)} %collective-permute-done.14.refs_3_) | copy-start | bytes 3096580
  138.6 1.0 copy-start.17
  139.6 3.0 %collective-permute-start.15 = (bf16[36,112,128]{2,1,0:T(8,128)(2,1)}, bf16[36,112,128]{2,1,0:T(8,128)(2,1)}, u32[]{:S(2)}, u32[]{:S(2)}) collective-permute-start(bf16[36,112,128]{2,1,0:T(8,128)(2,1)} %collective-permute-done.8.refs_14_), channel_id=1, source_target_pairs={{0,8},{1,9},{2,10},{3,11},{4,12},{5,13},{6,14},{7,15},{8,0},{9,1},... | collective-permute-start | bytes 3096584 | tf_op jit(solution)/shard_map/ppermute | solution.py:407
